TPU v7x, 256 devices: a whole 4x4x8 slice. The times are simulated.
256 devices in a mesh: dp: 32 (over y_hi, z, core), pipe: 2 (over y_lo), mp: 4 (over x).
Axes of the slice: x: 4, y: 4 (y_hi: 2, y_lo: 2; y = y_hi * 2 + y_lo), z: 8, core: 2. Of those that a mesh axis runs over, the one named last changes fastest.
Arguments:
- streams: bfloat16 [2, 64, 128, 2048], P('pipe', 'dp', None, 'mp'), may hold values from -14 to 14
- lengths: int32 [64], P('dp'), may hold values from 32 to 128, as said below
- encoder_gain: bfloat16 [2048], replicated, may hold values from 0.25 to 1.75
- ffn_gate: bfloat16 [2048, 8192], P('dp', 'mp'), may hold values from -0.125 to 0.125
- ffn_lift: bfloat16 [2048, 8192], P('dp', 'mp'), may hold values from -0.125 to 0.125
- ffn_down: bfloat16 [8192, 2048], P('mp', 'dp'), may hold values from -0.0625 to 0.0625
- final_gain: bfloat16 [2048], P('mp'), may hold values from 0.25 to 1.75
- decoder_gain: bfloat16 [2048], replicated, may hold values from 0.25 to 1.75
- query_weight: bfloat16 [2048, 2048], P(None, 'mp'), may hold values from -0.15191747 to 0.15191747
- key_weight: bfloat16 [2048, 2048], P(None, 'mp'), may hold values from -0.125 to 0.125
- value_weight: bfloat16 [2048, 2048], P(None, 'mp'), may hold values from -0.125 to 0.125
- output_weight: bfloat16 [2048, 2048], P('mp'), may hold values from -0.125 to 0.125
Outputs:
- sections: bfloat16 [2, 64, 128, 2048], P('pipe', 'dp', None, 'mp')
Inputs may be any that keep to these rules, and one draw needn't show every extreme that they name: `lengths`: every draw holds an example with 128 unpadded tokens and one with a quarter of 128.
All inputs are finite; a program needn't handle non-finite values.
Results may differ from a plain program's by a relative error of at most 0.024.
The roundings to bfloat16 on the way count: a program that leaves them out, or rounds other values in their place, can miss the bound.
Values may be sent and summed in bfloat16 or wider, within the bound.
No kernel may reach another device: no remote copies, remote signals or barrier semaphores. Data moves between devices by JAX's collectives and lax.ppermute only.
A program may use at most 128 MiB of HBM per device.

v0:
```python
import jax
import jax.numpy as jnp
from jax import lax
from jax.sharding import PartitionSpec as P

HEAD_DIM = 256


epsilon = 1e-06


def from_behind(value, axis, by):
    count = lax.axis_size(axis)
    pairs = [(i, i + by) for i in range(count) if 0 <= i + by < count]
    return lax.ppermute(value, axis, pairs)


def scale_rows(values, gain):
    mean_square = jnp.mean(values * values, axis=-1, keepdims=True)
    return values * lax.rsqrt(mean_square + epsilon) * gain.astype(jnp.float32)


def shards(
    streams,
    lengths,
    encoder_gain,
    ffn_gate,
    ffn_lift,
    ffn_down,
    final_gain,
    decoder_gain,
    query_weight,
    key_weight,
    value_weight,
    output_weight,
):
    segment = lax.axis_index("pipe")
    local = streams[0]
    micro, length, narrow = local.shape
    column = lax.axis_index("mp") * narrow
    tokens_all = local.reshape(micro * length, narrow)
    full = lax.all_gather(tokens_all, "mp", axis=1, tiled=True)
    normed = scale_rows(full.astype(jnp.float32), encoder_gain).astype(jnp.bfloat16)
    gate = jnp.dot(
        normed,
        lax.all_gather(ffn_gate, "dp", axis=0, tiled=True),
        preferred_element_type=jnp.float32,
    )
    lift = jnp.dot(
        normed,
        lax.all_gather(ffn_lift, "dp", axis=0, tiled=True),
        preferred_element_type=jnp.float32,
    )
    hidden = (jax.nn.gelu(gate, approximate=True) * lift).astype(jnp.bfloat16)
    terms = jnp.dot(
        hidden,
        lax.all_gather(ffn_down, "dp", axis=1, tiled=True),
        preferred_element_type=jnp.float32,
    )
    summed = lax.psum(terms, "mp")
    merged = full.astype(jnp.float32) + summed
    mean_square = jnp.mean(merged * merged, axis=-1, keepdims=True)
    own = lax.dynamic_slice_in_dim(merged, column, narrow, 1)
    memory = (own * lax.rsqrt(mean_square + epsilon) * final_gain.astype(jnp.float32)).astype(
        jnp.bfloat16
    )
    arrived = from_behind(memory, "pipe", 1)
    full = lax.all_gather(tokens_all, "mp", axis=1, tiled=True)
    source = lax.all_gather(arrived, "mp", axis=1, tiled=True)
    query_in = scale_rows(full.astype(jnp.float32), decoder_gain).astype(jnp.bfloat16)
    queries = jnp.dot(query_in, query_weight, preferred_element_type=jnp.float32)
    keys = jnp.dot(source, key_weight, preferred_element_type=jnp.float32)
    values = jnp.dot(source, value_weight, preferred_element_type=jnp.float32)
    blocks = lengths.shape[0]
    heads = queries.shape[1] // HEAD_DIM
    shape4 = (blocks, length, heads, HEAD_DIM)
    queries = queries.astype(jnp.bfloat16).reshape(shape4)
    keys = keys.astype(jnp.bfloat16).reshape(shape4)
    values = values.astype(jnp.bfloat16).reshape(shape4)
    scores = jnp.einsum("eqhd,ekhd->ehqk", queries, keys, preferred_element_type=jnp.float32)
    positions = lax.broadcasted_iota(jnp.int32, (1, 1, 1, length), 3)
    valid = positions < lengths[:, None, None, None]
    scores = jnp.where(valid, scores, -1e30)
    highest = jnp.max(scores, axis=-1, keepdims=True)
    weights = jnp.exp(scores - highest)
    probs = (weights / jnp.sum(weights, axis=-1, keepdims=True)).astype(jnp.bfloat16)
    context = jnp.einsum("ehqk,ekhd->eqhd", probs, values, preferred_element_type=jnp.float32)
    context = context.astype(jnp.bfloat16).reshape(blocks * length, heads * HEAD_DIM)
    terms = jnp.dot(context, output_weight, preferred_element_type=jnp.float32)
    summed = lax.psum(terms, "mp")
    merged = full.astype(jnp.float32) + summed
    decoded = lax.dynamic_slice_in_dim(merged, column, narrow, 1).astype(jnp.bfloat16)
    result = jnp.where(segment == 0, memory, decoded).reshape(1, micro, length, narrow)
    return result


def solution(mesh):
    placed = (
        P("pipe", "dp", None, "mp"),
        P("dp"),
        P(),
        P("dp", "mp"),
        P("dp", "mp"),
        P("mp", "dp"),
        P("mp"),
        P(),
        P(None, "mp"),
        P(None, "mp"),
        P(None, "mp"),
        P("mp", None),
    )
    return jax.shard_map(
        shards, mesh=mesh, in_specs=placed, out_specs=P("pipe", "dp", None, "mp"), check_vma=False
    )
```

profile of v0, /device:TPU:6, one launch (start us, length us, event | category | flops | bytes accessed | tf_op | source)
XLA Modules:
  0.0 546.1 jit_solution(4915814437907135609)
XLA Ops:
  6.5 0.7 all-gather.6.cloned.1.call-update
  7.3 0.0 all-gather.8.cloned.1.call-start
  7.3 0.7 all-gather.8.cloned.1.call-update
  8.0 0.0 all-gather.10.cloned.1.call-start
  8.1 0.7 all-gather.10.cloned.1.call-update
  8.7 0.0 all-gather.12.cloned.1.call-start
  8.8 0.5 all-gather.12.cloned.1.call-update
  9.3 0.0 all-reduce.3.cloned.1.call-start
  9.4 0.7 convert_element_type.49
  10.1 27.6 %all-gather.6.cloned.1.call-done = bf16[256,2048]{1,0:T(8,128)(2,1)} async-done(((bf16[256,512]{1,0:T(8,128)(2,1)}), bf16[256,2048]{1,0:T(8,128)(2,1)}) %all-gather.6.cloned.1.call-update) | async-done | bytes 1048592 | tf_op jit(solution)/shard_map/all_gather | solution.py:42
  37.7 1.5 multiply_reduce_fusion.1
  39.2 0.0 copy-start.1
  39.2 104.0 %all-gather.8.cloned.1.call-done = bf16[2048,2048]{1,0:T(8,128)(2,1)} async-done(((bf16[64,2048]{1,0:T(8,128)(2,1)}), bf16[2048,2048]{1,0:T(8,128)(2,1)}) %all-gather.8.cloned.1.call-update) | async-done | bytes 8388624 | tf_op jit(solution)/shard_map/all_gather | solution.py:46
  143.2 7.5 %fusion.16 = f32[256,2048]{1,0:T(8,128)} fusion(bf16[2048,2048]{1,0:T(8,128)(2,1)} %all-gather.8.cloned.1.call-done, bf16[256,2048]{1,0:T(8,128)(2,1)} %all-gather.6.cloned.1.call-done, f32[2048]{0:T(1024)S(1)} %convert_element_type.49, f32[256]{0:T(256)S(1)} %add_rsqrt_fusion.1), kind=kOutput, calls=%fused_computation.30 | convolution fusion | flops 2149580800 | bytes 11543552 | tf_op jit(solution)/shard_map/dot_general | solution.py:44
  150.7 93.3 %all-gather.10.cloned.1.call-done = bf16[2048,2048]{1,0:T(8,128)(2,1)} async-done(((bf16[64,2048]{1,0:T(8,128)(2,1)}), bf16[2048,2048]{1,0:T(8,128)(2,1)}) %all-gather.10.cloned.1.call-update) | async-done | bytes 8388624 | tf_op jit(solution)/shard_map/all_gather | solution.py:51
  244.0 100.6 %all-gather.12.cloned.1.call-done = bf16[2048,2048]{0,1:T(8,128)(2,1)} async-done(((bf16[2048,64]{0,1:T(8,128)(2,1)}), bf16[2048,2048]{0,1:T(8,128)(2,1)}) %all-gather.12.cloned.1.call-update) | async-done | bytes 8388624 | tf_op jit(solution)/shard_map/all_gather | solution.py:57
  344.6 12.6 %fusion.14 = f32[256,2048]{1,0:T(8,128)} fusion(bf16[2048,2048]{0,1:T(8,128)(2,1)} %all-gather.12.cloned.1.call-done, bf16[2048,2048]{1,0:T(8,128)(2,1)} %all-gather.10.cloned.1.call-done, f32[256,2048]{1,0:T(8,128)} %fusion.16, bf16[256,2048]{1,0:T(8,128)(2,1)S(1)} %copy-done.1, f32[2048]{0:T(1024)S(1)} %convert_element_type.49, f32[256]{0:T(256)S(1)} %add_rsqrt_fusion.1), kind=kOutput, calls=%fused_computation.26 | convolution fusion | flops 4302307328 | bytes 22029312 | tf_op jit(solution)/shard_map/dot_general | solution.py:55
  357.2 0.0 all-reduce.3.cloned.1.call-update
  357.2 0.0 all-gather.14.cloned.1.call-start
  357.3 0.6 copy-done.6
  357.9 57.9 %all-reduce.3.cloned.1.call-done = f32[256,2048]{1,0:T(8,128)} async-done(((f32[256,2048]{1,0:T(8,128)}), f32[256,2048]{1,0:T(8,128)}) %all-reduce.3.cloned.1.call-update) | async-done | bytes 2097168 | tf_op jit(solution)/shard_map/psum | solution.py:60
  415.8 1.9 multiply_reduce_fusion
  417.8 1.3 copy-done.2
  419.1 0.1 multiply_convert_fusion.3
  419.2 3.4 collective-permute-start
  422.6 5.5 %collective-permute-done = bf16[256,512]{1,0:T(8,128)(2,1)S(1)} collective-permute-done((bf16[256,512]{1,0:T(8,128)(2,1)S(1)}, bf16[256,512]{1,0:T(8,128)(2,1)S(1)}, u32[]{:S(2)}, u32[]{:S(2)}) %collective-permute-start) | collective-permute-done | bytes 262176 | tf_op jit(solution)/shard_map/ppermute | solution.py:15
  428.2 0.7 copy-done.3
  428.9 0.0 all-gather.14.cloned.1.call-update
  428.9 0.0 all-reduce.5.cloned.1.call-start
  429.0 0.1 iota_compare_fusion
  429.1 3.1 convolution_convert_fusion.2
  432.1 1.0 reshape.58
  433.1 23.9 %all-gather.14.cloned.1.call-done = bf16[256,2048]{1,0:T(8,128)(2,1)} async-done(((bf16[256,512]{1,0:T(8,128)(2,1)}), bf16[256,2048]{1,0:T(8,128)(2,1)}) %all-gather.14.cloned.1.call-update) | async-done | bytes 1048592 | tf_op jit(solution)/shard_map/all_gather | solution.py:69
  457.0 3.3 convolution_convert_fusion.1
  460.4 1.7 reshape.59
  462.1 1.2 convolution_select_fusion
  463.3 0.0 copy-start.4
  463.3 0.7 copy-done.4
  464.0 0.1 fusion.27
  464.1 3.3 convolution_convert_fusion.3
  467.4 1.0 reshape.57
  468.4 2.0 fusion.10
  470.4 1.1 copy.21
  471.6 2.1 fusion.28
  473.7 0.0 all-reduce.5.cloned.1.call-update
  473.7 1.6 convert_element_type.48
  475.3 61.8 %all-reduce.5.cloned.1.call-done = f32[256,2048]{1,0:T(8,128)} async-done(((f32[256,2048]{1,0:T(8,128)}), f32[256,2048]{1,0:T(8,128)}) %all-reduce.5.cloned.1.call-update) | async-done | bytes 2097168 | tf_op jit(solution)/shard_map/psum | solution.py:90
  537.1 2.2 fusion.17
  (16 shorter events, 0.1 us)
Async XLA Ops:
  6.5 465.1 %copy-start = (bf16[512,2048]{1,0:T(8,128)(2,1)S(1)}, bf16[512,2048]{1,0:T(8,128)(2,1)}, u32[]{:S(2)}) copy-start(bf16[512,2048]{1,0:T(8,128)(2,1)} %param.23) | copy-start | bytes 6291460
  6.5 31.2 %all-gather.6.cloned.1.call-start = ((), (), s32[]{:S(2)}) async-start(), calls=%async_computation | async-start | bytes 1310720 | tf_op jit(solution)/shard_map/all_gather | solution.py:42
  7.3 136.0 %all-gather.8.cloned.1.call-start = ((), (), s32[]{:S(2)}) async-start(), calls=%async_computation.1 | async-start | bytes 8650752 | tf_op jit(solution)/shard_map/all_gather | solution.py:46
  8.0 235.9 %all-gather.10.cloned.1.call-start = ((), (), s32[]{:S(2)}) async-start(), calls=%async_computation.2 | async-start | bytes 8650752 | tf_op jit(solution)/shard_map/all_gather | solution.py:51
  8.7 335.8 %all-gather.12.cloned.1.call-start = ((), (), s32[]{:S(2)}) async-start(), calls=%async_computation.3 | async-start | bytes 8650752 | tf_op jit(solution)/shard_map/all_gather | solution.py:57
  9.3 406.5 %all-reduce.3.cloned.1.call-start = ((), (), s32[]{:S(2)}) async-start(), calls=%async_computation.4 | async-start | bytes 4194304 | tf_op jit(solution)/shard_map/psum | solution.py:60
  39.2 305.3 %copy-start.1 = (bf16[256,2048]{1,0:T(8,128)(2,1)S(1)}, bf16[256,2048]{1,0:T(8,128)(2,1)}, u32[]{:S(2)}) copy-start(bf16[256,2048]{1,0:T(8,128)(2,1)} %all-gather.6.cloned.1.call-done) | copy-start | bytes 3145732
  357.2 0.7 copy-start.6
  357.2 99.8 %all-gather.14.cloned.1.call-start = ((), (), s32[]{:S(2)}) async-start(), calls=%async_computation.5 | async-start | bytes 1310720 | tf_op jit(solution)/shard_map/all_gather | solution.py:69
  357.9 71.1 %copy-start.5 = (bf16[2048]{0:T(1024)(128)(2,1)S(1)}, bf16[2048]{0:T(1024)(128)(2,1)}, u32[]{:S(2)}) copy-start(bf16[2048]{0:T(1024)(128)(2,1)} %param.19) | copy-start | bytes 12292
  357.9 71.1 %copy-start.7 = (s32[2]{0:T(128)S(1)}, s32[2]{0:T(128)}, u32[]{:S(2)}) copy-start(s32[2]{0:T(128)} %param.13) | copy-start | bytes 28
  417.8 1.3 copy-start.2
  419.2 8.9 %collective-permute-start = (bf16[256,512]{1,0:T(8,128)(2,1)S(1)}, bf16[256,512]{1,0:T(8,128)(2,1)S(1)}, u32[]{:S(2)}, u32[]{:S(2)}) collective-permute-start(bf16[256,512]{1,0:T(8,128)(2,1)S(1)} %multiply_convert_fusion.3), channel_id=1, source_target_pairs={{0,4},{1,5},{2,6},{3,7},{8,12},{9,13},{10,14},{11,15},{16,20},{17,... | collective-permute-start | bytes 786440 | tf_op jit(solution)/shard_map/ppermute | solution.py:15
  428.2 0.7 copy-start.3
  428.9 108.2 %all-reduce.5.cloned.1.call-start = ((), (), s32[]{:S(2)}) async-start(), calls=%async_computation.6 | async-start | bytes 4194304 | tf_op jit(solution)/shard_map/psum | solution.py:90
  463.3 0.7 copy-start.4
Sparse Core Ops, SparseCore 0:
  9.2 28.4 all-gather.5
  40.5 102.6 all-gather.7
  146.0 97.9 all-gather.9
  246.6 97.9 all-gather.11
  357.3 58.4 all-reduce.2
  429.0 27.9 all-gather.13
  473.8 63.2 all-reduce.4
where the time goes:
time: 549 us; the launch traced here: 546 us
  waiting for transfers between devices  477 us (87%)
  matrix products  35.1 us (6%)
  between operations  13.6 us (2%)
  local copies, waits for them, and re-layouts  8.24 us (2%)
  other arithmetic  8.2 us (1%)
    psum x2, waiting for transfers between devices, shards(): summed = lax.psum(terms, 'mp')  120 us
    all_gather x1, waiting for transfers between devices, shards(): lax.all_gather(ffn_gate, 'dp', axis=0, tiled=True)  104 us
    all_gather x1, waiting for transfers between devices, shards(): lax.all_gather(ffn_down, 'dp', axis=1, tiled=True)  101 us
    all_gather x1, waiting for transfers between devices, shards(): lax.all_gather(ffn_lift, 'dp', axis=0, tiled=True)  93.3 us
    all_gather x1, waiting for transfers between devices, shards(): full = lax.all_gather(tokens_all, 'mp', axis=1, tiled=True)  27.6 us
    all_gather x1, waiting for transfers between devices, shards(): source = lax.all_gather(arrived, 'mp', axis=1, tiled=True)  23.9 us
    dot_general x1, matrix products, shards(): jnp.dot(hidden, lax.all_gather(ffn_down, 'dp', axis=1, tiled=True), prefe...  12.6 us
  transfers between devices with their start and end apart: 8, of which 8 were waited for; matrix products, arithmetic and copies ran while one was open for 3% of the time, Pallas kernels for 0%

commit v1 on v0

v1 whole, which is shorter than its diff:
```python
import jax
import jax.numpy as jnp
import numpy as np
from jax import lax
from jax.experimental import pallas as pl
from jax.experimental.pallas import tpu as pltpu
from jax.sharding import Mesh, PartitionSpec as P

HEAD_DIM = 256
epsilon = 1e-06
SIZES = {"yh": 2, "z": 8, "c": 2, "p": 2, "x": 4}
LINE = ("z", "c")
PLANE = ("yh", "p", "x")
bf16, f32 = jnp.bfloat16, jnp.float32
MIB = 1 << 20


def moved(value, axes, route):
    dims = [SIZES[a] for a in axes]
    pairs = []
    for at in np.ndindex(*dims):
        to = route(*at)
        if to is not None:
            pairs.append((int(np.ravel_multi_index(at, dims)), int(np.ravel_multi_index(to, dims))))
    return lax.ppermute(value, axes, pairs)


def gathered(value, axis):
    spread = jnp.broadcast_to(value[None], (SIZES[axis],) + value.shape)
    return lax.all_to_all(spread, axis, 0, 0)


def whole(shape):
    return pl.BlockSpec(shape, lambda *_: (0,) * len(shape))


def ffn_kernel(tokens, gain, weights, out):
    square = 0.0
    for b in range(4):
        t = tokens[b].astype(f32)
        square = square + jnp.sum(t * t, axis=-1, keepdims=True)
    scale = lax.rsqrt(square * (1.0 / 2048) + epsilon)
    gate = lift = 0.0
    for yh in range(2):
        for zz in range(4):
            b, at = yh * 2 + zz // 2, (zz % 2) * 256
            t = tokens[b, :, at : at + 256].astype(f32)
            n = (t * scale * gain[b : b + 1, at : at + 256].astype(f32)).astype(bf16)
            parts = [[weights[zz * 4 + k, yh, m] for k in range(4)] for m in range(2)]
            gate += jnp.dot(n, jnp.concatenate(parts[0], 0), preferred_element_type=f32)
            lift += jnp.dot(n, jnp.concatenate(parts[1], 0), preferred_element_type=f32)
    inner = 0.7978845608028654 * (gate + 0.044715 * (gate * gate * gate))
    hidden = (0.5 * gate * (1.0 + jnp.tanh(inner)) * lift).astype(bf16)
    for yh in range(2):
        for zz in range(4):
            at = yh * 1024 + zz * 256
            down = jnp.concatenate([weights[zz * 4 + k, yh, 2] for k in range(4)], 0)
            part = lax.dot_general(hidden, down, (((1,), (1,)), ((), ())), preferred_element_type=f32)
            out[:, at : at + 256] = part.astype(bf16)


def ffn(tokens, gain, weights):
    rows = tokens.shape[1]
    tile = 256
    return pl.pallas_call(
        ffn_kernel,
        grid=(rows // tile,),
        in_specs=[
            pl.BlockSpec((4, tile, 512), lambda i: (0, i, 0)),
            whole(gain.shape),
            whole(weights.shape),
        ],
        out_specs=pl.BlockSpec((tile, 2048), lambda i: (i, 0)),
        out_shape=jax.ShapeDtypeStruct((rows, 2048), bf16),
        compiler_params=pltpu.CompilerParams(vmem_limit_bytes=48 * MIB),
        cost_estimate=pl.CostEstimate(
            flops=rows * 2048 * 512 * 6, bytes_accessed=10 * MIB, transcendentals=rows * 512
        ),
    )(tokens, gain, weights)


def memory_kernel(terms, tokens, gain, out):
    square, kept = 0.0, []
    for b in range(4):
        at = slice(b * 512, (b + 1) * 512)
        total = terms[0, :, at].astype(f32)
        for k in range(1, 16):
            total = total + terms[k, :, at].astype(f32)
        merged = tokens[b].astype(f32) + total
        square = square + jnp.sum(merged * merged, axis=-1, keepdims=True)
        kept.append(merged)
    scale = lax.rsqrt(square * (1.0 / 2048) + epsilon)
    for b in range(4):
        at = slice(b * 512, (b + 1) * 512)
        rounded = (kept[b] * scale * gain[b : b + 1].astype(f32)).astype(bf16)
        for k in range(4):
            out[k, :, at] = rounded


def attention_kernel(lengths, query, memory, key_weight, value_weight, output_weight, out):
    source = memory[...]
    keys = jnp.dot(source, key_weight[...], preferred_element_type=f32).astype(bf16)
    values = jnp.dot(source, value_weight[...], preferred_element_type=f32).astype(bf16)
    positions = lax.broadcasted_iota(jnp.int32, (128, 128), 1)
    valid = positions < lengths[0]
    contexts = []
    for h in range(2):
        at = slice(h * HEAD_DIM, (h + 1) * HEAD_DIM)
        scores = lax.dot_general(
            query[:, at], keys[:, at], (((1,), (1,)), ((), ())), preferred_element_type=f32
        )
        scores = jnp.where(valid, scores, -1e30)
        weights = jnp.exp(scores - jnp.max(scores, axis=-1, keepdims=True))
        probs = (weights / jnp.sum(weights, axis=-1, keepdims=True)).astype(bf16)
        contexts.append(jnp.dot(probs, values[:, at], preferred_element_type=f32).astype(bf16))
    context = jnp.concatenate(contexts, axis=1)
    for b in range(4):
        part = jnp.dot(
            context, output_weight[:, b * 512 : (b + 1) * 512], preferred_element_type=f32
        )
        out[b] = part.astype(bf16)


def vmem():
    return pl.BlockSpec(memory_space=pltpu.VMEM)


def shards(
    streams,
    lengths,
    encoder_gain,
    ffn_gate,
    ffn_lift,
    ffn_down,
    final_gain,
    decoder_gain,
    query_weight,
    key_weight,
    value_weight,
    output_weight,
):
    yh, p, x = lax.axis_index("yh"), lax.axis_index("p"), lax.axis_index("x")
    local = streams[0].reshape(256, 512)

    stack = jnp.stack([ffn_gate, ffn_lift, ffn_down.T])

    def quarter(at):
        return lax.dynamic_slice_in_dim(stack, (p * 2 + at) * 512, 512, 2)

    own = quarter(yh)
    other = moved(quarter(1 - yh), ("yh",), lambda a: (1 - a,))
    both = jnp.where(yh == 0, jnp.stack([own, other]), jnp.stack([other, own]))
    weights = lax.all_gather(both, LINE, axis=0)

    swapped = moved(local, ("p",), lambda a: (1 - a,))
    across = moved(local, ("yh", "p"), lambda a, b: (1 - a, 0) if b == 0 else None)
    corner = moved(local, ("yh", "p"), lambda a, b: (1 - a, 1) if b == 0 else None)
    mine = jnp.where(p == 0, local, swapped)
    theirs = jnp.where(p == 0, across, corner)
    encoded = jnp.where(yh == 0, jnp.concatenate([mine, theirs]), jnp.concatenate([theirs, mine]))
    encoded = gathered(encoded, "x")
    decoding = jnp.where(p == 0, swapped[:128], local[128:])
    gain_rows = jnp.broadcast_to(final_gain[None], (16, 512))
    decoder_side = gathered(jnp.concatenate([decoding, gain_rows]), "x")

    full = decoder_side[:, :128].transpose(1, 0, 2).reshape(128, 2048).astype(f32)
    mean_square = jnp.mean(full * full, axis=-1, keepdims=True)
    query_in = full * lax.rsqrt(mean_square + epsilon) * decoder_gain.astype(f32)
    query = jnp.dot(query_in.astype(bf16), query_weight, preferred_element_type=f32).astype(bf16)

    terms = ffn(encoded, encoder_gain.reshape(4, 512), weights)
    terms = lax.all_to_all(terms.reshape(16, 32, 2048), PLANE, 0, 0)
    rows = lax.dynamic_slice_in_dim(encoded, ((yh * 2 + p) * 4 + x) * 32, 32, 1)
    memory = pl.pallas_call(
        memory_kernel,
        in_specs=[vmem()] * 3,
        out_specs=vmem(),
        out_shape=jax.ShapeDtypeStruct((4, 32, 2048), bf16),
        compiler_params=pltpu.CompilerParams(vmem_limit_bytes=16 * MIB),
    )(terms, rows, decoder_side[:, 128])
    memory = lax.all_to_all(memory, "x", 0, 0).reshape(128, 2048)

    attended = pl.pallas_call(
        attention_kernel,
        in_specs=[pl.BlockSpec(memory_space=pltpu.SMEM)] + [vmem()] * 5,
        out_specs=vmem(),
        out_shape=jax.ShapeDtypeStruct((4, 128, 512), bf16),
        compiler_params=pltpu.CompilerParams(vmem_limit_bytes=32 * MIB),
    )(
        lax.dynamic_slice_in_dim(lengths, p, 1, 0),
        query,
        memory,
        key_weight,
        value_weight,
        output_weight,
    )
    columns = lax.dynamic_slice_in_dim(memory, x * 512, 512, 1)
    later = moved(columns, ("p",), lambda a: (0,) if a == 1 else None)
    attended = lax.all_to_all(attended, "x", 0, 0)
    summed = jnp.sum(attended.astype(f32), axis=0)
    decoded = (decoding.astype(f32) + summed).astype(bf16)
    earlier = moved(decoded, ("p",), lambda a: (1,) if a == 0 else None)
    first = jnp.where(p == 0, columns, earlier)
    second = jnp.where(p == 0, later, decoded)
    return jnp.concatenate([first, second]).reshape(1, 2, 128, 512)


def solution(mesh):
    names = tuple(SIZES)
    fine = Mesh(mesh.devices.reshape(tuple(SIZES.values())), names)
    dp = ("yh", "z", "c")
    placed = (
        P("p", dp, None, "x"),
        P(dp),
        P(),
        P(dp, "x"),
        P(dp, "x"),
        P("x", dp),
        P("x"),
        P(),
        P(None, "x"),
        P(None, "x"),
        P(None, "x"),
        P("x", None),
    )
    return jax.shard_map(
        shards, mesh=fine, in_specs=placed, out_specs=P("p", dp, None, "x"), check_vma=False
    )
```

time: 549 us -> 165 us (0.30)
  waiting for transfers between devices: 477 us -> 70.6 us
  starting transfers between devices: 3.64 us -> 39.7 us
  matrix products: 35.1 us -> 0.47 us
  Pallas kernels: 0 us -> 12.3 us
  blocking collectives: 0 us -> 10.5 us
    all_gather x5 -> x1, waiting for transfers between devices: 349 us -> 0.02 us  [shards(): weights = lax.all_gather(both, LINE, axis=0)]
    psum x2 -> x0, waiting for transfers between devices: 120 us -> none  [shards(): summed = lax.psum(terms, 'mp')]
    all_to_all x0 -> x4, waiting for transfers between devices: none -> 50.1 us  [the longest x2 22.8 us: gathered(): return lax.all_to_all(spread, axis, 0, 0)]
    dot_general x8 -> x1, matrix products: 35.1 us -> 0.47 us  [shards(): jnp.dot(query_in.astype(bf16), query_weight, preferred_element_type=f32)]
    all_to_all x0 -> x4, starting transfers between devices: none -> 24.3 us  [the longest x2 10.5 us: gathered(): return lax.all_to_all(spread, axis, 0, 0)]
    ppermute x1 -> x6, waiting for transfers between devices: 5.53 us -> 20.5 us  [moved(): return lax.ppermute(value, axes, pairs)]
    pallas_call x0 -> x3, Pallas kernels: none -> 12.3 us  [the longest x1 7.42 us: ffn(): pl.pallas_call(ffn_kernel, grid=(rows // tile,), in_specs=[pl.BlockSpec((...]
    ppermute x1 -> x6, starting transfers between devices: 3.41 us -> 15.4 us  [moved(): return lax.ppermute(value, axes, pairs)]
  transfers between devices with their start and end apart: 8 -> 11, of which waited for: 8 -> 7; matrix products, arithmetic and copies ran while one was open for 3% -> 5% of each run, Pallas kernels for 0% -> 5%
where the time goes in v1:
time: 165 us; the launch traced here: 163 us
  waiting for transfers between devices  70.6 us (43%)
  starting transfers between devices  39.7 us (24%)
  between operations  13.6 us (8%)
  local copies, waits for them, and re-layouts  12.3 us (7%)
  Pallas kernels  12.3 us (7%)
  blocking collectives  10.5 us (6%)
  other arithmetic  3.98 us (2%)
    all_to_all x2, waiting for transfers between devices, gathered(): return lax.all_to_all(spread, axis, 0, 0)  22.8 us
    all_to_all x1, waiting for transfers between devices, shards(): terms = lax.all_to_all(terms.reshape(16, 32, 2048), PLANE, 0, 0)  22.1 us
    ppermute x6, waiting for transfers between devices, moved(): return lax.ppermute(value, axes, pairs)  20.5 us
    ppermute x6, starting transfers between devices, moved(): return lax.ppermute(value, axes, pairs)  15.4 us
    all_to_all x2, starting transfers between devices, gathered(): return lax.all_to_all(spread, axis, 0, 0)  10.5 us
    all_to_all x1, blocking collectives, shards(): attended = lax.all_to_all(attended, 'x', 0, 0)  10.5 us
    all_to_all x1, starting transfers between devices, shards(): memory = lax.all_to_all(memory, 'x', 0, 0).reshape(128, 2048)  7.86 us
    pallas_call x1, Pallas kernels, ffn(): pl.pallas_call(ffn_kernel, grid=(rows // tile,), in_specs=[pl.BlockSpec((...  7.42 us
  transfers between devices with their start and end apart: 11, of which 7 were waited for; matrix products, arithmetic and copies ran while one was open for 5% of the time, Pallas kernels for 5%

profile of v1, /device:TPU:6, one launch (start us, length us, event | category | flops | bytes accessed | tf_op | source)
XLA Modules:
  0.0 163.4 jit_solution(3850848051435225595)
XLA Ops:
  6.5 0.0 copy-start
  6.5 0.0 all-gather.2.cloned.1.call-start
  6.5 1.3 pad_maximum_fusion
  7.9 3.3 %collective-permute-start.3 = (bf16[3,64,512]{2,1,0:T(8,128)(2,1)S(1)}, bf16[3,64,512]{2,1,0:T(8,128)(2,1)S(1)}, u32[]{:S(2)}, u32[]{:S(2)}) collective-permute-start(bf16[3,64,512]{2,1,0:T(8,128)(2,1)S(1)} %get-tuple-element.8), channel_id=1, source_target_pairs={{0,128},{128,0},{1,129},{129,1},{2,130},{130,2},{3,131},{131,3},{4... | collective-permute-start | bytes 589832 | tf_op jit(solution)/shard_map/ppermute | solution.py:25
  11.2 5.0 %collective-permute-done.3 = bf16[3,64,512]{2,1,0:T(8,128)(2,1)S(1)} collective-permute-done((bf16[3,64,512]{2,1,0:T(8,128)(2,1)S(1)}, bf16[3,64,512]{2,1,0:T(8,128)(2,1)S(1)}, u32[]{:S(2)}, u32[]{:S(2)}) %collective-permute-start.3) | collective-permute-done | bytes 196640 | tf_op jit(solution)/shard_map/ppermute | solution.py:25
  16.2 0.8 maximum_select_fusion.1
  17.0 0.0 all-gather.2.cloned.1.call-update
  17.0 1.7 %collective-permute-start = (bf16[256,512]{1,0:T(8,128)(2,1)S(1)}, bf16[256,512]{1,0:T(8,128)(2,1)S(1)}, u32[]{:S(2)}, u32[]{:S(2)}) collective-permute-start(bf16[256,512]{1,0:T(8,128)(2,1)S(1)} %bitcast.32), channel_id=1, source_target_pairs={{0,4},{4,0},{1,5},{5,1},{2,6},{6,2},{3,7},{7,3},{8,12},{12,8},{9,1... | collective-permute-start | bytes 786440 | tf_op jit(solution)/shard_map/ppermute | solution.py:25
  18.7 4.8 %collective-permute-start.1 = (bf16[256,512]{1,0:T(8,128)(2,1)S(1)}, bf16[256,512]{1,0:T(8,128)(2,1)S(1)}, u32[]{:S(2)}, u32[]{:S(2)}) collective-permute-start(bf16[256,512]{1,0:T(8,128)(2,1)S(1)} %bitcast.33), channel_id=1, source_target_pairs={{0,128},{128,0},{1,129},{129,1},{2,130},{130,2},{3,131},{131,3},{8... | collective-permute-start | bytes 786440 | tf_op jit(solution)/shard_map/ppermute | solution.py:25
  23.5 1.3 collective-permute-start.2
  24.8 0.0 collective-permute-done
  24.9 7.5 %collective-permute-done.1 = bf16[256,512]{1,0:T(8,128)(2,1)S(1)} collective-permute-done((bf16[256,512]{1,0:T(8,128)(2,1)S(1)}, bf16[256,512]{1,0:T(8,128)(2,1)S(1)}, u32[]{:S(2)}, u32[]{:S(2)}) %collective-permute-start.1) | collective-permute-done | bytes 262176 | tf_op jit(solution)/shard_map/ppermute | solution.py:25
  32.3 0.0 collective-permute-done.2
  32.4 0.2 maximum_select_fusion
  32.6 1.6 broadcast_in_dim.6
  34.2 5.0 %all-to-all-start = ((bf16[4,512,512]{2,1,0:T(8,128)(2,1)}), bf16[4,512,512]{2,1,0:T(8,128)(2,1)}, u32[]{:S(2)}, u32[]{:S(2)}) async-start(bf16[4,512,512]{2,1,0:T(8,128)(2,1)} %broadcast_in_dim.6), calls=%async_computation | async-start | bytes 4194304 | tf_op jit(solution)/shard_map/all_to_all | solution.py:30
  39.2 22.8 %all-to-all-done.tokens = bf16[4,512,512]{2,1,0:T(8,128)(2,1)} async-done(((bf16[4,512,512]{2,1,0:T(8,128)(2,1)}), bf16[4,512,512]{2,1,0:T(8,128)(2,1)}, u32[]{:S(2)}, u32[]{:S(2)}) %all-to-all-start) | async-done | bytes 2097184 | tf_op jit(solution)/shard_map/all_to_all | solution.py:30
  62.0 0.9 broadcast_in_dim.8
  63.0 5.5 %all-to-all-start.2 = ((bf16[4,144,512]{2,1,0:T(8,128)(2,1)}), bf16[4,144,512]{2,1,0:T(8,128)(2,1)S(1)}, u32[]{:S(2)}, u32[]{:S(2)}) async-start(bf16[4,144,512]{2,1,0:T(8,128)(2,1)} %broadcast_in_dim.8), calls=%async_computation.2 | async-start | bytes 1179648 | tf_op jit(solution)/shard_map/all_to_all | solution.py:30
  68.5 0.0 all-gather.2.cloned.1.call-done.weights
  68.5 7.4 %shard_map.118 = bf16[512,2048]{1,0:T(8,128)(2,1)S(1)} custom-call(bf16[4,512,512]{2,1,0:T(8,128)(2,1)} %all-to-all-done.tokens, bf16[4,512]{1,0:T(4,128)(2,1)S(1)} %reshape.115.gain, bf16[16,2,3,64,512]{4,3,2,1,0:T(8,128)(2,1)} %all-gather.2.cloned.1.call-done.weights), custom_call_target="tpu_custom_call" | custom-call | flops 3221225472 | bytes 10485760 | tf_op jit(solution)/shard_map/pallas_call | solution.py:65
  75.9 1.3 copy-done.1
  77.2 0.0 all-to-all-done.2
  77.2 5.9 %all-to-all-start.1 = ((bf16[16,32,2048]{2,1,0:T(8,128)(2,1)}), bf16[16,32,2048]{2,1,0:T(8,128)(2,1)}, u32[]{:S(2)}, u32[]{:S(2)}) async-start(bf16[16,32,2048]{2,1,0:T(8,128)(2,1)} %bitcast.30), calls=%async_computation.1 | async-start | bytes 4194304 | tf_op jit(solution)/shard_map/all_to_all | solution.py:172
  83.1 0.0 copy-done.6
  83.2 0.6 dynamic_slice.19.lengths
  83.8 0.8 slice.22
  84.6 1.3 copy.17
  85.9 0.3 multiply_reduce_fusion
  86.2 0.9 constant_dynamic-slice_fusion.1.tokens
  87.2 22.1 %all-to-all-done.1.terms = bf16[16,32,2048]{2,1,0:T(8,128)(2,1)} async-done(((bf16[16,32,2048]{2,1,0:T(8,128)(2,1)}), bf16[16,32,2048]{2,1,0:T(8,128)(2,1)}, u32[]{:S(2)}, u32[]{:S(2)}) %all-to-all-start.1) | async-done | bytes 2097184 | tf_op jit(solution)/shard_map/all_to_all | solution.py:172
  109.3 2.8 %shard_map.119 = bf16[4,32,2048]{2,1,0:T(8,128)(2,1)} custom-call(bf16[16,32,2048]{2,1,0:T(8,128)(2,1)} %all-to-all-done.1.terms, bf16[4,32,512]{2,1,0:T(8,128)(2,1)S(1)} %constant_dynamic-slice_fusion.1.tokens, bf16[4,512]{1,0:T(4,128)(2,1)S(1)} %bitcast.31), custom_call_target="tpu_custom_call" | custom-call | tf_op jit(solution)/shard_map/pallas_call | solution.py:174
  112.0 7.9 %all-to-all-start.3 = ((bf16[4,32,2048]{2,1,0:T(8,128)(2,1)}), bf16[4,32,2048]{2,1,0:T(8,128)(2,1)S(1)}, u32[]{:S(2)}, u32[]{:S(2)}) async-start(bf16[4,32,2048]{2,1,0:T(8,128)(2,1)} %shard_map.119), calls=%async_computation.3 | async-start | bytes 1048576 | tf_op jit(solution)/shard_map/all_to_all | solution.py:181
  119.9 0.3 fusion.1
  120.2 0.0 copy-done
  120.2 0.5 convolution_convert_fusion.query
  120.7 5.2 %all-to-all-done.3 = bf16[4,32,2048]{2,1,0:T(8,128)(2,1)S(1)} async-done(((bf16[4,32,2048]{2,1,0:T(8,128)(2,1)}), bf16[4,32,2048]{2,1,0:T(8,128)(2,1)S(1)}, u32[]{:S(2)}, u32[]{:S(2)}) %all-to-all-start.3) | async-done | bytes 524320 | tf_op jit(solution)/shard_map/all_to_all | solution.py:181
  125.9 1.6 copy-done.2
  127.5 1.6 copy-done.3
  129.1 1.6 copy-done.4
  130.7 2.1 %shard_map.120 = bf16[4,128,512]{2,1,0:T(8,128)(2,1)S(1)} custom-call(s32[1]{0:T(128)} %dynamic_slice.19.lengths, bf16[128,512]{1,0:T(8,128)(2,1)S(1)} %convolution_convert_fusion.query, bf16[128,2048]{1,0:T(8,128)(2,1)S(1)} %bitcast.28, bf16[2048,512]{1,0:T(8,128)(2,1)S(1)} %copy-done.2, bf16[2048,512]{1,0:T(8,128)(2,1)S(1)} %copy-done.3, ...), custom_call_target="tpu_custom_call" | custom-call | tf_op jit(solution)/shard_map/pallas_call | solution.py:183
  132.8 10.5 %all_to_all.25 = bf16[4,128,512]{2,1,0:T(8,128)(2,1)S(1)} all-to-all(bf16[4,128,512]{2,1,0:T(8,128)(2,1)S(1)} %shard_map.120), channel_id=1, replica_groups=mesh['yh'=2,'z'=8,'c'=2,'p'=2,'x'=4] {'x'}, dimensions={0} | all-to-all | bytes 1048576 | tf_op jit(solution)/shard_map/all_to_all | solution.py:199
  143.3 0.1 convert_reduce_fusion
  143.4 3.1 %collective-permute-start.4 = (bf16[128,512]{1,0:T(8,128)(2,1)S(1)}, bf16[128,512]{1,0:T(8,128)(2,1)S(1)}, u32[]{:S(2)}, u32[]{:S(2)}) collective-permute-start(bf16[128,512]{1,0:T(8,128)(2,1)S(1)} %add_convert_fusion), channel_id=1, source_target_pairs={{0,4},{1,5},{2,6},{3,7},{8,12},{9,13},{10,14},{11,15},{16,20},{17,... | collective-permute-start | bytes 393224 | tf_op jit(solution)/shard_map/ppermute | solution.py:25
  146.5 2.5 %collective-permute-done.4 = bf16[128,512]{1,0:T(8,128)(2,1)S(1)} collective-permute-done((bf16[128,512]{1,0:T(8,128)(2,1)S(1)}, bf16[128,512]{1,0:T(8,128)(2,1)S(1)}, u32[]{:S(2)}, u32[]{:S(2)}) %collective-permute-start.4) | collective-permute-done | bytes 131104 | tf_op jit(solution)/shard_map/ppermute | solution.py:25
  149.0 1.3 collective-permute-start.5
  150.3 5.6 %collective-permute-done.5 = bf16[128,512]{1,0:T(8,128)(2,1)S(1)} collective-permute-done((bf16[128,512]{1,0:T(8,128)(2,1)S(1)}, bf16[128,512]{1,0:T(8,128)(2,1)S(1)}, u32[]{:S(2)}, u32[]{:S(2)}) %collective-permute-start.5) | collective-permute-done | bytes 131104 | tf_op jit(solution)/shard_map/ppermute | solution.py:25
  155.9 0.7 pad_maximum_fusion.1
  (27 shorter events, 0.3 us)
Async XLA Ops:
  6.5 113.7 %copy-start = (bf16[2048,512]{1,0:T(8,128)(2,1)S(1)}, bf16[2048,512]{1,0:T(8,128)(2,1)}, u32[]{:S(2)}) copy-start(bf16[2048,512]{1,0:T(8,128)(2,1)} %param.20) | copy-start | bytes 6291460
  6.5 10.5 %copy-start.5 = (bf16[1,2,128,512]{3,2,1,0:T(8,128)(2,1)S(1)}, bf16[1,2,128,512]{3,2,1,0:T(8,128)(2,1)}, u32[]{:S(2)}) copy-start(bf16[1,2,128,512]{3,2,1,0:T(8,128)(2,1)} %param.12) | copy-start | bytes 786436
  6.5 62.0 %all-gather.2.cloned.1.call-start = ((), (), s32[]{:S(2)}) async-start(), calls=%async_computation.5 | async-start | bytes 6684672 | tf_op jit(solution)/shard_map/all_gather | solution.py:153
  7.9 8.2 %collective-permute-start.3 = (bf16[3,64,512]{2,1,0:T(8,128)(2,1)S(1)}, bf16[3,64,512]{2,1,0:T(8,128)(2,1)S(1)}, u32[]{:S(2)}, u32[]{:S(2)}) collective-permute-start(bf16[3,64,512]{2,1,0:T(8,128)(2,1)S(1)} %get-tuple-element.8), channel_id=1, source_target_pairs={{0,128},{128,0},{1,129},{129,1},{2,130},{130,2},{3,131},{131,3},{4... | collective-permute-start | bytes 589832 | tf_op jit(solution)/shard_map/ppermute | solution.py:25
  17.0 7.8 %collective-permute-start = (bf16[256,512]{1,0:T(8,128)(2,1)S(1)}, bf16[256,512]{1,0:T(8,128)(2,1)S(1)}, u32[]{:S(2)}, u32[]{:S(2)}) collective-permute-start(bf16[256,512]{1,0:T(8,128)(2,1)S(1)} %bitcast.32), channel_id=1, source_target_pairs={{0,4},{4,0},{1,5},{5,1},{2,6},{6,2},{3,7},{7,3},{8,12},{12,8},{9,1... | collective-permute-start | bytes 786440 | tf_op jit(solution)/shard_map/ppermute | solution.py:25
  18.7 13.7 %collective-permute-start.1 = (bf16[256,512]{1,0:T(8,128)(2,1)S(1)}, bf16[256,512]{1,0:T(8,128)(2,1)S(1)}, u32[]{:S(2)}, u32[]{:S(2)}) collective-permute-start(bf16[256,512]{1,0:T(8,128)(2,1)S(1)} %bitcast.33), channel_id=1, source_target_pairs={{0,128},{128,0},{1,129},{129,1},{2,130},{130,2},{3,131},{131,3},{8... | collective-permute-start | bytes 786440 | tf_op jit(solution)/shard_map/ppermute | solution.py:25
  23.5 8.9 %collective-permute-start.2 = (bf16[256,512]{1,0:T(8,128)(2,1)S(1)}, bf16[256,512]{1,0:T(8,128)(2,1)S(1)}, u32[]{:S(2)}, u32[]{:S(2)}) collective-permute-start(bf16[256,512]{1,0:T(8,128)(2,1)S(1)} %bitcast.34), channel_id=1, source_target_pairs={{0,132},{128,4},{1,133},{129,5},{2,134},{130,6},{3,135},{131,7},{8... | collective-permute-start | bytes 786440 | tf_op jit(solution)/shard_map/ppermute | solution.py:25
  34.1 5.0 %copy-start.8 = (bf16[512]{0:T(512)(128)(2,1)S(1)}, bf16[512]{0:T(512)(128)(2,1)}, u32[]{:S(2)}) copy-start(bf16[512]{0:T(512)(128)(2,1)} %param.18) | copy-start | bytes 3076
  34.2 27.9 %all-to-all-start = ((bf16[4,512,512]{2,1,0:T(8,128)(2,1)}), bf16[4,512,512]{2,1,0:T(8,128)(2,1)}, u32[]{:S(2)}, u32[]{:S(2)}) async-start(bf16[4,512,512]{2,1,0:T(8,128)(2,1)} %broadcast_in_dim.6), calls=%async_computation | async-start | bytes 4194304 | tf_op jit(solution)/shard_map/all_to_all | solution.py:30
  39.2 29.3 %copy-start.7 = (bf16[2048]{0:T(1024)(128)(2,1)S(1)}, bf16[2048]{0:T(1024)(128)(2,1)}, u32[]{:S(2)}) copy-start(bf16[2048]{0:T(1024)(128)(2,1)} %param.14) | copy-start | bytes 12292
  63.0 14.3 %all-to-all-start.2 = ((bf16[4,144,512]{2,1,0:T(8,128)(2,1)}), bf16[4,144,512]{2,1,0:T(8,128)(2,1)S(1)}, u32[]{:S(2)}, u32[]{:S(2)}) async-start(bf16[4,144,512]{2,1,0:T(8,128)(2,1)} %broadcast_in_dim.8), calls=%async_computation.2 | async-start | bytes 1179648 | tf_op jit(solution)/shard_map/all_to_all | solution.py:30
  75.9 1.3 copy-start.1
  77.2 5.9 %copy-start.6 = (bf16[2048]{0:T(1024)(128)(2,1)S(1)}, bf16[2048]{0:T(1024)(128)(2,1)}, u32[]{:S(2)}) copy-start(bf16[2048]{0:T(1024)(128)(2,1)} %param.19) | copy-start | bytes 12292
  77.2 5.9 %copy-start.9 = (s32[2]{0:T(128)S(1)}, s32[2]{0:T(128)}, u32[]{:S(2)}) copy-start(s32[2]{0:T(128)} %param.13) | copy-start | bytes 28
  77.2 32.0 %all-to-all-start.1 = ((bf16[16,32,2048]{2,1,0:T(8,128)(2,1)}), bf16[16,32,2048]{2,1,0:T(8,128)(2,1)}, u32[]{:S(2)}, u32[]{:S(2)}) async-start(bf16[16,32,2048]{2,1,0:T(8,128)(2,1)} %bitcast.30), calls=%async_computation.1 | async-start | bytes 4194304 | tf_op jit(solution)/shard_map/all_to_all | solution.py:172
  112.0 13.9 %all-to-all-start.3 = ((bf16[4,32,2048]{2,1,0:T(8,128)(2,1)}), bf16[4,32,2048]{2,1,0:T(8,128)(2,1)S(1)}, u32[]{:S(2)}, u32[]{:S(2)}) async-start(bf16[4,32,2048]{2,1,0:T(8,128)(2,1)} %shard_map.119), calls=%async_computation.3 | async-start | bytes 1048576 | tf_op jit(solution)/shard_map/all_to_all | solution.py:181
  125.9 1.6 copy-start.2
  127.5 1.6 copy-start.3
  129.1 1.6 copy-start.4
  143.4 5.6 %collective-permute-start.4 = (bf16[128,512]{1,0:T(8,128)(2,1)S(1)}, bf16[128,512]{1,0:T(8,128)(2,1)S(1)}, u32[]{:S(2)}, u32[]{:S(2)}) collective-permute-start(bf16[128,512]{1,0:T(8,128)(2,1)S(1)} %add_convert_fusion), channel_id=1, source_target_pairs={{0,4},{1,5},{2,6},{3,7},{8,12},{9,13},{10,14},{11,15},{16,20},{17,... | collective-permute-start | bytes 393224 | tf_op jit(solution)/shard_map/ppermute | solution.py:25
  149.0 6.9 %collective-permute-start.5 = (bf16[128,512]{1,0:T(8,128)(2,1)S(1)}, bf16[128,512]{1,0:T(8,128)(2,1)S(1)}, u32[]{:S(2)}, u32[]{:S(2)}) collective-permute-start(bf16[128,512]{1,0:T(8,128)(2,1)S(1)} %get-tuple-element.6), channel_id=1, source_target_pairs={{4,0},{5,1},{6,2},{7,3},{12,8},{13,9},{14,10},{15,11},{20,16},{21,... | collective-permute-start | bytes 393224 | tf_op jit(solution)/shard_map/ppermute | solution.py:25
Sparse Core Ops, SparseCore 0:
  17.1 48.9 all-gather.1

commit v2 on v1

--- a/solution.py
+++ b/solution.py
@@ -10,7 +10,6 @@
 epsilon = 1e-06
 SIZES = {"yh": 2, "z": 8, "c": 2, "p": 2, "x": 4}
 LINE = ("z", "c")
-PLANE = ("yh", "p", "x")
 bf16, f32 = jnp.bfloat16, jnp.float32
 MIB = 1 << 20
 
@@ -30,11 +29,16 @@
     return lax.all_to_all(spread, axis, 0, 0)
 
 
+def over(value, way):
+    return moved(value, ("yh", "p"), lambda a, b: (a ^ (way // 2), b ^ (way % 2)))
+
+
 def whole(shape):
     return pl.BlockSpec(shape, lambda *_: (0,) * len(shape))
 
 
-def ffn_kernel(tokens, gain, weights, out):
+def ffn_kernel(place, tokens, gain, weights, left, *rest):
+    right, tile = rest[:4], rest[4]
     square = 0.0
     for b in range(4):
         t = tokens[b].astype(f32)
@@ -53,39 +57,69 @@
     hidden = (0.5 * gate * (1.0 + jnp.tanh(inner)) * lift).astype(bf16)
     for yh in range(2):
         for zz in range(4):
-            at = yh * 1024 + zz * 256
+            half, at = zz // 2, (zz % 2) * 256
             down = jnp.concatenate([weights[zz * 4 + k, yh, 2] for k in range(4)], 0)
             part = lax.dot_general(hidden, down, (((1,), (1,)), ((), ())), preferred_element_type=f32)
-            out[:, at : at + 256] = part.astype(bf16)
-
-
-def ffn(tokens, gain, weights):
+            part = part.astype(bf16)
+            for p in range(2):
+                for x in range(4):
+                    rows = part[(p * 4 + x) * 32 : (p * 4 + x + 1) * 32]
+                    if yh == 0:
+                        left[x, p, half, :, at : at + 256] = rows
+                    else:
+                        tile[p, x, half, :, at : at + 256] = rows
+    for way in range(4):
+
+        @pl.when(pl.program_id(0) == place[0] ^ (way // 2))
+        def _():
+            right[way][...] = tile[place[1] ^ (way % 2)]
+
+
+def ffn(place, tokens, gain, weights):
     rows = tokens.shape[1]
-    tile = 256
     return pl.pallas_call(
         ffn_kernel,
-        grid=(rows // tile,),
+        grid=(2,),
         in_specs=[
-            pl.BlockSpec((4, tile, 512), lambda i: (0, i, 0)),
+            pl.BlockSpec(memory_space=pltpu.SMEM),
+            pl.BlockSpec((4, 256, 512), lambda i: (0, i, 0)),
             whole(gain.shape),
             whole(weights.shape),
         ],
-        out_specs=pl.BlockSpec((tile, 2048), lambda i: (i, 0)),
-        out_shape=jax.ShapeDtypeStruct((rows, 2048), bf16),
+        out_specs=[pl.BlockSpec((4, 2, 2, 32, 512), lambda i: (0, i, 0, 0, 0))]
+        + [whole((4, 2, 32, 512))] * 4,
+        out_shape=[jax.ShapeDtypeStruct((4, 4, 2, 32, 512), bf16)]
+        + [jax.ShapeDtypeStruct((4, 2, 32, 512), bf16)] * 4,
+        scratch_shapes=[pltpu.VMEM((2, 4, 2, 32, 512), bf16)],
         compiler_params=pltpu.CompilerParams(vmem_limit_bytes=48 * MIB),
         cost_estimate=pl.CostEstimate(
             flops=rows * 2048 * 512 * 6, bytes_accessed=10 * MIB, transcendentals=rows * 512
         ),
-    )(tokens, gain, weights)
-
-
-def memory_kernel(terms, tokens, gain, out):
+    )(place, tokens, gain, weights)
+
+
+def added(refs):
+    total = refs[0].astype(f32)
+    for value in refs[1:]:
+        total = total + value.astype(f32)
+    return total
+
+
+def between_kernel(place, left, r0, r1, r2, r3, o0, o1, o2, o3, right):
+    for way, out in enumerate((o0, o1, o2, o3)):
+        to = (place[0] * 2 + place[1]) ^ way
+        out[...] = added([left[k, to] for k in range(4)]).astype(bf16)
+    for x in range(4):
+        right[x] = added([r[x] for r in (r0, r1, r2, r3)]).astype(bf16)
+
+
+def memory_kernel(l0, l1, l2, l3, right, tokens, gain, out):
     square, kept = 0.0, []
     for b in range(4):
-        at = slice(b * 512, (b + 1) * 512)
-        total = terms[0, :, at].astype(f32)
-        for k in range(1, 16):
-            total = total + terms[k, :, at].astype(f32)
+        if b < 2:
+            total = added([r[b] for r in (l0, l1, l2, l3)])
+        else:
+            total = added([right[k, b - 2] for k in range(4)])
         merged = tokens[b].astype(f32) + total
         square = square + jnp.sum(merged * merged, axis=-1, keepdims=True)
         kept.append(merged)
@@ -95,6 +129,27 @@
         rounded = (kept[b] * scale * gain[b : b + 1].astype(f32)).astype(bf16)
         for k in range(4):
             out[k, :, at] = rounded
+
+
+def prepare_kernel(tokens, gain, after, wq, wk, wv, wo, query, key_out, value_out, output_out, sems):
+    copies = [
+        pltpu.make_async_copy(src, dst, sems.at[i])
+        for i, (src, dst) in enumerate(((wk, key_out), (wv, value_out), (wo, output_out)))
+    ]
+    for copy in copies:
+        copy.start()
+    square = 0.0
+    for b in range(4):
+        t = tokens[b].astype(f32)
+        square = square + jnp.sum(t * t, axis=-1, keepdims=True)
+    scale = lax.rsqrt(square * (1.0 / 2048) + epsilon)
+    total = 0.0
+    for b in range(4):
+        n = (tokens[b].astype(f32) * scale * gain[b : b + 1].astype(f32)).astype(bf16)
+        total += jnp.dot(n, wq[b * 512 : (b + 1) * 512], preferred_element_type=f32)
+    query[...] = total.astype(bf16)
+    for copy in copies:
+        copy.wait()
 
 
 def attention_kernel(lengths, query, memory, key_weight, value_weight, output_weight, out):
@@ -163,21 +218,49 @@
     gain_rows = jnp.broadcast_to(final_gain[None], (16, 512))
     decoder_side = gathered(jnp.concatenate([decoding, gain_rows]), "x")
 
-    full = decoder_side[:, :128].transpose(1, 0, 2).reshape(128, 2048).astype(f32)
-    mean_square = jnp.mean(full * full, axis=-1, keepdims=True)
-    query_in = full * lax.rsqrt(mean_square + epsilon) * decoder_gain.astype(f32)
-    query = jnp.dot(query_in.astype(bf16), query_weight, preferred_element_type=f32).astype(bf16)
-
-    terms = ffn(encoded, encoder_gain.reshape(4, 512), weights)
-    terms = lax.all_to_all(terms.reshape(16, 32, 2048), PLANE, 0, 0)
+    place = jnp.stack([yh, p, x]).astype(jnp.int32)
+    left, *right = ffn(place, encoded, encoder_gain.reshape(4, 512), weights)
+    left = lax.all_to_all(left, "x", 0, 0)
+    right = [right[0]] + [over(right[way], way) for way in (1, 2, 3)]
+    *left, right = pl.pallas_call(
+        between_kernel,
+        in_specs=[pl.BlockSpec(memory_space=pltpu.SMEM)] + [vmem()] * 5,
+        out_specs=[vmem()] * 5,
+        out_shape=[jax.ShapeDtypeStruct((2, 32, 512), bf16)] * 4
+        + [jax.ShapeDtypeStruct((4, 2, 32, 512), bf16)],
+        compiler_params=pltpu.CompilerParams(vmem_limit_bytes=16 * MIB),
+    )(place, left, *right)
     rows = lax.dynamic_slice_in_dim(encoded, ((yh * 2 + p) * 4 + x) * 32, 32, 1)
+    left = [left[0]] + [over(left[way], way) for way in (1, 2, 3)]
+    right = lax.all_to_all(right, "x", 0, 0)
     memory = pl.pallas_call(
         memory_kernel,
-        in_specs=[vmem()] * 3,
+        in_specs=[vmem()] * 7,
         out_specs=vmem(),
         out_shape=jax.ShapeDtypeStruct((4, 32, 2048), bf16),
         compiler_params=pltpu.CompilerParams(vmem_limit_bytes=16 * MIB),
-    )(terms, rows, decoder_side[:, 128])
+    )(*left, right, rows, decoder_side[:, 128])
+    anyplace = pl.BlockSpec(memory_space=pl.ANY)
+    prepared = pl.pallas_call(
+        prepare_kernel,
+        in_specs=[vmem()] * 2 + [anyplace, vmem()] + [anyplace] * 3,
+        out_specs=[vmem()] * 4,
+        out_shape=[jax.ShapeDtypeStruct((128, 512), bf16)]
+        + [jax.ShapeDtypeStruct(w.shape, bf16) for w in (key_weight, value_weight, output_weight)],
+        scratch_shapes=[pltpu.SemaphoreType.DMA((3,))],
+        compiler_params=pltpu.CompilerParams(vmem_limit_bytes=16 * MIB),
+        cost_estimate=pl.CostEstimate(
+            flops=2 * 128 * 2048 * 512, bytes_accessed=14 * MIB, transcendentals=0
+        ),
+    )(
+        decoder_side[:, :128],
+        decoder_gain.reshape(4, 512),
+        memory,
+        query_weight,
+        key_weight,
+        value_weight,
+        output_weight,
+    )
     memory = lax.all_to_all(memory, "x", 0, 0).reshape(128, 2048)
 
     attended = pl.pallas_call(
@@ -185,23 +268,18 @@
         in_specs=[pl.BlockSpec(memory_space=pltpu.SMEM)] + [vmem()] * 5,
         out_specs=vmem(),
         out_shape=jax.ShapeDtypeStruct((4, 128, 512), bf16),
-        compiler_params=pltpu.CompilerParams(vmem_limit_bytes=32 * MIB),
-    )(
-        lax.dynamic_slice_in_dim(lengths, p, 1, 0),
-        query,
-        memory,
-        key_weight,
-        value_weight,
-        output_weight,
-    )
+        compiler_params=pltpu.CompilerParams(vmem_limit_bytes=16 * MIB),
+        cost_estimate=pl.CostEstimate(
+            flops=6 * 128 * 2048 * 512, bytes_accessed=10 * MIB, transcendentals=0
+        ),
+    )(lax.dynamic_slice_in_dim(lengths, p, 1, 0), prepared[0], memory, *prepared[1:])
     columns = lax.dynamic_slice_in_dim(memory, x * 512, 512, 1)
-    later = moved(columns, ("p",), lambda a: (0,) if a == 1 else None)
     attended = lax.all_to_all(attended, "x", 0, 0)
     summed = jnp.sum(attended.astype(f32), axis=0)
     decoded = (decoding.astype(f32) + summed).astype(bf16)
-    earlier = moved(decoded, ("p",), lambda a: (1,) if a == 0 else None)
-    first = jnp.where(p == 0, columns, earlier)
-    second = jnp.where(p == 0, later, decoded)
+    swapped = moved(jnp.where(p == 0, decoded, columns), ("p",), lambda a: (1 - a,))
+    kept = jnp.where(p == 0, columns, decoded)
+    first, second = jnp.where(p == 0, kept, swapped), jnp.where(p == 0, swapped, kept)
     return jnp.concatenate([first, second]).reshape(1, 2, 128, 512)
 
 

time: 165 us -> 187 us (1.13)
  local copies, waits for them, and re-layouts: 12.3 us -> 25.2 us
  starting transfers between devices: 39.7 us -> 51.5 us
  blocking collectives: 10.5 us -> 0 us
  waiting for transfers between devices: 70.6 us -> 76.6 us
    ppermute x6 -> x11, waiting for transfers between devices: 20.5 us -> 32.5 us  [moved(): return lax.ppermute(value, axes, pairs)]
    unnamed x22 -> x51, local copies, waits for them, and re-layouts: 7.4 us -> 19.3 us
    all_to_all x1 -> x0, blocking collectives: 10.5 us -> none  [shards(): attended = lax.all_to_all(attended, 'x', 0, 0)]
    all_to_all x1 -> x3, starting transfers between devices: 5.88 us -> 14.4 us  [the longest x1 4.8 us: shards(): attended = lax.all_to_all(attended, 'x', 0, 0)]
    ppermute x6 -> x11, starting transfers between devices: 15.4 us -> 21.2 us  [moved(): return lax.ppermute(value, axes, pairs)]
    all_to_all x1, waiting for transfers between devices: 5.18 us -> 0.01 us  [shards(): memory = lax.all_to_all(memory, 'x', 0, 0).reshape(128, 2048)]
    all_to_all x1 -> x3, waiting for transfers between devices: 22.1 us -> 17.2 us  [the longest x1 11.1 us: shards(): left = lax.all_to_all(left, 'x', 0, 0)]
    all_gather x1, waiting for transfers between devices: 0.02 us -> 4.57 us  [shards(): weights = lax.all_gather(both, LINE, axis=0)]
  transfers between devices with their start and end apart: 11 -> 18, of which waited for: 7 -> 12; matrix products, arithmetic and copies ran while one was open for 5% -> 3% of each run, Pallas kernels for 5% -> 1%
where the time goes in v2:
time: 187 us; the launch traced here: 185 us
  waiting for transfers between devices  76.6 us (41%)
  starting transfers between devices  51.5 us (28%)
  local copies, waits for them, and re-layouts  25.2 us (13%)
  between operations  13.6 us (7%)
  Pallas kernels  13.1 us (7%)
  other arithmetic  5 us (3%)
    ppermute x11, waiting for transfers between devices, moved(): return lax.ppermute(value, axes, pairs)  32.5 us
    all_to_all x2, waiting for transfers between devices, gathered(): return lax.all_to_all(spread, axis, 0, 0)  22.4 us
    ppermute x11, starting transfers between devices, moved(): return lax.ppermute(value, axes, pairs)  21.2 us
    unnamed x51, local copies, waits for them, and re-layouts  19.3 us
    all_to_all x1, waiting for transfers between devices, shards(): left = lax.all_to_all(left, 'x', 0, 0)  11.1 us
    all_to_all x2, starting transfers between devices, gathered(): return lax.all_to_all(spread, axis, 0, 0)  11.1 us
    pallas_call x1, Pallas kernels, ffn(): pl.pallas_call(ffn_kernel, grid=(2,), in_specs=[pl.BlockSpec(memory_space...  7.34 us
    all_to_all x1, waiting for transfers between devices, shards(): attended = lax.all_to_all(attended, 'x', 0, 0)  6.02 us
  transfers between devices with their start and end apart: 18, of which 12 were waited for; matrix products, arithmetic and copies ran while one was open for 3% of the time, Pallas kernels for 1%

profile of v2, /device:TPU:6, one launch (start us, length us, event | category | flops | bytes accessed | tf_op | source)
XLA Modules:
  0.0 185.1 jit_solution(14503683928957891650)
XLA Ops:
  6.5 1.2 pad_maximum_fusion
  7.8 3.3 %collective-permute-start.3 = (bf16[3,64,512]{2,1,0:T(8,128)(2,1)S(1)}, bf16[3,64,512]{2,1,0:T(8,128)(2,1)S(1)}, u32[]{:S(2)}, u32[]{:S(2)}) collective-permute-start(bf16[3,64,512]{2,1,0:T(8,128)(2,1)S(1)} %get-tuple-element.38), channel_id=1, source_target_pairs={{0,128},{128,0},{1,129},{129,1},{2,130},{130,2},{3,131},{131,3},{4... | collective-permute-start | bytes 589832 | tf_op jit(solution)/shard_map/ppermute | solution.py:24
  11.1 5.0 %collective-permute-done.3 = bf16[3,64,512]{2,1,0:T(8,128)(2,1)S(1)} collective-permute-done((bf16[3,64,512]{2,1,0:T(8,128)(2,1)S(1)}, bf16[3,64,512]{2,1,0:T(8,128)(2,1)S(1)}, u32[]{:S(2)}, u32[]{:S(2)}) %collective-permute-start.3) | collective-permute-done | bytes 196640 | tf_op jit(solution)/shard_map/ppermute | solution.py:24
  16.1 0.8 maximum_select_fusion.1
  16.9 1.7 collective-permute-start
  18.6 4.8 %collective-permute-start.1 = (bf16[256,512]{1,0:T(8,128)(2,1)S(1)}, bf16[256,512]{1,0:T(8,128)(2,1)S(1)}, u32[]{:S(2)}, u32[]{:S(2)}) collective-permute-start(bf16[256,512]{1,0:T(8,128)(2,1)S(1)} %bitcast.25), channel_id=1, source_target_pairs={{0,128},{128,0},{1,129},{129,1},{2,130},{130,2},{3,131},{131,3},{8... | collective-permute-start | bytes 786440 | tf_op jit(solution)/shard_map/ppermute | solution.py:24
  23.4 1.3 collective-permute-start.2
  24.8 7.5 %collective-permute-done.1 = bf16[256,512]{1,0:T(8,128)(2,1)S(1)} collective-permute-done((bf16[256,512]{1,0:T(8,128)(2,1)S(1)}, bf16[256,512]{1,0:T(8,128)(2,1)S(1)}, u32[]{:S(2)}, u32[]{:S(2)}) %collective-permute-start.1) | collective-permute-done | bytes 262176 | tf_op jit(solution)/shard_map/ppermute | solution.py:24
  32.5 1.6 broadcast_in_dim.6
  34.0 4.9 %all-to-all-start = ((bf16[4,512,512]{2,1,0:T(8,128)(2,1)}), bf16[4,512,512]{2,1,0:T(8,128)(2,1)S(1)}, u32[]{:S(2)}, u32[]{:S(2)}) async-start(bf16[4,512,512]{2,1,0:T(8,128)(2,1)} %broadcast_in_dim.6), calls=%async_computation | async-start | bytes 4194304 | tf_op jit(solution)/shard_map/all_to_all | solution.py:29
  39.0 22.4 %all-to-all-done.tokens = bf16[4,512,512]{2,1,0:T(8,128)(2,1)S(1)} async-done(((bf16[4,512,512]{2,1,0:T(8,128)(2,1)}), bf16[4,512,512]{2,1,0:T(8,128)(2,1)S(1)}, u32[]{:S(2)}, u32[]{:S(2)}) %all-to-all-start) | async-done | bytes 2097184 | tf_op jit(solution)/shard_map/all_to_all | solution.py:29
  61.4 4.6 %all-gather.2.cloned.1.call-done.weights = bf16[16,2,3,64,512]{4,3,2,1,0:T(8,128)(2,1)} async-done(((bf16[1,2,3,64,512]{4,3,2,1,0:T(8,128)(2,1)}), bf16[16,2,3,64,512]{4,3,2,1,0:T(8,128)(2,1)}) %all-gather.2.cloned.1.call-update) | async-done | bytes 6291472 | tf_op jit(solution)/shard_map/all_gather | solution.py:208
  66.0 7.3 %shard_map.118 = (bf16[4,4,2,32,512]{4,3,2,1,0:T(8,128)(2,1)S(1)}, bf16[4,2,32,512]{3,2,1,0:T(8,128)(2,1)S(1)}, bf16[4,2,32,512]{3,2,1,0:T(8,128)(2,1)S(1)}, bf1...) custom-call(s32[3]{0:T(128)S(1)} %pad_add_fusion.place, bf16[4,512,512]{2,1,0:T(8,128)(2,1)S(1)} %all-to-all-done.tokens, ...), custom_call_target="tpu_custom_call" | custom-call | flops 3221225472 | bytes 10485760 | tf_op jit(solution)/shard_map/pallas_call | solution.py:80
  73.4 1.0 copy-done.10
  76.5 4.8 %all-to-all-start.1 = ((bf16[4,4,2,32,512]{4,3,2,1,0:T(8,128)(2,1)}), bf16[4,4,2,32,512]{4,3,2,1,0:T(8,128)(2,1)S(1)}, u32[]{:S(2)}, u32[]{:S(2)}) async-start(bf16[4,4,2,32,512]{4,3,2,1,0:T(8,128)(2,1)} %copy-done.10), calls=%async_computation.1 | async-start | bytes 2097152 | tf_op jit(solution)/shard_map/all_to_all | solution.py:223
  81.3 1.0 slice_select_fusion
  83.6 11.1 %all-to-all-done.1.left = bf16[4,4,2,32,512]{4,3,2,1,0:T(8,128)(2,1)S(1)} async-done(((bf16[4,4,2,32,512]{4,3,2,1,0:T(8,128)(2,1)}), bf16[4,4,2,32,512]{4,3,2,1,0:T(8,128)(2,1)S(1)}, u32[]{:S(2)}, u32[]{:S(2)}) %all-to-all-start.1) | async-done | bytes 1048608 | tf_op jit(solution)/shard_map/all_to_all | solution.py:223
  94.7 1.8 broadcast_in_dim.8
  96.5 6.2 %all-to-all-start.3 = ((bf16[4,144,512]{2,1,0:T(8,128)(2,1)}), bf16[4,144,512]{2,1,0:T(8,128)(2,1)}, u32[]{:S(2)}, u32[]{:S(2)}) async-start(bf16[4,144,512]{2,1,0:T(8,128)(2,1)} %broadcast_in_dim.8), calls=%async_computation.3 | async-start | bytes 1179648 | tf_op jit(solution)/shard_map/all_to_all | solution.py:29
  102.7 1.5 collective-permute-start.4
  104.2 2.7 %collective-permute-start.5 = (bf16[4,2,32,512]{3,2,1,0:T(8,128)(2,1)}, bf16[4,2,32,512]{3,2,1,0:T(8,128)(2,1)S(1)}, u32[]{:S(2)}, u32[]{:S(2)}) collective-permute-start(bf16[4,2,32,512]{3,2,1,0:T(8,128)(2,1)} %copy-done.13), channel_id=1, source_target_pairs={{0,128},{4,132},{128,0},{132,4},{1,129},{5,133},{129,1},{133,5},{2... | collective-permute-start | bytes 786440 | tf_op jit(solution)/shard_map/ppermute | solution.py:24
  107.4 4.8 %collective-permute-done.4.r1 = bf16[4,2,32,512]{3,2,1,0:T(8,128)(2,1)S(1)} collective-permute-done((bf16[4,2,32,512]{3,2,1,0:T(8,128)(2,1)}, bf16[4,2,32,512]{3,2,1,0:T(8,128)(2,1)S(1)}, u32[]{:S(2)}, u32[]{:S(2)}) %collective-permute-start.4) | collective-permute-done | bytes 262176 | tf_op jit(solution)/shard_map/ppermute | solution.py:24
  112.2 5.7 %collective-permute-done.5.r2 = bf16[4,2,32,512]{3,2,1,0:T(8,128)(2,1)S(1)} collective-permute-done((bf16[4,2,32,512]{3,2,1,0:T(8,128)(2,1)}, bf16[4,2,32,512]{3,2,1,0:T(8,128)(2,1)S(1)}, u32[]{:S(2)}, u32[]{:S(2)}) %collective-permute-start.5) | collective-permute-done | bytes 262176 | tf_op jit(solution)/shard_map/ppermute | solution.py:24
  117.9 2.6 %collective-permute-done.6.r3 = bf16[4,2,32,512]{3,2,1,0:T(8,128)(2,1)S(1)} collective-permute-done((bf16[4,2,32,512]{3,2,1,0:T(8,128)(2,1)}, bf16[4,2,32,512]{3,2,1,0:T(8,128)(2,1)S(1)}, u32[]{:S(2)}, u32[]{:S(2)}) %collective-permute-start.6) | collective-permute-done | bytes 262176 | tf_op jit(solution)/shard_map/ppermute | solution.py:24
  120.5 0.8 shard_map.119
  123.3 4.8 %all-to-all-start.2 = ((bf16[4,2,32,512]{3,2,1,0:T(8,128)(2,1)}), bf16[4,2,32,512]{3,2,1,0:T(8,128)(2,1)S(1)}, u32[]{:S(2)}, u32[]{:S(2)}) async-start(bf16[4,2,32,512]{3,2,1,0:T(8,128)(2,1)} %copy-done.11), calls=%async_computation.2 | async-start | bytes 524288 | tf_op jit(solution)/shard_map/all_to_all | solution.py:235
  128.1 0.8 slice.21
  128.9 1.9 %collective-permute-start.8 = (bf16[2,32,512]{2,1,0:T(8,128)(2,1)}, bf16[2,32,512]{2,1,0:T(8,128)(2,1)S(1)}, u32[]{:S(2)}, u32[]{:S(2)}) collective-permute-start(bf16[2,32,512]{2,1,0:T(8,128)(2,1)} %copy-done.15), channel_id=1, source_target_pairs={{0,128},{4,132},{128,0},{132,4},{1,129},{5,133},{129,1},{133,5},{2... | collective-permute-start | bytes 196616 | tf_op jit(solution)/shard_map/ppermute | solution.py:24
  130.8 2.8 %collective-permute-start.9 = (bf16[2,32,512]{2,1,0:T(8,128)(2,1)S(1)}, bf16[2,32,512]{2,1,0:T(8,128)(2,1)S(1)}, u32[]{:S(2)}, u32[]{:S(2)}) collective-permute-start(bf16[2,32,512]{2,1,0:T(8,128)(2,1)S(1)} %get-tuple-element.27), channel_id=1, source_target_pairs={{0,132},{4,128},{128,4},{132,0},{1,133},{5,129},{129,5},{133,1},{2... | collective-permute-start | bytes 196616 | tf_op jit(solution)/shard_map/ppermute | solution.py:24
  133.6 1.3 collective-permute-done.8.l2
  135.0 1.3 collective-permute-done.9.l3
  136.3 1.0 shard_map.120.after
  137.3 4.8 %all-to-all-start.4 = ((bf16[4,32,2048]{2,1,0:T(8,128)(2,1)}), bf16[4,32,2048]{2,1,0:T(8,128)(2,1)S(1)}, u32[]{:S(2)}, u32[]{:S(2)}) async-start(bf16[4,32,2048]{2,1,0:T(8,128)(2,1)} %shard_map.120.after), calls=%async_computation.4 | async-start | bytes 1048576 | tf_op jit(solution)/shard_map/all_to_all | solution.py:264
  142.7 1.1 slice.22.tokens
  143.8 1.6 copy-done.1
  145.4 1.6 copy-done.2
  147.0 1.6 copy-done.3
  148.6 1.0 shard_map.121
  149.6 1.3 copy-done.4
  150.9 1.4 copy-done.6
  152.3 1.4 copy-done.8
  153.7 1.6 copy-done.5
  155.3 1.6 copy-done.7
  156.8 1.6 copy-done.9
  158.4 2.9 %shard_map.122 = bf16[4,128,512]{2,1,0:T(8,128)(2,1)} custom-call(s32[1]{0:T(128)} %dynamic_slice.19.lengths, bf16[128,512]{1,0:T(8,128)(2,1)S(1)} %get-tuple-element.29.query, bf16[128,2048]{1,0:T(8,128)(2,1)S(1)} %bitcast.20, bf16[2048,512]{1,0:T(8,128)(2,1)S(1)} %copy-done.5, bf16[2048,512]{1,0:T(8,128)(2,1)S(1)} %copy-done.7, bf16[512,2048]{1,0:T(8,128)(2,1)S(1)} %copy-done.9), custom_call_target="tpu_custom_call" | custom-call | flops 805306368 | bytes 10485760 | tf_op jit(solution)/shard_map/pallas_call | solution.py:266
  161.4 4.8 %all-to-all-start.5 = ((bf16[4,128,512]{2,1,0:T(8,128)(2,1)}), bf16[4,128,512]{2,1,0:T(8,128)(2,1)S(1)}, u32[]{:S(2)}, u32[]{:S(2)}) async-start(bf16[4,128,512]{2,1,0:T(8,128)(2,1)} %shard_map.122), calls=%async_computation.5 | async-start | bytes 1048576 | tf_op jit(solution)/shard_map/all_to_all | solution.py:277
  166.2 6.0 %all-to-all-done.5 = bf16[4,128,512]{2,1,0:T(8,128)(2,1)S(1)} async-done(((bf16[4,128,512]{2,1,0:T(8,128)(2,1)}), bf16[4,128,512]{2,1,0:T(8,128)(2,1)S(1)}, u32[]{:S(2)}, u32[]{:S(2)}) %all-to-all-start.5) | async-done | bytes 524320 | tf_op jit(solution)/shard_map/all_to_all | solution.py:277
  173.1 4.3 %collective-permute-done.10 = bf16[128,512]{1,0:T(8,128)(2,1)S(1)} collective-permute-done((bf16[128,512]{1,0:T(8,128)(2,1)S(1)}, bf16[128,512]{1,0:T(8,128)(2,1)S(1)}, u32[]{:S(2)}, u32[]{:S(2)}) %collective-permute-start.10) | collective-permute-done | bytes 131104 | tf_op jit(solution)/shard_map/ppermute | solution.py:24
  (67 shorter events, 8.7 us)
Async XLA Ops:
  6.5 10.4 %copy-start.19 = (bf16[1,2,128,512]{3,2,1,0:T(8,128)(2,1)S(1)}, bf16[1,2,128,512]{3,2,1,0:T(8,128)(2,1)}, u32[]{:S(2)}) copy-start(bf16[1,2,128,512]{3,2,1,0:T(8,128)(2,1)} %param.12) | copy-start | bytes 786436
  6.5 59.5 %all-gather.2.cloned.1.call-start = ((), (), s32[]{:S(2)}) async-start(), calls=%async_computation.6 | async-start | bytes 6684672 | tf_op jit(solution)/shard_map/all_gather | solution.py:208
  7.8 8.2 %collective-permute-start.3 = (bf16[3,64,512]{2,1,0:T(8,128)(2,1)S(1)}, bf16[3,64,512]{2,1,0:T(8,128)(2,1)S(1)}, u32[]{:S(2)}, u32[]{:S(2)}) collective-permute-start(bf16[3,64,512]{2,1,0:T(8,128)(2,1)S(1)} %get-tuple-element.38), channel_id=1, source_target_pairs={{0,128},{128,0},{1,129},{129,1},{2,130},{130,2},{3,131},{131,3},{4... | collective-permute-start | bytes 589832 | tf_op jit(solution)/shard_map/ppermute | solution.py:24
  16.9 7.8 %collective-permute-start = (bf16[256,512]{1,0:T(8,128)(2,1)S(1)}, bf16[256,512]{1,0:T(8,128)(2,1)S(1)}, u32[]{:S(2)}, u32[]{:S(2)}) collective-permute-start(bf16[256,512]{1,0:T(8,128)(2,1)S(1)} %bitcast.24), channel_id=1, source_target_pairs={{0,4},{4,0},{1,5},{5,1},{2,6},{6,2},{3,7},{7,3},{8,12},{12,8},{9,1... | collective-permute-start | bytes 786440 | tf_op jit(solution)/shard_map/ppermute | solution.py:24
  18.6 13.7 %collective-permute-start.1 = (bf16[256,512]{1,0:T(8,128)(2,1)S(1)}, bf16[256,512]{1,0:T(8,128)(2,1)S(1)}, u32[]{:S(2)}, u32[]{:S(2)}) collective-permute-start(bf16[256,512]{1,0:T(8,128)(2,1)S(1)} %bitcast.25), channel_id=1, source_target_pairs={{0,128},{128,0},{1,129},{129,1},{2,130},{130,2},{3,131},{131,3},{8... | collective-permute-start | bytes 786440 | tf_op jit(solution)/shard_map/ppermute | solution.py:24
  23.4 8.9 %collective-permute-start.2 = (bf16[256,512]{1,0:T(8,128)(2,1)S(1)}, bf16[256,512]{1,0:T(8,128)(2,1)S(1)}, u32[]{:S(2)}, u32[]{:S(2)}) collective-permute-start(bf16[256,512]{1,0:T(8,128)(2,1)S(1)} %bitcast.26), channel_id=1, source_target_pairs={{0,132},{128,4},{1,133},{129,5},{2,134},{130,6},{3,135},{131,7},{8... | collective-permute-start | bytes 786440 | tf_op jit(solution)/shard_map/ppermute | solution.py:24
  24.7 9.3 %copy-start.20 = (bf16[256,512]{1,0:T(8,128)(2,1)}, bf16[256,512]{1,0:T(8,128)(2,1)S(1)}, u32[]{:S(2)}) copy-start(bf16[256,512]{1,0:T(8,128)(2,1)S(1)} %collective-permute-done) | copy-start | bytes 786436
  34.0 4.9 %copy-start.21 = (bf16[2048]{0:T(1024)(128)(2,1)S(1)}, bf16[2048]{0:T(1024)(128)(2,1)}, u32[]{:S(2)}) copy-start(bf16[2048]{0:T(1024)(128)(2,1)} %param.14) | copy-start | bytes 12292
  34.0 27.4 %all-to-all-start = ((bf16[4,512,512]{2,1,0:T(8,128)(2,1)}), bf16[4,512,512]{2,1,0:T(8,128)(2,1)S(1)}, u32[]{:S(2)}, u32[]{:S(2)}) async-start(bf16[4,512,512]{2,1,0:T(8,128)(2,1)} %broadcast_in_dim.6), calls=%async_computation | async-start | bytes 4194304 | tf_op jit(solution)/shard_map/all_to_all | solution.py:29
  73.3 1.0 copy-start.10
  74.3 0.7 copy-start.12
  75.1 0.7 copy-start.14
  75.8 0.7 copy-start.13
  75.8 6.5 %copy-start.23 = (bf16[512]{0:T(512)(128)(2,1)S(1)}, bf16[512]{0:T(512)(128)(2,1)}, u32[]{:S(2)}) copy-start(bf16[512]{0:T(512)(128)(2,1)} %param.18) | copy-start | bytes 3076
  76.5 18.2 %all-to-all-start.1 = ((bf16[4,4,2,32,512]{4,3,2,1,0:T(8,128)(2,1)}), bf16[4,4,2,32,512]{4,3,2,1,0:T(8,128)(2,1)S(1)}, u32[]{:S(2)}, u32[]{:S(2)}) async-start(bf16[4,4,2,32,512]{4,3,2,1,0:T(8,128)(2,1)} %copy-done.10), calls=%async_computation.1 | async-start | bytes 2097152 | tf_op jit(solution)/shard_map/all_to_all | solution.py:223
  82.3 0.6 copy-start.17
  96.5 26.7 %all-to-all-start.3 = ((bf16[4,144,512]{2,1,0:T(8,128)(2,1)}), bf16[4,144,512]{2,1,0:T(8,128)(2,1)}, u32[]{:S(2)}, u32[]{:S(2)}) async-start(bf16[4,144,512]{2,1,0:T(8,128)(2,1)} %broadcast_in_dim.8), calls=%async_computation.3 | async-start | bytes 1179648 | tf_op jit(solution)/shard_map/all_to_all | solution.py:29
  102.7 9.5 %collective-permute-start.4 = (bf16[4,2,32,512]{3,2,1,0:T(8,128)(2,1)}, bf16[4,2,32,512]{3,2,1,0:T(8,128)(2,1)S(1)}, u32[]{:S(2)}, u32[]{:S(2)}) collective-permute-start(bf16[4,2,32,512]{3,2,1,0:T(8,128)(2,1)} %copy-done.14), channel_id=1, source_target_pairs={{0,4},{4,0},{128,132},{132,128},{1,5},{5,1},{129,133},{133,129},{2... | collective-permute-start | bytes 786440 | tf_op jit(solution)/shard_map/ppermute | solution.py:24
  104.2 13.7 %collective-permute-start.5 = (bf16[4,2,32,512]{3,2,1,0:T(8,128)(2,1)}, bf16[4,2,32,512]{3,2,1,0:T(8,128)(2,1)S(1)}, u32[]{:S(2)}, u32[]{:S(2)}) collective-permute-start(bf16[4,2,32,512]{3,2,1,0:T(8,128)(2,1)} %copy-done.13), channel_id=1, source_target_pairs={{0,128},{4,132},{128,0},{132,4},{1,129},{5,133},{129,1},{133,5},{2... | collective-permute-start | bytes 786440 | tf_op jit(solution)/shard_map/ppermute | solution.py:24
  106.9 13.5 %collective-permute-start.6 = (bf16[4,2,32,512]{3,2,1,0:T(8,128)(2,1)}, bf16[4,2,32,512]{3,2,1,0:T(8,128)(2,1)S(1)}, u32[]{:S(2)}, u32[]{:S(2)}) collective-permute-start(bf16[4,2,32,512]{3,2,1,0:T(8,128)(2,1)} %copy-done.12), channel_id=1, source_target_pairs={{0,132},{4,128},{128,4},{132,0},{1,133},{5,129},{129,5},{133,1},{2... | collective-permute-start | bytes 786440 | tf_op jit(solution)/shard_map/ppermute | solution.py:24
  120.5 21.6 %copy-start.22 = (bf16[2048]{0:T(1024)(128)(2,1)S(1)}, bf16[2048]{0:T(1024)(128)(2,1)}, u32[]{:S(2)}) copy-start(bf16[2048]{0:T(1024)(128)(2,1)} %param.19) | copy-start | bytes 12292
  120.5 21.6 %copy-start.24 = (s32[2]{0:T(128)S(1)}, s32[2]{0:T(128)}, u32[]{:S(2)}) copy-start(s32[2]{0:T(128)} %param.13) | copy-start | bytes 28
  121.3 0.7 copy-start.11
  122.0 0.6 copy-start.15
  122.6 0.6 copy-start.16
  123.3 13.0 %all-to-all-start.2 = ((bf16[4,2,32,512]{3,2,1,0:T(8,128)(2,1)}), bf16[4,2,32,512]{3,2,1,0:T(8,128)(2,1)S(1)}, u32[]{:S(2)}, u32[]{:S(2)}) async-start(bf16[4,2,32,512]{3,2,1,0:T(8,128)(2,1)} %copy-done.11), calls=%async_computation.2 | async-start | bytes 524288 | tf_op jit(solution)/shard_map/all_to_all | solution.py:235
  128.8 4.8 %collective-permute-start.7 = (bf16[2,32,512]{2,1,0:T(8,128)(2,1)}, bf16[2,32,512]{2,1,0:T(8,128)(2,1)S(1)}, u32[]{:S(2)}, u32[]{:S(2)}) collective-permute-start(bf16[2,32,512]{2,1,0:T(8,128)(2,1)} %copy-done.16), channel_id=1, source_target_pairs={{0,4},{4,0},{128,132},{132,128},{1,5},{5,1},{129,133},{133,129},{2... | collective-permute-start | bytes 196616 | tf_op jit(solution)/shard_map/ppermute | solution.py:24
  128.9 6.1 %collective-permute-start.8 = (bf16[2,32,512]{2,1,0:T(8,128)(2,1)}, bf16[2,32,512]{2,1,0:T(8,128)(2,1)S(1)}, u32[]{:S(2)}, u32[]{:S(2)}) collective-permute-start(bf16[2,32,512]{2,1,0:T(8,128)(2,1)} %copy-done.15), channel_id=1, source_target_pairs={{0,128},{4,132},{128,0},{132,4},{1,129},{5,133},{129,1},{133,5},{2... | collective-permute-start | bytes 196616 | tf_op jit(solution)/shard_map/ppermute | solution.py:24
  130.8 5.5 %collective-permute-start.9 = (bf16[2,32,512]{2,1,0:T(8,128)(2,1)S(1)}, bf16[2,32,512]{2,1,0:T(8,128)(2,1)S(1)}, u32[]{:S(2)}, u32[]{:S(2)}) collective-permute-start(bf16[2,32,512]{2,1,0:T(8,128)(2,1)S(1)} %get-tuple-element.27), channel_id=1, source_target_pairs={{0,132},{4,128},{128,4},{132,0},{1,133},{5,129},{129,5},{133,1},{2... | collective-permute-start | bytes 196616 | tf_op jit(solution)/shard_map/ppermute | solution.py:24
  133.6 10.2 %copy-start = (bf16[2048,512]{1,0:T(8,128)(2,1)S(1)}, bf16[2048,512]{1,0:T(8,128)(2,1)}, u32[]{:S(2)}) copy-start(bf16[2048,512]{1,0:T(8,128)(2,1)} %wq.1) | copy-start | bytes 6291460
  137.3 16.4 %all-to-all-start.4 = ((bf16[4,32,2048]{2,1,0:T(8,128)(2,1)}), bf16[4,32,2048]{2,1,0:T(8,128)(2,1)S(1)}, u32[]{:S(2)}, u32[]{:S(2)}) async-start(bf16[4,32,2048]{2,1,0:T(8,128)(2,1)} %shard_map.120.after), calls=%async_computation.4 | async-start | bytes 1048576 | tf_op jit(solution)/shard_map/all_to_all | solution.py:264
  143.8 1.6 copy-start.1
  145.4 1.6 copy-start.2
  147.0 1.6 copy-start.3
  149.6 1.3 copy-start.4
  150.9 1.4 copy-start.6
  152.3 1.4 copy-start.8
  153.7 1.6 copy-start.5
  155.3 1.6 copy-start.7
  156.8 1.6 copy-start.9
  158.4 13.8 %copy-start.18 = (bf16[128,512]{1,0:T(8,128)(2,1)S(1)}, bf16[128,512]{1,0:T(8,128)(2,1)}, u32[]{:S(2)}) copy-start(bf16[128,512]{1,0:T(8,128)(2,1)} %copy-done.17) | copy-start | bytes 393220
  161.4 10.8 %all-to-all-start.5 = ((bf16[4,128,512]{2,1,0:T(8,128)(2,1)}), bf16[4,128,512]{2,1,0:T(8,128)(2,1)S(1)}, u32[]{:S(2)}, u32[]{:S(2)}) async-start(bf16[4,128,512]{2,1,0:T(8,128)(2,1)} %shard_map.122), calls=%async_computation.5 | async-start | bytes 1048576 | tf_op jit(solution)/shard_map/all_to_all | solution.py:277
  172.4 5.1 %collective-permute-start.10 = (bf16[128,512]{1,0:T(8,128)(2,1)S(1)}, bf16[128,512]{1,0:T(8,128)(2,1)S(1)}, u32[]{:S(2)}, u32[]{:S(2)}) collective-permute-start(bf16[128,512]{1,0:T(8,128)(2,1)S(1)} %get-tuple-element.33), channel_id=1, source_target_pairs={{0,4},{4,0},{1,5},{5,1},{2,6},{6,2},{3,7},{7,3},{8,12},{12,8},{9,1... | collective-permute-start | bytes 393224 | tf_op jit(solution)/shard_map/ppermute | solution.py:24
Sparse Core Ops, SparseCore 0:
  17.0 48.9 all-gather.1

commit v3 on v1

v3 whole, which is shorter than its diff:
```python
import jax
import jax.numpy as jnp
import numpy as np
from jax import lax
from jax.experimental import pallas as pl
from jax.experimental.pallas import tpu as pltpu
from jax.sharding import Mesh, PartitionSpec as P

HEAD_DIM = 256
epsilon = 1e-06
SIZES = {"yh": 2, "z": 8, "c": 2, "p": 2, "x": 4}
PLANE = ("yh", "p", "x")
bf16, f32 = jnp.bfloat16, jnp.float32
MIB = 1 << 20


def moved(value, axes, route):
    dims = [SIZES[a] for a in axes]
    pairs = []
    for at in np.ndindex(*dims):
        to = route(*at)
        if to is not None:
            pairs.append((int(np.ravel_multi_index(at, dims)), int(np.ravel_multi_index(to, dims))))
    return lax.ppermute(value, axes, pairs)


def passed(value):
    return moved(
        value, ("z", "c"), lambda z, c: ((z + 1) % 8, c) if c == 0 else ((z - 1) % 8, c)
    )


def after(value, *others):
    def kernel(*refs):
        del refs

    return pl.pallas_call(
        kernel,
        in_specs=[anyplace()] * (1 + len(others)),
        out_specs=anyplace(),
        out_shape=jax.ShapeDtypeStruct(value.shape, value.dtype),
        input_output_aliases={0: 0},
        compiler_params=params(),
    )(value, *others)


def gather_lines(near, far, *ready):
    near, far = [near], [far]
    for k in range(3):
        near.append(after(passed(near[k]), *ready[k]))
        far.append(passed(far[k]))
    near.append(passed(near[3][:192]))
    far.append(passed(far[3][:192]))
    return [v for line in (near, far) for v in line + [twin(chunk) for chunk in line[1:]]]


def opposite(value):
    return moved(value, ("yh", "p"), lambda a, b: (1 - a, 1 - b))


def around(value):
    return [value] + [moved(value, ("x",), lambda a: ((a + k) % 4,)) for k in (1, 2, 3)]


def twin(value):
    return moved(value, ("c",), lambda a: (1 - a,))


def whole(shape):
    return pl.BlockSpec(shape, lambda *_: (0,) * len(shape))


def params(mib=60):
    return pltpu.CompilerParams(vmem_limit_bytes=mib * MIB)


def smem():
    return pl.BlockSpec(memory_space=pltpu.SMEM)


def vmem():
    return pl.BlockSpec(memory_space=pltpu.VMEM)


def anyplace():
    return pl.BlockSpec(memory_space=pl.ANY)


CHUNKS = 9


def normed_block(block, scale, gain):
    return (block[...].astype(f32) * scale * gain.astype(f32)).astype(bf16)


def scale_of(blocks):
    square = 0.0
    for block in blocks:
        t = block[...].astype(f32)
        square = square + jnp.sum(t * t, axis=-1, keepdims=True)
    return lax.rsqrt(square * (1.0 / 2048) + epsilon)


def ffn_kernel(place, *refs):
    tokens, gain, refs = refs[:8], refs[8], refs[9:]
    chunks, (out, held, normed, sems) = refs[: 2 * CHUNKS], refs[2 * CHUNKS :]
    yh, x, z, c = place[0], place[2], place[3], place[4]
    first = pl.program_id(0) == 0
    ways = [(m, side) for side in range(2) for m in range(2)] + [(2, 0), (2, 1)]

    @pl.when(first)
    def _():
        for m, side in ways:
            for k in range(CHUNKS):
                chunk = chunks[side * CHUNKS + k]
                step, core = (k, c) if k < 5 else (k - 4, 1 - c)
                at = (z - step * (1 - 2 * core)) & 7
                for half in range(chunk.shape[0] // 192):
                    source = chunk.at[pl.ds(half * 192 + m * 64, 64)]
                    target = held.at[m, side, at, core ^ half]
                    pltpu.make_async_copy(source, target, sems.at[m, side]).start()

    def wait(*those):
        @pl.when(first)
        def _():
            for spot in those:
                pltpu.make_async_copy(held.at[spot], held.at[spot], sems.at[spot]).wait()

    for i in range(2):

        @pl.when(pl.program_id(0) == i)
        def _():
            blocks = tokens[i * 4 : (i + 1) * 4]
            scale = scale_of(blocks)
            for k, block in enumerate(blocks):
                b = (x - k) & 3
                normed[b] = normed_block(block, scale, gain[b])

    gate = lift = 0.0
    for side in range(2):
        b = (yh ^ side) * 2
        n = jnp.concatenate([normed[b], normed[b + 1]], 1)
        wait((0, side), (1, side))
        gate += jnp.dot(n, held[0, side].reshape(1024, 512), preferred_element_type=f32)
        lift += jnp.dot(n, held[1, side].reshape(1024, 512), preferred_element_type=f32)
    inner = 0.7978845608028654 * (gate + 0.044715 * (gate * gate * gate))
    hidden = (0.5 * gate * (1.0 + jnp.tanh(inner)) * lift).astype(bf16)
    wait((2, 0), (2, 1))
    for side in range(2):
        for k in range(2):
            rows = held[2, side, k * 4 : (k + 1) * 4].reshape(512, 512)
            part = lax.dot_general(
                hidden, rows, (((1,), (1,)), ((), ())), preferred_element_type=f32
            )
            out[:, (yh ^ side) * 2 + k] = part.astype(bf16).reshape(8, 32, 512)


def ffn(place, tokens, gain, chunks):
    grid_spec = pltpu.PrefetchScalarGridSpec(
        num_scalar_prefetch=1,
        grid=(2,),
        in_specs=[pl.BlockSpec((256, 512), lambda i, place: (0, 0))] * 8
        + [whole(gain.shape)]
        + [anyplace()] * len(chunks),
        out_specs=pl.BlockSpec((8, 4, 32, 512), lambda i, place: (place[0] ^ i, 0, 0, 0)),
        scratch_shapes=[
            pltpu.VMEM((3, 2, 8, 2, 64, 512), bf16),
            pltpu.VMEM((4, 256, 512), bf16),
            pltpu.SemaphoreType.DMA((3, 2)),
        ],
    )
    return pl.pallas_call(
        ffn_kernel,
        grid_spec=grid_spec,
        out_shape=jax.ShapeDtypeStruct((16, 4, 32, 512), bf16),
        compiler_params=params(),
        cost_estimate=pl.CostEstimate(
            flops=512 * 2048 * 512 * 6, bytes_accessed=10 * MIB, transcendentals=512 * 512
        ),
    )(place, *tokens, gain, *chunks)


def memory_kernel(place, terms, tokens, gain, out):
    square, kept = 0.0, []
    for i in range(4):
        b = (place[2] - i) & 3
        total = terms[0, b].astype(f32)
        for k in range(1, 16):
            total = total + terms[k, b].astype(f32)
        merged = tokens[i].astype(f32) + total
        square = square + jnp.sum(merged * merged, axis=-1, keepdims=True)
        kept.append(merged)
    scale = lax.rsqrt(square * (1.0 / 2048) + epsilon)
    for i in range(4):
        at = pl.ds(pl.multiple_of(((place[2] - i) & 3) * 512, 512), 512)
        rounded = (kept[i] * scale * gain[i : i + 1].astype(f32)).astype(bf16)
        for k in range(4):
            out[k, :, at] = rounded


def memory_rows(place, terms, tokens, gain):
    return pl.pallas_call(
        memory_kernel,
        in_specs=[smem()] + [vmem()] * 3,
        out_specs=vmem(),
        out_shape=jax.ShapeDtypeStruct((4, 32, 2048), bf16),
        compiler_params=params(16),
    )(place, terms, tokens, gain)


def query_kernel(place, t0, t1, t2, t3, gain, weight, out):
    blocks = (t0, t1, t2, t3)
    scale = scale_of(blocks)
    total = 0.0
    for k, block in enumerate(blocks):
        b = (place[2] - k) & 3
        rows = weight[pl.ds(pl.multiple_of(b * 512, 512), 512), :]
        n = normed_block(block, scale, gain[b])
        total += jnp.dot(n, rows, preferred_element_type=f32)
    out[...] = total.astype(bf16)


def query_rows(place, tokens, gain, weight):
    grid_spec = pltpu.PrefetchScalarGridSpec(
        num_scalar_prefetch=1,
        grid=(1,),
        in_specs=[pl.BlockSpec((128, 512), lambda i, place: (2, 0))] * 4
        + [whole(gain.shape), whole(weight.shape)],
        out_specs=whole((128, 512)),
    )
    return pl.pallas_call(
        query_kernel,
        grid_spec=grid_spec,
        out_shape=jax.ShapeDtypeStruct((128, 512), bf16),
        compiler_params=params(),
        cost_estimate=pl.CostEstimate(
            flops=2 * 128 * 2048 * 512, bytes_accessed=3 * MIB, transcendentals=0
        ),
    )(place, *tokens, gain, weight)


def attention_kernel(place, lengths, query, memory, wk, wv, wo, out, columns, held, sems):
    held_in, held_out = held
    columns[...] = memory[:, pl.ds(pl.multiple_of(place[2] * 512, 512), 512)]
    copies = []
    for k in range(8):
        source = (wk, wv)[k // 4].at[pl.ds((k % 4) * 512, 512)]
        copies.append(pltpu.make_async_copy(source, held_in.at[k], sems.at[k]))
    for k in range(2):
        rows = pl.ds(k * 256, 256)
        copies.append(pltpu.make_async_copy(wo.at[rows], held_out.at[rows], sems.at[8 + k]))
    for copy in copies:
        copy.start()
    made = []
    for m in range(2):
        total = 0.0
        for k in range(4):
            copies[m * 4 + k].wait()
            total += jnp.dot(
                memory[:, k * 512 : (k + 1) * 512], held_in[m * 4 + k], preferred_element_type=f32
            )
        made.append(total.astype(bf16))
    keys, values = made
    positions = lax.broadcasted_iota(jnp.int32, (128, 128), 1)
    valid = positions < lengths[place[1]]
    contexts = []
    for h in range(2):
        at = slice(h * HEAD_DIM, (h + 1) * HEAD_DIM)
        scores = lax.dot_general(
            query[:, at], keys[:, at], (((1,), (1,)), ((), ())), preferred_element_type=f32
        )
        scores = jnp.where(valid, scores, -1e30)
        weights = jnp.exp(scores - jnp.max(scores, axis=-1, keepdims=True))
        probs = (weights / jnp.sum(weights, axis=-1, keepdims=True)).astype(bf16)
        contexts.append(jnp.dot(probs, values[:, at], preferred_element_type=f32).astype(bf16))
    copies[8].wait()
    copies[9].wait()
    context = jnp.concatenate(contexts, axis=1)
    for b in range(4):
        part = jnp.dot(
            context, held_out[:, b * 512 : (b + 1) * 512], preferred_element_type=f32
        )
        out[b] = part.astype(bf16)


def attention(place, lengths, query, memory, wk, wv, wo):
    return pl.pallas_call(
        attention_kernel,
        in_specs=[smem()] * 2 + [vmem()] * 2 + [anyplace()] * 3,
        out_specs=[vmem()] * 2,
        out_shape=[
            jax.ShapeDtypeStruct((4, 128, 512), bf16),
            jax.ShapeDtypeStruct((128, 512), bf16),
        ],
        scratch_shapes=[
            (pltpu.VMEM((8, 512, 512), bf16), pltpu.VMEM((512, 2048), bf16)),
            pltpu.SemaphoreType.DMA((10,)),
        ],
        compiler_params=params(),
        cost_estimate=pl.CostEstimate(
            flops=6 * 128 * 2048 * 512, bytes_accessed=8 * MIB, transcendentals=128 * 256
        ),
    )(place, lengths, query, memory, wk, wv, wo)


def shards(
    streams,
    lengths,
    encoder_gain,
    ffn_gate,
    ffn_lift,
    ffn_down,
    final_gain,
    decoder_gain,
    query_weight,
    key_weight,
    value_weight,
    output_weight,
):
    place = jnp.stack([lax.axis_index(a) for a in ("yh", "p", "x", "z", "c")]).astype(jnp.int32)
    p, x = place[1], place[2]
    local = streams[0].reshape(256, 512)

    def quarter(yh, p):
        start = (p * 2 + yh) * 512
        return jnp.concatenate(
            [lax.dynamic_slice_in_dim(w, start, 512, 1) for w in (ffn_gate, ffn_lift, ffn_down.T)]
        )

    own, rest = quarter(place[0], p), opposite(quarter(1 - place[0], 1 - p))
    near, far = jnp.concatenate([own, twin(own)]), jnp.concatenate([rest, twin(rest)])

    swapped = moved(local, ("p",), lambda a: (1 - a,))
    mine = jnp.where(p == 0, local, swapped)
    theirs = opposite(mine)
    decoding = jnp.where(p == 0, swapped[:128], local[128:])
    gain_rows = jnp.broadcast_to(final_gain[None], (16, 512))
    tokens = around(jnp.concatenate([mine, decoding, gain_rows]))
    others = around(theirs)
    chunks = gather_lines(near, far, (swapped,), (theirs,), tokens[1:] + others[1:])

    terms = ffn(place, tokens + others, encoder_gain.reshape(4, 1, 512), chunks)
    terms = lax.all_to_all(terms, ("yh", "p", "x"), 0, 0)
    query = query_rows(place, tokens, decoder_gain.reshape(4, 1, 512), query_weight)
    rows = [lax.dynamic_slice_in_dim(t, (p * 4 + x) * 32, 32, 0) for t in tokens]
    gains = [t[384] for t in tokens]
    memory = memory_rows(place, terms, jnp.stack(rows), jnp.stack(gains))
    memory = lax.all_to_all(memory, "x", 0, 0).reshape(128, 2048)
    attended, columns = attention(
        place, lengths, query, memory, key_weight, value_weight, output_weight
    )
    attended = lax.all_to_all(attended, "x", 0, 0)
    summed = jnp.sum(attended.astype(f32), axis=0)
    decoded = (decoding.astype(f32) + summed).astype(bf16)
    swapped = moved(jnp.where(p == 0, decoded, columns), ("p",), lambda a: (1 - a,))
    first = jnp.where(p == 0, columns, swapped)
    second = jnp.where(p == 0, swapped, decoded)
    return jnp.concatenate([first, second]).reshape(1, 2, 128, 512)


def solution(mesh):
    names = tuple(SIZES)
    fine = Mesh(mesh.devices.reshape(tuple(SIZES.values())), names)
    dp = ("yh", "z", "c")
    placed = (
        P("p", dp, None, "x"),
        P(dp),
        P(),
        P(dp, "x"),
        P(dp, "x"),
        P("x", dp),
        P("x"),
        P(),
        P(None, "x"),
        P(None, "x"),
        P(None, "x"),
        P("x", None),
    )
    return jax.shard_map(
        shards, mesh=fine, in_specs=placed, out_specs=P("p", dp, None, "x"), check_vma=False
    )
```

time: 165 us -> 158 us (0.958)
  waiting for transfers between devices: 70.6 us -> 55.5 us
  between operations: 13.6 us -> 0.37 us
  starting transfers between devices: 39.7 us -> 51.8 us
  Pallas kernels: 12.3 us -> 21 us
  other arithmetic: 3.98 us -> 1.11 us
  local copies, waits for them, and re-layouts: 12.3 us -> 14.5 us
    ppermute x6 -> x28, starting transfers between devices: 15.4 us -> 38.1 us  [moved(): return lax.ppermute(value, axes, pairs)]
    all_to_all x3 -> x1, waiting for transfers between devices: 44.9 us -> 25.9 us  [shards(): terms = lax.all_to_all(terms, ('yh', 'p', 'x'), 0, 0)]
    all_to_all x3 -> x1, starting transfers between devices: 16.4 us -> 7.14 us  [shards(): terms = lax.all_to_all(terms, ('yh', 'p', 'x'), 0, 0)]
    pallas_call x3 -> x7, Pallas kernels: 12.3 us -> 21 us  [the longest x1 10.2 us: ffn(): pl.pallas_call(ffn_kernel, grid_spec=grid_spec, out_shape=jax.ShapeDtypeS...]
    ppermute x6 -> x28, waiting for transfers between devices: 20.5 us -> 26.7 us  [moved(): return lax.ppermute(value, axes, pairs)]
    another operation x1 -> x5, local copies, waits for them, and re-layouts: 0.04 us -> 3.68 us  [the longest x4 3.07 us: shards(): memory = memory_rows(place, terms, jnp.stack(rows), jnp.stack(gains))]
    unnamed x22 -> x57, local copies, waits for them, and re-layouts: 7.4 us -> 3.97 us
    broadcast_in_dim x2 -> x0, local copies, waits for them, and re-layouts: 2.49 us -> none  [gathered(): spread = jnp.broadcast_to(value[None], (SIZES[axis],) + value.shape)]
  transfers between devices with their start and end apart: 11 -> 30, of which waited for: 7 -> 15; matrix products, arithmetic and copies ran while one was open for 5% -> 6% of each run, Pallas kernels for 5% -> 2%
where the time goes in v3:
time: 158 us; the launch traced here: 156 us
  waiting for transfers between devices  55.5 us (35%)
  starting transfers between devices  51.8 us (33%)
  Pallas kernels  21 us (13%)
  local copies, waits for them, and re-layouts  14.5 us (9%)
  blocking collectives  11.7 us (7%)
    ppermute x28, starting transfers between devices, moved(): return lax.ppermute(value, axes, pairs)  38.1 us
    ppermute x28, waiting for transfers between devices, moved(): return lax.ppermute(value, axes, pairs)  26.7 us
    all_to_all x1, waiting for transfers between devices, shards(): terms = lax.all_to_all(terms, ('yh', 'p', 'x'), 0, 0)  25.9 us
    all_to_all x1, blocking collectives, shards(): attended = lax.all_to_all(attended, 'x', 0, 0)  11.7 us
    pallas_call x1, Pallas kernels, ffn(): pl.pallas_call(ffn_kernel, grid_spec=grid_spec, out_shape=jax.ShapeDtypeS...  10.2 us
    all_to_all x1, starting transfers between devices, shards(): terms = lax.all_to_all(terms, ('yh', 'p', 'x'), 0, 0)  7.14 us
    all_to_all x1, starting transfers between devices, shards(): memory = lax.all_to_all(memory, 'x', 0, 0).reshape(128, 2048)  6.54 us
    pallas_call x1, Pallas kernels, attention(): pl.pallas_call(attention_kernel, in_specs=[smem()] * 2 + [vmem()] * 2 + [...  5.27 us
  transfers between devices with their start and end apart: 30, of which 15 were waited for; matrix products, arithmetic and copies ran while one was open for 6% of the time, Pallas kernels for 2%

profile of v3, /device:TPU:6, one launch (start us, length us, event | category | flops | bytes accessed | tf_op | source)
XLA Modules:
  0.0 156.0 jit_solution(12600302516189202619)
XLA Ops:
  0.0 0.9 dynamic-slice_bitcast_fusion
  0.9 1.0 constant_dynamic-slice_fusion
  2.1 3.1 %collective-permute-start.17 = (bf16[192,512]{1,0:T(8,128)(2,1)S(1)}, bf16[192,512]{1,0:T(8,128)(2,1)S(1)}, u32[]{:S(2)}, u32[]{:S(2)}) collective-permute-start(bf16[192,512]{1,0:T(8,128)(2,1)S(1)} %pad_maximum_fusion.4), channel_id=1, source_target_pairs={{0,132},{4,128},{128,4},{132,0},{1,133},{5,129},{129,5},{133,1},{2... | collective-permute-start | bytes 589832 | tf_op jit(solution)/shard_map/ppermute | solution.py:24
  5.3 2.0 %collective-permute-start.9 = (bf16[384,512]{1,0:T(8,128)(2,1)S(1)}, bf16[384,512]{1,0:T(8,128)(2,1)S(1)}, u32[]{:S(2)}, u32[]{:S(2)}) collective-permute-start(bf16[384,512]{1,0:T(8,128)(2,1)S(1)} %pad_maximum_fusion.1.refs_9_), channel_id=1, source_target_pairs={{0,16},{8,120},{16,32},{24,8},{32,48},{40,24},{48,64},{56,40},{64,... | collective-permute-start | bytes 1179656 | tf_op jit(solution)/shard_map/ppermute | solution.py:24
  7.3 3.4 %collective-permute-done.17 = bf16[192,512]{1,0:T(8,128)(2,1)S(1)} collective-permute-done((bf16[192,512]{1,0:T(8,128)(2,1)S(1)}, bf16[192,512]{1,0:T(8,128)(2,1)S(1)}, u32[]{:S(2)}, u32[]{:S(2)}) %collective-permute-start.17) | collective-permute-done | bytes 196640 | tf_op jit(solution)/shard_map/ppermute | solution.py:24
  11.1 2.7 %collective-permute-done.refs_1_ = bf16[256,512]{1,0:T(8,128)(2,1)S(1)} collective-permute-done((bf16[256,512]{1,0:T(8,128)(2,1)}, bf16[256,512]{1,0:T(8,128)(2,1)S(1)}, u32[]{:S(2)}, u32[]{:S(2)}) %collective-permute-start) | collective-permute-done | bytes 262176 | tf_op jit(solution)/shard_map/ppermute | solution.py:24
  14.4 2.0 %collective-permute-start.19 = (bf16[384,512]{1,0:T(8,128)(2,1)S(1)}, bf16[384,512]{1,0:T(8,128)(2,1)}, u32[]{:S(2)}, u32[]{:S(2)}) collective-permute-start(bf16[384,512]{1,0:T(8,128)(2,1)S(1)} %constant_dynamic-update-slice_fusion.refs_18_), channel_id=1, source_target_pairs={{0,16},{8,120},{16,32},{24,8},{32,48},{40,24},{48,64},{56,40},{64,... | collective-permute-start | bytes 1179656 | tf_op jit(solution)/shard_map/ppermute | solution.py:24
  17.0 2.4 %collective-permute-start.2 = (bf16[400,512]{1,0:T(8,128)(2,1)S(1)}, bf16[400,512]{1,0:T(8,128)(2,1)S(1)}, u32[]{:S(2)}, u32[]{:S(2)}) collective-permute-start(bf16[400,512]{1,0:T(8,128)(2,1)S(1)} %pad_maximum_fusion.t0.refs_0_), channel_id=1, source_target_pairs={{0,2},{1,3},{2,0},{3,1},{4,6},{5,7},{6,4},{7,5},{8,10},{9,11},{10,... | collective-permute-start | bytes 1228808 | tf_op jit(solution)/shard_map/ppermute | solution.py:24
  19.4 0.7 copy-done.11
  20.1 1.9 %collective-permute-start.10 = (bf16[384,512]{1,0:T(8,128)(2,1)}, bf16[384,512]{1,0:T(8,128)(2,1)S(1)}, u32[]{:S(2)}, u32[]{:S(2)}) collective-permute-start(bf16[384,512]{1,0:T(8,128)(2,1)} %shard_map.119.refs_10_), channel_id=1, source_target_pairs={{0,16},{8,120},{16,32},{24,8},{32,48},{40,24},{48,64},{56,40},{64,... | collective-permute-start | bytes 1179656 | tf_op jit(solution)/shard_map/ppermute | solution.py:24
  22.7 0.8 collective-permute-start.3
  23.6 2.6 %collective-permute-done.19.refs_19_ = bf16[384,512]{1,0:T(8,128)(2,1)} collective-permute-done((bf16[384,512]{1,0:T(8,128)(2,1)S(1)}, bf16[384,512]{1,0:T(8,128)(2,1)}, u32[]{:S(2)}, u32[]{:S(2)}) %collective-permute-start.19) | collective-permute-done | bytes 393248 | tf_op jit(solution)/shard_map/ppermute | solution.py:24
  26.3 1.7 %collective-permute-start.5 = (bf16[256,512]{1,0:T(8,128)(2,1)S(1)}, bf16[256,512]{1,0:T(8,128)(2,1)S(1)}, u32[]{:S(2)}, u32[]{:S(2)}) collective-permute-start(bf16[256,512]{1,0:T(8,128)(2,1)S(1)} %collective-permute-done.4.refs_1_.refs_4_), channel_id=1, source_target_pairs={{0,1},{1,2},{2,3},{3,0},{4,5},{5,6},{6,7},{7,4},{8,9},{9,10},{10,1... | collective-permute-start | bytes 786440 | tf_op jit(solution)/shard_map/ppermute | solution.py:24
  28.7 2.4 %collective-permute-start.6 = (bf16[256,512]{1,0:T(8,128)(2,1)S(1)}, bf16[256,512]{1,0:T(8,128)(2,1)S(1)}, u32[]{:S(2)}, u32[]{:S(2)}) collective-permute-start(bf16[256,512]{1,0:T(8,128)(2,1)S(1)} %collective-permute-done.4.refs_1_.refs_4_), channel_id=1, source_target_pairs={{0,2},{1,3},{2,0},{3,1},{4,6},{5,7},{6,4},{7,5},{8,10},{9,11},{10,... | collective-permute-start | bytes 786440 | tf_op jit(solution)/shard_map/ppermute | solution.py:24
  31.1 7.6 %collective-permute-start.7 = (bf16[256,512]{1,0:T(8,128)(2,1)S(1)}, bf16[256,512]{1,0:T(8,128)(2,1)S(1)}, u32[]{:S(2)}, u32[]{:S(2)}) collective-permute-start(bf16[256,512]{1,0:T(8,128)(2,1)S(1)} %collective-permute-done.4.refs_1_.refs_4_), channel_id=1, source_target_pairs={{0,3},{1,0},{2,1},{3,2},{4,7},{5,4},{6,5},{7,6},{8,11},{9,8},{10,9... | collective-permute-start | bytes 786440 | tf_op jit(solution)/shard_map/ppermute | solution.py:24
  38.7 3.1 %collective-permute-done.3.t3.refs_3_ = bf16[400,512]{1,0:T(8,128)(2,1)S(1)} collective-permute-done((bf16[400,512]{1,0:T(8,128)(2,1)S(1)}, bf16[400,512]{1,0:T(8,128)(2,1)S(1)}, u32[]{:S(2)}, u32[]{:S(2)}) %collective-permute-start.3) | collective-permute-done | bytes 409632 | tf_op jit(solution)/shard_map/ppermute | solution.py:24
  41.8 1.9 %collective-permute-start.11 = (bf16[384,512]{1,0:T(8,128)(2,1)}, bf16[384,512]{1,0:T(8,128)(2,1)S(1)}, u32[]{:S(2)}, u32[]{:S(2)}) collective-permute-start(bf16[384,512]{1,0:T(8,128)(2,1)} %shard_map.120.refs_11_), channel_id=1, source_target_pairs={{0,16},{8,120},{16,32},{24,8},{32,48},{40,24},{48,64},{56,40},{64,... | collective-permute-start | bytes 1179656 | tf_op jit(solution)/shard_map/ppermute | solution.py:24
  43.7 2.7 %collective-permute-start.21 = (bf16[384,512]{1,0:T(8,128)(2,1)}, bf16[384,512]{1,0:T(8,128)(2,1)S(1)}, u32[]{:S(2)}, u32[]{:S(2)}) collective-permute-start(bf16[384,512]{1,0:T(8,128)(2,1)} %collective-permute-done.20.refs_20_), channel_id=1, source_target_pairs={{0,16},{8,120},{16,32},{24,8},{32,48},{40,24},{48,64},{56,40},{64,... | collective-permute-start | bytes 1179656 | tf_op jit(solution)/shard_map/ppermute | solution.py:24
  46.4 0.9 collective-permute-start.23
  47.3 2.9 %collective-permute-done.7.refs_6_.refs_7_ = bf16[256,512]{1,0:T(8,128)(2,1)S(1)} collective-permute-done((bf16[256,512]{1,0:T(8,128)(2,1)S(1)}, bf16[256,512]{1,0:T(8,128)(2,1)S(1)}, u32[]{:S(2)}, u32[]{:S(2)}) %collective-permute-start.7) | collective-permute-done | bytes 262176 | tf_op jit(solution)/shard_map/ppermute | solution.py:24
  50.2 0.7 collective-permute-start.14
  51.2 0.7 copy-done.7
  52.0 0.9 slice.37
  52.9 2.5 %collective-permute-done.21.refs_21_ = bf16[384,512]{1,0:T(8,128)(2,1)S(1)} collective-permute-done((bf16[384,512]{1,0:T(8,128)(2,1)}, bf16[384,512]{1,0:T(8,128)(2,1)S(1)}, u32[]{:S(2)}, u32[]{:S(2)}) %collective-permute-start.21) | collective-permute-done | bytes 393248 | tf_op jit(solution)/shard_map/ppermute | solution.py:24
  55.4 0.9 collective-permute-start.12
  56.3 2.4 %collective-permute-start.22 = (bf16[192,512]{1,0:T(8,128)(2,1)S(1)}, bf16[192,512]{1,0:T(8,128)(2,1)S(1)}, u32[]{:S(2)}, u32[]{:S(2)}) collective-permute-start(bf16[192,512]{1,0:T(8,128)(2,1)S(1)} %slice.38), channel_id=1, source_target_pairs={{0,16},{8,120},{16,32},{24,8},{32,48},{40,24},{48,64},{56,40},{64,... | collective-permute-start | bytes 589832 | tf_op jit(solution)/shard_map/ppermute | solution.py:24
  58.7 1.8 %collective-permute-start.25 = (bf16[384,512]{1,0:T(8,128)(2,1)S(1)}, bf16[384,512]{1,0:T(8,128)(2,1)S(1)}, u32[]{:S(2)}, u32[]{:S(2)}) collective-permute-start(bf16[384,512]{1,0:T(8,128)(2,1)S(1)} %collective-permute-done.21.refs_21_), channel_id=1, source_target_pairs={{0,8},{8,0},{1,9},{9,1},{2,10},{10,2},{3,11},{11,3},{4,12},{12,4},... | collective-permute-start | bytes 1179656 | tf_op jit(solution)/shard_map/ppermute | solution.py:24
  60.5 1.8 %collective-permute-done.12.refs_13_ = bf16[192,512]{1,0:T(8,128)(2,1)S(1)} collective-permute-done((bf16[192,512]{1,0:T(8,128)(2,1)S(1)}, bf16[192,512]{1,0:T(8,128)(2,1)S(1)}, u32[]{:S(2)}, u32[]{:S(2)}) %collective-permute-start.12) | collective-permute-done | bytes 196640 | tf_op jit(solution)/shard_map/ppermute | solution.py:24
  62.4 2.1 %collective-permute-done.22.refs_22_ = bf16[192,512]{1,0:T(8,128)(2,1)S(1)} collective-permute-done((bf16[192,512]{1,0:T(8,128)(2,1)S(1)}, bf16[192,512]{1,0:T(8,128)(2,1)S(1)}, u32[]{:S(2)}, u32[]{:S(2)}) %collective-permute-start.22) | collective-permute-done | bytes 196640 | tf_op jit(solution)/shard_map/ppermute | solution.py:24
  64.5 1.3 reshape.20.refs_8_
  67.3 0.8 copy-done.23
  68.1 10.2 %shard_map.122 = bf16[16,4,32,512]{3,2,1,0:T(8,128)(2,1)} custom-call(s32[5]{0:T(128)} %stack.41.place, bf16[400,512]{1,0:T(8,128)(2,1)} %copy-done.5, bf16[400,512]{1,0:T(8,128)(2,1)} %copy-done.2, bf16[400,512]{1,0:T(8,128)(2,1)} %copy-done.3, bf16[400,512]{1,0:T(8,128)(2,1)} %copy-done.4, bf16[256,512]{1,0:T(8,128)(2,1)} %copy-done.13, ...), custom_call_target="tpu_custom_call" | custom-call | flops 3221225472 | bytes 10485760 | tf_op jit(solution)/shard_map/pallas_call | solution.py:172
  78.4 7.1 %all-to-all-start = ((bf16[16,4,32,512]{3,2,1,0:T(8,128)(2,1)}), bf16[16,4,32,512]{3,2,1,0:T(8,128)(2,1)S(1)}, u32[]{:S(2)}, u32[]{:S(2)}) async-start(bf16[16,4,32,512]{3,2,1,0:T(8,128)(2,1)} %shard_map.122), calls=%async_computation | async-start | bytes 4194304 | tf_op jit(solution)/shard_map/all_to_all | solution.py:343
  85.5 0.8 dynamic-slice_bitcast_fusion.5
  88.4 0.8 dynamic-slice_bitcast_fusion.2
  89.2 0.8 dynamic-slice_bitcast_fusion.3
  90.0 0.8 dynamic-slice_bitcast_fusion.4
  90.7 25.9 %all-to-all-done.terms = bf16[16,4,32,512]{3,2,1,0:T(8,128)(2,1)S(1)} async-done(((bf16[16,4,32,512]{3,2,1,0:T(8,128)(2,1)}), bf16[16,4,32,512]{3,2,1,0:T(8,128)(2,1)S(1)}, u32[]{:S(2)}, u32[]{:S(2)}) %all-to-all-start) | async-done | bytes 2097184 | tf_op jit(solution)/shard_map/all_to_all | solution.py:343
  116.7 1.8 %shard_map.123 = bf16[4,32,2048]{2,1,0:T(8,128)(2,1)} custom-call(s32[5]{0:T(128)S(1)} %copy-done, bf16[16,4,32,512]{3,2,1,0:T(8,128)(2,1)S(1)} %all-to-all-done.terms, bf16[4,32,512]{2,1,0:T(8,128)(2,1)S(1)} %pad_maximum_fusion.5.tokens, bf16[4,512]{1,0:T(4,128)(2,1)S(1)} %pad_maximum_fusion.6.gain), custom_call_target="tpu_custom_call" | custom-call | tf_op jit(solution)/shard_map/pallas_call | solution.py:202
  118.4 6.5 %all-to-all-start.1 = ((bf16[4,32,2048]{2,1,0:T(8,128)(2,1)}), bf16[4,32,2048]{2,1,0:T(8,128)(2,1)S(1)}, u32[]{:S(2)}, u32[]{:S(2)}) async-start(bf16[4,32,2048]{2,1,0:T(8,128)(2,1)} %shard_map.123), calls=%async_computation.1 | async-start | bytes 1048576 | tf_op jit(solution)/shard_map/all_to_all | solution.py:348
  125.6 3.8 %shard_map.118.query = bf16[128,512]{1,0:T(8,128)(2,1)} custom-call(s32[5]{0:T(128)} %stack.41.place, bf16[400,512]{1,0:T(8,128)(2,1)} %copy-done.5, bf16[400,512]{1,0:T(8,128)(2,1)} %copy-done.2, bf16[400,512]{1,0:T(8,128)(2,1)} %copy-done.3, bf16[400,512]{1,0:T(8,128)(2,1)} %copy-done.4, bf16[4,1,512]{2,1,0:T(2,128)(2,1)} %reshape.19.gain, ...), custom_call_target="tpu_custom_call" | custom-call | flops 268435456 | bytes 3145728 | tf_op jit(solution)/shard_map/pallas_call | solution.py:231
  129.3 2.9 %all-to-all-done.1 = bf16[4,32,2048]{2,1,0:T(8,128)(2,1)S(1)} async-done(((bf16[4,32,2048]{2,1,0:T(8,128)(2,1)}), bf16[4,32,2048]{2,1,0:T(8,128)(2,1)S(1)}, u32[]{:S(2)}, u32[]{:S(2)}) %all-to-all-start.1) | async-done | bytes 524320 | tf_op jit(solution)/shard_map/all_to_all | solution.py:348
  132.2 0.8 copy-done.1
  133.0 5.3 %shard_map.124 = (bf16[4,128,512]{2,1,0:T(8,128)(2,1)}, bf16[128,512]{1,0:T(8,128)(2,1)}) custom-call(s32[5]{0:T(128)} %stack.41.place, s32[2]{0:T(128)} %lengths.1, bf16[128,512]{1,0:T(8,128)(2,1)} %shard_map.118.query, bf16[128,2048]{1,0:T(8,128)(2,1)} %bitcast.23, bf16[2048,512]{1,0:T(8,128)(2,1)} %wk.1, bf16[2048,512]{1,0:T(8,128)(2,1)} %wv.1, ...), custom_call_target="tpu_custom_call" | custom-call | flops 805306368 | bytes 8388608 | tf_op jit(solution)/shard_map/pallas_call | solution.py:287
  138.3 11.7 %all_to_all.15 = bf16[4,128,512]{2,1,0:T(8,128)(2,1)S(1)} all-to-all(bf16[4,128,512]{2,1,0:T(8,128)(2,1)} %get-tuple-element.8), channel_id=1, replica_groups=mesh['yh'=2,'z'=8,'c'=2,'p'=2,'x'=4] {'x'}, dimensions={0} | all-to-all | bytes 1048576 | tf_op jit(solution)/shard_map/all_to_all | solution.py:352
  150.1 1.2 collective-permute-start.27
  151.3 3.9 %collective-permute-done.27 = bf16[128,512]{1,0:T(8,128)(2,1)S(1)} collective-permute-done((bf16[128,512]{1,0:T(8,128)(2,1)S(1)}, bf16[128,512]{1,0:T(8,128)(2,1)S(1)}, u32[]{:S(2)}, u32[]{:S(2)}) %collective-permute-start.27) | collective-permute-done | bytes 131104 | tf_op jit(solution)/shard_map/ppermute | solution.py:24
  155.2 0.7 pad_maximum_fusion.2
  (106 shorter events, 8.0 us)
Async XLA Ops:
  0.0 13.8 %copy-start.8 = (bf16[1,2,128,512]{3,2,1,0:T(8,128)(2,1)S(1)}, bf16[1,2,128,512]{3,2,1,0:T(8,128)(2,1)}, u32[]{:S(2)}) copy-start(bf16[1,2,128,512]{3,2,1,0:T(8,128)(2,1)} %param.12) | copy-start | bytes 786436
  0.9 15.4 %copy-start.20 = (bf16[512]{0:T(512)(128)(2,1)S(1)}, bf16[512]{0:T(512)(128)(2,1)}, u32[]{:S(2)}) copy-start(bf16[512]{0:T(512)(128)(2,1)} %param.18) | copy-start | bytes 3076
  1.9 3.4 %collective-permute-start.8 = (bf16[192,512]{1,0:T(8,128)(2,1)S(1)}, bf16[192,512]{1,0:T(8,128)(2,1)S(1)}, u32[]{:S(2)}, u32[]{:S(2)}) collective-permute-start(bf16[192,512]{1,0:T(8,128)(2,1)S(1)} %pad_maximum_fusion.3), channel_id=1, source_target_pairs={{0,8},{8,0},{1,9},{9,1},{2,10},{10,2},{3,11},{11,3},{4,12},{12,4},... | collective-permute-start | bytes 589832 | tf_op jit(solution)/shard_map/ppermute | solution.py:24
  2.1 8.7 %collective-permute-start.17 = (bf16[192,512]{1,0:T(8,128)(2,1)S(1)}, bf16[192,512]{1,0:T(8,128)(2,1)S(1)}, u32[]{:S(2)}, u32[]{:S(2)}) collective-permute-start(bf16[192,512]{1,0:T(8,128)(2,1)S(1)} %pad_maximum_fusion.4), channel_id=1, source_target_pairs={{0,132},{4,128},{128,4},{132,0},{1,133},{5,129},{129,5},{133,1},{2... | collective-permute-start | bytes 589832 | tf_op jit(solution)/shard_map/ppermute | solution.py:24
  5.2 8.6 %collective-permute-start = (bf16[256,512]{1,0:T(8,128)(2,1)}, bf16[256,512]{1,0:T(8,128)(2,1)S(1)}, u32[]{:S(2)}, u32[]{:S(2)}) collective-permute-start(bf16[256,512]{1,0:T(8,128)(2,1)} %bitcast.24), channel_id=1, source_target_pairs={{0,4},{4,0},{1,5},{5,1},{2,6},{6,2},{3,7},{7,3},{8,12},{12,8},{9,1... | collective-permute-start | bytes 786440 | tf_op jit(solution)/shard_map/ppermute | solution.py:24
  5.3 33.4 %copy-start.10 = (bf16[384,512]{1,0:T(8,128)(2,1)}, bf16[384,512]{1,0:T(8,128)(2,1)S(1)}, u32[]{:S(2)}) copy-start(bf16[384,512]{1,0:T(8,128)(2,1)S(1)} %pad_maximum_fusion.1.refs_9_) | copy-start | bytes 1179652
  5.3 14.1 %collective-permute-start.9 = (bf16[384,512]{1,0:T(8,128)(2,1)S(1)}, bf16[384,512]{1,0:T(8,128)(2,1)S(1)}, u32[]{:S(2)}, u32[]{:S(2)}) collective-permute-start(bf16[384,512]{1,0:T(8,128)(2,1)S(1)} %pad_maximum_fusion.1.refs_9_), channel_id=1, source_target_pairs={{0,16},{8,120},{16,32},{24,8},{32,48},{40,24},{48,64},{56,40},{64,... | collective-permute-start | bytes 1179656 | tf_op jit(solution)/shard_map/ppermute | solution.py:24
  10.7 3.6 %collective-permute-start.18 = (bf16[192,512]{1,0:T(8,128)(2,1)S(1)}, bf16[192,512]{1,0:T(8,128)(2,1)S(1)}, u32[]{:S(2)}, u32[]{:S(2)}) collective-permute-start(bf16[192,512]{1,0:T(8,128)(2,1)S(1)} %collective-permute-done.17), channel_id=1, source_target_pairs={{0,8},{8,0},{1,9},{9,1},{2,10},{10,2},{3,11},{11,3},{4,12},{12,4},... | collective-permute-start | bytes 589832 | tf_op jit(solution)/shard_map/ppermute | solution.py:24
  13.8 5.6 %copy-start.6 = (bf16[256,512]{1,0:T(8,128)(2,1)}, bf16[256,512]{1,0:T(8,128)(2,1)S(1)}, u32[]{:S(2)}) copy-start(bf16[256,512]{1,0:T(8,128)(2,1)S(1)} %collective-permute-done.refs_1_) | copy-start | bytes 786436
  13.8 8.9 %collective-permute-start.4 = (bf16[256,512]{1,0:T(8,128)(2,1)S(1)}, bf16[256,512]{1,0:T(8,128)(2,1)S(1)}, u32[]{:S(2)}, u32[]{:S(2)}) collective-permute-start(bf16[256,512]{1,0:T(8,128)(2,1)S(1)} %broadcast_select_fusion), channel_id=1, source_target_pairs={{0,132},{4,128},{128,4},{132,0},{1,133},{5,129},{129,5},{133,1},{2... | collective-permute-start | bytes 786440 | tf_op jit(solution)/shard_map/ppermute | solution.py:24
  14.4 37.6 %copy-start.18 = (bf16[384,512]{1,0:T(8,128)(2,1)}, bf16[384,512]{1,0:T(8,128)(2,1)S(1)}, u32[]{:S(2)}) copy-start(bf16[384,512]{1,0:T(8,128)(2,1)S(1)} %constant_dynamic-update-slice_fusion.refs_18_) | copy-start | bytes 1179652
  14.4 11.8 %collective-permute-start.19 = (bf16[384,512]{1,0:T(8,128)(2,1)S(1)}, bf16[384,512]{1,0:T(8,128)(2,1)}, u32[]{:S(2)}, u32[]{:S(2)}) collective-permute-start(bf16[384,512]{1,0:T(8,128)(2,1)S(1)} %constant_dynamic-update-slice_fusion.refs_18_), channel_id=1, source_target_pairs={{0,16},{8,120},{16,32},{24,8},{32,48},{40,24},{48,64},{56,40},{64,... | collective-permute-start | bytes 1179656 | tf_op jit(solution)/shard_map/ppermute | solution.py:24
  16.4 35.5 %copy-start.5 = (bf16[400,512]{1,0:T(8,128)(2,1)}, bf16[400,512]{1,0:T(8,128)(2,1)S(1)}, u32[]{:S(2)}) copy-start(bf16[400,512]{1,0:T(8,128)(2,1)S(1)} %pad_maximum_fusion.t0.refs_0_) | copy-start | bytes 1228804
  16.4 9.9 %collective-permute-start.1 = (bf16[400,512]{1,0:T(8,128)(2,1)S(1)}, bf16[400,512]{1,0:T(8,128)(2,1)S(1)}, u32[]{:S(2)}, u32[]{:S(2)}) collective-permute-start(bf16[400,512]{1,0:T(8,128)(2,1)S(1)} %pad_maximum_fusion.t0.refs_0_), channel_id=1, source_target_pairs={{0,1},{1,2},{2,3},{3,0},{4,5},{5,6},{6,7},{7,4},{8,9},{9,10},{10,1... | collective-permute-start | bytes 1228808 | tf_op jit(solution)/shard_map/ppermute | solution.py:24
  17.0 11.7 %collective-permute-start.2 = (bf16[400,512]{1,0:T(8,128)(2,1)S(1)}, bf16[400,512]{1,0:T(8,128)(2,1)S(1)}, u32[]{:S(2)}, u32[]{:S(2)}) collective-permute-start(bf16[400,512]{1,0:T(8,128)(2,1)S(1)} %pad_maximum_fusion.t0.refs_0_), channel_id=1, source_target_pairs={{0,2},{1,3},{2,0},{3,1},{4,6},{5,7},{6,4},{7,5},{8,10},{9,11},{10,... | collective-permute-start | bytes 1228808 | tf_op jit(solution)/shard_map/ppermute | solution.py:24
  20.1 10.9 %collective-permute-start.10 = (bf16[384,512]{1,0:T(8,128)(2,1)}, bf16[384,512]{1,0:T(8,128)(2,1)S(1)}, u32[]{:S(2)}, u32[]{:S(2)}) collective-permute-start(bf16[384,512]{1,0:T(8,128)(2,1)} %shard_map.119.refs_10_), channel_id=1, source_target_pairs={{0,16},{8,120},{16,32},{24,8},{32,48},{40,24},{48,64},{56,40},{64,... | collective-permute-start | bytes 1179656 | tf_op jit(solution)/shard_map/ppermute | solution.py:24
  22.7 16.0 %copy-start.13 = (bf16[256,512]{1,0:T(8,128)(2,1)}, bf16[256,512]{1,0:T(8,128)(2,1)S(1)}, u32[]{:S(2)}) copy-start(bf16[256,512]{1,0:T(8,128)(2,1)S(1)} %collective-permute-done.4.refs_1_.refs_4_) | copy-start | bytes 786436
  22.7 19.1 %collective-permute-start.3 = (bf16[400,512]{1,0:T(8,128)(2,1)S(1)}, bf16[400,512]{1,0:T(8,128)(2,1)S(1)}, u32[]{:S(2)}, u32[]{:S(2)}) collective-permute-start(bf16[400,512]{1,0:T(8,128)(2,1)S(1)} %pad_maximum_fusion.t0.refs_0_), channel_id=1, source_target_pairs={{0,3},{1,0},{2,1},{3,2},{4,7},{5,4},{6,5},{7,6},{8,11},{9,8},{10,9... | collective-permute-start | bytes 1228808 | tf_op jit(solution)/shard_map/ppermute | solution.py:24
  26.2 17.6 %collective-permute-start.20 = (bf16[384,512]{1,0:T(8,128)(2,1)}, bf16[384,512]{1,0:T(8,128)(2,1)}, u32[]{:S(2)}, u32[]{:S(2)}) collective-permute-start(bf16[384,512]{1,0:T(8,128)(2,1)} %collective-permute-done.19.refs_19_), channel_id=1, source_target_pairs={{0,16},{8,120},{16,32},{24,8},{32,48},{40,24},{48,64},{56,40},{64,... | collective-permute-start | bytes 1179656 | tf_op jit(solution)/shard_map/ppermute | solution.py:24
  26.3 24.9 %copy-start.2 = (bf16[400,512]{1,0:T(8,128)(2,1)}, bf16[400,512]{1,0:T(8,128)(2,1)S(1)}, u32[]{:S(2)}) copy-start(bf16[400,512]{1,0:T(8,128)(2,1)S(1)} %collective-permute-done.1.t1.refs_1_) | copy-start | bytes 1228804
  26.3 20.1 %collective-permute-start.5 = (bf16[256,512]{1,0:T(8,128)(2,1)S(1)}, bf16[256,512]{1,0:T(8,128)(2,1)S(1)}, u32[]{:S(2)}, u32[]{:S(2)}) collective-permute-start(bf16[256,512]{1,0:T(8,128)(2,1)S(1)} %collective-permute-done.4.refs_1_.refs_4_), channel_id=1, source_target_pairs={{0,1},{1,2},{2,3},{3,0},{4,5},{5,6},{6,7},{7,4},{8,9},{9,10},{10,1... | collective-permute-start | bytes 786440 | tf_op jit(solution)/shard_map/ppermute | solution.py:24
  28.7 22.5 %copy-start.3 = (bf16[400,512]{1,0:T(8,128)(2,1)}, bf16[400,512]{1,0:T(8,128)(2,1)S(1)}, u32[]{:S(2)}) copy-start(bf16[400,512]{1,0:T(8,128)(2,1)S(1)} %collective-permute-done.2.t2.refs_2_) | copy-start | bytes 1228804
  28.7 17.8 %collective-permute-start.6 = (bf16[256,512]{1,0:T(8,128)(2,1)S(1)}, bf16[256,512]{1,0:T(8,128)(2,1)S(1)}, u32[]{:S(2)}, u32[]{:S(2)}) collective-permute-start(bf16[256,512]{1,0:T(8,128)(2,1)S(1)} %collective-permute-done.4.refs_1_.refs_4_), channel_id=1, source_target_pairs={{0,2},{1,3},{2,0},{3,1},{4,6},{5,7},{6,4},{7,5},{8,10},{9,11},{10,... | collective-permute-start | bytes 786440 | tf_op jit(solution)/shard_map/ppermute | solution.py:24
  31.1 7.6 %copy-start.12 = (bf16[384,512]{1,0:T(8,128)(2,1)}, bf16[384,512]{1,0:T(8,128)(2,1)S(1)}, u32[]{:S(2)}) copy-start(bf16[384,512]{1,0:T(8,128)(2,1)S(1)} %collective-permute-done.10.refs_0_) | copy-start | bytes 1179652
  31.1 19.1 %collective-permute-start.7 = (bf16[256,512]{1,0:T(8,128)(2,1)S(1)}, bf16[256,512]{1,0:T(8,128)(2,1)S(1)}, u32[]{:S(2)}, u32[]{:S(2)}) collective-permute-start(bf16[256,512]{1,0:T(8,128)(2,1)S(1)} %collective-permute-done.4.refs_1_.refs_4_), channel_id=1, source_target_pairs={{0,3},{1,0},{2,1},{3,2},{4,7},{5,4},{6,5},{7,6},{8,11},{9,8},{10,9... | collective-permute-start | bytes 786440 | tf_op jit(solution)/shard_map/ppermute | solution.py:24
  41.8 9.4 %copy-start.4 = (bf16[400,512]{1,0:T(8,128)(2,1)}, bf16[400,512]{1,0:T(8,128)(2,1)S(1)}, u32[]{:S(2)}) copy-start(bf16[400,512]{1,0:T(8,128)(2,1)S(1)} %collective-permute-done.3.t3.refs_3_) | copy-start | bytes 1228804
  41.8 9.3 %collective-permute-start.11 = (bf16[384,512]{1,0:T(8,128)(2,1)}, bf16[384,512]{1,0:T(8,128)(2,1)S(1)}, u32[]{:S(2)}, u32[]{:S(2)}) collective-permute-start(bf16[384,512]{1,0:T(8,128)(2,1)} %shard_map.120.refs_11_), channel_id=1, source_target_pairs={{0,16},{8,120},{16,32},{24,8},{32,48},{40,24},{48,64},{56,40},{64,... | collective-permute-start | bytes 1179656 | tf_op jit(solution)/shard_map/ppermute | solution.py:24
  43.7 11.6 %collective-permute-start.21 = (bf16[384,512]{1,0:T(8,128)(2,1)}, bf16[384,512]{1,0:T(8,128)(2,1)S(1)}, u32[]{:S(2)}, u32[]{:S(2)}) collective-permute-start(bf16[384,512]{1,0:T(8,128)(2,1)} %collective-permute-done.20.refs_20_), channel_id=1, source_target_pairs={{0,16},{8,120},{16,32},{24,8},{32,48},{40,24},{48,64},{56,40},{64,... | collective-permute-start | bytes 1179656 | tf_op jit(solution)/shard_map/ppermute | solution.py:24
  46.4 4.8 %copy-start.14 = (bf16[256,512]{1,0:T(8,128)(2,1)}, bf16[256,512]{1,0:T(8,128)(2,1)S(1)}, u32[]{:S(2)}) copy-start(bf16[256,512]{1,0:T(8,128)(2,1)S(1)} %collective-permute-done.5.refs_4_.refs_5_) | copy-start | bytes 786436
  46.4 9.0 %collective-permute-start.13 = (bf16[384,512]{1,0:T(8,128)(2,1)}, bf16[384,512]{1,0:T(8,128)(2,1)}, u32[]{:S(2)}, u32[]{:S(2)}) collective-permute-start(bf16[384,512]{1,0:T(8,128)(2,1)} %shard_map.119.refs_10_), channel_id=1, source_target_pairs={{0,8},{8,0},{1,9},{9,1},{2,10},{10,2},{3,11},{11,3},{4,12},{12,4},... | collective-permute-start | bytes 1179656 | tf_op jit(solution)/shard_map/ppermute | solution.py:24
  46.4 4.8 %copy-start.15 = (bf16[256,512]{1,0:T(8,128)(2,1)}, bf16[256,512]{1,0:T(8,128)(2,1)S(1)}, u32[]{:S(2)}) copy-start(bf16[256,512]{1,0:T(8,128)(2,1)S(1)} %collective-permute-done.6.refs_5_.refs_6_) | copy-start | bytes 786436
  46.4 9.9 %collective-permute-start.23 = (bf16[384,512]{1,0:T(8,128)(2,1)}, bf16[384,512]{1,0:T(8,128)(2,1)}, u32[]{:S(2)}, u32[]{:S(2)}) collective-permute-start(bf16[384,512]{1,0:T(8,128)(2,1)} %collective-permute-done.19.refs_19_), channel_id=1, source_target_pairs={{0,8},{8,0},{1,9},{9,1},{2,10},{10,2},{3,11},{11,3},{4,12},{12,4},... | collective-permute-start | bytes 1179656 | tf_op jit(solution)/shard_map/ppermute | solution.py:24
  50.2 8.5 %collective-permute-start.14 = (bf16[384,512]{1,0:T(8,128)(2,1)}, bf16[384,512]{1,0:T(8,128)(2,1)}, u32[]{:S(2)}, u32[]{:S(2)}) collective-permute-start(bf16[384,512]{1,0:T(8,128)(2,1)} %shard_map.120.refs_11_), channel_id=1, source_target_pairs={{0,8},{8,0},{1,9},{9,1},{2,10},{10,2},{3,11},{11,3},{4,12},{12,4},... | collective-permute-start | bytes 1179656 | tf_op jit(solution)/shard_map/ppermute | solution.py:24
  51.2 15.2 %collective-permute-start.24 = (bf16[384,512]{1,0:T(8,128)(2,1)}, bf16[384,512]{1,0:T(8,128)(2,1)}, u32[]{:S(2)}, u32[]{:S(2)}) collective-permute-start(bf16[384,512]{1,0:T(8,128)(2,1)} %collective-permute-done.20.refs_20_), channel_id=1, source_target_pairs={{0,8},{8,0},{1,9},{9,1},{2,10},{10,2},{3,11},{11,3},{4,12},{12,4},... | collective-permute-start | bytes 1179656 | tf_op jit(solution)/shard_map/ppermute | solution.py:24
  55.4 11.1 %copy-start.17 = (bf16[384,512]{1,0:T(8,128)(2,1)}, bf16[384,512]{1,0:T(8,128)(2,1)S(1)}, u32[]{:S(2)}) copy-start(bf16[384,512]{1,0:T(8,128)(2,1)S(1)} %collective-permute-done.21.refs_21_) | copy-start | bytes 1179652
  55.4 11.0 %collective-permute-start.15 = (bf16[384,512]{1,0:T(8,128)(2,1)}, bf16[384,512]{1,0:T(8,128)(2,1)S(1)}, u32[]{:S(2)}, u32[]{:S(2)}) collective-permute-start(bf16[384,512]{1,0:T(8,128)(2,1)} %shard_map.121.refs_12_), channel_id=1, source_target_pairs={{0,8},{8,0},{1,9},{9,1},{2,10},{10,2},{3,11},{11,3},{4,12},{12,4},... | collective-permute-start | bytes 1179656 | tf_op jit(solution)/shard_map/ppermute | solution.py:24
  55.4 7.0 %collective-permute-start.12 = (bf16[192,512]{1,0:T(8,128)(2,1)S(1)}, bf16[192,512]{1,0:T(8,128)(2,1)S(1)}, u32[]{:S(2)}, u32[]{:S(2)}) collective-permute-start(bf16[192,512]{1,0:T(8,128)(2,1)S(1)} %slice.37), channel_id=1, source_target_pairs={{0,16},{8,120},{16,32},{24,8},{32,48},{40,24},{48,64},{56,40},{64,... | collective-permute-start | bytes 589832 | tf_op jit(solution)/shard_map/ppermute | solution.py:24
  56.3 8.1 %collective-permute-start.22 = (bf16[192,512]{1,0:T(8,128)(2,1)S(1)}, bf16[192,512]{1,0:T(8,128)(2,1)S(1)}, u32[]{:S(2)}, u32[]{:S(2)}) collective-permute-start(bf16[192,512]{1,0:T(8,128)(2,1)S(1)} %slice.38), channel_id=1, source_target_pairs={{0,16},{8,120},{16,32},{24,8},{32,48},{40,24},{48,64},{56,40},{64,... | collective-permute-start | bytes 589832 | tf_op jit(solution)/shard_map/ppermute | solution.py:24
  58.7 7.7 %collective-permute-start.25 = (bf16[384,512]{1,0:T(8,128)(2,1)S(1)}, bf16[384,512]{1,0:T(8,128)(2,1)S(1)}, u32[]{:S(2)}, u32[]{:S(2)}) collective-permute-start(bf16[384,512]{1,0:T(8,128)(2,1)S(1)} %collective-permute-done.21.refs_21_), channel_id=1, source_target_pairs={{0,8},{8,0},{1,9},{9,1},{2,10},{10,2},{3,11},{11,3},{4,12},{12,4},... | collective-permute-start | bytes 1179656 | tf_op jit(solution)/shard_map/ppermute | solution.py:24
  62.4 4.0 %collective-permute-start.16 = (bf16[192,512]{1,0:T(8,128)(2,1)S(1)}, bf16[192,512]{1,0:T(8,128)(2,1)S(1)}, u32[]{:S(2)}, u32[]{:S(2)}) collective-permute-start(bf16[192,512]{1,0:T(8,128)(2,1)S(1)} %collective-permute-done.12.refs_13_), channel_id=1, source_target_pairs={{0,8},{8,0},{1,9},{9,1},{2,10},{10,2},{3,11},{11,3},{4,12},{12,4},... | collective-permute-start | bytes 589832 | tf_op jit(solution)/shard_map/ppermute | solution.py:24
  64.5 2.0 %collective-permute-start.26 = (bf16[192,512]{1,0:T(8,128)(2,1)S(1)}, bf16[192,512]{1,0:T(8,128)(2,1)S(1)}, u32[]{:S(2)}, u32[]{:S(2)}) collective-permute-start(bf16[192,512]{1,0:T(8,128)(2,1)S(1)} %collective-permute-done.22.refs_22_), channel_id=1, source_target_pairs={{0,8},{8,0},{1,9},{9,1},{2,10},{10,2},{3,11},{11,3},{4,12},{12,4},... | collective-permute-start | bytes 589832 | tf_op jit(solution)/shard_map/ppermute | solution.py:24
  78.3 7.2 %copy-start.21 = (bf16[512]{0:T(512)(128)(2,1)S(1)}, bf16[512]{0:T(512)(128)(2,1)}, u32[]{:S(2)}) copy-start(bf16[512]{0:T(512)(128)(2,1)} %param.18) | copy-start | bytes 3076
  78.3 38.3 %copy-start = (s32[5]{0:T(128)S(1)}, s32[5]{0:T(128)}, u32[]{:S(2)}) copy-start(s32[5]{0:T(128)} %stack.41.place) | copy-start | bytes 64
  78.4 38.3 %all-to-all-start = ((bf16[16,4,32,512]{3,2,1,0:T(8,128)(2,1)}), bf16[16,4,32,512]{3,2,1,0:T(8,128)(2,1)S(1)}, u32[]{:S(2)}, u32[]{:S(2)}) async-start(bf16[16,4,32,512]{3,2,1,0:T(8,128)(2,1)} %shard_map.122), calls=%async_computation | async-start | bytes 4194304 | tf_op jit(solution)/shard_map/all_to_all | solution.py:343
  89.2 35.8 %copy-start.19 = (bf16[2048]{0:T(1024)(128)(2,1)S(1)}, bf16[2048]{0:T(1024)(128)(2,1)}, u32[]{:S(2)}) copy-start(bf16[2048]{0:T(1024)(128)(2,1)} %param.19) | copy-start | bytes 12292
  118.4 13.8 %all-to-all-start.1 = ((bf16[4,32,2048]{2,1,0:T(8,128)(2,1)}), bf16[4,32,2048]{2,1,0:T(8,128)(2,1)S(1)}, u32[]{:S(2)}, u32[]{:S(2)}) async-start(bf16[4,32,2048]{2,1,0:T(8,128)(2,1)} %shard_map.123), calls=%async_computation.1 | async-start | bytes 1048576 | tf_op jit(solution)/shard_map/all_to_all | solution.py:348
  138.3 16.9 %copy-start.9 = (bf16[128,512]{1,0:T(8,128)(2,1)S(1)}, bf16[128,512]{1,0:T(8,128)(2,1)}, u32[]{:S(2)}) copy-start(bf16[128,512]{1,0:T(8,128)(2,1)} %get-tuple-element.7) | copy-start | bytes 393220
  150.1 5.1 %collective-permute-start.27 = (bf16[128,512]{1,0:T(8,128)(2,1)S(1)}, bf16[128,512]{1,0:T(8,128)(2,1)S(1)}, u32[]{:S(2)}, u32[]{:S(2)}) collective-permute-start(bf16[128,512]{1,0:T(8,128)(2,1)S(1)} %broadcast_select_fusion.3), channel_id=1, source_target_pairs={{0,4},{4,0},{1,5},{5,1},{2,6},{6,2},{3,7},{7,3},{8,12},{12,8},{9,1... | collective-permute-start | bytes 393224 | tf_op jit(solution)/shard_map/ppermute | solution.py:24
  (10 other events, 12.6 us)

commit v4 on v3

--- a/solution.py
+++ b/solution.py
@@ -31,6 +31,9 @@
 
 
 def after(value, *others):
+    if not others:
+        return value
+
     def kernel(*refs):
         del refs
 
@@ -44,12 +47,12 @@
     )(value, *others)
 
 
-def gather_lines(near, far, *ready):
+def gather_lines(near, far, ready):
     near, far = [near], [far]
     for k in range(3):
         near.append(after(passed(near[k]), *ready[k]))
         far.append(passed(far[k]))
-    near.append(passed(near[3][:192]))
+    near.append(after(passed(near[3][:192]), *ready[3]))
     far.append(passed(far[3][:192]))
     return [v for line in (near, far) for v in line + [twin(chunk) for chunk in line[1:]]]
 
@@ -58,8 +61,15 @@
     return moved(value, ("yh", "p"), lambda a, b: (1 - a, 1 - b))
 
 
-def around(value):
-    return [value] + [moved(value, ("x",), lambda a: ((a + k) % 4,)) for k in (1, 2, 3)]
+def shifted(value, k):
+    return moved(value, ("x",), lambda a: ((a + k) % 4,)) if k else value
+
+
+def around(value, cut):
+    up, down = (lambda a: ((a + 1) % 4,)), (lambda a: ((a - 1) % 4,))
+    first, third = moved(value, ("x",), up), moved(value, ("x",), down)
+    second = moved(first[:cut], ("x",), up), moved(third[cut:], ("x",), down)
+    return value, first, second, third
 
 
 def twin(value):
@@ -155,11 +165,17 @@
             out[:, (yh ^ side) * 2 + k] = part.astype(bf16).reshape(8, 32, 512)
 
 
+def rows_at(rows, at):
+    return pl.BlockSpec((rows, 512), lambda i, place: (at, 0))
+
+
 def ffn(place, tokens, gain, chunks):
+    first, second, (third, third_rest), fourth = tokens
+    mine, theirs = (first, second, third, fourth), (first, second, third_rest, fourth)
     grid_spec = pltpu.PrefetchScalarGridSpec(
         num_scalar_prefetch=1,
         grid=(2,),
-        in_specs=[pl.BlockSpec((256, 512), lambda i, place: (0, 0))] * 8
+        in_specs=[rows_at(256, at) for at in (0, 0, 0, 0, 1, 1, 0, 1)]
         + [whole(gain.shape)]
         + [anyplace()] * len(chunks),
         out_specs=pl.BlockSpec((8, 4, 32, 512), lambda i, place: (place[0] ^ i, 0, 0, 0)),
@@ -177,35 +193,43 @@
         cost_estimate=pl.CostEstimate(
             flops=512 * 2048 * 512 * 6, bytes_accessed=10 * MIB, transcendentals=512 * 512
         ),
-    )(place, *tokens, gain, *chunks)
-
-
-def memory_kernel(place, terms, tokens, gain, out):
+    )(place, *mine, *theirs, gain, *chunks)
+
+
+def memory_kernel(place, terms, *refs):
+    tokens, gains, out = refs[:4], refs[4:8], refs[8]
     square, kept = 0.0, []
     for i in range(4):
         b = (place[2] - i) & 3
         total = terms[0, b].astype(f32)
         for k in range(1, 16):
             total = total + terms[k, b].astype(f32)
-        merged = tokens[i].astype(f32) + total
+        merged = tokens[i][...].astype(f32) + total
         square = square + jnp.sum(merged * merged, axis=-1, keepdims=True)
         kept.append(merged)
     scale = lax.rsqrt(square * (1.0 / 2048) + epsilon)
     for i in range(4):
         at = pl.ds(pl.multiple_of(((place[2] - i) & 3) * 512, 512), 512)
-        rounded = (kept[i] * scale * gain[i : i + 1].astype(f32)).astype(bf16)
-        for k in range(4):
-            out[k, :, at] = rounded
-
-
-def memory_rows(place, terms, tokens, gain):
+        rounded = (kept[i] * scale * gains[i][:1].astype(f32)).astype(bf16)
+        out[:, at] = rounded
+
+
+def memory_rows(place, terms, tokens):
+    first, second, (third, third_rest), fourth = tokens
+    grid_spec = pltpu.PrefetchScalarGridSpec(
+        num_scalar_prefetch=1,
+        grid=(1,),
+        in_specs=[whole(terms.shape)]
+        + [pl.BlockSpec((32, 512), lambda i, place: (place[1] * 4 + place[2], 0))] * 4
+        + [rows_at(16, at) for at in (40, 40, 24, 40)],
+        out_specs=whole((32, 2048)),
+    )
     return pl.pallas_call(
         memory_kernel,
-        in_specs=[smem()] + [vmem()] * 3,
-        out_specs=vmem(),
-        out_shape=jax.ShapeDtypeStruct((4, 32, 2048), bf16),
+        grid_spec=grid_spec,
+        out_shape=jax.ShapeDtypeStruct((32, 2048), bf16),
         compiler_params=params(16),
-    )(place, terms, tokens, gain)
+    )(place, terms, first, second, third, fourth, first, second, third_rest, fourth)
 
 
 def query_kernel(place, t0, t1, t2, t3, gain, weight, out):
@@ -224,7 +248,7 @@
     grid_spec = pltpu.PrefetchScalarGridSpec(
         num_scalar_prefetch=1,
         grid=(1,),
-        in_specs=[pl.BlockSpec((128, 512), lambda i, place: (2, 0))] * 4
+        in_specs=[rows_at(128, at) for at in (4, 4, 2, 4)]
         + [whole(gain.shape), whole(weight.shape)],
         out_specs=whole((128, 512)),
     )
@@ -236,12 +260,12 @@
         cost_estimate=pl.CostEstimate(
             flops=2 * 128 * 2048 * 512, bytes_accessed=3 * MIB, transcendentals=0
         ),
-    )(place, *tokens, gain, weight)
-
-
-def attention_kernel(place, lengths, query, memory, wk, wv, wo, out, columns, held, sems):
-    held_in, held_out = held
-    columns[...] = memory[:, pl.ds(pl.multiple_of(place[2] * 512, 512), 512)]
+    )(place, tokens[0], tokens[1], tokens[2][1], tokens[3], gain, weight)
+
+
+def attention_kernel(place, lengths, query, m0, m1, m2, m3, wk, wv, wo, *refs):
+    outs, columns, held_in, held_out, sems = refs[:4], *refs[4:]
+    x = place[2]
     copies = []
     for k in range(8):
         source = (wk, wv)[k // 4].at[pl.ds((k % 4) * 512, 512)]
@@ -251,6 +275,11 @@
         copies.append(pltpu.make_async_copy(wo.at[rows], held_out.at[rows], sems.at[8 + k]))
     for copy in copies:
         copy.start()
+    blocks = (m0, m1, m2, m3)
+    mine = pl.ds(pl.multiple_of(x * 512, 512), 512)
+    for k, block in enumerate(blocks):
+        columns[pl.ds(pl.multiple_of(((x - k) & 3) * 32, 32), 32), :] = block[:, mine]
+    memory = jnp.concatenate([block[...] for block in blocks], 0)
     made = []
     for m in range(2):
         total = 0.0
@@ -261,7 +290,8 @@
             )
         made.append(total.astype(bf16))
     keys, values = made
-    positions = lax.broadcasted_iota(jnp.int32, (128, 128), 1)
+    spots = lax.broadcasted_iota(jnp.int32, (128, 128), 1)
+    positions = (((x - (spots >> 5)) & 3) << 5) + (spots & 31)
     valid = positions < lengths[place[1]]
     contexts = []
     for h in range(2):
@@ -276,31 +306,28 @@
     copies[8].wait()
     copies[9].wait()
     context = jnp.concatenate(contexts, axis=1)
-    for b in range(4):
-        part = jnp.dot(
-            context, held_out[:, b * 512 : (b + 1) * 512], preferred_element_type=f32
-        )
-        out[b] = part.astype(bf16)
+    for k in range(4):
+        at = pl.ds(pl.multiple_of(((x + k) & 3) * 512, 512), 512)
+        part = jnp.dot(context, held_out[:, at], preferred_element_type=f32)
+        outs[k][...] = part.astype(bf16)
 
 
 def attention(place, lengths, query, memory, wk, wv, wo):
     return pl.pallas_call(
         attention_kernel,
-        in_specs=[smem()] * 2 + [vmem()] * 2 + [anyplace()] * 3,
-        out_specs=[vmem()] * 2,
-        out_shape=[
-            jax.ShapeDtypeStruct((4, 128, 512), bf16),
-            jax.ShapeDtypeStruct((128, 512), bf16),
-        ],
+        in_specs=[smem()] * 2 + [vmem()] * 5 + [anyplace()] * 3,
+        out_specs=[vmem()] * 5,
+        out_shape=[jax.ShapeDtypeStruct((128, 512), bf16)] * 5,
         scratch_shapes=[
-            (pltpu.VMEM((8, 512, 512), bf16), pltpu.VMEM((512, 2048), bf16)),
+            pltpu.VMEM((8, 512, 512), bf16),
+            pltpu.VMEM((512, 2048), bf16),
             pltpu.SemaphoreType.DMA((10,)),
         ],
         compiler_params=params(),
         cost_estimate=pl.CostEstimate(
             flops=6 * 128 * 2048 * 512, bytes_accessed=8 * MIB, transcendentals=128 * 256
         ),
-    )(place, lengths, query, memory, wk, wv, wo)
+    )(place, lengths, query, *memory, wk, wv, wo)
 
 
 def shards(
@@ -332,26 +359,29 @@
 
     swapped = moved(local, ("p",), lambda a: (1 - a,))
     mine = jnp.where(p == 0, local, swapped)
-    theirs = opposite(mine)
+    across = moved(local, ("yh", "p"), lambda a, b: (1 - a, 0) if b == 0 else None)
+    corner = moved(local, ("yh", "p"), lambda a, b: (1 - a, 1) if b == 0 else None)
+    theirs = jnp.where(p == 0, across, corner)
     decoding = jnp.where(p == 0, swapped[:128], local[128:])
     gain_rows = jnp.broadcast_to(final_gain[None], (16, 512))
-    tokens = around(jnp.concatenate([mine, decoding, gain_rows]))
-    others = around(theirs)
-    chunks = gather_lines(near, far, (swapped,), (theirs,), tokens[1:] + others[1:])
-
-    terms = ffn(place, tokens + others, encoder_gain.reshape(4, 1, 512), chunks)
+    tokens = around(jnp.concatenate([mine, theirs, decoding, gain_rows]), 256)
+    gain = encoder_gain.reshape(4, 1, 512)
+    query_gain = decoder_gain.reshape(4, 1, 512)
+    early = swapped, across, corner
+    chunks = gather_lines(near, far, (early, (place, gain, query_gain), tokens[1:4:2], tokens[2]))
+
+    terms = ffn(place, tokens, gain, chunks)
     terms = lax.all_to_all(terms, ("yh", "p", "x"), 0, 0)
-    query = query_rows(place, tokens, decoder_gain.reshape(4, 1, 512), query_weight)
-    rows = [lax.dynamic_slice_in_dim(t, (p * 4 + x) * 32, 32, 0) for t in tokens]
-    gains = [t[384] for t in tokens]
-    memory = memory_rows(place, terms, jnp.stack(rows), jnp.stack(gains))
-    memory = lax.all_to_all(memory, "x", 0, 0).reshape(128, 2048)
-    attended, columns = attention(
+    query = query_rows(place, tokens, query_gain, query_weight)
+    memory = memory_rows(place, terms, tokens)
+    memory = [shifted(memory, k) for k in range(4)]
+    *attended, columns = attention(
         place, lengths, query, memory, key_weight, value_weight, output_weight
     )
-    attended = lax.all_to_all(attended, "x", 0, 0)
-    summed = jnp.sum(attended.astype(f32), axis=0)
-    decoded = (decoding.astype(f32) + summed).astype(bf16)
+    summed = decoding.astype(f32)
+    for k in range(4):
+        summed = summed + shifted(attended[k], k).astype(f32)
+    decoded = summed.astype(bf16)
     swapped = moved(jnp.where(p == 0, decoded, columns), ("p",), lambda a: (1 - a,))
     first = jnp.where(p == 0, columns, swapped)
     second = jnp.where(p == 0, swapped, decoded)

time: 158 us -> 142 us (0.90); the launches traced: 156 us -> 142 us
  blocking collectives: 11.7 us -> 32.2 us
  starting transfers between devices: 51.8 us -> 31.4 us
  waiting for transfers between devices: 55.5 us -> 43.4 us
  local copies, waits for them, and re-layouts: 14.5 us -> 11.2 us
  other arithmetic: 1.11 us -> 2.87 us
    all_to_all x2 -> x0, waiting for transfers between devices: 28.8 us -> none  [the longest x1 25.9 us: shards(): terms = lax.all_to_all(terms, ('yh', 'p', 'x'), 0, 0)]
    all_to_all x1, blocking collectives: 11.7 us -> 32.2 us  [shards(): terms = lax.all_to_all(terms, ('yh', 'p', 'x'), 0, 0)]
    ppermute x28 -> x33, waiting for transfers between devices: 26.7 us -> 43.4 us  [moved(): return lax.ppermute(value, axes, pairs)]
    all_to_all x2 -> x0, starting transfers between devices: 13.7 us -> none  [the longest x1 7.14 us: shards(): terms = lax.all_to_all(terms, ('yh', 'p', 'x'), 0, 0)]
    ppermute x28 -> x33, starting transfers between devices: 38.1 us -> 31.4 us  [moved(): return lax.ppermute(value, axes, pairs)]
    another operation x4 -> x0, local copies, waits for them, and re-layouts: 3.07 us -> none  [shards(): memory = memory_rows(place, terms, jnp.stack(rows), jnp.stack(gains))]
    unnamed x57 -> x75, local copies, waits for them, and re-layouts: 3.97 us -> 4.9 us
  transfers between devices with their start and end apart: 30 -> 33, of which waited for: 15 -> 17; matrix products, arithmetic and copies ran while one was open for 6% -> 3% of each run, Pallas kernels for 2% -> 3%
where the time goes in v4:
time: 142 us
  waiting for transfers between devices  43.4 us (31%)
  blocking collectives  32.2 us (23%)
  starting transfers between devices  31.4 us (22%)
  Pallas kernels  20.2 us (14%)
  local copies, waits for them, and re-layouts  11.2 us (8%)
  other arithmetic  2.87 us (2%)
    ppermute x33, waiting for transfers between devices, moved(): return lax.ppermute(value, axes, pairs)  43.4 us
    all_to_all x1, blocking collectives, shards(): terms = lax.all_to_all(terms, ('yh', 'p', 'x'), 0, 0)  32.2 us
    ppermute x33, starting transfers between devices, moved(): return lax.ppermute(value, axes, pairs)  31.4 us
    pallas_call x1, Pallas kernels, ffn(): pl.pallas_call(ffn_kernel, grid_spec=grid_spec, out_shape=jax.ShapeDtypeS...  10.2 us
    pallas_call x1, Pallas kernels, attention(): pl.pallas_call(attention_kernel, in_specs=[smem()] * 2 + [vmem()] * 5 + [...  5.24 us
    unnamed x75, local copies, waits for them, and re-layouts  4.9 us
    pallas_call x1, Pallas kernels, query_rows(): pl.pallas_call(query_kernel, grid_spec=grid_spec, out_shape=jax.ShapeDtyp...  3.78 us
  transfers between devices with their start and end apart: 33, of which 17 were waited for; matrix products, arithmetic and copies ran while one was open for 3% of the time, Pallas kernels for 3%

profile of v4, /device:TPU:6, one launch (start us, length us, event | category | flops | bytes accessed | tf_op | source)
XLA Modules:
  0.0 141.8 jit_solution(9846485624585876262)
XLA Ops:
  0.0 0.9 dynamic-slice_bitcast_fusion
  0.9 1.0 constant_dynamic-slice_fusion
  2.0 3.1 %collective-permute-start.16 = (bf16[192,512]{1,0:T(8,128)(2,1)S(1)}, bf16[192,512]{1,0:T(8,128)(2,1)S(1)}, u32[]{:S(2)}, u32[]{:S(2)}) collective-permute-start(bf16[192,512]{1,0:T(8,128)(2,1)S(1)} %pad_maximum_fusion.4), channel_id=1, source_target_pairs={{0,132},{4,128},{128,4},{132,0},{1,133},{5,129},{129,5},{133,1},{2... | collective-permute-start | bytes 589832 | tf_op jit(solution)/shard_map/ppermute | solution.py:24
  5.3 3.5 %collective-permute-start.1 = (bf16[256,512]{1,0:T(8,128)(2,1)S(1)}, bf16[256,512]{1,0:T(8,128)(2,1)S(1)}, u32[]{:S(2)}, u32[]{:S(2)}) collective-permute-start(bf16[256,512]{1,0:T(8,128)(2,1)S(1)} %bitcast.15), channel_id=1, source_target_pairs={{0,128},{128,0},{1,129},{129,1},{2,130},{130,2},{3,131},{131,3},{8... | collective-permute-start | bytes 786440 | tf_op jit(solution)/shard_map/ppermute | solution.py:24
  8.8 1.3 collective-permute-start.2
  10.1 2.0 %collective-permute-start.8 = (bf16[384,512]{1,0:T(8,128)(2,1)S(1)}, bf16[384,512]{1,0:T(8,128)(2,1)S(1)}, u32[]{:S(2)}, u32[]{:S(2)}) collective-permute-start(bf16[384,512]{1,0:T(8,128)(2,1)S(1)} %pad_maximum_fusion.1.refs_9_), channel_id=1, source_target_pairs={{0,16},{8,120},{16,32},{24,8},{32,48},{40,24},{48,64},{56,40},{64,... | collective-permute-start | bytes 1179656 | tf_op jit(solution)/shard_map/ppermute | solution.py:24
  12.2 3.5 %collective-permute-start.17 = (bf16[192,512]{1,0:T(8,128)(2,1)S(1)}, bf16[192,512]{1,0:T(8,128)(2,1)S(1)}, u32[]{:S(2)}, u32[]{:S(2)}) collective-permute-start(bf16[192,512]{1,0:T(8,128)(2,1)S(1)} %collective-permute-done.16), channel_id=1, source_target_pairs={{0,8},{8,0},{1,9},{9,1},{2,10},{10,2},{3,11},{11,3},{4,12},{12,4},... | collective-permute-start | bytes 589832 | tf_op jit(solution)/shard_map/ppermute | solution.py:24
  15.8 3.3 %collective-permute-done.1.refs_2_ = bf16[256,512]{1,0:T(8,128)(2,1)S(1)} collective-permute-done((bf16[256,512]{1,0:T(8,128)(2,1)S(1)}, bf16[256,512]{1,0:T(8,128)(2,1)S(1)}, u32[]{:S(2)}, u32[]{:S(2)}) %collective-permute-start.1) | collective-permute-done | bytes 262176 | tf_op jit(solution)/shard_map/ppermute | solution.py:24
  19.1 2.0 %collective-permute-start.18 = (bf16[384,512]{1,0:T(8,128)(2,1)S(1)}, bf16[384,512]{1,0:T(8,128)(2,1)}, u32[]{:S(2)}, u32[]{:S(2)}) collective-permute-start(bf16[384,512]{1,0:T(8,128)(2,1)S(1)} %constant_dynamic-update-slice_fusion.refs_18_), channel_id=1, source_target_pairs={{0,16},{8,120},{16,32},{24,8},{32,48},{40,24},{48,64},{56,40},{64,... | collective-permute-start | bytes 1179656 | tf_op jit(solution)/shard_map/ppermute | solution.py:24
  21.3 0.9 collective-permute-start.4
  22.2 2.4 %collective-permute-start.3 = (bf16[656,512]{1,0:T(8,128)(2,1)S(1)}, bf16[656,512]{1,0:T(8,128)(2,1)S(1)}, u32[]{:S(2)}, u32[]{:S(2)}) collective-permute-start(bf16[656,512]{1,0:T(8,128)(2,1)S(1)} %pad_maximum_fusion.t0.refs_0_.refs_4_), channel_id=1, source_target_pairs={{0,1},{1,2},{2,3},{3,0},{4,5},{5,6},{6,7},{7,4},{8,9},{9,10},{10,1... | collective-permute-start | bytes 2015240 | tf_op jit(solution)/shard_map/ppermute | solution.py:24
  24.6 0.8 copy-done.15
  25.3 1.9 %collective-permute-start.9 = (bf16[384,512]{1,0:T(8,128)(2,1)}, bf16[384,512]{1,0:T(8,128)(2,1)S(1)}, u32[]{:S(2)}, u32[]{:S(2)}) collective-permute-start(bf16[384,512]{1,0:T(8,128)(2,1)} %shard_map.119.refs_10_), channel_id=1, source_target_pairs={{0,16},{8,120},{16,32},{24,8},{32,48},{40,24},{48,64},{56,40},{64,... | collective-permute-start | bytes 1179656 | tf_op jit(solution)/shard_map/ppermute | solution.py:24
  27.3 3.6 %collective-permute-done.18.refs_19_ = bf16[384,512]{1,0:T(8,128)(2,1)} collective-permute-done((bf16[384,512]{1,0:T(8,128)(2,1)S(1)}, bf16[384,512]{1,0:T(8,128)(2,1)}, u32[]{:S(2)}, u32[]{:S(2)}) %collective-permute-start.18) | collective-permute-done | bytes 393248 | tf_op jit(solution)/shard_map/ppermute | solution.py:24
  32.8 2.9 %collective-permute-done.9.refs_0_ = bf16[384,512]{1,0:T(8,128)(2,1)S(1)} collective-permute-done((bf16[384,512]{1,0:T(8,128)(2,1)}, bf16[384,512]{1,0:T(8,128)(2,1)S(1)}, u32[]{:S(2)}, u32[]{:S(2)}) %collective-permute-start.9) | collective-permute-done | bytes 393248 | tf_op jit(solution)/shard_map/ppermute | solution.py:24
  35.6 0.8 copy-done.16
  36.4 1.4 %collective-permute-start.12 = (bf16[384,512]{1,0:T(8,128)(2,1)}, bf16[384,512]{1,0:T(8,128)(2,1)}, u32[]{:S(2)}, u32[]{:S(2)}) collective-permute-start(bf16[384,512]{1,0:T(8,128)(2,1)} %shard_map.119.refs_10_), channel_id=1, source_target_pairs={{0,8},{8,0},{1,9},{9,1},{2,10},{10,2},{3,11},{11,3},{4,12},{12,4},... | collective-permute-start | bytes 1179656 | tf_op jit(solution)/shard_map/ppermute | solution.py:24
  37.9 2.3 %collective-permute-done.19.refs_20_ = bf16[384,512]{1,0:T(8,128)(2,1)} collective-permute-done((bf16[384,512]{1,0:T(8,128)(2,1)}, bf16[384,512]{1,0:T(8,128)(2,1)}, u32[]{:S(2)}, u32[]{:S(2)}) %collective-permute-start.19) | collective-permute-done | bytes 393248 | tf_op jit(solution)/shard_map/ppermute | solution.py:24
  40.2 0.8 slice.29
  41.1 0.8 collective-permute-start.5
  42.3 0.7 slice.30
  43.0 2.6 %collective-permute-done.10.refs_0_ = bf16[384,512]{1,0:T(8,128)(2,1)S(1)} collective-permute-done((bf16[384,512]{1,0:T(8,128)(2,1)}, bf16[384,512]{1,0:T(8,128)(2,1)S(1)}, u32[]{:S(2)}, u32[]{:S(2)}) %collective-permute-start.10) | collective-permute-done | bytes 393248 | tf_op jit(solution)/shard_map/ppermute | solution.py:24
  46.4 0.9 slice.31
  47.3 2.5 %collective-permute-done.20.refs_21_ = bf16[384,512]{1,0:T(8,128)(2,1)S(1)} collective-permute-done((bf16[384,512]{1,0:T(8,128)(2,1)}, bf16[384,512]{1,0:T(8,128)(2,1)S(1)}, u32[]{:S(2)}, u32[]{:S(2)}) %collective-permute-start.20) | collective-permute-done | bytes 393248 | tf_op jit(solution)/shard_map/ppermute | solution.py:24
  50.5 1.7 %collective-permute-done.6.refs_1_.refs_2_ = bf16[256,512]{1,0:T(8,128)(2,1)S(1)} collective-permute-done((bf16[256,512]{1,0:T(8,128)(2,1)}, bf16[256,512]{1,0:T(8,128)(2,1)S(1)}, u32[]{:S(2)}, u32[]{:S(2)}) %collective-permute-start.6) | collective-permute-done | bytes 262176 | tf_op jit(solution)/shard_map/ppermute | solution.py:24
  52.2 2.5 %collective-permute-done.5.t2.refs_2_.refs_6_ = bf16[400,512]{1,0:T(8,128)(2,1)S(1)} collective-permute-done((bf16[400,512]{1,0:T(8,128)(2,1)}, bf16[400,512]{1,0:T(8,128)(2,1)S(1)}, u32[]{:S(2)}, u32[]{:S(2)}) %collective-permute-start.5) | collective-permute-done | bytes 409632 | tf_op jit(solution)/shard_map/ppermute | solution.py:24
  54.9 1.9 %collective-permute-done.11.refs_0_ = bf16[192,512]{1,0:T(8,128)(2,1)S(1)} collective-permute-done((bf16[192,512]{1,0:T(8,128)(2,1)S(1)}, bf16[192,512]{1,0:T(8,128)(2,1)S(1)}, u32[]{:S(2)}, u32[]{:S(2)}) %collective-permute-start.11) | collective-permute-done | bytes 196640 | tf_op jit(solution)/shard_map/ppermute | solution.py:24
  57.4 4.2 %collective-permute-done.21.refs_22_ = bf16[192,512]{1,0:T(8,128)(2,1)S(1)} collective-permute-done((bf16[192,512]{1,0:T(8,128)(2,1)S(1)}, bf16[192,512]{1,0:T(8,128)(2,1)S(1)}, u32[]{:S(2)}, u32[]{:S(2)}) %collective-permute-start.21) | collective-permute-done | bytes 196640 | tf_op jit(solution)/shard_map/ppermute | solution.py:24
  61.7 1.4 collective-permute-done.25.refs_26_
  63.7 0.8 copy-done.27
  64.5 10.2 %shard_map.123 = bf16[16,4,32,512]{3,2,1,0:T(8,128)(2,1)} custom-call(s32[5]{0:T(128)} %stack.23.place.refs_1_, bf16[656,512]{1,0:T(8,128)(2,1)} %copy-done.4, bf16[656,512]{1,0:T(8,128)(2,1)} %copy-done.2, bf16[256,512]{1,0:T(8,128)(2,1)} %copy-done.8, bf16[656,512]{1,0:T(8,128)(2,1)} %copy-done, bf16[656,512]{1,0:T(8,128)(2,1)} %copy-done.4, ...), custom_call_target="tpu_custom_call" | custom-call | flops 3221225472 | bytes 10485760 | tf_op jit(solution)/shard_map/pallas_call | solution.py:188
  74.7 32.2 %all_to_all.5.terms = bf16[16,4,32,512]{3,2,1,0:T(8,128)(2,1)S(1)} all-to-all(bf16[16,4,32,512]{3,2,1,0:T(8,128)(2,1)} %shard_map.123), channel_id=1, replica_groups=mesh['yh'=2,'z'=8,'c'=2,'p'=2,'x'=4] {'yh','p','x'}, dimensions={0} | all-to-all | bytes 4194304 | tf_op jit(solution)/shard_map/all_to_all | solution.py:374
  107.0 0.9 shard_map.124.m0
  107.9 2.8 %collective-permute-start.26 = (bf16[32,2048]{1,0:T(8,128)(2,1)S(1)}, bf16[32,2048]{1,0:T(8,128)(2,1)S(1)}, u32[]{:S(2)}, u32[]{:S(2)}) collective-permute-start(bf16[32,2048]{1,0:T(8,128)(2,1)S(1)} %shard_map.124.m0), channel_id=1, source_target_pairs={{0,1},{1,2},{2,3},{3,0},{4,5},{5,6},{6,7},{7,4},{8,9},{9,10},{10,1... | collective-permute-start | bytes 393224 | tf_op jit(solution)/shard_map/ppermute | solution.py:24
  110.9 1.2 collective-permute-start.28
  112.1 3.8 %shard_map.118.query = bf16[128,512]{1,0:T(8,128)(2,1)} custom-call(s32[5]{0:T(128)} %stack.23.place.refs_1_, bf16[656,512]{1,0:T(8,128)(2,1)} %copy-done.4, bf16[656,512]{1,0:T(8,128)(2,1)} %copy-done.2, bf16[400,512]{1,0:T(8,128)(2,1)} %copy-done.6, bf16[656,512]{1,0:T(8,128)(2,1)} %copy-done, bf16[4,1,512]{2,1,0:T(2,128)(2,1)} %reshape.14.gain.refs_3_, ...), custom_call_target="tpu_custom_call" | custom-call | flops 268435456 | bytes 3145728 | tf_op jit(solution)/shard_map/pallas_call | solution.py:255
  115.9 1.7 %collective-permute-done.27.m2 = bf16[32,2048]{1,0:T(8,128)(2,1)S(1)} collective-permute-done((bf16[32,2048]{1,0:T(8,128)(2,1)S(1)}, bf16[32,2048]{1,0:T(8,128)(2,1)S(1)}, u32[]{:S(2)}, u32[]{:S(2)}) %collective-permute-start.27) | collective-permute-done | bytes 131104 | tf_op jit(solution)/shard_map/ppermute | solution.py:24
  117.6 1.3 collective-permute-done.28.m3
  119.5 5.2 %shard_map.125 = (bf16[128,512]{1,0:T(8,128)(2,1)}, bf16[128,512]{1,0:T(8,128)(2,1)}, bf16[128,512]{1,0:T(8,128)(2,1)}, bf16[128,512]{1,0:T(8,128)(2,1)}, bf16[128,512]{1,0:T(8,128)(2,1)}) custom-call(s32[5]{0:T(128)} %stack.23.place.refs_1_, s32[2]{0:T(128)} %lengths.1, bf16[128,512]{1,0:T(8,128)(2,1)} %shard_map.118.query, bf16[32,2048]{1,0:T(8,128)(2,1)} %copy-done.10, ...), custom_call_target="tpu_custom_call" | custom-call | flops 805306368 | bytes 8388608 | tf_op jit(solution)/shard_map/pallas_call | solution.py:316
  124.8 0.8 collective-permute-start.29
  125.5 1.2 collective-permute-start.30
  127.4 3.5 %collective-permute-done.29 = bf16[128,512]{1,0:T(8,128)(2,1)S(1)} collective-permute-done((bf16[128,512]{1,0:T(8,128)(2,1)}, bf16[128,512]{1,0:T(8,128)(2,1)S(1)}, u32[]{:S(2)}, u32[]{:S(2)}) %collective-permute-start.29) | collective-permute-done | bytes 131104 | tf_op jit(solution)/shard_map/ppermute | solution.py:24
  130.9 2.2 %collective-permute-done.30 = bf16[128,512]{1,0:T(8,128)(2,1)S(1)} collective-permute-done((bf16[128,512]{1,0:T(8,128)(2,1)}, bf16[128,512]{1,0:T(8,128)(2,1)S(1)}, u32[]{:S(2)}, u32[]{:S(2)}) %collective-permute-start.30) | collective-permute-done | bytes 131104 | tf_op jit(solution)/shard_map/ppermute | solution.py:24
  133.1 0.9 collective-permute-done.31
  134.0 1.0 broadcast_select_fusion.4
  135.2 5.0 %collective-permute-done.32 = bf16[128,512]{1,0:T(8,128)(2,1)S(1)} collective-permute-done((bf16[128,512]{1,0:T(8,128)(2,1)S(1)}, bf16[128,512]{1,0:T(8,128)(2,1)S(1)}, u32[]{:S(2)}, u32[]{:S(2)}) %collective-permute-start.32) | collective-permute-done | bytes 131104 | tf_op jit(solution)/shard_map/ppermute | solution.py:24
  140.1 0.9 broadcast_select_fusion.3
  141.1 0.7 pad_maximum_fusion.2
  (123 shorter events, 7.3 us)
Async XLA Ops:
  1.9 8.2 %collective-permute-start.7 = (bf16[192,512]{1,0:T(8,128)(2,1)S(1)}, bf16[192,512]{1,0:T(8,128)(2,1)S(1)}, u32[]{:S(2)}, u32[]{:S(2)}) collective-permute-start(bf16[192,512]{1,0:T(8,128)(2,1)S(1)} %pad_maximum_fusion.3), channel_id=1, source_target_pairs={{0,8},{8,0},{1,9},{9,1},{2,10},{10,2},{3,11},{11,3},{4,12},{12,4},... | collective-permute-start | bytes 589832 | tf_op jit(solution)/shard_map/ppermute | solution.py:24
  2.0 10.1 %collective-permute-start.16 = (bf16[192,512]{1,0:T(8,128)(2,1)S(1)}, bf16[192,512]{1,0:T(8,128)(2,1)S(1)}, u32[]{:S(2)}, u32[]{:S(2)}) collective-permute-start(bf16[192,512]{1,0:T(8,128)(2,1)S(1)} %pad_maximum_fusion.4), channel_id=1, source_target_pairs={{0,132},{4,128},{128,4},{132,0},{1,133},{5,129},{129,5},{133,1},{2... | collective-permute-start | bytes 589832 | tf_op jit(solution)/shard_map/ppermute | solution.py:24
  5.1 10.6 %collective-permute-start = (bf16[256,512]{1,0:T(8,128)(2,1)S(1)}, bf16[256,512]{1,0:T(8,128)(2,1)S(1)}, u32[]{:S(2)}, u32[]{:S(2)}) collective-permute-start(bf16[256,512]{1,0:T(8,128)(2,1)S(1)} %bitcast.14), channel_id=1, source_target_pairs={{0,4},{4,0},{1,5},{5,1},{2,6},{6,2},{3,7},{7,3},{8,12},{12,8},{9,1... | collective-permute-start | bytes 786440 | tf_op jit(solution)/shard_map/ppermute | solution.py:24
  5.3 13.7 %collective-permute-start.1 = (bf16[256,512]{1,0:T(8,128)(2,1)S(1)}, bf16[256,512]{1,0:T(8,128)(2,1)S(1)}, u32[]{:S(2)}, u32[]{:S(2)}) collective-permute-start(bf16[256,512]{1,0:T(8,128)(2,1)S(1)} %bitcast.15), channel_id=1, source_target_pairs={{0,128},{128,0},{1,129},{129,1},{2,130},{130,2},{3,131},{131,3},{8... | collective-permute-start | bytes 786440 | tf_op jit(solution)/shard_map/ppermute | solution.py:24
  8.8 10.3 %collective-permute-start.2 = (bf16[256,512]{1,0:T(8,128)(2,1)S(1)}, bf16[256,512]{1,0:T(8,128)(2,1)S(1)}, u32[]{:S(2)}, u32[]{:S(2)}) collective-permute-start(bf16[256,512]{1,0:T(8,128)(2,1)S(1)} %bitcast.16), channel_id=1, source_target_pairs={{0,132},{128,4},{1,133},{129,5},{2,134},{130,6},{3,135},{131,7},{8... | collective-permute-start | bytes 786440 | tf_op jit(solution)/shard_map/ppermute | solution.py:24
  10.1 11.0 %copy-start.14 = (bf16[384,512]{1,0:T(8,128)(2,1)}, bf16[384,512]{1,0:T(8,128)(2,1)S(1)}, u32[]{:S(2)}) copy-start(bf16[384,512]{1,0:T(8,128)(2,1)S(1)} %pad_maximum_fusion.1.refs_9_) | copy-start | bytes 1179652
  10.1 11.0 %copy-start.36 = (bf16[512]{0:T(512)(128)(2,1)S(1)}, bf16[512]{0:T(512)(128)(2,1)}, u32[]{:S(2)}) copy-start(bf16[512]{0:T(512)(128)(2,1)} %param.18) | copy-start | bytes 3076
  10.1 14.4 %collective-permute-start.8 = (bf16[384,512]{1,0:T(8,128)(2,1)S(1)}, bf16[384,512]{1,0:T(8,128)(2,1)S(1)}, u32[]{:S(2)}, u32[]{:S(2)}) collective-permute-start(bf16[384,512]{1,0:T(8,128)(2,1)S(1)} %pad_maximum_fusion.1.refs_9_), channel_id=1, source_target_pairs={{0,16},{8,120},{16,32},{24,8},{32,48},{40,24},{48,64},{56,40},{64,... | collective-permute-start | bytes 1179656 | tf_op jit(solution)/shard_map/ppermute | solution.py:24
  12.2 6.9 %collective-permute-start.17 = (bf16[192,512]{1,0:T(8,128)(2,1)S(1)}, bf16[192,512]{1,0:T(8,128)(2,1)S(1)}, u32[]{:S(2)}, u32[]{:S(2)}) collective-permute-start(bf16[192,512]{1,0:T(8,128)(2,1)S(1)} %collective-permute-done.16), channel_id=1, source_target_pairs={{0,8},{8,0},{1,9},{9,1},{2,10},{10,2},{3,11},{11,3},{4,12},{12,4},... | collective-permute-start | bytes 589832 | tf_op jit(solution)/shard_map/ppermute | solution.py:24
  19.1 6.3 %copy-start.21 = (bf16[384,512]{1,0:T(8,128)(2,1)}, bf16[384,512]{1,0:T(8,128)(2,1)S(1)}, u32[]{:S(2)}) copy-start(bf16[384,512]{1,0:T(8,128)(2,1)S(1)} %constant_dynamic-update-slice_fusion.refs_18_) | copy-start | bytes 1179652
  19.1 11.8 %collective-permute-start.18 = (bf16[384,512]{1,0:T(8,128)(2,1)S(1)}, bf16[384,512]{1,0:T(8,128)(2,1)}, u32[]{:S(2)}, u32[]{:S(2)}) collective-permute-start(bf16[384,512]{1,0:T(8,128)(2,1)S(1)} %constant_dynamic-update-slice_fusion.refs_18_), channel_id=1, source_target_pairs={{0,16},{8,120},{16,32},{24,8},{32,48},{40,24},{48,64},{56,40},{64,... | collective-permute-start | bytes 1179656 | tf_op jit(solution)/shard_map/ppermute | solution.py:24
  21.1 9.8 %copy-start.34 = (bf16[2048]{0:T(1024)(128)(2,1)S(1)}, bf16[2048]{0:T(1024)(128)(2,1)}, u32[]{:S(2)}) copy-start(bf16[2048]{0:T(1024)(128)(2,1)} %param.19) | copy-start | bytes 12292
  21.2 10.4 %copy-start.35 = (bf16[2048]{0:T(1024)(128)(2,1)S(1)}, bf16[2048]{0:T(1024)(128)(2,1)}, u32[]{:S(2)}) copy-start(bf16[2048]{0:T(1024)(128)(2,1)} %param.14) | copy-start | bytes 12292
  21.3 19.8 %copy-start.4 = (bf16[656,512]{1,0:T(8,128)(2,1)}, bf16[656,512]{1,0:T(8,128)(2,1)S(1)}, u32[]{:S(2)}) copy-start(bf16[656,512]{1,0:T(8,128)(2,1)S(1)} %pad_maximum_fusion.t0.refs_0_.refs_4_) | copy-start | bytes 2015236
  21.3 18.9 %collective-permute-start.4 = (bf16[656,512]{1,0:T(8,128)(2,1)S(1)}, bf16[656,512]{1,0:T(8,128)(2,1)S(1)}, u32[]{:S(2)}, u32[]{:S(2)}) collective-permute-start(bf16[656,512]{1,0:T(8,128)(2,1)S(1)} %pad_maximum_fusion.t0.refs_0_.refs_4_), channel_id=1, source_target_pairs={{0,3},{1,0},{2,1},{3,2},{4,7},{5,4},{6,5},{7,6},{8,11},{9,8},{10,9... | collective-permute-start | bytes 2015240 | tf_op jit(solution)/shard_map/ppermute | solution.py:24
  22.2 19.7 %collective-permute-start.3 = (bf16[656,512]{1,0:T(8,128)(2,1)S(1)}, bf16[656,512]{1,0:T(8,128)(2,1)S(1)}, u32[]{:S(2)}, u32[]{:S(2)}) collective-permute-start(bf16[656,512]{1,0:T(8,128)(2,1)S(1)} %pad_maximum_fusion.t0.refs_0_.refs_4_), channel_id=1, source_target_pairs={{0,1},{1,2},{2,3},{3,0},{4,5},{5,6},{6,7},{7,4},{8,9},{9,10},{10,1... | collective-permute-start | bytes 2015240 | tf_op jit(solution)/shard_map/ppermute | solution.py:24
  25.3 10.3 %collective-permute-start.9 = (bf16[384,512]{1,0:T(8,128)(2,1)}, bf16[384,512]{1,0:T(8,128)(2,1)S(1)}, u32[]{:S(2)}, u32[]{:S(2)}) collective-permute-start(bf16[384,512]{1,0:T(8,128)(2,1)} %shard_map.119.refs_10_), channel_id=1, source_target_pairs={{0,16},{8,120},{16,32},{24,8},{32,48},{40,24},{48,64},{56,40},{64,... | collective-permute-start | bytes 1179656 | tf_op jit(solution)/shard_map/ppermute | solution.py:24
  30.9 9.3 %collective-permute-start.19 = (bf16[384,512]{1,0:T(8,128)(2,1)}, bf16[384,512]{1,0:T(8,128)(2,1)}, u32[]{:S(2)}, u32[]{:S(2)}) collective-permute-start(bf16[384,512]{1,0:T(8,128)(2,1)} %collective-permute-done.18.refs_19_), channel_id=1, source_target_pairs={{0,16},{8,120},{16,32},{24,8},{32,48},{40,24},{48,64},{56,40},{64,... | collective-permute-start | bytes 1179656 | tf_op jit(solution)/shard_map/ppermute | solution.py:24
  36.4 9.2 %collective-permute-start.10 = (bf16[384,512]{1,0:T(8,128)(2,1)}, bf16[384,512]{1,0:T(8,128)(2,1)S(1)}, u32[]{:S(2)}, u32[]{:S(2)}) collective-permute-start(bf16[384,512]{1,0:T(8,128)(2,1)} %shard_map.120.refs_11_), channel_id=1, source_target_pairs={{0,16},{8,120},{16,32},{24,8},{32,48},{40,24},{48,64},{56,40},{64,... | collective-permute-start | bytes 1179656 | tf_op jit(solution)/shard_map/ppermute | solution.py:24
  36.4 10.0 %collective-permute-start.12 = (bf16[384,512]{1,0:T(8,128)(2,1)}, bf16[384,512]{1,0:T(8,128)(2,1)}, u32[]{:S(2)}, u32[]{:S(2)}) collective-permute-start(bf16[384,512]{1,0:T(8,128)(2,1)} %shard_map.119.refs_10_), channel_id=1, source_target_pairs={{0,8},{8,0},{1,9},{9,1},{2,10},{10,2},{3,11},{11,3},{4,12},{12,4},... | collective-permute-start | bytes 1179656 | tf_op jit(solution)/shard_map/ppermute | solution.py:24
  40.2 9.6 %collective-permute-start.20 = (bf16[384,512]{1,0:T(8,128)(2,1)}, bf16[384,512]{1,0:T(8,128)(2,1)S(1)}, u32[]{:S(2)}, u32[]{:S(2)}) collective-permute-start(bf16[384,512]{1,0:T(8,128)(2,1)} %collective-permute-done.19.refs_20_), channel_id=1, source_target_pairs={{0,16},{8,120},{16,32},{24,8},{32,48},{40,24},{48,64},{56,40},{64,... | collective-permute-start | bytes 1179656 | tf_op jit(solution)/shard_map/ppermute | solution.py:24
  41.1 13.6 %collective-permute-start.5 = (bf16[400,512]{1,0:T(8,128)(2,1)}, bf16[400,512]{1,0:T(8,128)(2,1)S(1)}, u32[]{:S(2)}, u32[]{:S(2)}) collective-permute-start(bf16[400,512]{1,0:T(8,128)(2,1)} %slice.29), channel_id=1, source_target_pairs={{0,3},{1,0},{2,1},{3,2},{4,7},{5,4},{6,5},{7,6},{8,11},{9,8},{10,9... | collective-permute-start | bytes 1228808 | tf_op jit(solution)/shard_map/ppermute | solution.py:24
  41.9 8.0 %collective-permute-start.22 = (bf16[384,512]{1,0:T(8,128)(2,1)}, bf16[384,512]{1,0:T(8,128)(2,1)}, u32[]{:S(2)}, u32[]{:S(2)}) collective-permute-start(bf16[384,512]{1,0:T(8,128)(2,1)} %collective-permute-done.18.refs_19_), channel_id=1, source_target_pairs={{0,8},{8,0},{1,9},{9,1},{2,10},{10,2},{3,11},{11,3},{4,12},{12,4},... | collective-permute-start | bytes 1179656 | tf_op jit(solution)/shard_map/ppermute | solution.py:24
  45.6 6.6 %collective-permute-start.6 = (bf16[256,512]{1,0:T(8,128)(2,1)}, bf16[256,512]{1,0:T(8,128)(2,1)S(1)}, u32[]{:S(2)}, u32[]{:S(2)}) collective-permute-start(bf16[256,512]{1,0:T(8,128)(2,1)} %slice.30), channel_id=1, source_target_pairs={{0,1},{1,2},{2,3},{3,0},{4,5},{5,6},{6,7},{7,4},{8,9},{9,10},{10,1... | collective-permute-start | bytes 786440 | tf_op jit(solution)/shard_map/ppermute | solution.py:24
  46.4 11.0 %collective-permute-start.13 = (bf16[384,512]{1,0:T(8,128)(2,1)S(1)}, bf16[384,512]{1,0:T(8,128)(2,1)S(1)}, u32[]{:S(2)}, u32[]{:S(2)}) collective-permute-start(bf16[384,512]{1,0:T(8,128)(2,1)S(1)} %copy-done.17), channel_id=1, source_target_pairs={{0,8},{8,0},{1,9},{9,1},{2,10},{10,2},{3,11},{11,3},{4,12},{12,4},... | collective-permute-start | bytes 1179656 | tf_op jit(solution)/shard_map/ppermute | solution.py:24
  49.8 13.2 %copy-start.20 = (bf16[384,512]{1,0:T(8,128)(2,1)}, bf16[384,512]{1,0:T(8,128)(2,1)S(1)}, u32[]{:S(2)}) copy-start(bf16[384,512]{1,0:T(8,128)(2,1)S(1)} %collective-permute-done.20.refs_21_) | copy-start | bytes 1179652
  49.8 6.9 %collective-permute-start.11 = (bf16[192,512]{1,0:T(8,128)(2,1)S(1)}, bf16[192,512]{1,0:T(8,128)(2,1)S(1)}, u32[]{:S(2)}, u32[]{:S(2)}) collective-permute-start(bf16[192,512]{1,0:T(8,128)(2,1)S(1)} %slice.31), channel_id=1, source_target_pairs={{0,16},{8,120},{16,32},{24,8},{32,48},{40,24},{48,64},{56,40},{64,... | collective-permute-start | bytes 589832 | tf_op jit(solution)/shard_map/ppermute | solution.py:24
  49.9 11.7 %collective-permute-start.23 = (bf16[384,512]{1,0:T(8,128)(2,1)}, bf16[384,512]{1,0:T(8,128)(2,1)S(1)}, u32[]{:S(2)}, u32[]{:S(2)}) collective-permute-start(bf16[384,512]{1,0:T(8,128)(2,1)} %collective-permute-done.19.refs_20_), channel_id=1, source_target_pairs={{0,8},{8,0},{1,9},{9,1},{2,10},{10,2},{3,11},{11,3},{4,12},{12,4},... | collective-permute-start | bytes 1179656 | tf_op jit(solution)/shard_map/ppermute | solution.py:24
  52.2 9.4 %collective-permute-start.14 = (bf16[384,512]{1,0:T(8,128)(2,1)}, bf16[384,512]{1,0:T(8,128)(2,1)S(1)}, u32[]{:S(2)}, u32[]{:S(2)}) collective-permute-start(bf16[384,512]{1,0:T(8,128)(2,1)} %shard_map.121.refs_12_), channel_id=1, source_target_pairs={{0,8},{8,0},{1,9},{9,1},{2,10},{10,2},{3,11},{11,3},{4,12},{12,4},... | collective-permute-start | bytes 1179656 | tf_op jit(solution)/shard_map/ppermute | solution.py:24
  54.7 6.9 %collective-permute-start.21 = (bf16[192,512]{1,0:T(8,128)(2,1)S(1)}, bf16[192,512]{1,0:T(8,128)(2,1)S(1)}, u32[]{:S(2)}, u32[]{:S(2)}) collective-permute-start(bf16[192,512]{1,0:T(8,128)(2,1)S(1)} %slice.32), channel_id=1, source_target_pairs={{0,16},{8,120},{16,32},{24,8},{32,48},{40,24},{48,64},{56,40},{64,... | collective-permute-start | bytes 589832 | tf_op jit(solution)/shard_map/ppermute | solution.py:24
  56.7 6.3 %collective-permute-start.24 = (bf16[384,512]{1,0:T(8,128)(2,1)S(1)}, bf16[384,512]{1,0:T(8,128)(2,1)S(1)}, u32[]{:S(2)}, u32[]{:S(2)}) collective-permute-start(bf16[384,512]{1,0:T(8,128)(2,1)S(1)} %collective-permute-done.20.refs_21_), channel_id=1, source_target_pairs={{0,8},{8,0},{1,9},{9,1},{2,10},{10,2},{3,11},{11,3},{4,12},{12,4},... | collective-permute-start | bytes 1179656 | tf_op jit(solution)/shard_map/ppermute | solution.py:24
  57.4 5.6 %copy-start.24 = (bf16[384,512]{1,0:T(8,128)(2,1)}, bf16[384,512]{1,0:T(8,128)(2,1)S(1)}, u32[]{:S(2)}) copy-start(bf16[384,512]{1,0:T(8,128)(2,1)S(1)} %collective-permute-done.13.refs_15_) | copy-start | bytes 1179652
  57.4 4.2 %collective-permute-start.15 = (bf16[192,512]{1,0:T(8,128)(2,1)}, bf16[192,512]{1,0:T(8,128)(2,1)S(1)}, u32[]{:S(2)}, u32[]{:S(2)}) collective-permute-start(bf16[192,512]{1,0:T(8,128)(2,1)} %shard_map.122.refs_13_), channel_id=1, source_target_pairs={{0,8},{8,0},{1,9},{9,1},{2,10},{10,2},{3,11},{11,3},{4,12},{12,4},... | collective-permute-start | bytes 589832 | tf_op jit(solution)/shard_map/ppermute | solution.py:24
  61.6 1.4 %collective-permute-start.25 = (bf16[192,512]{1,0:T(8,128)(2,1)S(1)}, bf16[192,512]{1,0:T(8,128)(2,1)S(1)}, u32[]{:S(2)}, u32[]{:S(2)}) collective-permute-start(bf16[192,512]{1,0:T(8,128)(2,1)S(1)} %collective-permute-done.21.refs_22_), channel_id=1, source_target_pairs={{0,8},{8,0},{1,9},{9,1},{2,10},{10,2},{3,11},{11,3},{4,12},{12,4},... | collective-permute-start | bytes 589832 | tf_op jit(solution)/shard_map/ppermute | solution.py:24
  74.7 32.2 %copy-start.1 = (bf16[656,512]{1,0:T(8,128)(2,1)S(1)}, bf16[656,512]{1,0:T(8,128)(2,1)}, u32[]{:S(2)}) copy-start(bf16[656,512]{1,0:T(8,128)(2,1)} %copy-done) | copy-start | bytes 2015236
  74.7 32.2 %copy-start.3 = (bf16[656,512]{1,0:T(8,128)(2,1)S(1)}, bf16[656,512]{1,0:T(8,128)(2,1)}, u32[]{:S(2)}) copy-start(bf16[656,512]{1,0:T(8,128)(2,1)} %copy-done.2) | copy-start | bytes 2015236
  74.7 32.2 %copy-start.5 = (bf16[656,512]{1,0:T(8,128)(2,1)S(1)}, bf16[656,512]{1,0:T(8,128)(2,1)}, u32[]{:S(2)}) copy-start(bf16[656,512]{1,0:T(8,128)(2,1)} %copy-done.4) | copy-start | bytes 2015236
  74.7 32.2 %copy-start.7 = (bf16[400,512]{1,0:T(8,128)(2,1)S(1)}, bf16[400,512]{1,0:T(8,128)(2,1)}, u32[]{:S(2)}) copy-start(bf16[400,512]{1,0:T(8,128)(2,1)} %copy-done.6) | copy-start | bytes 1228804
  74.7 32.2 %copy-start.9 = (bf16[256,512]{1,0:T(8,128)(2,1)S(1)}, bf16[256,512]{1,0:T(8,128)(2,1)}, u32[]{:S(2)}) copy-start(bf16[256,512]{1,0:T(8,128)(2,1)} %copy-done.8) | copy-start | bytes 786436
  74.7 32.2 %copy-start.11 = (s32[5]{0:T(128)S(1)}, s32[5]{0:T(128)}, u32[]{:S(2)}) copy-start(s32[5]{0:T(128)} %stack.23.place.refs_1_) | copy-start | bytes 64
  107.9 8.0 %copy-start.10 = (bf16[32,2048]{1,0:T(8,128)(2,1)}, bf16[32,2048]{1,0:T(8,128)(2,1)S(1)}, u32[]{:S(2)}) copy-start(bf16[32,2048]{1,0:T(8,128)(2,1)S(1)} %shard_map.124.m0) | copy-start | bytes 393220
  107.9 8.0 %collective-permute-start.26 = (bf16[32,2048]{1,0:T(8,128)(2,1)S(1)}, bf16[32,2048]{1,0:T(8,128)(2,1)S(1)}, u32[]{:S(2)}, u32[]{:S(2)}) collective-permute-start(bf16[32,2048]{1,0:T(8,128)(2,1)S(1)} %shard_map.124.m0), channel_id=1, source_target_pairs={{0,1},{1,2},{2,3},{3,0},{4,5},{5,6},{6,7},{7,4},{8,9},{9,10},{10,1... | collective-permute-start | bytes 393224 | tf_op jit(solution)/shard_map/ppermute | solution.py:24
  110.7 6.9 %collective-permute-start.27 = (bf16[32,2048]{1,0:T(8,128)(2,1)S(1)}, bf16[32,2048]{1,0:T(8,128)(2,1)S(1)}, u32[]{:S(2)}, u32[]{:S(2)}) collective-permute-start(bf16[32,2048]{1,0:T(8,128)(2,1)S(1)} %shard_map.124.m0), channel_id=1, source_target_pairs={{0,2},{1,3},{2,0},{3,1},{4,6},{5,7},{6,4},{7,5},{8,10},{9,11},{10,... | collective-permute-start | bytes 393224 | tf_op jit(solution)/shard_map/ppermute | solution.py:24
  110.9 8.0 %collective-permute-start.28 = (bf16[32,2048]{1,0:T(8,128)(2,1)S(1)}, bf16[32,2048]{1,0:T(8,128)(2,1)S(1)}, u32[]{:S(2)}, u32[]{:S(2)}) collective-permute-start(bf16[32,2048]{1,0:T(8,128)(2,1)S(1)} %shard_map.124.m0), channel_id=1, source_target_pairs={{0,3},{1,0},{2,1},{3,2},{4,7},{5,4},{6,5},{7,6},{8,11},{9,8},{10,9... | collective-permute-start | bytes 393224 | tf_op jit(solution)/shard_map/ppermute | solution.py:24
  124.8 6.1 %collective-permute-start.29 = (bf16[128,512]{1,0:T(8,128)(2,1)}, bf16[128,512]{1,0:T(8,128)(2,1)S(1)}, u32[]{:S(2)}, u32[]{:S(2)}) collective-permute-start(bf16[128,512]{1,0:T(8,128)(2,1)} %get-tuple-element.12), channel_id=1, source_target_pairs={{0,1},{1,2},{2,3},{3,0},{4,5},{5,6},{6,7},{7,4},{8,9},{9,10},{10,1... | collective-permute-start | bytes 393224 | tf_op jit(solution)/shard_map/ppermute | solution.py:24
  125.5 7.6 %collective-permute-start.30 = (bf16[128,512]{1,0:T(8,128)(2,1)}, bf16[128,512]{1,0:T(8,128)(2,1)S(1)}, u32[]{:S(2)}, u32[]{:S(2)}) collective-permute-start(bf16[128,512]{1,0:T(8,128)(2,1)} %get-tuple-element.13), channel_id=1, source_target_pairs={{0,2},{1,3},{2,0},{3,1},{4,6},{5,7},{6,4},{7,5},{8,10},{9,11},{10,... | collective-permute-start | bytes 393224 | tf_op jit(solution)/shard_map/ppermute | solution.py:24
  126.7 7.3 %collective-permute-start.31 = (bf16[128,512]{1,0:T(8,128)(2,1)}, bf16[128,512]{1,0:T(8,128)(2,1)S(1)}, u32[]{:S(2)}, u32[]{:S(2)}) collective-permute-start(bf16[128,512]{1,0:T(8,128)(2,1)} %get-tuple-element.14), channel_id=1, source_target_pairs={{0,3},{1,0},{2,1},{3,2},{4,7},{5,4},{6,5},{7,6},{8,11},{9,8},{10,9... | collective-permute-start | bytes 393224 | tf_op jit(solution)/shard_map/ppermute | solution.py:24
  135.1 5.1 %collective-permute-start.32 = (bf16[128,512]{1,0:T(8,128)(2,1)S(1)}, bf16[128,512]{1,0:T(8,128)(2,1)S(1)}, u32[]{:S(2)}, u32[]{:S(2)}) collective-permute-start(bf16[128,512]{1,0:T(8,128)(2,1)S(1)} %get-tuple-element.15), channel_id=1, source_target_pairs={{0,4},{4,0},{1,5},{5,1},{2,6},{6,2},{3,7},{7,3},{8,12},{12,8},{9,1... | collective-permute-start | bytes 393224 | tf_op jit(solution)/shard_map/ppermute | solution.py:24
  (22 other events, 51.7 us)

commit v5 on v4

--- a/solution.py
+++ b/solution.py
@@ -43,7 +43,7 @@
         out_specs=anyplace(),
         out_shape=jax.ShapeDtypeStruct(value.shape, value.dtype),
         input_output_aliases={0: 0},
-        compiler_params=params(),
+        compiler_params=params(1),
     )(value, *others)
 
 
@@ -232,7 +232,14 @@
     )(place, terms, first, second, third, fourth, first, second, third_rest, fourth)
 
 
-def query_kernel(place, t0, t1, t2, t3, gain, weight, out):
+def query_kernel(place, t0, t1, t2, t3, gain, weight, wk, wv, wo, out, *held):
+    kept, sems = held[:3], held[3]
+    copies = [
+        pltpu.make_async_copy(source, target, sems.at[i])
+        for i, (source, target) in enumerate(zip((wk, wv, wo), kept))
+    ]
+    for copy in copies:
+        copy.start()
     blocks = (t0, t1, t2, t3)
     scale = scale_of(blocks)
     total = 0.0
@@ -242,54 +249,43 @@
         n = normed_block(block, scale, gain[b])
         total += jnp.dot(n, rows, preferred_element_type=f32)
     out[...] = total.astype(bf16)
-
-
-def query_rows(place, tokens, gain, weight):
+    for copy in copies:
+        copy.wait()
+
+
+def query_rows(place, tokens, gain, weight, others):
     grid_spec = pltpu.PrefetchScalarGridSpec(
         num_scalar_prefetch=1,
         grid=(1,),
         in_specs=[rows_at(128, at) for at in (4, 4, 2, 4)]
-        + [whole(gain.shape), whole(weight.shape)],
-        out_specs=whole((128, 512)),
+        + [whole(gain.shape), whole(weight.shape)]
+        + [anyplace()] * 3,
+        out_specs=[whole((128, 512))] + [vmem()] * 3,
+        scratch_shapes=[pltpu.SemaphoreType.DMA((3,))],
     )
     return pl.pallas_call(
         query_kernel,
         grid_spec=grid_spec,
-        out_shape=jax.ShapeDtypeStruct((128, 512), bf16),
-        compiler_params=params(),
+        out_shape=[jax.ShapeDtypeStruct((128, 512), bf16)]
+        + [jax.ShapeDtypeStruct(w.shape, bf16) for w in others],
+        compiler_params=params(40),
         cost_estimate=pl.CostEstimate(
-            flops=2 * 128 * 2048 * 512, bytes_accessed=3 * MIB, transcendentals=0
+            flops=2 * 128 * 2048 * 512, bytes_accessed=10 * MIB, transcendentals=0
         ),
-    )(place, tokens[0], tokens[1], tokens[2][1], tokens[3], gain, weight)
+    )(place, tokens[0], tokens[1], tokens[2][1], tokens[3], gain, weight, *others)
 
 
 def attention_kernel(place, lengths, query, m0, m1, m2, m3, wk, wv, wo, *refs):
-    outs, columns, held_in, held_out, sems = refs[:4], *refs[4:]
+    outs, columns = refs[:4], refs[4]
     x = place[2]
-    copies = []
-    for k in range(8):
-        source = (wk, wv)[k // 4].at[pl.ds((k % 4) * 512, 512)]
-        copies.append(pltpu.make_async_copy(source, held_in.at[k], sems.at[k]))
-    for k in range(2):
-        rows = pl.ds(k * 256, 256)
-        copies.append(pltpu.make_async_copy(wo.at[rows], held_out.at[rows], sems.at[8 + k]))
-    for copy in copies:
-        copy.start()
     blocks = (m0, m1, m2, m3)
     mine = pl.ds(pl.multiple_of(x * 512, 512), 512)
     for k, block in enumerate(blocks):
         columns[pl.ds(pl.multiple_of(((x - k) & 3) * 32, 32), 32), :] = block[:, mine]
     memory = jnp.concatenate([block[...] for block in blocks], 0)
-    made = []
-    for m in range(2):
-        total = 0.0
-        for k in range(4):
-            copies[m * 4 + k].wait()
-            total += jnp.dot(
-                memory[:, k * 512 : (k + 1) * 512], held_in[m * 4 + k], preferred_element_type=f32
-            )
-        made.append(total.astype(bf16))
-    keys, values = made
+    keys, values = (
+        jnp.dot(memory, w[...], preferred_element_type=f32).astype(bf16) for w in (wk, wv)
+    )
     spots = lax.broadcasted_iota(jnp.int32, (128, 128), 1)
     positions = (((x - (spots >> 5)) & 3) << 5) + (spots & 31)
     valid = positions < lengths[place[1]]
@@ -303,27 +299,20 @@
         weights = jnp.exp(scores - jnp.max(scores, axis=-1, keepdims=True))
         probs = (weights / jnp.sum(weights, axis=-1, keepdims=True)).astype(bf16)
         contexts.append(jnp.dot(probs, values[:, at], preferred_element_type=f32).astype(bf16))
-    copies[8].wait()
-    copies[9].wait()
     context = jnp.concatenate(contexts, axis=1)
     for k in range(4):
         at = pl.ds(pl.multiple_of(((x + k) & 3) * 512, 512), 512)
-        part = jnp.dot(context, held_out[:, at], preferred_element_type=f32)
+        part = jnp.dot(context, wo[:, at], preferred_element_type=f32)
         outs[k][...] = part.astype(bf16)
 
 
 def attention(place, lengths, query, memory, wk, wv, wo):
     return pl.pallas_call(
         attention_kernel,
-        in_specs=[smem()] * 2 + [vmem()] * 5 + [anyplace()] * 3,
+        in_specs=[smem()] * 2 + [vmem()] * 8,
         out_specs=[vmem()] * 5,
         out_shape=[jax.ShapeDtypeStruct((128, 512), bf16)] * 5,
-        scratch_shapes=[
-            pltpu.VMEM((8, 512, 512), bf16),
-            pltpu.VMEM((512, 2048), bf16),
-            pltpu.SemaphoreType.DMA((10,)),
-        ],
-        compiler_params=params(),
+        compiler_params=params(16),
         cost_estimate=pl.CostEstimate(
             flops=6 * 128 * 2048 * 512, bytes_accessed=8 * MIB, transcendentals=128 * 256
         ),
@@ -372,12 +361,12 @@
 
     terms = ffn(place, tokens, gain, chunks)
     terms = lax.all_to_all(terms, ("yh", "p", "x"), 0, 0)
-    query = query_rows(place, tokens, query_gain, query_weight)
+    query, *others = query_rows(
+        place, tokens, query_gain, query_weight, (key_weight, value_weight, output_weight)
+    )
     memory = memory_rows(place, terms, tokens)
     memory = [shifted(memory, k) for k in range(4)]
-    *attended, columns = attention(
-        place, lengths, query, memory, key_weight, value_weight, output_weight
-    )
+    *attended, columns = attention(place, lengths, query, memory, *others)
     summed = decoding.astype(f32)
     for k in range(4):
         summed = summed + shifted(attended[k], k).astype(f32)

time: 142 us -> 135 us (0.951)
  local copies, waits for them, and re-layouts: 11.2 us -> 3.4 us
  Pallas kernels: 20.2 us -> 16.1 us
  starting transfers between devices: 31.4 us -> 34.4 us
  waiting for transfers between devices: 43.4 us -> 46.4 us
  other arithmetic: 2.87 us -> 1.05 us
    pallas_call x2, Pallas kernels: 9.02 us -> 5 us  [the longest x1 2.99 us: query_rows(): pl.pallas_call(query_kernel, grid_spec=grid_spec, out_shape=[jax.ShapeDty...]
    unnamed x75, local copies, waits for them, and re-layouts: 4.9 us -> 1.31 us
    ppermute x33, waiting for transfers between devices: 43.4 us -> 46.4 us  [moved(): return lax.ppermute(value, axes, pairs)]
    ppermute x33, starting transfers between devices: 31.4 us -> 34.4 us  [moved(): return lax.ppermute(value, axes, pairs)]
    slice x2, local copies, waits for them, and re-layouts: 1.57 us -> 0.05 us  [around(): second = (moved(first[:cut], ('x',), up), moved(third[cut:], ('x',), down))]
  transfers between devices with their start and end apart: 33 -> 33, of which waited for: 17 -> 17; matrix products, arithmetic and copies ran while one was open for 3% -> 0% of each run, Pallas kernels for 3% -> 2%
where the time goes in v5:
time: 135 us; the launch traced here: 134 us
  waiting for transfers between devices  46.4 us (34%)
  starting transfers between devices  34.4 us (25%)
  blocking collectives  32.1 us (24%)
  Pallas kernels  16.1 us (12%)
  local copies, waits for them, and re-layouts  3.4 us (3%)
    ppermute x33, waiting for transfers between devices, moved(): return lax.ppermute(value, axes, pairs)  46.4 us
    ppermute x33, starting transfers between devices, moved(): return lax.ppermute(value, axes, pairs)  34.4 us
    all_to_all x1, blocking collectives, shards(): terms = lax.all_to_all(terms, ('yh', 'p', 'x'), 0, 0)  32.1 us
    pallas_call x1, Pallas kernels, ffn(): pl.pallas_call(ffn_kernel, grid_spec=grid_spec, out_shape=jax.ShapeDtypeS...  10.2 us
    pallas_call x1, Pallas kernels, query_rows(): pl.pallas_call(query_kernel, grid_spec=grid_spec, out_shape=[jax.ShapeDty...  2.99 us
  transfers between devices with their start and end apart: 33, of which 17 were waited for; matrix products, arithmetic and copies ran while one was open for 0% of the time, Pallas kernels for 2%

profile of v5, /device:TPU:6, one launch (start us, length us, event | category | flops | bytes accessed | tf_op | source)
XLA Modules:
  0.0 134.2 jit_solution(15811966021102087411)
XLA Ops:
  0.0 0.9 dynamic-slice_bitcast_fusion
  0.9 1.0 constant_dynamic-slice_fusion
  2.1 3.1 %collective-permute-start.16 = (bf16[192,512]{1,0:T(8,128)(2,1)S(1)}, bf16[192,512]{1,0:T(8,128)(2,1)S(1)}, u32[]{:S(2)}, u32[]{:S(2)}) collective-permute-start(bf16[192,512]{1,0:T(8,128)(2,1)S(1)} %pad_maximum_fusion.4), channel_id=1, source_target_pairs={{0,132},{4,128},{128,4},{132,0},{1,133},{5,129},{129,5},{133,1},{2... | collective-permute-start | bytes 589832 | tf_op jit(solution)/shard_map/ppermute | solution.py:24
  5.2 0.1 collective-permute-start
  5.3 3.5 %collective-permute-start.1 = (bf16[256,512]{1,0:T(8,128)(2,1)}, bf16[256,512]{1,0:T(8,128)(2,1)S(1)}, u32[]{:S(2)}, u32[]{:S(2)}) collective-permute-start(bf16[256,512]{1,0:T(8,128)(2,1)} %bitcast.15), channel_id=1, source_target_pairs={{0,128},{128,0},{1,129},{129,1},{2,130},{130,2},{3,131},{131,3},{8... | collective-permute-start | bytes 786440 | tf_op jit(solution)/shard_map/ppermute | solution.py:24
  8.8 1.3 collective-permute-start.2
  10.1 2.0 %collective-permute-start.8 = (bf16[384,512]{1,0:T(8,128)(2,1)S(1)}, bf16[384,512]{1,0:T(8,128)(2,1)S(1)}, u32[]{:S(2)}, u32[]{:S(2)}) collective-permute-start(bf16[384,512]{1,0:T(8,128)(2,1)S(1)} %pad_maximum_fusion.1.refs_9_), channel_id=1, source_target_pairs={{0,16},{8,120},{16,32},{24,8},{32,48},{40,24},{48,64},{56,40},{64,... | collective-permute-start | bytes 1179656 | tf_op jit(solution)/shard_map/ppermute | solution.py:24
  12.1 3.5 %collective-permute-start.17 = (bf16[192,512]{1,0:T(8,128)(2,1)S(1)}, bf16[192,512]{1,0:T(8,128)(2,1)S(1)}, u32[]{:S(2)}, u32[]{:S(2)}) collective-permute-start(bf16[192,512]{1,0:T(8,128)(2,1)S(1)} %collective-permute-done.16), channel_id=1, source_target_pairs={{0,8},{8,0},{1,9},{9,1},{2,10},{10,2},{3,11},{11,3},{4,12},{12,4},... | collective-permute-start | bytes 589832 | tf_op jit(solution)/shard_map/ppermute | solution.py:24
  15.7 3.5 %collective-permute-done.1.refs_2_ = bf16[256,512]{1,0:T(8,128)(2,1)S(1)} collective-permute-done((bf16[256,512]{1,0:T(8,128)(2,1)}, bf16[256,512]{1,0:T(8,128)(2,1)S(1)}, u32[]{:S(2)}, u32[]{:S(2)}) %collective-permute-start.1) | collective-permute-done | bytes 262176 | tf_op jit(solution)/shard_map/ppermute | solution.py:24
  19.3 2.0 %collective-permute-start.18 = (bf16[384,512]{1,0:T(8,128)(2,1)S(1)}, bf16[384,512]{1,0:T(8,128)(2,1)}, u32[]{:S(2)}, u32[]{:S(2)}) collective-permute-start(bf16[384,512]{1,0:T(8,128)(2,1)S(1)} %constant_dynamic-update-slice_fusion.refs_18_), channel_id=1, source_target_pairs={{0,16},{8,120},{16,32},{24,8},{32,48},{40,24},{48,64},{56,40},{64,... | collective-permute-start | bytes 1179656 | tf_op jit(solution)/shard_map/ppermute | solution.py:24
  21.4 0.6 copy-done.21
  22.0 0.8 collective-permute-start.4
  22.8 2.4 %collective-permute-start.3 = (bf16[656,512]{1,0:T(8,128)(2,1)S(1)}, bf16[656,512]{1,0:T(8,128)(2,1)S(1)}, u32[]{:S(2)}, u32[]{:S(2)}) collective-permute-start(bf16[656,512]{1,0:T(8,128)(2,1)S(1)} %pad_maximum_fusion.t0.refs_0_.refs_4_), channel_id=1, source_target_pairs={{0,1},{1,2},{2,3},{3,0},{4,5},{5,6},{6,7},{7,4},{8,9},{9,10},{10,1... | collective-permute-start | bytes 2015240 | tf_op jit(solution)/shard_map/ppermute | solution.py:24
  25.2 2.0 %collective-permute-start.9 = (bf16[384,512]{1,0:T(8,128)(2,1)S(1)}, bf16[384,512]{1,0:T(8,128)(2,1)S(1)}, u32[]{:S(2)}, u32[]{:S(2)}) collective-permute-start(bf16[384,512]{1,0:T(8,128)(2,1)S(1)} %shard_map.119.refs_10_), channel_id=1, source_target_pairs={{0,16},{8,120},{16,32},{24,8},{32,48},{40,24},{48,64},{56,40},{64,... | collective-permute-start | bytes 1179656 | tf_op jit(solution)/shard_map/ppermute | solution.py:24
  27.2 3.9 %collective-permute-done.18.refs_19_ = bf16[384,512]{1,0:T(8,128)(2,1)} collective-permute-done((bf16[384,512]{1,0:T(8,128)(2,1)S(1)}, bf16[384,512]{1,0:T(8,128)(2,1)}, u32[]{:S(2)}, u32[]{:S(2)}) %collective-permute-start.18) | collective-permute-done | bytes 393248 | tf_op jit(solution)/shard_map/ppermute | solution.py:24
  31.2 4.0 %collective-permute-done.9.refs_0_ = bf16[384,512]{1,0:T(8,128)(2,1)S(1)} collective-permute-done((bf16[384,512]{1,0:T(8,128)(2,1)S(1)}, bf16[384,512]{1,0:T(8,128)(2,1)S(1)}, u32[]{:S(2)}, u32[]{:S(2)}) %collective-permute-start.9) | collective-permute-done | bytes 393248 | tf_op jit(solution)/shard_map/ppermute | solution.py:24
  35.2 1.6 %collective-permute-start.12 = (bf16[384,512]{1,0:T(8,128)(2,1)S(1)}, bf16[384,512]{1,0:T(8,128)(2,1)S(1)}, u32[]{:S(2)}, u32[]{:S(2)}) collective-permute-start(bf16[384,512]{1,0:T(8,128)(2,1)S(1)} %shard_map.119.refs_10_), channel_id=1, source_target_pairs={{0,8},{8,0},{1,9},{9,1},{2,10},{10,2},{3,11},{11,3},{4,12},{12,4},... | collective-permute-start | bytes 1179656 | tf_op jit(solution)/shard_map/ppermute | solution.py:24
  36.9 3.5 %collective-permute-done.19.refs_20_ = bf16[384,512]{1,0:T(8,128)(2,1)} collective-permute-done((bf16[384,512]{1,0:T(8,128)(2,1)}, bf16[384,512]{1,0:T(8,128)(2,1)}, u32[]{:S(2)}, u32[]{:S(2)}) %collective-permute-start.19) | collective-permute-done | bytes 393248 | tf_op jit(solution)/shard_map/ppermute | solution.py:24
  40.5 0.9 collective-permute-start.5
  41.4 0.2 collective-permute-start.22
  41.6 2.9 %collective-permute-done.10.refs_0_ = bf16[384,512]{1,0:T(8,128)(2,1)S(1)} collective-permute-done((bf16[384,512]{1,0:T(8,128)(2,1)S(1)}, bf16[384,512]{1,0:T(8,128)(2,1)S(1)}, u32[]{:S(2)}, u32[]{:S(2)}) %collective-permute-start.10) | collective-permute-done | bytes 393248 | tf_op jit(solution)/shard_map/ppermute | solution.py:24
  44.5 0.5 collective-permute-start.6
  45.0 0.3 collective-permute-start.13
  45.3 4.3 %collective-permute-done.20.refs_21_ = bf16[384,512]{1,0:T(8,128)(2,1)S(1)} collective-permute-done((bf16[384,512]{1,0:T(8,128)(2,1)}, bf16[384,512]{1,0:T(8,128)(2,1)S(1)}, u32[]{:S(2)}, u32[]{:S(2)}) %collective-permute-start.20) | collective-permute-done | bytes 393248 | tf_op jit(solution)/shard_map/ppermute | solution.py:24
  49.8 1.7 %collective-permute-done.6.refs_1_.refs_2_ = bf16[256,512]{1,0:T(8,128)(2,1)S(1)} collective-permute-done((bf16[256,512]{1,0:T(8,128)(2,1)S(1)}, bf16[256,512]{1,0:T(8,128)(2,1)S(1)}, u32[]{:S(2)}, u32[]{:S(2)}) %collective-permute-start.6) | collective-permute-done | bytes 262176 | tf_op jit(solution)/shard_map/ppermute | solution.py:24
  51.5 2.4 %collective-permute-done.5.t2.refs_2_.refs_6_ = bf16[400,512]{1,0:T(8,128)(2,1)S(1)} collective-permute-done((bf16[400,512]{1,0:T(8,128)(2,1)S(1)}, bf16[400,512]{1,0:T(8,128)(2,1)S(1)}, u32[]{:S(2)}, u32[]{:S(2)}) %collective-permute-start.5) | collective-permute-done | bytes 409632 | tf_op jit(solution)/shard_map/ppermute | solution.py:24
  54.0 2.5 %collective-permute-done.11.refs_0_ = bf16[192,512]{1,0:T(8,128)(2,1)S(1)} collective-permute-done((bf16[192,512]{1,0:T(8,128)(2,1)S(1)}, bf16[192,512]{1,0:T(8,128)(2,1)S(1)}, u32[]{:S(2)}, u32[]{:S(2)}) %collective-permute-start.11) | collective-permute-done | bytes 196640 | tf_op jit(solution)/shard_map/ppermute | solution.py:24
  56.5 0.6 collective-permute-start.15
  57.1 3.7 %collective-permute-done.21.refs_22_ = bf16[192,512]{1,0:T(8,128)(2,1)S(1)} collective-permute-done((bf16[192,512]{1,0:T(8,128)(2,1)S(1)}, bf16[192,512]{1,0:T(8,128)(2,1)S(1)}, u32[]{:S(2)}, u32[]{:S(2)}) %collective-permute-start.21) | collective-permute-done | bytes 196640 | tf_op jit(solution)/shard_map/ppermute | solution.py:24
  60.9 1.4 %collective-permute-done.25.refs_26_ = bf16[192,512]{1,0:T(8,128)(2,1)S(1)} collective-permute-done((bf16[192,512]{1,0:T(8,128)(2,1)S(1)}, bf16[192,512]{1,0:T(8,128)(2,1)S(1)}, u32[]{:S(2)}, u32[]{:S(2)}) %collective-permute-start.25) | collective-permute-done | bytes 196640 | tf_op jit(solution)/shard_map/ppermute | solution.py:24
  62.4 0.6 copy-done.33
  63.0 10.2 %shard_map.123 = bf16[16,4,32,512]{3,2,1,0:T(8,128)(2,1)} custom-call(s32[5]{0:T(128)} %copy-done.17, bf16[656,512]{1,0:T(8,128)(2,1)} %copy-done.4, bf16[656,512]{1,0:T(8,128)(2,1)} %copy-done.2, bf16[256,512]{1,0:T(8,128)(2,1)} %copy-done.9, bf16[656,512]{1,0:T(8,128)(2,1)} %copy-done, bf16[656,512]{1,0:T(8,128)(2,1)} %copy-done.4, ...), custom_call_target="tpu_custom_call" | custom-call | flops 3221225472 | bytes 10485760 | tf_op jit(solution)/shard_map/pallas_call | solution.py:188
  73.2 32.1 %all_to_all.5.terms = bf16[16,4,32,512]{3,2,1,0:T(8,128)(2,1)S(1)} all-to-all(bf16[16,4,32,512]{3,2,1,0:T(8,128)(2,1)} %shard_map.123), channel_id=1, replica_groups=mesh['yh'=2,'z'=8,'c'=2,'p'=2,'x'=4] {'yh','p','x'}, dimensions={0} | all-to-all | bytes 4194304 | tf_op jit(solution)/shard_map/all_to_all | solution.py:363
  105.5 0.9 shard_map.124.m0
  106.4 0.9 collective-permute-start.28
  107.3 3.3 %collective-permute-start.27 = (bf16[32,2048]{1,0:T(8,128)(2,1)S(1)}, bf16[32,2048]{1,0:T(8,128)(2,1)S(1)}, u32[]{:S(2)}, u32[]{:S(2)}) collective-permute-start(bf16[32,2048]{1,0:T(8,128)(2,1)S(1)} %shard_map.124.m0), channel_id=1, source_target_pairs={{0,2},{1,3},{2,0},{3,1},{4,6},{5,7},{6,4},{7,5},{8,10},{9,11},{10,... | collective-permute-start | bytes 393224 | tf_op jit(solution)/shard_map/ppermute | solution.py:24
  110.7 1.2 collective-permute-start.26
  111.8 3.0 %shard_map.118 = (bf16[128,512]{1,0:T(8,128)(2,1)S(1)}, bf16[2048,512]{1,0:T(8,128)(2,1)S(1)}, bf16[2048,512]{1,0:T(8,128)(2,1)S(1)}, bf16[512,2048]{1,0:T(8,128)(2,1)S(1)}) custom-call(s32[5]{0:T(128)S(1)} %copy-done.18, bf16[656,512]{1,0:T(8,128)(2,1)S(1)} %copy-done.5, bf16[656,512]{1,0:T(8,128)(2,1)S(1)} %copy-done.3, bf16[400,512]{1,0:T(8,128)(2,1)S(1)} %copy-done.7, ...), custom_call_target="tpu_custom_call" | custom-call | flops 268435456 | bytes 10485760 | tf_op jit(solution)/shard_map/pallas_call | solution.py:266
  114.8 0.7 collective-permute-done.27.m2
  115.6 2.0 %shard_map.125 = (bf16[128,512]{1,0:T(8,128)(2,1)S(1)}, bf16[128,512]{1,0:T(8,128)(2,1)S(1)}, bf16[128,512]{1,0:T(8,128)(2,1)S(1)}, bf16[128,512]{1,0:T(8,128)(2,1)S(1)}, bf16[128,512]{1,0:T(8,128)(2,1)S(1)}) custom-call(s32[5]{0:T(128)S(1)} %copy-done.18, s32[2]{0:T(128)S(1)} %copy-done.19, bf16[128,512]{1,0:T(8,128)(2,1)S(1)} %get-tuple-element.14.query, ...), custom_call_target="tpu_custom_call" | custom-call | flops 805306368 | bytes 8388608 | tf_op jit(solution)/shard_map/pallas_call | solution.py:310
  117.7 2.8 %collective-permute-start.29 = (bf16[128,512]{1,0:T(8,128)(2,1)S(1)}, bf16[128,512]{1,0:T(8,128)(2,1)S(1)}, u32[]{:S(2)}, u32[]{:S(2)}) collective-permute-start(bf16[128,512]{1,0:T(8,128)(2,1)S(1)} %get-tuple-element.20), channel_id=1, source_target_pairs={{0,1},{1,2},{2,3},{3,0},{4,5},{5,6},{6,7},{7,4},{8,9},{9,10},{10,1... | collective-permute-start | bytes 393224 | tf_op jit(solution)/shard_map/ppermute | solution.py:24
  120.4 0.7 collective-permute-start.30
  121.1 0.4 collective-permute-start.31
  121.6 2.8 %collective-permute-done.29 = bf16[128,512]{1,0:T(8,128)(2,1)S(1)} collective-permute-done((bf16[128,512]{1,0:T(8,128)(2,1)S(1)}, bf16[128,512]{1,0:T(8,128)(2,1)S(1)}, u32[]{:S(2)}, u32[]{:S(2)}) %collective-permute-start.29) | collective-permute-done | bytes 131104 | tf_op jit(solution)/shard_map/ppermute | solution.py:24
  124.3 2.7 %collective-permute-done.30 = bf16[128,512]{1,0:T(8,128)(2,1)S(1)} collective-permute-done((bf16[128,512]{1,0:T(8,128)(2,1)S(1)}, bf16[128,512]{1,0:T(8,128)(2,1)S(1)}, u32[]{:S(2)}, u32[]{:S(2)}) %collective-permute-start.30) | collective-permute-done | bytes 131104 | tf_op jit(solution)/shard_map/ppermute | solution.py:24
  127.0 1.3 collective-permute-done.31
  128.5 5.0 %collective-permute-done.32 = bf16[128,512]{1,0:T(8,128)(2,1)S(1)} collective-permute-done((bf16[128,512]{1,0:T(8,128)(2,1)S(1)}, bf16[128,512]{1,0:T(8,128)(2,1)S(1)}, u32[]{:S(2)}, u32[]{:S(2)}) %collective-permute-start.32) | collective-permute-done | bytes 131104 | tf_op jit(solution)/shard_map/ppermute | solution.py:24
  133.5 0.7 pad_maximum_fusion.2
  (123 shorter events, 1.1 us)
Async XLA Ops:
  0.0 15.6 %copy-start.25 = (bf16[1,2,128,512]{3,2,1,0:T(8,128)(2,1)S(1)}, bf16[1,2,128,512]{3,2,1,0:T(8,128)(2,1)}, u32[]{:S(2)}) copy-start(bf16[1,2,128,512]{3,2,1,0:T(8,128)(2,1)} %param.12) | copy-start | bytes 786436
  1.9 19.4 %copy-start.36 = (bf16[512]{0:T(512)(128)(2,1)S(1)}, bf16[512]{0:T(512)(128)(2,1)}, u32[]{:S(2)}) copy-start(bf16[512]{0:T(512)(128)(2,1)} %param.18) | copy-start | bytes 3076
  1.9 8.2 %collective-permute-start.7 = (bf16[192,512]{1,0:T(8,128)(2,1)S(1)}, bf16[192,512]{1,0:T(8,128)(2,1)S(1)}, u32[]{:S(2)}, u32[]{:S(2)}) collective-permute-start(bf16[192,512]{1,0:T(8,128)(2,1)S(1)} %pad_maximum_fusion.3), channel_id=1, source_target_pairs={{0,8},{8,0},{1,9},{9,1},{2,10},{10,2},{3,11},{11,3},{4,12},{12,4},... | collective-permute-start | bytes 589832 | tf_op jit(solution)/shard_map/ppermute | solution.py:24
  2.1 10.1 %collective-permute-start.16 = (bf16[192,512]{1,0:T(8,128)(2,1)S(1)}, bf16[192,512]{1,0:T(8,128)(2,1)S(1)}, u32[]{:S(2)}, u32[]{:S(2)}) collective-permute-start(bf16[192,512]{1,0:T(8,128)(2,1)S(1)} %pad_maximum_fusion.4), channel_id=1, source_target_pairs={{0,132},{4,128},{128,4},{132,0},{1,133},{5,129},{129,5},{133,1},{2... | collective-permute-start | bytes 589832 | tf_op jit(solution)/shard_map/ppermute | solution.py:24
  5.2 10.5 %collective-permute-start = (bf16[256,512]{1,0:T(8,128)(2,1)}, bf16[256,512]{1,0:T(8,128)(2,1)S(1)}, u32[]{:S(2)}, u32[]{:S(2)}) collective-permute-start(bf16[256,512]{1,0:T(8,128)(2,1)} %bitcast.14), channel_id=1, source_target_pairs={{0,4},{4,0},{1,5},{5,1},{2,6},{6,2},{3,7},{7,3},{8,12},{12,8},{9,1... | collective-permute-start | bytes 786440 | tf_op jit(solution)/shard_map/ppermute | solution.py:24
  5.3 13.9 %collective-permute-start.1 = (bf16[256,512]{1,0:T(8,128)(2,1)}, bf16[256,512]{1,0:T(8,128)(2,1)S(1)}, u32[]{:S(2)}, u32[]{:S(2)}) collective-permute-start(bf16[256,512]{1,0:T(8,128)(2,1)} %bitcast.15), channel_id=1, source_target_pairs={{0,128},{128,0},{1,129},{129,1},{2,130},{130,2},{3,131},{131,3},{8... | collective-permute-start | bytes 786440 | tf_op jit(solution)/shard_map/ppermute | solution.py:24
  8.8 10.5 %collective-permute-start.2 = (bf16[256,512]{1,0:T(8,128)(2,1)}, bf16[256,512]{1,0:T(8,128)(2,1)S(1)}, u32[]{:S(2)}, u32[]{:S(2)}) collective-permute-start(bf16[256,512]{1,0:T(8,128)(2,1)} %bitcast.16), channel_id=1, source_target_pairs={{0,132},{128,4},{1,133},{129,5},{2,134},{130,6},{3,135},{131,7},{8... | collective-permute-start | bytes 786440 | tf_op jit(solution)/shard_map/ppermute | solution.py:24
  10.1 15.1 %collective-permute-start.8 = (bf16[384,512]{1,0:T(8,128)(2,1)S(1)}, bf16[384,512]{1,0:T(8,128)(2,1)S(1)}, u32[]{:S(2)}, u32[]{:S(2)}) collective-permute-start(bf16[384,512]{1,0:T(8,128)(2,1)S(1)} %pad_maximum_fusion.1.refs_9_), channel_id=1, source_target_pairs={{0,16},{8,120},{16,32},{24,8},{32,48},{40,24},{48,64},{56,40},{64,... | collective-permute-start | bytes 1179656 | tf_op jit(solution)/shard_map/ppermute | solution.py:24
  12.1 7.1 %collective-permute-start.17 = (bf16[192,512]{1,0:T(8,128)(2,1)S(1)}, bf16[192,512]{1,0:T(8,128)(2,1)S(1)}, u32[]{:S(2)}, u32[]{:S(2)}) collective-permute-start(bf16[192,512]{1,0:T(8,128)(2,1)S(1)} %collective-permute-done.16), channel_id=1, source_target_pairs={{0,8},{8,0},{1,9},{9,1},{2,10},{10,2},{3,11},{11,3},{4,12},{12,4},... | collective-permute-start | bytes 589832 | tf_op jit(solution)/shard_map/ppermute | solution.py:24
  15.7 15.4 %copy-start.34 = (bf16[2048]{0:T(1024)(128)(2,1)S(1)}, bf16[2048]{0:T(1024)(128)(2,1)}, u32[]{:S(2)}) copy-start(bf16[2048]{0:T(1024)(128)(2,1)} %param.14) | copy-start | bytes 12292
  15.7 15.4 %copy-start.35 = (bf16[2048]{0:T(1024)(128)(2,1)S(1)}, bf16[2048]{0:T(1024)(128)(2,1)}, u32[]{:S(2)}) copy-start(bf16[2048]{0:T(1024)(128)(2,1)} %param.19) | copy-start | bytes 12292
  19.3 11.8 %collective-permute-start.18 = (bf16[384,512]{1,0:T(8,128)(2,1)S(1)}, bf16[384,512]{1,0:T(8,128)(2,1)}, u32[]{:S(2)}, u32[]{:S(2)}) collective-permute-start(bf16[384,512]{1,0:T(8,128)(2,1)S(1)} %constant_dynamic-update-slice_fusion.refs_18_), channel_id=1, source_target_pairs={{0,16},{8,120},{16,32},{24,8},{32,48},{40,24},{48,64},{56,40},{64,... | collective-permute-start | bytes 1179656 | tf_op jit(solution)/shard_map/ppermute | solution.py:24
  22.0 23.0 %copy-start.4 = (bf16[656,512]{1,0:T(8,128)(2,1)}, bf16[656,512]{1,0:T(8,128)(2,1)S(1)}, u32[]{:S(2)}) copy-start(bf16[656,512]{1,0:T(8,128)(2,1)S(1)} %pad_maximum_fusion.t0.refs_0_.refs_4_) | copy-start | bytes 2015236
  22.0 18.4 %collective-permute-start.4 = (bf16[656,512]{1,0:T(8,128)(2,1)S(1)}, bf16[656,512]{1,0:T(8,128)(2,1)S(1)}, u32[]{:S(2)}, u32[]{:S(2)}) collective-permute-start(bf16[656,512]{1,0:T(8,128)(2,1)S(1)} %pad_maximum_fusion.t0.refs_0_.refs_4_), channel_id=1, source_target_pairs={{0,3},{1,0},{2,1},{3,2},{4,7},{5,4},{6,5},{7,6},{8,11},{9,8},{10,9... | collective-permute-start | bytes 2015240 | tf_op jit(solution)/shard_map/ppermute | solution.py:24
  22.8 18.6 %collective-permute-start.3 = (bf16[656,512]{1,0:T(8,128)(2,1)S(1)}, bf16[656,512]{1,0:T(8,128)(2,1)S(1)}, u32[]{:S(2)}, u32[]{:S(2)}) collective-permute-start(bf16[656,512]{1,0:T(8,128)(2,1)S(1)} %pad_maximum_fusion.t0.refs_0_.refs_4_), channel_id=1, source_target_pairs={{0,1},{1,2},{2,3},{3,0},{4,5},{5,6},{6,7},{7,4},{8,9},{9,10},{10,1... | collective-permute-start | bytes 2015240 | tf_op jit(solution)/shard_map/ppermute | solution.py:24
  25.2 19.8 %copy-start.13 = (bf16[384,512]{1,0:T(8,128)(2,1)}, bf16[384,512]{1,0:T(8,128)(2,1)S(1)}, u32[]{:S(2)}) copy-start(bf16[384,512]{1,0:T(8,128)(2,1)S(1)} %shard_map.119.refs_10_) | copy-start | bytes 1179652
  25.2 10.0 %collective-permute-start.9 = (bf16[384,512]{1,0:T(8,128)(2,1)S(1)}, bf16[384,512]{1,0:T(8,128)(2,1)S(1)}, u32[]{:S(2)}, u32[]{:S(2)}) collective-permute-start(bf16[384,512]{1,0:T(8,128)(2,1)S(1)} %shard_map.119.refs_10_), channel_id=1, source_target_pairs={{0,16},{8,120},{16,32},{24,8},{32,48},{40,24},{48,64},{56,40},{64,... | collective-permute-start | bytes 1179656 | tf_op jit(solution)/shard_map/ppermute | solution.py:24
  31.1 9.3 %collective-permute-start.19 = (bf16[384,512]{1,0:T(8,128)(2,1)}, bf16[384,512]{1,0:T(8,128)(2,1)}, u32[]{:S(2)}, u32[]{:S(2)}) collective-permute-start(bf16[384,512]{1,0:T(8,128)(2,1)} %collective-permute-done.18.refs_19_), channel_id=1, source_target_pairs={{0,16},{8,120},{16,32},{24,8},{32,48},{40,24},{48,64},{56,40},{64,... | collective-permute-start | bytes 1179656 | tf_op jit(solution)/shard_map/ppermute | solution.py:24
  35.2 9.3 %collective-permute-start.10 = (bf16[384,512]{1,0:T(8,128)(2,1)S(1)}, bf16[384,512]{1,0:T(8,128)(2,1)S(1)}, u32[]{:S(2)}, u32[]{:S(2)}) collective-permute-start(bf16[384,512]{1,0:T(8,128)(2,1)S(1)} %shard_map.120.refs_11_), channel_id=1, source_target_pairs={{0,16},{8,120},{16,32},{24,8},{32,48},{40,24},{48,64},{56,40},{64,... | collective-permute-start | bytes 1179656 | tf_op jit(solution)/shard_map/ppermute | solution.py:24
  35.2 9.8 %collective-permute-start.12 = (bf16[384,512]{1,0:T(8,128)(2,1)S(1)}, bf16[384,512]{1,0:T(8,128)(2,1)S(1)}, u32[]{:S(2)}, u32[]{:S(2)}) collective-permute-start(bf16[384,512]{1,0:T(8,128)(2,1)S(1)} %shard_map.119.refs_10_), channel_id=1, source_target_pairs={{0,8},{8,0},{1,9},{9,1},{2,10},{10,2},{3,11},{11,3},{4,12},{12,4},... | collective-permute-start | bytes 1179656 | tf_op jit(solution)/shard_map/ppermute | solution.py:24
  40.4 9.2 %collective-permute-start.20 = (bf16[384,512]{1,0:T(8,128)(2,1)}, bf16[384,512]{1,0:T(8,128)(2,1)S(1)}, u32[]{:S(2)}, u32[]{:S(2)}) collective-permute-start(bf16[384,512]{1,0:T(8,128)(2,1)} %collective-permute-done.19.refs_20_), channel_id=1, source_target_pairs={{0,16},{8,120},{16,32},{24,8},{32,48},{40,24},{48,64},{56,40},{64,... | collective-permute-start | bytes 1179656 | tf_op jit(solution)/shard_map/ppermute | solution.py:24
  40.5 13.5 %collective-permute-start.5 = (bf16[400,512]{1,0:T(8,128)(2,1)S(1)}, bf16[400,512]{1,0:T(8,128)(2,1)S(1)}, u32[]{:S(2)}, u32[]{:S(2)}) collective-permute-start(bf16[400,512]{1,0:T(8,128)(2,1)S(1)} %slice.29), channel_id=1, source_target_pairs={{0,3},{1,0},{2,1},{3,2},{4,7},{5,4},{6,5},{7,6},{8,11},{9,8},{10,9... | collective-permute-start | bytes 1228808 | tf_op jit(solution)/shard_map/ppermute | solution.py:24
  41.4 15.1 %copy-start.2 = (bf16[656,512]{1,0:T(8,128)(2,1)}, bf16[656,512]{1,0:T(8,128)(2,1)S(1)}, u32[]{:S(2)}) copy-start(bf16[656,512]{1,0:T(8,128)(2,1)S(1)} %collective-permute-done.3.t1.refs_1_.refs_5_) | copy-start | bytes 2015236
  41.4 8.3 %collective-permute-start.22 = (bf16[384,512]{1,0:T(8,128)(2,1)}, bf16[384,512]{1,0:T(8,128)(2,1)S(1)}, u32[]{:S(2)}, u32[]{:S(2)}) collective-permute-start(bf16[384,512]{1,0:T(8,128)(2,1)} %collective-permute-done.18.refs_19_), channel_id=1, source_target_pairs={{0,8},{8,0},{1,9},{9,1},{2,10},{10,2},{3,11},{11,3},{4,12},{12,4},... | collective-permute-start | bytes 1179656 | tf_op jit(solution)/shard_map/ppermute | solution.py:24
  44.5 7.0 %collective-permute-start.6 = (bf16[256,512]{1,0:T(8,128)(2,1)S(1)}, bf16[256,512]{1,0:T(8,128)(2,1)S(1)}, u32[]{:S(2)}, u32[]{:S(2)}) collective-permute-start(bf16[256,512]{1,0:T(8,128)(2,1)S(1)} %slice.30), channel_id=1, source_target_pairs={{0,1},{1,2},{2,3},{3,0},{4,5},{5,6},{6,7},{7,4},{8,9},{9,10},{10,1... | collective-permute-start | bytes 786440 | tf_op jit(solution)/shard_map/ppermute | solution.py:24
  45.0 17.3 %copy-start.8 = (bf16[384,512]{1,0:T(8,128)(2,1)}, bf16[384,512]{1,0:T(8,128)(2,1)S(1)}, u32[]{:S(2)}) copy-start(bf16[384,512]{1,0:T(8,128)(2,1)S(1)} %shard_map.121.refs_12_) | copy-start | bytes 1179652
  45.0 17.2 %copy-start.26 = (bf16[384,512]{1,0:T(8,128)(2,1)}, bf16[384,512]{1,0:T(8,128)(2,1)S(1)}, u32[]{:S(2)}) copy-start(bf16[384,512]{1,0:T(8,128)(2,1)S(1)} %collective-permute-done.12.refs_14_) | copy-start | bytes 1179652
  45.0 11.5 %collective-permute-start.13 = (bf16[384,512]{1,0:T(8,128)(2,1)S(1)}, bf16[384,512]{1,0:T(8,128)(2,1)S(1)}, u32[]{:S(2)}, u32[]{:S(2)}) collective-permute-start(bf16[384,512]{1,0:T(8,128)(2,1)S(1)} %shard_map.120.refs_11_), channel_id=1, source_target_pairs={{0,8},{8,0},{1,9},{9,1},{2,10},{10,2},{3,11},{11,3},{4,12},{12,4},... | collective-permute-start | bytes 1179656 | tf_op jit(solution)/shard_map/ppermute | solution.py:24
  49.6 6.9 %collective-permute-start.11 = (bf16[192,512]{1,0:T(8,128)(2,1)S(1)}, bf16[192,512]{1,0:T(8,128)(2,1)S(1)}, u32[]{:S(2)}, u32[]{:S(2)}) collective-permute-start(bf16[192,512]{1,0:T(8,128)(2,1)S(1)} %slice.31), channel_id=1, source_target_pairs={{0,16},{8,120},{16,32},{24,8},{32,48},{40,24},{48,64},{56,40},{64,... | collective-permute-start | bytes 589832 | tf_op jit(solution)/shard_map/ppermute | solution.py:24
  49.7 11.2 %collective-permute-start.23 = (bf16[384,512]{1,0:T(8,128)(2,1)}, bf16[384,512]{1,0:T(8,128)(2,1)S(1)}, u32[]{:S(2)}, u32[]{:S(2)}) collective-permute-start(bf16[384,512]{1,0:T(8,128)(2,1)} %collective-permute-done.19.refs_20_), channel_id=1, source_target_pairs={{0,8},{8,0},{1,9},{9,1},{2,10},{10,2},{3,11},{11,3},{4,12},{12,4},... | collective-permute-start | bytes 1179656 | tf_op jit(solution)/shard_map/ppermute | solution.py:24
  51.5 9.4 %collective-permute-start.14 = (bf16[384,512]{1,0:T(8,128)(2,1)S(1)}, bf16[384,512]{1,0:T(8,128)(2,1)S(1)}, u32[]{:S(2)}, u32[]{:S(2)}) collective-permute-start(bf16[384,512]{1,0:T(8,128)(2,1)S(1)} %shard_map.121.refs_12_), channel_id=1, source_target_pairs={{0,8},{8,0},{1,9},{9,1},{2,10},{10,2},{3,11},{11,3},{4,12},{12,4},... | collective-permute-start | bytes 1179656 | tf_op jit(solution)/shard_map/ppermute | solution.py:24
  54.0 6.9 %collective-permute-start.21 = (bf16[192,512]{1,0:T(8,128)(2,1)S(1)}, bf16[192,512]{1,0:T(8,128)(2,1)S(1)}, u32[]{:S(2)}, u32[]{:S(2)}) collective-permute-start(bf16[192,512]{1,0:T(8,128)(2,1)S(1)} %slice.32), channel_id=1, source_target_pairs={{0,16},{8,120},{16,32},{24,8},{32,48},{40,24},{48,64},{56,40},{64,... | collective-permute-start | bytes 589832 | tf_op jit(solution)/shard_map/ppermute | solution.py:24
  56.5 5.8 %collective-permute-start.24 = (bf16[384,512]{1,0:T(8,128)(2,1)S(1)}, bf16[384,512]{1,0:T(8,128)(2,1)}, u32[]{:S(2)}, u32[]{:S(2)}) collective-permute-start(bf16[384,512]{1,0:T(8,128)(2,1)S(1)} %collective-permute-done.20.refs_21_), channel_id=1, source_target_pairs={{0,8},{8,0},{1,9},{9,1},{2,10},{10,2},{3,11},{11,3},{4,12},{12,4},... | collective-permute-start | bytes 1179656 | tf_op jit(solution)/shard_map/ppermute | solution.py:24
  56.5 4.3 %collective-permute-start.15 = (bf16[192,512]{1,0:T(8,128)(2,1)S(1)}, bf16[192,512]{1,0:T(8,128)(2,1)S(1)}, u32[]{:S(2)}, u32[]{:S(2)}) collective-permute-start(bf16[192,512]{1,0:T(8,128)(2,1)S(1)} %shard_map.122.refs_13_), channel_id=1, source_target_pairs={{0,8},{8,0},{1,9},{9,1},{2,10},{10,2},{3,11},{11,3},{4,12},{12,4},... | collective-permute-start | bytes 589832 | tf_op jit(solution)/shard_map/ppermute | solution.py:24
  60.8 1.4 %collective-permute-start.25 = (bf16[192,512]{1,0:T(8,128)(2,1)S(1)}, bf16[192,512]{1,0:T(8,128)(2,1)S(1)}, u32[]{:S(2)}, u32[]{:S(2)}) collective-permute-start(bf16[192,512]{1,0:T(8,128)(2,1)S(1)} %collective-permute-done.21.refs_22_), channel_id=1, source_target_pairs={{0,8},{8,0},{1,9},{9,1},{2,10},{10,2},{3,11},{11,3},{4,12},{12,4},... | collective-permute-start | bytes 589832 | tf_op jit(solution)/shard_map/ppermute | solution.py:24
  73.2 32.2 %copy-start.1 = (bf16[656,512]{1,0:T(8,128)(2,1)S(1)}, bf16[656,512]{1,0:T(8,128)(2,1)}, u32[]{:S(2)}) copy-start(bf16[656,512]{1,0:T(8,128)(2,1)} %copy-done) | copy-start | bytes 2015236
  73.2 32.2 %copy-start.3 = (bf16[656,512]{1,0:T(8,128)(2,1)S(1)}, bf16[656,512]{1,0:T(8,128)(2,1)}, u32[]{:S(2)}) copy-start(bf16[656,512]{1,0:T(8,128)(2,1)} %copy-done.2) | copy-start | bytes 2015236
  73.2 32.2 %copy-start.5 = (bf16[656,512]{1,0:T(8,128)(2,1)S(1)}, bf16[656,512]{1,0:T(8,128)(2,1)}, u32[]{:S(2)}) copy-start(bf16[656,512]{1,0:T(8,128)(2,1)} %copy-done.4) | copy-start | bytes 2015236
  73.2 32.2 %copy-start.7 = (bf16[400,512]{1,0:T(8,128)(2,1)S(1)}, bf16[400,512]{1,0:T(8,128)(2,1)}, u32[]{:S(2)}) copy-start(bf16[400,512]{1,0:T(8,128)(2,1)} %copy-done.6) | copy-start | bytes 1228804
  73.2 32.2 %copy-start.10 = (bf16[256,512]{1,0:T(8,128)(2,1)S(1)}, bf16[256,512]{1,0:T(8,128)(2,1)}, u32[]{:S(2)}) copy-start(bf16[256,512]{1,0:T(8,128)(2,1)} %copy-done.9) | copy-start | bytes 786436
  73.2 32.2 %copy-start.18 = (s32[5]{0:T(128)S(1)}, s32[5]{0:T(128)}, u32[]{:S(2)}) copy-start(s32[5]{0:T(128)} %copy-done.17) | copy-start | bytes 64
  106.4 8.4 %collective-permute-start.28 = (bf16[32,2048]{1,0:T(8,128)(2,1)S(1)}, bf16[32,2048]{1,0:T(8,128)(2,1)S(1)}, u32[]{:S(2)}, u32[]{:S(2)}) collective-permute-start(bf16[32,2048]{1,0:T(8,128)(2,1)S(1)} %shard_map.124.m0), channel_id=1, source_target_pairs={{0,3},{1,0},{2,1},{3,2},{4,7},{5,4},{6,5},{7,6},{8,11},{9,8},{10,9... | collective-permute-start | bytes 393224 | tf_op jit(solution)/shard_map/ppermute | solution.py:24
  107.3 8.2 %collective-permute-start.27 = (bf16[32,2048]{1,0:T(8,128)(2,1)S(1)}, bf16[32,2048]{1,0:T(8,128)(2,1)S(1)}, u32[]{:S(2)}, u32[]{:S(2)}) collective-permute-start(bf16[32,2048]{1,0:T(8,128)(2,1)S(1)} %shard_map.124.m0), channel_id=1, source_target_pairs={{0,2},{1,3},{2,0},{3,1},{4,6},{5,7},{6,4},{7,5},{8,10},{9,11},{10,... | collective-permute-start | bytes 393224 | tf_op jit(solution)/shard_map/ppermute | solution.py:24
  110.7 5.0 %collective-permute-start.26 = (bf16[32,2048]{1,0:T(8,128)(2,1)S(1)}, bf16[32,2048]{1,0:T(8,128)(2,1)S(1)}, u32[]{:S(2)}, u32[]{:S(2)}) collective-permute-start(bf16[32,2048]{1,0:T(8,128)(2,1)S(1)} %shard_map.124.m0), channel_id=1, source_target_pairs={{0,1},{1,2},{2,3},{3,0},{4,5},{5,6},{6,7},{7,4},{8,9},{9,10},{10,1... | collective-permute-start | bytes 393224 | tf_op jit(solution)/shard_map/ppermute | solution.py:24
  117.7 6.7 %collective-permute-start.29 = (bf16[128,512]{1,0:T(8,128)(2,1)S(1)}, bf16[128,512]{1,0:T(8,128)(2,1)S(1)}, u32[]{:S(2)}, u32[]{:S(2)}) collective-permute-start(bf16[128,512]{1,0:T(8,128)(2,1)S(1)} %get-tuple-element.20), channel_id=1, source_target_pairs={{0,1},{1,2},{2,3},{3,0},{4,5},{5,6},{6,7},{7,4},{8,9},{9,10},{10,1... | collective-permute-start | bytes 393224 | tf_op jit(solution)/shard_map/ppermute | solution.py:24
  120.4 6.6 %collective-permute-start.30 = (bf16[128,512]{1,0:T(8,128)(2,1)S(1)}, bf16[128,512]{1,0:T(8,128)(2,1)S(1)}, u32[]{:S(2)}, u32[]{:S(2)}) collective-permute-start(bf16[128,512]{1,0:T(8,128)(2,1)S(1)} %get-tuple-element.21), channel_id=1, source_target_pairs={{0,2},{1,3},{2,0},{3,1},{4,6},{5,7},{6,4},{7,5},{8,10},{9,11},{10,... | collective-permute-start | bytes 393224 | tf_op jit(solution)/shard_map/ppermute | solution.py:24
  121.1 7.2 %collective-permute-start.31 = (bf16[128,512]{1,0:T(8,128)(2,1)S(1)}, bf16[128,512]{1,0:T(8,128)(2,1)S(1)}, u32[]{:S(2)}, u32[]{:S(2)}) collective-permute-start(bf16[128,512]{1,0:T(8,128)(2,1)S(1)} %get-tuple-element.22), channel_id=1, source_target_pairs={{0,3},{1,0},{2,1},{3,2},{4,7},{5,4},{6,5},{7,6},{8,11},{9,8},{10,9... | collective-permute-start | bytes 393224 | tf_op jit(solution)/shard_map/ppermute | solution.py:24
  128.4 5.1 %collective-permute-start.32 = (bf16[128,512]{1,0:T(8,128)(2,1)S(1)}, bf16[128,512]{1,0:T(8,128)(2,1)S(1)}, u32[]{:S(2)}, u32[]{:S(2)}) collective-permute-start(bf16[128,512]{1,0:T(8,128)(2,1)S(1)} %get-tuple-element.23), channel_id=1, source_target_pairs={{0,4},{4,0},{1,5},{5,1},{2,6},{6,2},{3,7},{7,3},{8,12},{12,8},{9,1... | collective-permute-start | bytes 393224 | tf_op jit(solution)/shard_map/ppermute | solution.py:24
  (22 other events, 171.1 us)

commit v6 on v5

--- a/solution.py
+++ b/solution.py
@@ -111,58 +111,84 @@
     return lax.rsqrt(square * (1.0 / 2048) + epsilon)
 
 
-def ffn_kernel(place, *refs):
-    tokens, gain, refs = refs[:8], refs[8], refs[9:]
-    chunks, (out, held, normed, sems) = refs[: 2 * CHUNKS], refs[2 * CHUNKS :]
-    yh, x, z, c = place[0], place[2], place[3], place[4]
-    first = pl.program_id(0) == 0
-    ways = [(m, side) for side in range(2) for m in range(2)] + [(2, 0), (2, 1)]
-
-    @pl.when(first)
-    def _():
-        for m, side in ways:
-            for k in range(CHUNKS):
-                chunk = chunks[side * CHUNKS + k]
-                step, core = (k, c) if k < 5 else (k - 4, 1 - c)
-                at = (z - step * (1 - 2 * core)) & 7
-                for half in range(chunk.shape[0] // 192):
-                    source = chunk.at[pl.ds(half * 192 + m * 64, 64)]
-                    target = held.at[m, side, at, core ^ half]
-                    pltpu.make_async_copy(source, target, sems.at[m, side]).start()
-
-    def wait(*those):
-        @pl.when(first)
-        def _():
-            for spot in those:
-                pltpu.make_async_copy(held.at[spot], held.at[spot], sems.at[spot]).wait()
-
+def halves_of(chunk, core, part):
+    return [
+        chunk[pl.ds(pl.multiple_of((a ^ core) * 192 + part * 64, 64), 64), :] for a in range(2)
+    ]
+
+
+def whole_chunks(place, chunks):
+    yh, z, c = place[0], place[3], place[4]
+    found = []
+    for side in range(2):
+        for k in (0, 1, 2, 3, 5, 6, 7):
+            step, core = (k, c) if k < 5 else (k - 4, 1 - c)
+            at = (yh ^ side) * 8 + ((z - step * (1 - 2 * core)) & 7)
+            found.append((at, chunks[side * CHUNKS + k], core))
+    return found
+
+
+def first_kernel(place, *refs):
+    tokens, gain, given = refs[:8], refs[8], refs[9:23]
+    gate, lift, last, normed = refs[23:]
+    yh, x, z = place[0], place[2], place[3]
     for i in range(2):
-
-        @pl.when(pl.program_id(0) == i)
-        def _():
-            blocks = tokens[i * 4 : (i + 1) * 4]
-            scale = scale_of(blocks)
-            for k, block in enumerate(blocks):
-                b = (x - k) & 3
-                normed[b] = normed_block(block, scale, gain[b])
-
-    gate = lift = 0.0
+        rows = slice(i * 256, (i + 1) * 256)
+        blocks = tokens[i * 4 : (i + 1) * 4]
+        scale = scale_of(blocks)
+        for k, block in enumerate(blocks):
+            b = (x - k) & 3
+            value = normed_block(block, scale, gain[b])
+            for j in range(4):
+                normed[b * 4 + j, rows] = value[:, j * 128 : (j + 1) * 128]
+    chunks = [None] * (2 * CHUNKS)
+    for j, chunk in enumerate(given):
+        chunks[j // 7 * CHUNKS + (0, 1, 2, 3, 5, 6, 7)[j % 7]] = chunk
+    spots = whole_chunks(place, chunks)
+    for part, out in enumerate((gate, lift)):
+        w = jnp.concatenate(
+            [half for _, chunk, core in spots for half in halves_of(chunk, core, part)], 0
+        )
+        for i in range(2):
+            rows = slice(i * 256, (i + 1) * 256)
+            n = jnp.concatenate([normed[at, rows] for at, _, _ in spots], 1)
+            out[rows] = jnp.dot(n, w, preferred_element_type=f32)
     for side in range(2):
-        b = (yh ^ side) * 2
-        n = jnp.concatenate([normed[b], normed[b + 1]], 1)
-        wait((0, side), (1, side))
-        gate += jnp.dot(n, held[0, side].reshape(1024, 512), preferred_element_type=f32)
-        lift += jnp.dot(n, held[1, side].reshape(1024, 512), preferred_element_type=f32)
-    inner = 0.7978845608028654 * (gate + 0.044715 * (gate * gate * gate))
-    hidden = (0.5 * gate * (1.0 + jnp.tanh(inner)) * lift).astype(bf16)
-    wait((2, 0), (2, 1))
-    for side in range(2):
-        for k in range(2):
-            rows = held[2, side, k * 4 : (k + 1) * 4].reshape(512, 512)
-            part = lax.dot_general(
-                hidden, rows, (((1,), (1,)), ((), ())), preferred_element_type=f32
-            )
-            out[:, (yh ^ side) * 2 + k] = part.astype(bf16).reshape(8, 32, 512)
+        last[side] = normed[(yh ^ side) * 8 + ((z + 4) & 7)]
+
+
+def second_kernel(place, gate, lift, last, *refs):
+    chunks, out = refs[: 2 * CHUNKS], refs[2 * CHUNKS]
+    yh, z, c = place[0], place[3], place[4]
+
+    def rest_of(part):
+        rows = slice(part * 64, (part + 1) * 64)
+        found = []
+        for side in range(2):
+            own, twin = (chunks[side * CHUNKS + k][rows] for k in (4, 8))
+            found += [jnp.where(c == 0, own, twin), jnp.where(c == 0, twin, own)]
+        return jnp.concatenate(found, 0)
+
+    n = jnp.concatenate([last[0], last[1]], 1)
+    g = gate[...] + jnp.dot(n, rest_of(0), preferred_element_type=f32)
+    up = lift[...] + jnp.dot(n, rest_of(1), preferred_element_type=f32)
+    inner = 0.7978845608028654 * (g + 0.044715 * (g * g * g))
+    hidden = (0.5 * g * (1.0 + jnp.tanh(inner)) * up).astype(bf16)
+    spots = whole_chunks(place, chunks)
+    pairs = [
+        (
+            [spots[k][0], spots[k + 1][0]],
+            jnp.concatenate(halves_of(*spots[k][1:], 2) + halves_of(*spots[k + 1][1:], 2), 0),
+        )
+        for k in range(0, 14, 2)
+    ]
+    pairs.append(([(yh ^ side) * 8 + ((z + 4) & 7) for side in range(2)], rest_of(2)))
+    for places, w in pairs:
+        sums = lax.dot_general(hidden, w, (((1,), (1,)), ((), ())), preferred_element_type=f32)
+        sums = sums.astype(bf16)
+        for j, at in enumerate(places):
+            lanes = pl.ds(pl.multiple_of((at & 3) * 128, 128), 128)
+            out[:, at >> 2, :, lanes] = sums[:, j * 128 : (j + 1) * 128].reshape(8, 32, 128)
 
 
 def rows_at(rows, at):
@@ -172,28 +198,43 @@
 def ffn(place, tokens, gain, chunks):
     first, second, (third, third_rest), fourth = tokens
     mine, theirs = (first, second, third, fourth), (first, second, third_rest, fourth)
+    given = [chunk for chunk in chunks if chunk.shape[0] == 384]
+    grid_spec = pltpu.PrefetchScalarGridSpec(
+        num_scalar_prefetch=1,
+        grid=(1,),
+        in_specs=[rows_at(256, at) for at in (0, 0, 0, 0, 1, 1, 0, 1)]
+        + [whole(gain.shape)]
+        + [vmem()] * len(given),
+        out_specs=[vmem()] * 3,
+        scratch_shapes=[pltpu.VMEM((16, 512, 128), bf16)],
+    )
+    gate, lift, last = pl.pallas_call(
+        first_kernel,
+        grid_spec=grid_spec,
+        out_shape=[jax.ShapeDtypeStruct((512, 512), f32)] * 2
+        + [jax.ShapeDtypeStruct((2, 512, 128), bf16)],
+        compiler_params=params(24),
+        cost_estimate=pl.CostEstimate(
+            flops=512 * 1792 * 512 * 4, bytes_accessed=4 * MIB, transcendentals=0
+        ),
+    )(place, *mine, *theirs, gain, *given)
     grid_spec = pltpu.PrefetchScalarGridSpec(
         num_scalar_prefetch=1,
         grid=(2,),
-        in_specs=[rows_at(256, at) for at in (0, 0, 0, 0, 1, 1, 0, 1)]
-        + [whole(gain.shape)]
-        + [anyplace()] * len(chunks),
+        in_specs=[pl.BlockSpec((256, 512), lambda i, place: (i, 0))] * 2
+        + [pl.BlockSpec((2, 256, 128), lambda i, place: (0, i, 0))]
+        + [vmem()] * len(chunks),
         out_specs=pl.BlockSpec((8, 4, 32, 512), lambda i, place: (place[0] ^ i, 0, 0, 0)),
-        scratch_shapes=[
-            pltpu.VMEM((3, 2, 8, 2, 64, 512), bf16),
-            pltpu.VMEM((4, 256, 512), bf16),
-            pltpu.SemaphoreType.DMA((3, 2)),
-        ],
     )
     return pl.pallas_call(
-        ffn_kernel,
+        second_kernel,
         grid_spec=grid_spec,
         out_shape=jax.ShapeDtypeStruct((16, 4, 32, 512), bf16),
-        compiler_params=params(),
+        compiler_params=params(24),
         cost_estimate=pl.CostEstimate(
-            flops=512 * 2048 * 512 * 6, bytes_accessed=10 * MIB, transcendentals=512 * 512
+            flops=512 * 2304 * 512 * 2, bytes_accessed=4 * MIB, transcendentals=512 * 512
         ),
-    )(place, *mine, *theirs, gain, *chunks)
+    )(place, gate, lift, last, *chunks)
 
 
 def memory_kernel(place, terms, *refs):

time: 135 us -> 132 us (0.978)
  waiting for transfers between devices: 46.4 us -> 39.9 us
  starting transfers between devices: 34.4 us -> 40.3 us
    ppermute x33, waiting for transfers between devices: 46.4 us -> 39.9 us  [moved(): return lax.ppermute(value, axes, pairs)]
    ppermute x33, starting transfers between devices: 34.4 us -> 40.3 us  [moved(): return lax.ppermute(value, axes, pairs)]
    pallas_call x1 -> x2, Pallas kernels: 10.2 us -> 9.07 us  [the longest x1 4.89 us: ffn(): pl.pallas_call(first_kernel, grid_spec=grid_spec, out_shape=[jax.ShapeDty...]
  transfers between devices with their start and end apart: 33 -> 33, of which waited for: 17 -> 15; matrix products, arithmetic and copies ran while one was open for 0% -> 0% of each run, Pallas kernels for 2% -> 6%
where the time goes in v6:
time: 132 us
  starting transfers between devices  40.3 us (31%)
  waiting for transfers between devices  39.9 us (30%)
  blocking collectives  32.2 us (24%)
  Pallas kernels  15 us (11%)
  local copies, waits for them, and re-layouts  3.1 us (2%)
    ppermute x33, starting transfers between devices, moved(): return lax.ppermute(value, axes, pairs)  40.3 us
    ppermute x33, waiting for transfers between devices, moved(): return lax.ppermute(value, axes, pairs)  39.9 us
    all_to_all x1, blocking collectives, shards(): terms = lax.all_to_all(terms, ('yh', 'p', 'x'), 0, 0)  32.2 us
    pallas_call x1, Pallas kernels, ffn(): pl.pallas_call(first_kernel, grid_spec=grid_spec, out_shape=[jax.ShapeDty...  4.89 us
    pallas_call x1, Pallas kernels, ffn(): pl.pallas_call(second_kernel, grid_spec=grid_spec, out_shape=jax.ShapeDty...  4.18 us
    pallas_call x1, Pallas kernels, query_rows(): pl.pallas_call(query_kernel, grid_spec=grid_spec, out_shape=[jax.ShapeDty...  2.99 us
  transfers between devices with their start and end apart: 33, of which 15 were waited for; matrix products, arithmetic and copies ran while one was open for 0% of the time, Pallas kernels for 6%

profile of v6, /device:TPU:6, one launch (start us, length us, event | category | flops | bytes accessed | tf_op | source)
XLA Modules:
  0.0 131.9 jit_solution(15976191348562372456)
XLA Ops:
  0.0 0.9 dynamic-slice_bitcast_fusion
  0.9 1.0 constant_dynamic-slice_fusion
  1.9 0.1 collective-permute-start.7
  2.1 3.1 %collective-permute-start.14 = (bf16[192,512]{1,0:T(8,128)(2,1)S(1)}, bf16[192,512]{1,0:T(8,128)(2,1)S(1)}, u32[]{:S(2)}, u32[]{:S(2)}) collective-permute-start(bf16[192,512]{1,0:T(8,128)(2,1)S(1)} %pad_maximum_fusion.4), channel_id=1, source_target_pairs={{0,132},{4,128},{128,4},{132,0},{1,133},{5,129},{129,5},{133,1},{2... | collective-permute-start | bytes 589832 | tf_op jit(solution)/shard_map/ppermute | solution.py:24
  5.2 0.1 collective-permute-start
  5.3 3.5 %collective-permute-start.1 = (bf16[256,512]{1,0:T(8,128)(2,1)}, bf16[256,512]{1,0:T(8,128)(2,1)S(1)}, u32[]{:S(2)}, u32[]{:S(2)}) collective-permute-start(bf16[256,512]{1,0:T(8,128)(2,1)} %bitcast.15), channel_id=1, source_target_pairs={{0,128},{128,0},{1,129},{129,1},{2,130},{130,2},{3,131},{131,3},{8... | collective-permute-start | bytes 786440 | tf_op jit(solution)/shard_map/ppermute | solution.py:24
  8.8 1.3 collective-permute-start.2
  10.1 2.0 %collective-permute-start.8 = (bf16[384,512]{1,0:T(8,128)(2,1)S(1)}, bf16[384,512]{1,0:T(8,128)(2,1)S(1)}, u32[]{:S(2)}, u32[]{:S(2)}) collective-permute-start(bf16[384,512]{1,0:T(8,128)(2,1)S(1)} %pad_maximum_fusion.1.refs_9_.refs_0_), channel_id=1, source_target_pairs={{0,16},{8,120},{16,32},{24,8},{32,48},{40,24},{48,64},{56,40},{64,... | collective-permute-start | bytes 1179656 | tf_op jit(solution)/shard_map/ppermute | solution.py:24
  12.1 3.5 %collective-permute-start.15 = (bf16[192,512]{1,0:T(8,128)(2,1)S(1)}, bf16[192,512]{1,0:T(8,128)(2,1)S(1)}, u32[]{:S(2)}, u32[]{:S(2)}) collective-permute-start(bf16[192,512]{1,0:T(8,128)(2,1)S(1)} %collective-permute-done.14), channel_id=1, source_target_pairs={{0,8},{8,0},{1,9},{9,1},{2,10},{10,2},{3,11},{11,3},{4,12},{12,4},... | collective-permute-start | bytes 589832 | tf_op jit(solution)/shard_map/ppermute | solution.py:24
  15.7 3.5 %collective-permute-done.1.refs_2_ = bf16[256,512]{1,0:T(8,128)(2,1)S(1)} collective-permute-done((bf16[256,512]{1,0:T(8,128)(2,1)}, bf16[256,512]{1,0:T(8,128)(2,1)S(1)}, u32[]{:S(2)}, u32[]{:S(2)}) %collective-permute-start.1) | collective-permute-done | bytes 262176 | tf_op jit(solution)/shard_map/ppermute | solution.py:24
  19.3 2.0 %collective-permute-start.16 = (bf16[384,512]{1,0:T(8,128)(2,1)S(1)}, bf16[384,512]{1,0:T(8,128)(2,1)}, u32[]{:S(2)}, u32[]{:S(2)}) collective-permute-start(bf16[384,512]{1,0:T(8,128)(2,1)S(1)} %constant_dynamic-update-slice_fusion.refs_16_.refs_9_), channel_id=1, source_target_pairs={{0,16},{8,120},{16,32},{24,8},{32,48},{40,24},{48,64},{56,40},{64,... | collective-permute-start | bytes 1179656 | tf_op jit(solution)/shard_map/ppermute | solution.py:24
  21.4 0.9 collective-permute-start.4
  22.3 2.4 %collective-permute-start.3 = (bf16[656,512]{1,0:T(8,128)(2,1)S(1)}, bf16[656,512]{1,0:T(8,128)(2,1)S(1)}, u32[]{:S(2)}, u32[]{:S(2)}) collective-permute-start(bf16[656,512]{1,0:T(8,128)(2,1)S(1)} %pad_maximum_fusion.t0.refs_0_.refs_4_), channel_id=1, source_target_pairs={{0,1},{1,2},{2,3},{3,0},{4,5},{5,6},{6,7},{7,4},{8,9},{9,10},{10,1... | collective-permute-start | bytes 2015240 | tf_op jit(solution)/shard_map/ppermute | solution.py:24
  24.7 0.9 copy-done.5
  25.7 1.9 %collective-permute-start.9 = (bf16[384,512]{1,0:T(8,128)(2,1)S(1)}, bf16[384,512]{1,0:T(8,128)(2,1)S(1)}, u32[]{:S(2)}, u32[]{:S(2)}) collective-permute-start(bf16[384,512]{1,0:T(8,128)(2,1)S(1)} %shard_map.119.refs_10_.refs_1_), channel_id=1, source_target_pairs={{0,16},{8,120},{16,32},{24,8},{32,48},{40,24},{48,64},{56,40},{64,... | collective-permute-start | bytes 1179656 | tf_op jit(solution)/shard_map/ppermute | solution.py:24
  27.6 3.5 %collective-permute-done.16.refs_17_.refs_10_ = bf16[384,512]{1,0:T(8,128)(2,1)} collective-permute-done((bf16[384,512]{1,0:T(8,128)(2,1)S(1)}, bf16[384,512]{1,0:T(8,128)(2,1)}, u32[]{:S(2)}, u32[]{:S(2)}) %collective-permute-start.16) | collective-permute-done | bytes 393248 | tf_op jit(solution)/shard_map/ppermute | solution.py:24
  31.3 4.6 %collective-permute-done.9.refs_0_ = bf16[384,512]{1,0:T(8,128)(2,1)S(1)} collective-permute-done((bf16[384,512]{1,0:T(8,128)(2,1)S(1)}, bf16[384,512]{1,0:T(8,128)(2,1)S(1)}, u32[]{:S(2)}, u32[]{:S(2)}) %collective-permute-start.9) | collective-permute-done | bytes 393248 | tf_op jit(solution)/shard_map/ppermute | solution.py:24
  35.9 1.3 collective-permute-start.11
  37.2 1.2 collective-permute-done.4.t3.refs_2_.refs_3_.refs_7_
  38.3 2.4 %collective-permute-start.19 = (bf16[384,512]{1,0:T(8,128)(2,1)}, bf16[384,512]{1,0:T(8,128)(2,1)S(1)}, u32[]{:S(2)}, u32[]{:S(2)}) collective-permute-start(bf16[384,512]{1,0:T(8,128)(2,1)} %collective-permute-done.16.refs_17_.refs_10_), channel_id=1, source_target_pairs={{0,8},{8,0},{1,9},{9,1},{2,10},{10,2},{3,11},{11,3},{4,12},{12,4},... | collective-permute-start | bytes 1179656 | tf_op jit(solution)/shard_map/ppermute | solution.py:24
  41.0 3.8 %collective-permute-done.10.refs_0_ = bf16[384,512]{1,0:T(8,128)(2,1)S(1)} collective-permute-done((bf16[384,512]{1,0:T(8,128)(2,1)S(1)}, bf16[384,512]{1,0:T(8,128)(2,1)S(1)}, u32[]{:S(2)}, u32[]{:S(2)}) %collective-permute-start.10) | collective-permute-done | bytes 393248 | tf_op jit(solution)/shard_map/ppermute | solution.py:24
  44.9 0.2 collective-permute-start.6
  45.0 2.3 %collective-permute-start.12 = (bf16[384,512]{1,0:T(8,128)(2,1)S(1)}, bf16[384,512]{1,0:T(8,128)(2,1)S(1)}, u32[]{:S(2)}, u32[]{:S(2)}) collective-permute-start(bf16[384,512]{1,0:T(8,128)(2,1)S(1)} %shard_map.120.refs_11_.refs_2_), channel_id=1, source_target_pairs={{0,8},{8,0},{1,9},{9,1},{2,10},{10,2},{3,11},{11,3},{4,12},{12,4},... | collective-permute-start | bytes 1179656 | tf_op jit(solution)/shard_map/ppermute | solution.py:24
  47.3 5.3 %collective-permute-done.6.refs_2_.refs_1_ = bf16[256,512]{1,0:T(8,128)(2,1)S(1)} collective-permute-done((bf16[256,512]{1,0:T(8,128)(2,1)S(1)}, bf16[256,512]{1,0:T(8,128)(2,1)S(1)}, u32[]{:S(2)}, u32[]{:S(2)}) %collective-permute-start.6) | collective-permute-done | bytes 262176 | tf_op jit(solution)/shard_map/ppermute | solution.py:24
  52.7 1.0 collective-permute-done.5.t2.refs_6_.refs_2_
  53.6 0.5 collective-permute-start.21
  54.3 3.2 %collective-permute-start.23 = (bf16[192,512]{1,0:T(8,128)(2,1)S(1)}, bf16[192,512]{1,0:T(8,128)(2,1)S(1)}, u32[]{:S(2)}, u32[]{:S(2)}) collective-permute-start(bf16[192,512]{1,0:T(8,128)(2,1)S(1)} %shard_map.123.refs_4_), channel_id=1, source_target_pairs={{0,8},{8,0},{1,9},{9,1},{2,10},{10,2},{3,11},{11,3},{4,12},{12,4},... | collective-permute-start | bytes 589832 | tf_op jit(solution)/shard_map/ppermute | solution.py:24
  57.4 3.9 %collective-permute-done.24.refs_13_ = bf16[192,512]{1,0:T(8,128)(2,1)S(1)} collective-permute-done((bf16[192,512]{1,0:T(8,128)(2,1)S(1)}, bf16[192,512]{1,0:T(8,128)(2,1)S(1)}, u32[]{:S(2)}, u32[]{:S(2)}) %collective-permute-start.24) | collective-permute-done | bytes 196640 | tf_op jit(solution)/shard_map/ppermute | solution.py:24
  61.4 4.9 %shard_map.122 = (f32[512,512]{1,0:T(8,128)S(1)}, f32[512,512]{1,0:T(8,128)S(1)}, bf16[2,512,128]{2,1,0:T(8,128)(2,1)S(1)}) custom-call(s32[5]{0:T(128)S(1)} %stack.23.place.refs_1_, bf16[656,512]{1,0:T(8,128)(2,1)S(1)} %pad_maximum_fusion.t0.refs_0_.refs_4_, bf16[656,512]{1,0:T(8,128)(2,1)S(1)} %collective-permute-done.3.t1.refs_1_.refs_5_, ...), custom_call_target="tpu_custom_call" | custom-call | flops 1879048192 | bytes 4194304 | tf_op jit(solution)/shard_map/pallas_call | solution.py:211
  66.3 4.2 %shard_map.124 = bf16[16,4,32,512]{3,2,1,0:T(8,128)(2,1)S(1)} custom-call(s32[5]{0:T(128)S(1)} %stack.23.place.refs_1_, f32[512,512]{1,0:T(8,128)S(1)} %get-tuple-element.18.gate, f32[512,512]{1,0:T(8,128)S(1)} %get-tuple-element.19.lift, bf16[2,512,128]{2,1,0:T(8,128)(2,1)S(1)} %get-tuple-element.20.last, ...), custom_call_target="tpu_custom_call" | custom-call | flops 1207959552 | bytes 4194304 | tf_op jit(solution)/shard_map/pallas_call | solution.py:229
  70.5 32.2 %all_to_all.5.terms = bf16[16,4,32,512]{3,2,1,0:T(8,128)(2,1)S(1)} all-to-all(bf16[16,4,32,512]{3,2,1,0:T(8,128)(2,1)S(1)} %shard_map.124), channel_id=1, replica_groups=mesh['yh'=2,'z'=8,'c'=2,'p'=2,'x'=4] {'yh','p','x'}, dimensions={0} | all-to-all | bytes 4194304 | tf_op jit(solution)/shard_map/all_to_all | solution.py:404
  102.7 0.9 shard_map.125.m0
  103.6 0.9 collective-permute-start.28
  104.5 3.5 %collective-permute-start.27 = (bf16[32,2048]{1,0:T(8,128)(2,1)S(1)}, bf16[32,2048]{1,0:T(8,128)(2,1)S(1)}, u32[]{:S(2)}, u32[]{:S(2)}) collective-permute-start(bf16[32,2048]{1,0:T(8,128)(2,1)S(1)} %shard_map.125.m0), channel_id=1, source_target_pairs={{0,2},{1,3},{2,0},{3,1},{4,6},{5,7},{6,4},{7,5},{8,10},{9,11},{10,... | collective-permute-start | bytes 393224 | tf_op jit(solution)/shard_map/ppermute | solution.py:24
  108.0 1.2 collective-permute-start.26
  109.2 3.0 %shard_map.118 = (bf16[128,512]{1,0:T(8,128)(2,1)S(1)}, bf16[2048,512]{1,0:T(8,128)(2,1)S(1)}, bf16[2048,512]{1,0:T(8,128)(2,1)S(1)}, bf16[512,2048]{1,0:T(8,128)(2,1)S(1)}) custom-call(s32[5]{0:T(128)S(1)} %stack.23.place.refs_1_, bf16[656,512]{1,0:T(8,128)(2,1)S(1)} %pad_maximum_fusion.t0.refs_0_.refs_4_, ...), custom_call_target="tpu_custom_call" | custom-call | flops 268435456 | bytes 10485760 | tf_op jit(solution)/shard_map/pallas_call | solution.py:307
  112.2 1.1 collective-permute-done.27.m2
  113.4 2.0 %shard_map.126 = (bf16[128,512]{1,0:T(8,128)(2,1)S(1)}, bf16[128,512]{1,0:T(8,128)(2,1)S(1)}, bf16[128,512]{1,0:T(8,128)(2,1)S(1)}, bf16[128,512]{1,0:T(8,128)(2,1)S(1)}, bf16[128,512]{1,0:T(8,128)(2,1)S(1)}) custom-call(s32[5]{0:T(128)S(1)} %stack.23.place.refs_1_, s32[2]{0:T(128)S(1)} %copy-done.6, bf16[128,512]{1,0:T(8,128)(2,1)S(1)} %get-tuple-element.17.query, ...), custom_call_target="tpu_custom_call" | custom-call | flops 805306368 | bytes 8388608 | tf_op jit(solution)/shard_map/pallas_call | solution.py:351
  115.4 2.6 %collective-permute-start.29 = (bf16[128,512]{1,0:T(8,128)(2,1)S(1)}, bf16[128,512]{1,0:T(8,128)(2,1)S(1)}, u32[]{:S(2)}, u32[]{:S(2)}) collective-permute-start(bf16[128,512]{1,0:T(8,128)(2,1)S(1)} %get-tuple-element.26), channel_id=1, source_target_pairs={{0,1},{1,2},{2,3},{3,0},{4,5},{5,6},{6,7},{7,4},{8,9},{9,10},{10,1... | collective-permute-start | bytes 393224 | tf_op jit(solution)/shard_map/ppermute | solution.py:24
  118.0 1.1 collective-permute-start.30
  119.1 0.1 collective-permute-start.31
  119.2 3.2 %collective-permute-done.29 = bf16[128,512]{1,0:T(8,128)(2,1)S(1)} collective-permute-done((bf16[128,512]{1,0:T(8,128)(2,1)S(1)}, bf16[128,512]{1,0:T(8,128)(2,1)S(1)}, u32[]{:S(2)}, u32[]{:S(2)}) %collective-permute-start.29) | collective-permute-done | bytes 131104 | tf_op jit(solution)/shard_map/ppermute | solution.py:24
  122.4 2.1 %collective-permute-done.30 = bf16[128,512]{1,0:T(8,128)(2,1)S(1)} collective-permute-done((bf16[128,512]{1,0:T(8,128)(2,1)S(1)}, bf16[128,512]{1,0:T(8,128)(2,1)S(1)}, u32[]{:S(2)}, u32[]{:S(2)}) %collective-permute-start.30) | collective-permute-done | bytes 131104 | tf_op jit(solution)/shard_map/ppermute | solution.py:24
  124.5 1.5 %collective-permute-done.31 = bf16[128,512]{1,0:T(8,128)(2,1)S(1)} collective-permute-done((bf16[128,512]{1,0:T(8,128)(2,1)S(1)}, bf16[128,512]{1,0:T(8,128)(2,1)S(1)}, u32[]{:S(2)}, u32[]{:S(2)}) %collective-permute-start.31) | collective-permute-done | bytes 131104 | tf_op jit(solution)/shard_map/ppermute | solution.py:24
  126.0 0.1 broadcast_select_fusion.4
  126.1 0.1 collective-permute-start.32
  126.2 5.0 %collective-permute-done.32 = bf16[128,512]{1,0:T(8,128)(2,1)S(1)} collective-permute-done((bf16[128,512]{1,0:T(8,128)(2,1)S(1)}, bf16[128,512]{1,0:T(8,128)(2,1)S(1)}, u32[]{:S(2)}, u32[]{:S(2)}) %collective-permute-start.32) | collective-permute-done | bytes 131104 | tf_op jit(solution)/shard_map/ppermute | solution.py:24
  131.2 0.7 pad_maximum_fusion.2
  (72 shorter events, 0.9 us)
Async XLA Ops:
  0.0 15.6 %copy-start.7 = (bf16[1,2,128,512]{3,2,1,0:T(8,128)(2,1)S(1)}, bf16[1,2,128,512]{3,2,1,0:T(8,128)(2,1)}, u32[]{:S(2)}) copy-start(bf16[1,2,128,512]{3,2,1,0:T(8,128)(2,1)} %param.12) | copy-start | bytes 786436
  1.9 19.4 %copy-start.10 = (bf16[512]{0:T(512)(128)(2,1)S(1)}, bf16[512]{0:T(512)(128)(2,1)}, u32[]{:S(2)}) copy-start(bf16[512]{0:T(512)(128)(2,1)} %param.18) | copy-start | bytes 3076
  1.9 8.2 %collective-permute-start.7 = (bf16[192,512]{1,0:T(8,128)(2,1)S(1)}, bf16[192,512]{1,0:T(8,128)(2,1)S(1)}, u32[]{:S(2)}, u32[]{:S(2)}) collective-permute-start(bf16[192,512]{1,0:T(8,128)(2,1)S(1)} %pad_maximum_fusion.3), channel_id=1, source_target_pairs={{0,8},{8,0},{1,9},{9,1},{2,10},{10,2},{3,11},{11,3},{4,12},{12,4},... | collective-permute-start | bytes 589832 | tf_op jit(solution)/shard_map/ppermute | solution.py:24
  2.1 10.1 %collective-permute-start.14 = (bf16[192,512]{1,0:T(8,128)(2,1)S(1)}, bf16[192,512]{1,0:T(8,128)(2,1)S(1)}, u32[]{:S(2)}, u32[]{:S(2)}) collective-permute-start(bf16[192,512]{1,0:T(8,128)(2,1)S(1)} %pad_maximum_fusion.4), channel_id=1, source_target_pairs={{0,132},{4,128},{128,4},{132,0},{1,133},{5,129},{129,5},{133,1},{2... | collective-permute-start | bytes 589832 | tf_op jit(solution)/shard_map/ppermute | solution.py:24
  5.2 10.4 %collective-permute-start = (bf16[256,512]{1,0:T(8,128)(2,1)}, bf16[256,512]{1,0:T(8,128)(2,1)S(1)}, u32[]{:S(2)}, u32[]{:S(2)}) collective-permute-start(bf16[256,512]{1,0:T(8,128)(2,1)} %bitcast.14), channel_id=1, source_target_pairs={{0,4},{4,0},{1,5},{5,1},{2,6},{6,2},{3,7},{7,3},{8,12},{12,8},{9,1... | collective-permute-start | bytes 786440 | tf_op jit(solution)/shard_map/ppermute | solution.py:24
  5.3 13.9 %collective-permute-start.1 = (bf16[256,512]{1,0:T(8,128)(2,1)}, bf16[256,512]{1,0:T(8,128)(2,1)S(1)}, u32[]{:S(2)}, u32[]{:S(2)}) collective-permute-start(bf16[256,512]{1,0:T(8,128)(2,1)} %bitcast.15), channel_id=1, source_target_pairs={{0,128},{128,0},{1,129},{129,1},{2,130},{130,2},{3,131},{131,3},{8... | collective-permute-start | bytes 786440 | tf_op jit(solution)/shard_map/ppermute | solution.py:24
  8.8 10.5 %collective-permute-start.2 = (bf16[256,512]{1,0:T(8,128)(2,1)}, bf16[256,512]{1,0:T(8,128)(2,1)S(1)}, u32[]{:S(2)}, u32[]{:S(2)}) collective-permute-start(bf16[256,512]{1,0:T(8,128)(2,1)} %bitcast.16), channel_id=1, source_target_pairs={{0,132},{128,4},{1,133},{129,5},{2,134},{130,6},{3,135},{131,7},{8... | collective-permute-start | bytes 786440 | tf_op jit(solution)/shard_map/ppermute | solution.py:24
  10.1 14.6 %collective-permute-start.8 = (bf16[384,512]{1,0:T(8,128)(2,1)S(1)}, bf16[384,512]{1,0:T(8,128)(2,1)S(1)}, u32[]{:S(2)}, u32[]{:S(2)}) collective-permute-start(bf16[384,512]{1,0:T(8,128)(2,1)S(1)} %pad_maximum_fusion.1.refs_9_.refs_0_), channel_id=1, source_target_pairs={{0,16},{8,120},{16,32},{24,8},{32,48},{40,24},{48,64},{56,40},{64,... | collective-permute-start | bytes 1179656 | tf_op jit(solution)/shard_map/ppermute | solution.py:24
  12.1 7.2 %collective-permute-start.15 = (bf16[192,512]{1,0:T(8,128)(2,1)S(1)}, bf16[192,512]{1,0:T(8,128)(2,1)S(1)}, u32[]{:S(2)}, u32[]{:S(2)}) collective-permute-start(bf16[192,512]{1,0:T(8,128)(2,1)S(1)} %collective-permute-done.14), channel_id=1, source_target_pairs={{0,8},{8,0},{1,9},{9,1},{2,10},{10,2},{3,11},{11,3},{4,12},{12,4},... | collective-permute-start | bytes 589832 | tf_op jit(solution)/shard_map/ppermute | solution.py:24
  15.7 15.5 %copy-start.8 = (bf16[2048]{0:T(1024)(128)(2,1)S(1)}, bf16[2048]{0:T(1024)(128)(2,1)}, u32[]{:S(2)}) copy-start(bf16[2048]{0:T(1024)(128)(2,1)} %param.14) | copy-start | bytes 12292
  15.7 15.5 %copy-start.9 = (bf16[2048]{0:T(1024)(128)(2,1)S(1)}, bf16[2048]{0:T(1024)(128)(2,1)}, u32[]{:S(2)}) copy-start(bf16[2048]{0:T(1024)(128)(2,1)} %param.19) | copy-start | bytes 12292
  19.2 2.1 %copy-start.4 = (bf16[256,512]{1,0:T(8,128)(2,1)}, bf16[256,512]{1,0:T(8,128)(2,1)S(1)}, u32[]{:S(2)}) copy-start(bf16[256,512]{1,0:T(8,128)(2,1)S(1)} %collective-permute-done.2.refs_3_) | copy-start | bytes 786436
  19.3 6.3 %copy-start = (bf16[384,512]{1,0:T(8,128)(2,1)}, bf16[384,512]{1,0:T(8,128)(2,1)S(1)}, u32[]{:S(2)}) copy-start(bf16[384,512]{1,0:T(8,128)(2,1)S(1)} %constant_dynamic-update-slice_fusion.refs_16_.refs_9_) | copy-start | bytes 1179652
  19.3 11.8 %collective-permute-start.16 = (bf16[384,512]{1,0:T(8,128)(2,1)S(1)}, bf16[384,512]{1,0:T(8,128)(2,1)}, u32[]{:S(2)}, u32[]{:S(2)}) collective-permute-start(bf16[384,512]{1,0:T(8,128)(2,1)S(1)} %constant_dynamic-update-slice_fusion.refs_16_.refs_9_), channel_id=1, source_target_pairs={{0,16},{8,120},{16,32},{24,8},{32,48},{40,24},{48,64},{56,40},{64,... | collective-permute-start | bytes 1179656 | tf_op jit(solution)/shard_map/ppermute | solution.py:24
  21.4 16.9 %collective-permute-start.4 = (bf16[656,512]{1,0:T(8,128)(2,1)S(1)}, bf16[656,512]{1,0:T(8,128)(2,1)S(1)}, u32[]{:S(2)}, u32[]{:S(2)}) collective-permute-start(bf16[656,512]{1,0:T(8,128)(2,1)S(1)} %pad_maximum_fusion.t0.refs_0_.refs_4_), channel_id=1, source_target_pairs={{0,3},{1,0},{2,1},{3,2},{4,7},{5,4},{6,5},{7,6},{8,11},{9,8},{10,9... | collective-permute-start | bytes 2015240 | tf_op jit(solution)/shard_map/ppermute | solution.py:24
  22.3 18.5 %collective-permute-start.3 = (bf16[656,512]{1,0:T(8,128)(2,1)S(1)}, bf16[656,512]{1,0:T(8,128)(2,1)S(1)}, u32[]{:S(2)}, u32[]{:S(2)}) collective-permute-start(bf16[656,512]{1,0:T(8,128)(2,1)S(1)} %pad_maximum_fusion.t0.refs_0_.refs_4_), channel_id=1, source_target_pairs={{0,1},{1,2},{2,3},{3,0},{4,5},{5,6},{6,7},{7,4},{8,9},{9,10},{10,1... | collective-permute-start | bytes 2015240 | tf_op jit(solution)/shard_map/ppermute | solution.py:24
  24.7 1.0 copy-start.5
  25.7 10.2 %collective-permute-start.9 = (bf16[384,512]{1,0:T(8,128)(2,1)S(1)}, bf16[384,512]{1,0:T(8,128)(2,1)S(1)}, u32[]{:S(2)}, u32[]{:S(2)}) collective-permute-start(bf16[384,512]{1,0:T(8,128)(2,1)S(1)} %shard_map.119.refs_10_.refs_1_), channel_id=1, source_target_pairs={{0,16},{8,120},{16,32},{24,8},{32,48},{40,24},{48,64},{56,40},{64,... | collective-permute-start | bytes 1179656 | tf_op jit(solution)/shard_map/ppermute | solution.py:24
  31.1 9.8 %collective-permute-start.17 = (bf16[384,512]{1,0:T(8,128)(2,1)}, bf16[384,512]{1,0:T(8,128)(2,1)}, u32[]{:S(2)}, u32[]{:S(2)}) collective-permute-start(bf16[384,512]{1,0:T(8,128)(2,1)} %collective-permute-done.16.refs_17_.refs_10_), channel_id=1, source_target_pairs={{0,16},{8,120},{16,32},{24,8},{32,48},{40,24},{48,64},{56,40},{64,... | collective-permute-start | bytes 1179656 | tf_op jit(solution)/shard_map/ppermute | solution.py:24
  35.9 9.0 %collective-permute-start.10 = (bf16[384,512]{1,0:T(8,128)(2,1)S(1)}, bf16[384,512]{1,0:T(8,128)(2,1)S(1)}, u32[]{:S(2)}, u32[]{:S(2)}) collective-permute-start(bf16[384,512]{1,0:T(8,128)(2,1)S(1)} %shard_map.120.refs_11_.refs_2_), channel_id=1, source_target_pairs={{0,16},{8,120},{16,32},{24,8},{32,48},{40,24},{48,64},{56,40},{64,... | collective-permute-start | bytes 1179656 | tf_op jit(solution)/shard_map/ppermute | solution.py:24
  35.9 9.2 %collective-permute-start.11 = (bf16[384,512]{1,0:T(8,128)(2,1)S(1)}, bf16[384,512]{1,0:T(8,128)(2,1)S(1)}, u32[]{:S(2)}, u32[]{:S(2)}) collective-permute-start(bf16[384,512]{1,0:T(8,128)(2,1)S(1)} %shard_map.119.refs_10_.refs_1_), channel_id=1, source_target_pairs={{0,8},{8,0},{1,9},{9,1},{2,10},{10,2},{3,11},{11,3},{4,12},{12,4},... | collective-permute-start | bytes 1179656 | tf_op jit(solution)/shard_map/ppermute | solution.py:24
  38.3 9.0 %collective-permute-start.19 = (bf16[384,512]{1,0:T(8,128)(2,1)}, bf16[384,512]{1,0:T(8,128)(2,1)S(1)}, u32[]{:S(2)}, u32[]{:S(2)}) collective-permute-start(bf16[384,512]{1,0:T(8,128)(2,1)} %collective-permute-done.16.refs_17_.refs_10_), channel_id=1, source_target_pairs={{0,8},{8,0},{1,9},{9,1},{2,10},{10,2},{3,11},{11,3},{4,12},{12,4},... | collective-permute-start | bytes 1179656 | tf_op jit(solution)/shard_map/ppermute | solution.py:24
  40.8 12.8 %collective-permute-start.5 = (bf16[400,512]{1,0:T(8,128)(2,1)S(1)}, bf16[400,512]{1,0:T(8,128)(2,1)S(1)}, u32[]{:S(2)}, u32[]{:S(2)}) collective-permute-start(bf16[400,512]{1,0:T(8,128)(2,1)S(1)} %slice.29), channel_id=1, source_target_pairs={{0,3},{1,0},{2,1},{3,2},{4,7},{5,4},{6,5},{7,6},{8,11},{9,8},{10,9... | collective-permute-start | bytes 1228808 | tf_op jit(solution)/shard_map/ppermute | solution.py:24
  40.9 12.7 %collective-permute-start.18 = (bf16[384,512]{1,0:T(8,128)(2,1)}, bf16[384,512]{1,0:T(8,128)(2,1)S(1)}, u32[]{:S(2)}, u32[]{:S(2)}) collective-permute-start(bf16[384,512]{1,0:T(8,128)(2,1)} %collective-permute-done.17.refs_18_.refs_11_), channel_id=1, source_target_pairs={{0,16},{8,120},{16,32},{24,8},{32,48},{40,24},{48,64},{56,40},{64,... | collective-permute-start | bytes 1179656 | tf_op jit(solution)/shard_map/ppermute | solution.py:24
  41.0 20.4 %copy-start.1 = (bf16[384,512]{1,0:T(8,128)(2,1)S(1)}, bf16[384,512]{1,0:T(8,128)(2,1)}, u32[]{:S(2)}) copy-start(bf16[384,512]{1,0:T(8,128)(2,1)} %copy-done) | copy-start | bytes 1179652
  44.9 7.8 %collective-permute-start.6 = (bf16[256,512]{1,0:T(8,128)(2,1)S(1)}, bf16[256,512]{1,0:T(8,128)(2,1)S(1)}, u32[]{:S(2)}, u32[]{:S(2)}) collective-permute-start(bf16[256,512]{1,0:T(8,128)(2,1)S(1)} %slice.30), channel_id=1, source_target_pairs={{0,1},{1,2},{2,3},{3,0},{4,5},{5,6},{6,7},{7,4},{8,9},{9,10},{10,1... | collective-permute-start | bytes 786440 | tf_op jit(solution)/shard_map/ppermute | solution.py:24
  45.0 9.2 %collective-permute-start.12 = (bf16[384,512]{1,0:T(8,128)(2,1)S(1)}, bf16[384,512]{1,0:T(8,128)(2,1)S(1)}, u32[]{:S(2)}, u32[]{:S(2)}) collective-permute-start(bf16[384,512]{1,0:T(8,128)(2,1)S(1)} %shard_map.120.refs_11_.refs_2_), channel_id=1, source_target_pairs={{0,8},{8,0},{1,9},{9,1},{2,10},{10,2},{3,11},{11,3},{4,12},{12,4},... | collective-permute-start | bytes 1179656 | tf_op jit(solution)/shard_map/ppermute | solution.py:24
  47.3 6.9 %collective-permute-start.22 = (bf16[192,512]{1,0:T(8,128)(2,1)S(1)}, bf16[192,512]{1,0:T(8,128)(2,1)S(1)}, u32[]{:S(2)}, u32[]{:S(2)}) collective-permute-start(bf16[192,512]{1,0:T(8,128)(2,1)S(1)} %slice.31), channel_id=1, source_target_pairs={{0,16},{8,120},{16,32},{24,8},{32,48},{40,24},{48,64},{56,40},{64,... | collective-permute-start | bytes 589832 | tf_op jit(solution)/shard_map/ppermute | solution.py:24
  52.7 8.7 %collective-permute-start.20 = (bf16[384,512]{1,0:T(8,128)(2,1)}, bf16[384,512]{1,0:T(8,128)(2,1)S(1)}, u32[]{:S(2)}, u32[]{:S(2)}) collective-permute-start(bf16[384,512]{1,0:T(8,128)(2,1)} %collective-permute-done.17.refs_18_.refs_11_), channel_id=1, source_target_pairs={{0,8},{8,0},{1,9},{9,1},{2,10},{10,2},{3,11},{11,3},{4,12},{12,4},... | collective-permute-start | bytes 1179656 | tf_op jit(solution)/shard_map/ppermute | solution.py:24
  53.6 7.8 %collective-permute-start.13 = (bf16[384,512]{1,0:T(8,128)(2,1)S(1)}, bf16[384,512]{1,0:T(8,128)(2,1)S(1)}, u32[]{:S(2)}, u32[]{:S(2)}) collective-permute-start(bf16[384,512]{1,0:T(8,128)(2,1)S(1)} %shard_map.121.refs_12_.refs_3_), channel_id=1, source_target_pairs={{0,8},{8,0},{1,9},{9,1},{2,10},{10,2},{3,11},{11,3},{4,12},{12,4},... | collective-permute-start | bytes 1179656 | tf_op jit(solution)/shard_map/ppermute | solution.py:24
  53.6 7.8 %collective-permute-start.21 = (bf16[384,512]{1,0:T(8,128)(2,1)S(1)}, bf16[384,512]{1,0:T(8,128)(2,1)S(1)}, u32[]{:S(2)}, u32[]{:S(2)}) collective-permute-start(bf16[384,512]{1,0:T(8,128)(2,1)S(1)} %collective-permute-done.18.refs_19_.refs_12_), channel_id=1, source_target_pairs={{0,8},{8,0},{1,9},{9,1},{2,10},{10,2},{3,11},{11,3},{4,12},{12,4},... | collective-permute-start | bytes 1179656 | tf_op jit(solution)/shard_map/ppermute | solution.py:24
  54.2 7.1 %collective-permute-start.24 = (bf16[192,512]{1,0:T(8,128)(2,1)S(1)}, bf16[192,512]{1,0:T(8,128)(2,1)S(1)}, u32[]{:S(2)}, u32[]{:S(2)}) collective-permute-start(bf16[192,512]{1,0:T(8,128)(2,1)S(1)} %slice.32), channel_id=1, source_target_pairs={{0,16},{8,120},{16,32},{24,8},{32,48},{40,24},{48,64},{56,40},{64,... | collective-permute-start | bytes 589832 | tf_op jit(solution)/shard_map/ppermute | solution.py:24
  54.3 12.0 %collective-permute-start.23 = (bf16[192,512]{1,0:T(8,128)(2,1)S(1)}, bf16[192,512]{1,0:T(8,128)(2,1)S(1)}, u32[]{:S(2)}, u32[]{:S(2)}) collective-permute-start(bf16[192,512]{1,0:T(8,128)(2,1)S(1)} %shard_map.123.refs_4_), channel_id=1, source_target_pairs={{0,8},{8,0},{1,9},{9,1},{2,10},{10,2},{3,11},{11,3},{4,12},{12,4},... | collective-permute-start | bytes 589832 | tf_op jit(solution)/shard_map/ppermute | solution.py:24
  61.4 4.9 %collective-permute-start.25 = (bf16[192,512]{1,0:T(8,128)(2,1)S(1)}, bf16[192,512]{1,0:T(8,128)(2,1)S(1)}, u32[]{:S(2)}, u32[]{:S(2)}) collective-permute-start(bf16[192,512]{1,0:T(8,128)(2,1)S(1)} %collective-permute-done.24.refs_13_), channel_id=1, source_target_pairs={{0,8},{8,0},{1,9},{9,1},{2,10},{10,2},{3,11},{11,3},{4,12},{12,4},... | collective-permute-start | bytes 589832 | tf_op jit(solution)/shard_map/ppermute | solution.py:24
  102.7 6.5 %copy-start.2 = (bf16[2048,512]{1,0:T(8,128)(2,1)S(1)}, bf16[2048,512]{1,0:T(8,128)(2,1)}, u32[]{:S(2)}) copy-start(bf16[2048,512]{1,0:T(8,128)(2,1)} %weight.1) | copy-start | bytes 6291460
  102.7 6.5 %copy-start.3 = (bf16[2048,512]{1,0:T(8,128)(2,1)S(1)}, bf16[2048,512]{1,0:T(8,128)(2,1)}, u32[]{:S(2)}) copy-start(bf16[2048,512]{1,0:T(8,128)(2,1)} %wk.1) | copy-start | bytes 6291460
  103.6 9.8 %copy-start.6 = (s32[2]{0:T(128)S(1)}, s32[2]{0:T(128)}, u32[]{:S(2)}) copy-start(s32[2]{0:T(128)} %lengths.1) | copy-start | bytes 28
  103.6 8.6 %collective-permute-start.28 = (bf16[32,2048]{1,0:T(8,128)(2,1)S(1)}, bf16[32,2048]{1,0:T(8,128)(2,1)S(1)}, u32[]{:S(2)}, u32[]{:S(2)}) collective-permute-start(bf16[32,2048]{1,0:T(8,128)(2,1)S(1)} %shard_map.125.m0), channel_id=1, source_target_pairs={{0,3},{1,0},{2,1},{3,2},{4,7},{5,4},{6,5},{7,6},{8,11},{9,8},{10,9... | collective-permute-start | bytes 393224 | tf_op jit(solution)/shard_map/ppermute | solution.py:24
  104.5 8.7 %collective-permute-start.27 = (bf16[32,2048]{1,0:T(8,128)(2,1)S(1)}, bf16[32,2048]{1,0:T(8,128)(2,1)S(1)}, u32[]{:S(2)}, u32[]{:S(2)}) collective-permute-start(bf16[32,2048]{1,0:T(8,128)(2,1)S(1)} %shard_map.125.m0), channel_id=1, source_target_pairs={{0,2},{1,3},{2,0},{3,1},{4,6},{5,7},{6,4},{7,5},{8,10},{9,11},{10,... | collective-permute-start | bytes 393224 | tf_op jit(solution)/shard_map/ppermute | solution.py:24
  108.0 5.4 %collective-permute-start.26 = (bf16[32,2048]{1,0:T(8,128)(2,1)S(1)}, bf16[32,2048]{1,0:T(8,128)(2,1)S(1)}, u32[]{:S(2)}, u32[]{:S(2)}) collective-permute-start(bf16[32,2048]{1,0:T(8,128)(2,1)S(1)} %shard_map.125.m0), channel_id=1, source_target_pairs={{0,1},{1,2},{2,3},{3,0},{4,5},{5,6},{6,7},{7,4},{8,9},{9,10},{10,1... | collective-permute-start | bytes 393224 | tf_op jit(solution)/shard_map/ppermute | solution.py:24
  115.4 7.1 %collective-permute-start.29 = (bf16[128,512]{1,0:T(8,128)(2,1)S(1)}, bf16[128,512]{1,0:T(8,128)(2,1)S(1)}, u32[]{:S(2)}, u32[]{:S(2)}) collective-permute-start(bf16[128,512]{1,0:T(8,128)(2,1)S(1)} %get-tuple-element.26), channel_id=1, source_target_pairs={{0,1},{1,2},{2,3},{3,0},{4,5},{5,6},{6,7},{7,4},{8,9},{9,10},{10,1... | collective-permute-start | bytes 393224 | tf_op jit(solution)/shard_map/ppermute | solution.py:24
  118.0 6.6 %collective-permute-start.30 = (bf16[128,512]{1,0:T(8,128)(2,1)S(1)}, bf16[128,512]{1,0:T(8,128)(2,1)S(1)}, u32[]{:S(2)}, u32[]{:S(2)}) collective-permute-start(bf16[128,512]{1,0:T(8,128)(2,1)S(1)} %get-tuple-element.27), channel_id=1, source_target_pairs={{0,2},{1,3},{2,0},{3,1},{4,6},{5,7},{6,4},{7,5},{8,10},{9,11},{10,... | collective-permute-start | bytes 393224 | tf_op jit(solution)/shard_map/ppermute | solution.py:24
  119.1 6.9 %collective-permute-start.31 = (bf16[128,512]{1,0:T(8,128)(2,1)S(1)}, bf16[128,512]{1,0:T(8,128)(2,1)S(1)}, u32[]{:S(2)}, u32[]{:S(2)}) collective-permute-start(bf16[128,512]{1,0:T(8,128)(2,1)S(1)} %get-tuple-element.28), channel_id=1, source_target_pairs={{0,3},{1,0},{2,1},{3,2},{4,7},{5,4},{6,5},{7,6},{8,11},{9,8},{10,9... | collective-permute-start | bytes 393224 | tf_op jit(solution)/shard_map/ppermute | solution.py:24
  126.1 5.1 %collective-permute-start.32 = (bf16[128,512]{1,0:T(8,128)(2,1)S(1)}, bf16[128,512]{1,0:T(8,128)(2,1)S(1)}, u32[]{:S(2)}, u32[]{:S(2)}) collective-permute-start(bf16[128,512]{1,0:T(8,128)(2,1)S(1)} %get-tuple-element.29), channel_id=1, source_target_pairs={{0,4},{4,0},{1,5},{5,1},{2,6},{6,2},{3,7},{7,3},{8,12},{12,8},{9,1... | collective-permute-start | bytes 393224 | tf_op jit(solution)/shard_map/ppermute | solution.py:24

commit v7 on v6

--- a/solution.py
+++ b/solution.py
@@ -52,9 +52,9 @@
     for k in range(3):
         near.append(after(passed(near[k]), *ready[k]))
         far.append(passed(far[k]))
-    near.append(after(passed(near[3][:192]), *ready[3]))
+    near.append(passed(near[3][:192]))
     far.append(passed(far[3][:192]))
-    return [v for line in (near, far) for v in line + [twin(chunk) for chunk in line[1:]]]
+    return [v for line in (near, far) for v in line + [twin(chunk) for chunk in line[1:4]]]
 
 
 def opposite(value):
@@ -218,6 +218,11 @@
             flops=512 * 1792 * 512 * 4, bytes_accessed=4 * MIB, transcendentals=0
         ),
     )(place, *mine, *theirs, gain, *given)
+    lines = []
+    for line in (chunks[: CHUNKS - 1], chunks[CHUNKS - 1 :]):
+        arrived = after(line[4], last)
+        lines += line[:4] + [arrived] + line[5:] + [twin(arrived)]
+    chunks = lines
     grid_spec = pltpu.PrefetchScalarGridSpec(
         num_scalar_prefetch=1,
         grid=(2,),
@@ -398,7 +403,7 @@
     gain = encoder_gain.reshape(4, 1, 512)
     query_gain = decoder_gain.reshape(4, 1, 512)
     early = swapped, across, corner
-    chunks = gather_lines(near, far, (early, (place, gain, query_gain), tokens[1:4:2], tokens[2]))
+    chunks = gather_lines(near, far, (early, (place, gain, query_gain), tokens[1:4:2]))
 
     terms = ffn(place, tokens, gain, chunks)
     terms = lax.all_to_all(terms, ("yh", "p", "x"), 0, 0)

time: 132 us -> 130 us (0.985)
  waiting for transfers between devices: 39.9 us -> 37.1 us
    ppermute x33, waiting for transfers between devices: 39.9 us -> 37.1 us  [moved(): return lax.ppermute(value, axes, pairs)]
  transfers between devices with their start and end apart: 33 -> 33, of which waited for: 15 -> 18; matrix products, arithmetic and copies ran while one was open for 0% -> 0% of each run, Pallas kernels for 6% -> 6%
where the time goes in v7:
time: 130 us
  starting transfers between devices  41.6 us (32%)
  waiting for transfers between devices  37.1 us (29%)
  blocking collectives  31.8 us (24%)
  Pallas kernels  15.2 us (12%)
  local copies, waits for them, and re-layouts  3.1 us (2%)
    ppermute x33, starting transfers between devices, moved(): return lax.ppermute(value, axes, pairs)  41.6 us
    ppermute x33, waiting for transfers between devices, moved(): return lax.ppermute(value, axes, pairs)  37.1 us
    all_to_all x1, blocking collectives, shards(): terms = lax.all_to_all(terms, ('yh', 'p', 'x'), 0, 0)  31.8 us
    pallas_call x1, Pallas kernels, ffn(): pl.pallas_call(first_kernel, grid_spec=grid_spec, out_shape=[jax.ShapeDty...  5.01 us
    pallas_call x1, Pallas kernels, ffn(): pl.pallas_call(second_kernel, grid_spec=grid_spec, out_shape=jax.ShapeDty...  4.29 us
    pallas_call x1, Pallas kernels, query_rows(): pl.pallas_call(query_kernel, grid_spec=grid_spec, out_shape=[jax.ShapeDty...  2.99 us
  transfers between devices with their start and end apart: 33, of which 18 were waited for; matrix products, arithmetic and copies ran while one was open for 0% of the time, Pallas kernels for 6%

profile of v7, /device:TPU:6, one launch (start us, length us, event | category | flops | bytes accessed | tf_op | source)
XLA Modules:
  0.0 130.2 jit_solution(12355528399443794977)
XLA Ops:
  0.0 0.9 dynamic-slice_bitcast_fusion
  0.9 1.0 constant_dynamic-slice_fusion
  2.1 3.1 %collective-permute-start.14 = (bf16[192,512]{1,0:T(8,128)(2,1)S(1)}, bf16[192,512]{1,0:T(8,128)(2,1)S(1)}, u32[]{:S(2)}, u32[]{:S(2)}) collective-permute-start(bf16[192,512]{1,0:T(8,128)(2,1)S(1)} %pad_maximum_fusion.4), channel_id=1, source_target_pairs={{0,132},{4,128},{128,4},{132,0},{1,133},{5,129},{129,5},{133,1},{2... | collective-permute-start | bytes 589832 | tf_op jit(solution)/shard_map/ppermute | solution.py:24
  5.3 3.5 %collective-permute-start.1 = (bf16[256,512]{1,0:T(8,128)(2,1)}, bf16[256,512]{1,0:T(8,128)(2,1)S(1)}, u32[]{:S(2)}, u32[]{:S(2)}) collective-permute-start(bf16[256,512]{1,0:T(8,128)(2,1)} %bitcast.15), channel_id=1, source_target_pairs={{0,128},{128,0},{1,129},{129,1},{2,130},{130,2},{3,131},{131,3},{8... | collective-permute-start | bytes 786440 | tf_op jit(solution)/shard_map/ppermute | solution.py:24
  8.8 1.3 %collective-permute-start.2 = (bf16[256,512]{1,0:T(8,128)(2,1)}, bf16[256,512]{1,0:T(8,128)(2,1)S(1)}, u32[]{:S(2)}, u32[]{:S(2)}) collective-permute-start(bf16[256,512]{1,0:T(8,128)(2,1)} %bitcast.16), channel_id=1, source_target_pairs={{0,132},{128,4},{1,133},{129,5},{2,134},{130,6},{3,135},{131,7},{8... | collective-permute-start | bytes 786440 | tf_op jit(solution)/shard_map/ppermute | solution.py:24
  10.1 2.0 %collective-permute-start.8 = (bf16[384,512]{1,0:T(8,128)(2,1)S(1)}, bf16[384,512]{1,0:T(8,128)(2,1)S(1)}, u32[]{:S(2)}, u32[]{:S(2)}) collective-permute-start(bf16[384,512]{1,0:T(8,128)(2,1)S(1)} %pad_maximum_fusion.1.refs_9_.refs_0_), channel_id=1, source_target_pairs={{0,16},{8,120},{16,32},{24,8},{32,48},{40,24},{48,64},{56,40},{64,... | collective-permute-start | bytes 1179656 | tf_op jit(solution)/shard_map/ppermute | solution.py:24
  12.1 3.5 %collective-permute-start.15 = (bf16[192,512]{1,0:T(8,128)(2,1)S(1)}, bf16[192,512]{1,0:T(8,128)(2,1)S(1)}, u32[]{:S(2)}, u32[]{:S(2)}) collective-permute-start(bf16[192,512]{1,0:T(8,128)(2,1)S(1)} %collective-permute-done.14), channel_id=1, source_target_pairs={{0,8},{8,0},{1,9},{9,1},{2,10},{10,2},{3,11},{11,3},{4,12},{12,4},... | collective-permute-start | bytes 589832 | tf_op jit(solution)/shard_map/ppermute | solution.py:24
  15.7 3.5 %collective-permute-done.1.refs_2_ = bf16[256,512]{1,0:T(8,128)(2,1)S(1)} collective-permute-done((bf16[256,512]{1,0:T(8,128)(2,1)}, bf16[256,512]{1,0:T(8,128)(2,1)S(1)}, u32[]{:S(2)}, u32[]{:S(2)}) %collective-permute-start.1) | collective-permute-done | bytes 262176 | tf_op jit(solution)/shard_map/ppermute | solution.py:24
  19.3 2.0 %collective-permute-start.16 = (bf16[384,512]{1,0:T(8,128)(2,1)S(1)}, bf16[384,512]{1,0:T(8,128)(2,1)}, u32[]{:S(2)}, u32[]{:S(2)}) collective-permute-start(bf16[384,512]{1,0:T(8,128)(2,1)S(1)} %constant_dynamic-update-slice_fusion.refs_16_.refs_9_), channel_id=1, source_target_pairs={{0,16},{8,120},{16,32},{24,8},{32,48},{40,24},{48,64},{56,40},{64,... | collective-permute-start | bytes 1179656 | tf_op jit(solution)/shard_map/ppermute | solution.py:24
  21.4 0.6 collective-permute-start.3
  22.0 1.5 %collective-permute-start.4 = (bf16[656,512]{1,0:T(8,128)(2,1)S(1)}, bf16[656,512]{1,0:T(8,128)(2,1)S(1)}, u32[]{:S(2)}, u32[]{:S(2)}) collective-permute-start(bf16[656,512]{1,0:T(8,128)(2,1)S(1)} %pad_maximum_fusion.t0.refs_0_.refs_4_), channel_id=1, source_target_pairs={{0,3},{1,0},{2,1},{3,2},{4,7},{5,4},{6,5},{7,6},{8,11},{9,8},{10,9... | collective-permute-start | bytes 2015240 | tf_op jit(solution)/shard_map/ppermute | solution.py:24
  23.5 0.9 copy-done.5
  24.5 1.9 %collective-permute-start.9 = (bf16[384,512]{1,0:T(8,128)(2,1)S(1)}, bf16[384,512]{1,0:T(8,128)(2,1)S(1)}, u32[]{:S(2)}, u32[]{:S(2)}) collective-permute-start(bf16[384,512]{1,0:T(8,128)(2,1)S(1)} %shard_map.119.refs_10_.refs_1_), channel_id=1, source_target_pairs={{0,16},{8,120},{16,32},{24,8},{32,48},{40,24},{48,64},{56,40},{64,... | collective-permute-start | bytes 1179656 | tf_op jit(solution)/shard_map/ppermute | solution.py:24
  26.4 4.8 %collective-permute-done.16.refs_17_.refs_10_ = bf16[384,512]{1,0:T(8,128)(2,1)} collective-permute-done((bf16[384,512]{1,0:T(8,128)(2,1)S(1)}, bf16[384,512]{1,0:T(8,128)(2,1)}, u32[]{:S(2)}, u32[]{:S(2)}) %collective-permute-start.16) | collective-permute-done | bytes 393248 | tf_op jit(solution)/shard_map/ppermute | solution.py:24
  31.1 1.5 %collective-permute-start.11 = (bf16[384,512]{1,0:T(8,128)(2,1)S(1)}, bf16[384,512]{1,0:T(8,128)(2,1)}, u32[]{:S(2)}, u32[]{:S(2)}) collective-permute-start(bf16[384,512]{1,0:T(8,128)(2,1)S(1)} %shard_map.119.refs_10_.refs_1_), channel_id=1, source_target_pairs={{0,8},{8,0},{1,9},{9,1},{2,10},{10,2},{3,11},{11,3},{4,12},{12,4},... | collective-permute-start | bytes 1179656 | tf_op jit(solution)/shard_map/ppermute | solution.py:24
  32.8 2.4 %collective-permute-done.9.refs_0_ = bf16[384,512]{1,0:T(8,128)(2,1)S(1)} collective-permute-done((bf16[384,512]{1,0:T(8,128)(2,1)S(1)}, bf16[384,512]{1,0:T(8,128)(2,1)S(1)}, u32[]{:S(2)}, u32[]{:S(2)}) %collective-permute-start.9) | collective-permute-done | bytes 393248 | tf_op jit(solution)/shard_map/ppermute | solution.py:24
  35.2 1.9 %collective-permute-done.3.t1.refs_1_.refs_5_ = bf16[656,512]{1,0:T(8,128)(2,1)S(1)} collective-permute-done((bf16[656,512]{1,0:T(8,128)(2,1)S(1)}, bf16[656,512]{1,0:T(8,128)(2,1)S(1)}, u32[]{:S(2)}, u32[]{:S(2)}) %collective-permute-start.3) | collective-permute-done | bytes 671776 | tf_op jit(solution)/shard_map/ppermute | solution.py:24
  37.1 2.5 %collective-permute-start.19 = (bf16[384,512]{1,0:T(8,128)(2,1)}, bf16[384,512]{1,0:T(8,128)(2,1)S(1)}, u32[]{:S(2)}, u32[]{:S(2)}) collective-permute-start(bf16[384,512]{1,0:T(8,128)(2,1)} %collective-permute-done.16.refs_17_.refs_10_), channel_id=1, source_target_pairs={{0,8},{8,0},{1,9},{9,1},{2,10},{10,2},{3,11},{11,3},{4,12},{12,4},... | collective-permute-start | bytes 1179656 | tf_op jit(solution)/shard_map/ppermute | solution.py:24
  39.7 0.8 collective-permute-done.17.refs_18_.refs_11_
  40.5 0.9 collective-permute-start.6
  41.4 1.3 collective-permute-start.5
  42.7 1.8 %collective-permute-done.10.refs_0_ = bf16[384,512]{1,0:T(8,128)(2,1)S(1)} collective-permute-done((bf16[384,512]{1,0:T(8,128)(2,1)S(1)}, bf16[384,512]{1,0:T(8,128)(2,1)S(1)}, u32[]{:S(2)}, u32[]{:S(2)}) %collective-permute-start.10) | collective-permute-done | bytes 393248 | tf_op jit(solution)/shard_map/ppermute | solution.py:24
  45.1 3.1 %collective-permute-done.6.refs_2_ = bf16[256,512]{1,0:T(8,128)(2,1)S(1)} collective-permute-done((bf16[256,512]{1,0:T(8,128)(2,1)S(1)}, bf16[256,512]{1,0:T(8,128)(2,1)S(1)}, u32[]{:S(2)}, u32[]{:S(2)}) %collective-permute-start.6) | collective-permute-done | bytes 262176 | tf_op jit(solution)/shard_map/ppermute | solution.py:24
  48.2 1.7 %collective-permute-start.13 = (bf16[384,512]{1,0:T(8,128)(2,1)S(1)}, bf16[384,512]{1,0:T(8,128)(2,1)S(1)}, u32[]{:S(2)}, u32[]{:S(2)}) collective-permute-start(bf16[384,512]{1,0:T(8,128)(2,1)S(1)} %shard_map.121.refs_12_.refs_3_), channel_id=1, source_target_pairs={{0,8},{8,0},{1,9},{9,1},{2,10},{10,2},{3,11},{11,3},{4,12},{12,4},... | collective-permute-start | bytes 1179656 | tf_op jit(solution)/shard_map/ppermute | solution.py:24
  49.9 3.1 %collective-permute-done.5.t2.refs_6_ = bf16[400,512]{1,0:T(8,128)(2,1)S(1)} collective-permute-done((bf16[400,512]{1,0:T(8,128)(2,1)S(1)}, bf16[400,512]{1,0:T(8,128)(2,1)S(1)}, u32[]{:S(2)}, u32[]{:S(2)}) %collective-permute-start.5) | collective-permute-done | bytes 409632 | tf_op jit(solution)/shard_map/ppermute | solution.py:24
  52.9 2.6 %collective-permute-start.22 = (bf16[192,512]{1,0:T(8,128)(2,1)S(1)}, bf16[192,512]{1,0:T(8,128)(2,1)S(1)}, u32[]{:S(2)}, u32[]{:S(2)}) collective-permute-start(bf16[192,512]{1,0:T(8,128)(2,1)S(1)} %slice.31), channel_id=1, source_target_pairs={{0,16},{8,120},{16,32},{24,8},{32,48},{40,24},{48,64},{56,40},{64,... | collective-permute-start | bytes 589832 | tf_op jit(solution)/shard_map/ppermute | solution.py:24
  55.9 5.0 %shard_map.122 = (f32[512,512]{1,0:T(8,128)S(1)}, f32[512,512]{1,0:T(8,128)S(1)}, bf16[2,512,128]{2,1,0:T(8,128)(2,1)S(1)}) custom-call(s32[5]{0:T(128)S(1)} %stack.23.place.refs_1_, bf16[656,512]{1,0:T(8,128)(2,1)S(1)} %pad_maximum_fusion.t0.refs_0_.refs_4_, bf16[656,512]{1,0:T(8,128)(2,1)S(1)} %collective-permute-done.3.t1.refs_1_.refs_5_, ...), custom_call_target="tpu_custom_call" | custom-call | flops 1879048192 | bytes 4194304 | tf_op jit(solution)/shard_map/pallas_call | solution.py:211
  60.9 0.9 collective-permute-done.22.refs_0_
  61.8 1.3 %collective-permute-start.23 = (bf16[192,512]{1,0:T(8,128)(2,1)S(1)}, bf16[192,512]{1,0:T(8,128)(2,1)S(1)}, u32[]{:S(2)}, u32[]{:S(2)}) collective-permute-start(bf16[192,512]{1,0:T(8,128)(2,1)S(1)} %shard_map.123.refs_4_), channel_id=1, source_target_pairs={{0,8},{8,0},{1,9},{9,1},{2,10},{10,2},{3,11},{11,3},{4,12},{12,4},... | collective-permute-start | bytes 589832 | tf_op jit(solution)/shard_map/ppermute | solution.py:24
  63.1 0.8 collective-permute-done.24.refs_0_
  64.2 1.2 collective-permute-done.25.refs_17_
  65.3 4.3 %shard_map.125 = bf16[16,4,32,512]{3,2,1,0:T(8,128)(2,1)S(1)} custom-call(s32[5]{0:T(128)S(1)} %stack.23.place.refs_1_, f32[512,512]{1,0:T(8,128)S(1)} %get-tuple-element.18.gate, f32[512,512]{1,0:T(8,128)S(1)} %get-tuple-element.19.lift, bf16[2,512,128]{2,1,0:T(8,128)(2,1)S(1)} %get-tuple-element.20.refs_1_.last, ...), custom_call_target="tpu_custom_call" | custom-call | flops 1207959552 | bytes 4194304 | tf_op jit(solution)/shard_map/pallas_call | solution.py:234
  69.6 31.8 %all_to_all.5.terms = bf16[16,4,32,512]{3,2,1,0:T(8,128)(2,1)S(1)} all-to-all(bf16[16,4,32,512]{3,2,1,0:T(8,128)(2,1)S(1)} %shard_map.125), channel_id=1, replica_groups=mesh['yh'=2,'z'=8,'c'=2,'p'=2,'x'=4] {'yh','p','x'}, dimensions={0} | all-to-all | bytes 4194304 | tf_op jit(solution)/shard_map/all_to_all | solution.py:409
  101.4 0.9 shard_map.126.m0
  102.4 0.9 collective-permute-start.28
  103.3 3.3 %collective-permute-start.27 = (bf16[32,2048]{1,0:T(8,128)(2,1)S(1)}, bf16[32,2048]{1,0:T(8,128)(2,1)S(1)}, u32[]{:S(2)}, u32[]{:S(2)}) collective-permute-start(bf16[32,2048]{1,0:T(8,128)(2,1)S(1)} %shard_map.126.m0), channel_id=1, source_target_pairs={{0,2},{1,3},{2,0},{3,1},{4,6},{5,7},{6,4},{7,5},{8,10},{9,11},{10,... | collective-permute-start | bytes 393224 | tf_op jit(solution)/shard_map/ppermute | solution.py:24
  106.6 1.2 collective-permute-start.26
  107.8 3.0 %shard_map.118 = (bf16[128,512]{1,0:T(8,128)(2,1)S(1)}, bf16[2048,512]{1,0:T(8,128)(2,1)S(1)}, bf16[2048,512]{1,0:T(8,128)(2,1)S(1)}, bf16[512,2048]{1,0:T(8,128)(2,1)S(1)}) custom-call(s32[5]{0:T(128)S(1)} %stack.23.place.refs_1_, bf16[656,512]{1,0:T(8,128)(2,1)S(1)} %pad_maximum_fusion.t0.refs_0_.refs_4_, ...), custom_call_target="tpu_custom_call" | custom-call | flops 268435456 | bytes 10485760 | tf_op jit(solution)/shard_map/pallas_call | solution.py:312
  110.8 0.7 collective-permute-done.27.m2
  111.6 2.0 %shard_map.127 = (bf16[128,512]{1,0:T(8,128)(2,1)S(1)}, bf16[128,512]{1,0:T(8,128)(2,1)S(1)}, bf16[128,512]{1,0:T(8,128)(2,1)S(1)}, bf16[128,512]{1,0:T(8,128)(2,1)S(1)}, bf16[128,512]{1,0:T(8,128)(2,1)S(1)}) custom-call(s32[5]{0:T(128)S(1)} %stack.23.place.refs_1_, s32[2]{0:T(128)S(1)} %copy-done.6, bf16[128,512]{1,0:T(8,128)(2,1)S(1)} %get-tuple-element.17.query, ...), custom_call_target="tpu_custom_call" | custom-call | flops 805306368 | bytes 8388608 | tf_op jit(solution)/shard_map/pallas_call | solution.py:356
  113.7 2.7 %collective-permute-start.29 = (bf16[128,512]{1,0:T(8,128)(2,1)S(1)}, bf16[128,512]{1,0:T(8,128)(2,1)S(1)}, u32[]{:S(2)}, u32[]{:S(2)}) collective-permute-start(bf16[128,512]{1,0:T(8,128)(2,1)S(1)} %get-tuple-element.26), channel_id=1, source_target_pairs={{0,1},{1,2},{2,3},{3,0},{4,5},{5,6},{6,7},{7,4},{8,9},{9,10},{10,1... | collective-permute-start | bytes 393224 | tf_op jit(solution)/shard_map/ppermute | solution.py:24
  116.4 0.7 collective-permute-start.30
  117.1 0.4 collective-permute-start.31
  117.5 2.8 %collective-permute-done.29 = bf16[128,512]{1,0:T(8,128)(2,1)S(1)} collective-permute-done((bf16[128,512]{1,0:T(8,128)(2,1)S(1)}, bf16[128,512]{1,0:T(8,128)(2,1)S(1)}, u32[]{:S(2)}, u32[]{:S(2)}) %collective-permute-start.29) | collective-permute-done | bytes 131104 | tf_op jit(solution)/shard_map/ppermute | solution.py:24
  120.3 2.7 %collective-permute-done.30 = bf16[128,512]{1,0:T(8,128)(2,1)S(1)} collective-permute-done((bf16[128,512]{1,0:T(8,128)(2,1)S(1)}, bf16[128,512]{1,0:T(8,128)(2,1)S(1)}, u32[]{:S(2)}, u32[]{:S(2)}) %collective-permute-start.30) | collective-permute-done | bytes 131104 | tf_op jit(solution)/shard_map/ppermute | solution.py:24
  123.0 1.3 collective-permute-done.31
  124.5 5.0 %collective-permute-done.32 = bf16[128,512]{1,0:T(8,128)(2,1)S(1)} collective-permute-done((bf16[128,512]{1,0:T(8,128)(2,1)S(1)}, bf16[128,512]{1,0:T(8,128)(2,1)S(1)}, u32[]{:S(2)}, u32[]{:S(2)}) %collective-permute-start.32) | collective-permute-done | bytes 131104 | tf_op jit(solution)/shard_map/ppermute | solution.py:24
  129.5 0.7 pad_maximum_fusion.2
  (73 shorter events, 2.1 us)
Async XLA Ops:
  0.0 15.6 %copy-start.7 = (bf16[1,2,128,512]{3,2,1,0:T(8,128)(2,1)S(1)}, bf16[1,2,128,512]{3,2,1,0:T(8,128)(2,1)}, u32[]{:S(2)}) copy-start(bf16[1,2,128,512]{3,2,1,0:T(8,128)(2,1)} %param.12) | copy-start | bytes 786436
  1.9 19.4 %copy-start.10 = (bf16[512]{0:T(512)(128)(2,1)S(1)}, bf16[512]{0:T(512)(128)(2,1)}, u32[]{:S(2)}) copy-start(bf16[512]{0:T(512)(128)(2,1)} %param.18) | copy-start | bytes 3076
  1.9 8.2 %collective-permute-start.7 = (bf16[192,512]{1,0:T(8,128)(2,1)S(1)}, bf16[192,512]{1,0:T(8,128)(2,1)S(1)}, u32[]{:S(2)}, u32[]{:S(2)}) collective-permute-start(bf16[192,512]{1,0:T(8,128)(2,1)S(1)} %pad_maximum_fusion.3), channel_id=1, source_target_pairs={{0,8},{8,0},{1,9},{9,1},{2,10},{10,2},{3,11},{11,3},{4,12},{12,4},... | collective-permute-start | bytes 589832 | tf_op jit(solution)/shard_map/ppermute | solution.py:24
  2.1 10.1 %collective-permute-start.14 = (bf16[192,512]{1,0:T(8,128)(2,1)S(1)}, bf16[192,512]{1,0:T(8,128)(2,1)S(1)}, u32[]{:S(2)}, u32[]{:S(2)}) collective-permute-start(bf16[192,512]{1,0:T(8,128)(2,1)S(1)} %pad_maximum_fusion.4), channel_id=1, source_target_pairs={{0,132},{4,128},{128,4},{132,0},{1,133},{5,129},{129,5},{133,1},{2... | collective-permute-start | bytes 589832 | tf_op jit(solution)/shard_map/ppermute | solution.py:24
  5.2 10.4 %collective-permute-start = (bf16[256,512]{1,0:T(8,128)(2,1)}, bf16[256,512]{1,0:T(8,128)(2,1)S(1)}, u32[]{:S(2)}, u32[]{:S(2)}) collective-permute-start(bf16[256,512]{1,0:T(8,128)(2,1)} %bitcast.14), channel_id=1, source_target_pairs={{0,4},{4,0},{1,5},{5,1},{2,6},{6,2},{3,7},{7,3},{8,12},{12,8},{9,1... | collective-permute-start | bytes 786440 | tf_op jit(solution)/shard_map/ppermute | solution.py:24
  5.3 13.9 %collective-permute-start.1 = (bf16[256,512]{1,0:T(8,128)(2,1)}, bf16[256,512]{1,0:T(8,128)(2,1)S(1)}, u32[]{:S(2)}, u32[]{:S(2)}) collective-permute-start(bf16[256,512]{1,0:T(8,128)(2,1)} %bitcast.15), channel_id=1, source_target_pairs={{0,128},{128,0},{1,129},{129,1},{2,130},{130,2},{3,131},{131,3},{8... | collective-permute-start | bytes 786440 | tf_op jit(solution)/shard_map/ppermute | solution.py:24
  8.8 10.5 %collective-permute-start.2 = (bf16[256,512]{1,0:T(8,128)(2,1)}, bf16[256,512]{1,0:T(8,128)(2,1)S(1)}, u32[]{:S(2)}, u32[]{:S(2)}) collective-permute-start(bf16[256,512]{1,0:T(8,128)(2,1)} %bitcast.16), channel_id=1, source_target_pairs={{0,132},{128,4},{1,133},{129,5},{2,134},{130,6},{3,135},{131,7},{8... | collective-permute-start | bytes 786440 | tf_op jit(solution)/shard_map/ppermute | solution.py:24
  10.1 13.4 %collective-permute-start.8 = (bf16[384,512]{1,0:T(8,128)(2,1)S(1)}, bf16[384,512]{1,0:T(8,128)(2,1)S(1)}, u32[]{:S(2)}, u32[]{:S(2)}) collective-permute-start(bf16[384,512]{1,0:T(8,128)(2,1)S(1)} %pad_maximum_fusion.1.refs_9_.refs_0_), channel_id=1, source_target_pairs={{0,16},{8,120},{16,32},{24,8},{32,48},{40,24},{48,64},{56,40},{64,... | collective-permute-start | bytes 1179656 | tf_op jit(solution)/shard_map/ppermute | solution.py:24
  12.1 7.2 %collective-permute-start.15 = (bf16[192,512]{1,0:T(8,128)(2,1)S(1)}, bf16[192,512]{1,0:T(8,128)(2,1)S(1)}, u32[]{:S(2)}, u32[]{:S(2)}) collective-permute-start(bf16[192,512]{1,0:T(8,128)(2,1)S(1)} %collective-permute-done.14), channel_id=1, source_target_pairs={{0,8},{8,0},{1,9},{9,1},{2,10},{10,2},{3,11},{11,3},{4,12},{12,4},... | collective-permute-start | bytes 589832 | tf_op jit(solution)/shard_map/ppermute | solution.py:24
  15.7 17.0 %copy-start.8 = (bf16[2048]{0:T(1024)(128)(2,1)S(1)}, bf16[2048]{0:T(1024)(128)(2,1)}, u32[]{:S(2)}) copy-start(bf16[2048]{0:T(1024)(128)(2,1)} %param.14) | copy-start | bytes 12292
  15.7 17.0 %copy-start.9 = (bf16[2048]{0:T(1024)(128)(2,1)S(1)}, bf16[2048]{0:T(1024)(128)(2,1)}, u32[]{:S(2)}) copy-start(bf16[2048]{0:T(1024)(128)(2,1)} %param.19) | copy-start | bytes 12292
  19.2 2.2 %copy-start.4 = (bf16[256,512]{1,0:T(8,128)(2,1)}, bf16[256,512]{1,0:T(8,128)(2,1)S(1)}, u32[]{:S(2)}) copy-start(bf16[256,512]{1,0:T(8,128)(2,1)S(1)} %collective-permute-done.2.refs_3_) | copy-start | bytes 786436
  19.3 11.8 %copy-start = (bf16[384,512]{1,0:T(8,128)(2,1)}, bf16[384,512]{1,0:T(8,128)(2,1)S(1)}, u32[]{:S(2)}) copy-start(bf16[384,512]{1,0:T(8,128)(2,1)S(1)} %constant_dynamic-update-slice_fusion.refs_16_.refs_9_) | copy-start | bytes 1179652
  19.3 11.8 %collective-permute-start.16 = (bf16[384,512]{1,0:T(8,128)(2,1)S(1)}, bf16[384,512]{1,0:T(8,128)(2,1)}, u32[]{:S(2)}, u32[]{:S(2)}) collective-permute-start(bf16[384,512]{1,0:T(8,128)(2,1)S(1)} %constant_dynamic-update-slice_fusion.refs_16_.refs_9_), channel_id=1, source_target_pairs={{0,16},{8,120},{16,32},{24,8},{32,48},{40,24},{48,64},{56,40},{64,... | collective-permute-start | bytes 1179656 | tf_op jit(solution)/shard_map/ppermute | solution.py:24
  21.4 15.7 %collective-permute-start.3 = (bf16[656,512]{1,0:T(8,128)(2,1)S(1)}, bf16[656,512]{1,0:T(8,128)(2,1)S(1)}, u32[]{:S(2)}, u32[]{:S(2)}) collective-permute-start(bf16[656,512]{1,0:T(8,128)(2,1)S(1)} %pad_maximum_fusion.t0.refs_0_.refs_4_), channel_id=1, source_target_pairs={{0,1},{1,2},{2,3},{3,0},{4,5},{5,6},{6,7},{7,4},{8,9},{9,10},{10,1... | collective-permute-start | bytes 2015240 | tf_op jit(solution)/shard_map/ppermute | solution.py:24
  22.0 18.5 %collective-permute-start.4 = (bf16[656,512]{1,0:T(8,128)(2,1)S(1)}, bf16[656,512]{1,0:T(8,128)(2,1)S(1)}, u32[]{:S(2)}, u32[]{:S(2)}) collective-permute-start(bf16[656,512]{1,0:T(8,128)(2,1)S(1)} %pad_maximum_fusion.t0.refs_0_.refs_4_), channel_id=1, source_target_pairs={{0,3},{1,0},{2,1},{3,2},{4,7},{5,4},{6,5},{7,6},{8,11},{9,8},{10,9... | collective-permute-start | bytes 2015240 | tf_op jit(solution)/shard_map/ppermute | solution.py:24
  23.5 1.0 copy-start.5
  24.5 10.8 %collective-permute-start.9 = (bf16[384,512]{1,0:T(8,128)(2,1)S(1)}, bf16[384,512]{1,0:T(8,128)(2,1)S(1)}, u32[]{:S(2)}, u32[]{:S(2)}) collective-permute-start(bf16[384,512]{1,0:T(8,128)(2,1)S(1)} %shard_map.119.refs_10_.refs_1_), channel_id=1, source_target_pairs={{0,16},{8,120},{16,32},{24,8},{32,48},{40,24},{48,64},{56,40},{64,... | collective-permute-start | bytes 1179656 | tf_op jit(solution)/shard_map/ppermute | solution.py:24
  31.1 9.3 %collective-permute-start.17 = (bf16[384,512]{1,0:T(8,128)(2,1)}, bf16[384,512]{1,0:T(8,128)(2,1)}, u32[]{:S(2)}, u32[]{:S(2)}) collective-permute-start(bf16[384,512]{1,0:T(8,128)(2,1)} %collective-permute-done.16.refs_17_.refs_10_), channel_id=1, source_target_pairs={{0,16},{8,120},{16,32},{24,8},{32,48},{40,24},{48,64},{56,40},{64,... | collective-permute-start | bytes 1179656 | tf_op jit(solution)/shard_map/ppermute | solution.py:24
  31.1 10.3 %collective-permute-start.11 = (bf16[384,512]{1,0:T(8,128)(2,1)S(1)}, bf16[384,512]{1,0:T(8,128)(2,1)}, u32[]{:S(2)}, u32[]{:S(2)}) collective-permute-start(bf16[384,512]{1,0:T(8,128)(2,1)S(1)} %shard_map.119.refs_10_.refs_1_), channel_id=1, source_target_pairs={{0,8},{8,0},{1,9},{9,1},{2,10},{10,2},{3,11},{11,3},{4,12},{12,4},... | collective-permute-start | bytes 1179656 | tf_op jit(solution)/shard_map/ppermute | solution.py:24
  35.2 20.6 %copy-start.1 = (bf16[384,512]{1,0:T(8,128)(2,1)S(1)}, bf16[384,512]{1,0:T(8,128)(2,1)}, u32[]{:S(2)}) copy-start(bf16[384,512]{1,0:T(8,128)(2,1)} %copy-done) | copy-start | bytes 1179652
  35.2 9.3 %collective-permute-start.10 = (bf16[384,512]{1,0:T(8,128)(2,1)S(1)}, bf16[384,512]{1,0:T(8,128)(2,1)S(1)}, u32[]{:S(2)}, u32[]{:S(2)}) collective-permute-start(bf16[384,512]{1,0:T(8,128)(2,1)S(1)} %shard_map.120.refs_11_.refs_2_), channel_id=1, source_target_pairs={{0,16},{8,120},{16,32},{24,8},{32,48},{40,24},{48,64},{56,40},{64,... | collective-permute-start | bytes 1179656 | tf_op jit(solution)/shard_map/ppermute | solution.py:24
  37.1 7.7 %collective-permute-start.19 = (bf16[384,512]{1,0:T(8,128)(2,1)}, bf16[384,512]{1,0:T(8,128)(2,1)S(1)}, u32[]{:S(2)}, u32[]{:S(2)}) collective-permute-start(bf16[384,512]{1,0:T(8,128)(2,1)} %collective-permute-done.16.refs_17_.refs_10_), channel_id=1, source_target_pairs={{0,8},{8,0},{1,9},{9,1},{2,10},{10,2},{3,11},{11,3},{4,12},{12,4},... | collective-permute-start | bytes 1179656 | tf_op jit(solution)/shard_map/ppermute | solution.py:24
  40.4 9.4 %collective-permute-start.18 = (bf16[384,512]{1,0:T(8,128)(2,1)}, bf16[384,512]{1,0:T(8,128)(2,1)S(1)}, u32[]{:S(2)}, u32[]{:S(2)}) collective-permute-start(bf16[384,512]{1,0:T(8,128)(2,1)} %collective-permute-done.17.refs_18_.refs_11_), channel_id=1, source_target_pairs={{0,16},{8,120},{16,32},{24,8},{32,48},{40,24},{48,64},{56,40},{64,... | collective-permute-start | bytes 1179656 | tf_op jit(solution)/shard_map/ppermute | solution.py:24
  40.5 7.7 %collective-permute-start.6 = (bf16[256,512]{1,0:T(8,128)(2,1)S(1)}, bf16[256,512]{1,0:T(8,128)(2,1)S(1)}, u32[]{:S(2)}, u32[]{:S(2)}) collective-permute-start(bf16[256,512]{1,0:T(8,128)(2,1)S(1)} %slice.30), channel_id=1, source_target_pairs={{0,1},{1,2},{2,3},{3,0},{4,5},{5,6},{6,7},{7,4},{8,9},{9,10},{10,1... | collective-permute-start | bytes 786440 | tf_op jit(solution)/shard_map/ppermute | solution.py:24
  41.4 11.5 %collective-permute-start.5 = (bf16[400,512]{1,0:T(8,128)(2,1)S(1)}, bf16[400,512]{1,0:T(8,128)(2,1)S(1)}, u32[]{:S(2)}, u32[]{:S(2)}) collective-permute-start(bf16[400,512]{1,0:T(8,128)(2,1)S(1)} %slice.29), channel_id=1, source_target_pairs={{0,3},{1,0},{2,1},{3,2},{4,7},{5,4},{6,5},{7,6},{8,11},{9,8},{10,9... | collective-permute-start | bytes 1228808 | tf_op jit(solution)/shard_map/ppermute | solution.py:24
  44.5 11.0 %collective-permute-start.12 = (bf16[384,512]{1,0:T(8,128)(2,1)S(1)}, bf16[384,512]{1,0:T(8,128)(2,1)S(1)}, u32[]{:S(2)}, u32[]{:S(2)}) collective-permute-start(bf16[384,512]{1,0:T(8,128)(2,1)S(1)} %shard_map.120.refs_11_.refs_2_), channel_id=1, source_target_pairs={{0,8},{8,0},{1,9},{9,1},{2,10},{10,2},{3,11},{11,3},{4,12},{12,4},... | collective-permute-start | bytes 1179656 | tf_op jit(solution)/shard_map/ppermute | solution.py:24
  44.8 11.0 %collective-permute-start.20 = (bf16[384,512]{1,0:T(8,128)(2,1)}, bf16[384,512]{1,0:T(8,128)(2,1)S(1)}, u32[]{:S(2)}, u32[]{:S(2)}) collective-permute-start(bf16[384,512]{1,0:T(8,128)(2,1)} %collective-permute-done.17.refs_18_.refs_11_), channel_id=1, source_target_pairs={{0,8},{8,0},{1,9},{9,1},{2,10},{10,2},{3,11},{11,3},{4,12},{12,4},... | collective-permute-start | bytes 1179656 | tf_op jit(solution)/shard_map/ppermute | solution.py:24
  48.2 7.7 %collective-permute-start.13 = (bf16[384,512]{1,0:T(8,128)(2,1)S(1)}, bf16[384,512]{1,0:T(8,128)(2,1)S(1)}, u32[]{:S(2)}, u32[]{:S(2)}) collective-permute-start(bf16[384,512]{1,0:T(8,128)(2,1)S(1)} %shard_map.121.refs_12_.refs_3_), channel_id=1, source_target_pairs={{0,8},{8,0},{1,9},{9,1},{2,10},{10,2},{3,11},{11,3},{4,12},{12,4},... | collective-permute-start | bytes 1179656 | tf_op jit(solution)/shard_map/ppermute | solution.py:24
  49.8 6.0 %collective-permute-start.21 = (bf16[384,512]{1,0:T(8,128)(2,1)S(1)}, bf16[384,512]{1,0:T(8,128)(2,1)S(1)}, u32[]{:S(2)}, u32[]{:S(2)}) collective-permute-start(bf16[384,512]{1,0:T(8,128)(2,1)S(1)} %collective-permute-done.18.refs_19_.refs_12_), channel_id=1, source_target_pairs={{0,8},{8,0},{1,9},{9,1},{2,10},{10,2},{3,11},{11,3},{4,12},{12,4},... | collective-permute-start | bytes 1179656 | tf_op jit(solution)/shard_map/ppermute | solution.py:24
  52.9 8.9 %collective-permute-start.22 = (bf16[192,512]{1,0:T(8,128)(2,1)S(1)}, bf16[192,512]{1,0:T(8,128)(2,1)S(1)}, u32[]{:S(2)}, u32[]{:S(2)}) collective-permute-start(bf16[192,512]{1,0:T(8,128)(2,1)S(1)} %slice.31), channel_id=1, source_target_pairs={{0,16},{8,120},{16,32},{24,8},{32,48},{40,24},{48,64},{56,40},{64,... | collective-permute-start | bytes 589832 | tf_op jit(solution)/shard_map/ppermute | solution.py:24
  55.6 8.3 %collective-permute-start.24 = (bf16[192,512]{1,0:T(8,128)(2,1)S(1)}, bf16[192,512]{1,0:T(8,128)(2,1)S(1)}, u32[]{:S(2)}, u32[]{:S(2)}) collective-permute-start(bf16[192,512]{1,0:T(8,128)(2,1)S(1)} %slice.32), channel_id=1, source_target_pairs={{0,16},{8,120},{16,32},{24,8},{32,48},{40,24},{48,64},{56,40},{64,... | collective-permute-start | bytes 589832 | tf_op jit(solution)/shard_map/ppermute | solution.py:24
  61.8 2.4 %collective-permute-start.23 = (bf16[192,512]{1,0:T(8,128)(2,1)S(1)}, bf16[192,512]{1,0:T(8,128)(2,1)S(1)}, u32[]{:S(2)}, u32[]{:S(2)}) collective-permute-start(bf16[192,512]{1,0:T(8,128)(2,1)S(1)} %shard_map.123.refs_4_), channel_id=1, source_target_pairs={{0,8},{8,0},{1,9},{9,1},{2,10},{10,2},{3,11},{11,3},{4,12},{12,4},... | collective-permute-start | bytes 589832 | tf_op jit(solution)/shard_map/ppermute | solution.py:24
  63.9 1.4 %collective-permute-start.25 = (bf16[192,512]{1,0:T(8,128)(2,1)S(1)}, bf16[192,512]{1,0:T(8,128)(2,1)S(1)}, u32[]{:S(2)}, u32[]{:S(2)}) collective-permute-start(bf16[192,512]{1,0:T(8,128)(2,1)S(1)} %shard_map.124.refs_13_), channel_id=1, source_target_pairs={{0,8},{8,0},{1,9},{9,1},{2,10},{10,2},{3,11},{11,3},{4,12},{12,4},... | collective-permute-start | bytes 589832 | tf_op jit(solution)/shard_map/ppermute | solution.py:24
  101.4 6.4 %copy-start.2 = (bf16[2048,512]{1,0:T(8,128)(2,1)S(1)}, bf16[2048,512]{1,0:T(8,128)(2,1)}, u32[]{:S(2)}) copy-start(bf16[2048,512]{1,0:T(8,128)(2,1)} %weight.1) | copy-start | bytes 6291460
  101.4 6.4 %copy-start.3 = (bf16[2048,512]{1,0:T(8,128)(2,1)S(1)}, bf16[2048,512]{1,0:T(8,128)(2,1)}, u32[]{:S(2)}) copy-start(bf16[2048,512]{1,0:T(8,128)(2,1)} %wk.1) | copy-start | bytes 6291460
  102.4 9.3 %copy-start.6 = (s32[2]{0:T(128)S(1)}, s32[2]{0:T(128)}, u32[]{:S(2)}) copy-start(s32[2]{0:T(128)} %lengths.1) | copy-start | bytes 28
  102.4 8.4 %collective-permute-start.28 = (bf16[32,2048]{1,0:T(8,128)(2,1)S(1)}, bf16[32,2048]{1,0:T(8,128)(2,1)S(1)}, u32[]{:S(2)}, u32[]{:S(2)}) collective-permute-start(bf16[32,2048]{1,0:T(8,128)(2,1)S(1)} %shard_map.126.m0), channel_id=1, source_target_pairs={{0,3},{1,0},{2,1},{3,2},{4,7},{5,4},{6,5},{7,6},{8,11},{9,8},{10,9... | collective-permute-start | bytes 393224 | tf_op jit(solution)/shard_map/ppermute | solution.py:24
  103.3 8.3 %collective-permute-start.27 = (bf16[32,2048]{1,0:T(8,128)(2,1)S(1)}, bf16[32,2048]{1,0:T(8,128)(2,1)S(1)}, u32[]{:S(2)}, u32[]{:S(2)}) collective-permute-start(bf16[32,2048]{1,0:T(8,128)(2,1)S(1)} %shard_map.126.m0), channel_id=1, source_target_pairs={{0,2},{1,3},{2,0},{3,1},{4,6},{5,7},{6,4},{7,5},{8,10},{9,11},{10,... | collective-permute-start | bytes 393224 | tf_op jit(solution)/shard_map/ppermute | solution.py:24
  106.6 5.0 %collective-permute-start.26 = (bf16[32,2048]{1,0:T(8,128)(2,1)S(1)}, bf16[32,2048]{1,0:T(8,128)(2,1)S(1)}, u32[]{:S(2)}, u32[]{:S(2)}) collective-permute-start(bf16[32,2048]{1,0:T(8,128)(2,1)S(1)} %shard_map.126.m0), channel_id=1, source_target_pairs={{0,1},{1,2},{2,3},{3,0},{4,5},{5,6},{6,7},{7,4},{8,9},{9,10},{10,1... | collective-permute-start | bytes 393224 | tf_op jit(solution)/shard_map/ppermute | solution.py:24
  113.7 6.7 %collective-permute-start.29 = (bf16[128,512]{1,0:T(8,128)(2,1)S(1)}, bf16[128,512]{1,0:T(8,128)(2,1)S(1)}, u32[]{:S(2)}, u32[]{:S(2)}) collective-permute-start(bf16[128,512]{1,0:T(8,128)(2,1)S(1)} %get-tuple-element.26), channel_id=1, source_target_pairs={{0,1},{1,2},{2,3},{3,0},{4,5},{5,6},{6,7},{7,4},{8,9},{9,10},{10,1... | collective-permute-start | bytes 393224 | tf_op jit(solution)/shard_map/ppermute | solution.py:24
  116.4 6.6 %collective-permute-start.30 = (bf16[128,512]{1,0:T(8,128)(2,1)S(1)}, bf16[128,512]{1,0:T(8,128)(2,1)S(1)}, u32[]{:S(2)}, u32[]{:S(2)}) collective-permute-start(bf16[128,512]{1,0:T(8,128)(2,1)S(1)} %get-tuple-element.27), channel_id=1, source_target_pairs={{0,2},{1,3},{2,0},{3,1},{4,6},{5,7},{6,4},{7,5},{8,10},{9,11},{10,... | collective-permute-start | bytes 393224 | tf_op jit(solution)/shard_map/ppermute | solution.py:24
  117.1 7.2 %collective-permute-start.31 = (bf16[128,512]{1,0:T(8,128)(2,1)S(1)}, bf16[128,512]{1,0:T(8,128)(2,1)S(1)}, u32[]{:S(2)}, u32[]{:S(2)}) collective-permute-start(bf16[128,512]{1,0:T(8,128)(2,1)S(1)} %get-tuple-element.28), channel_id=1, source_target_pairs={{0,3},{1,0},{2,1},{3,2},{4,7},{5,4},{6,5},{7,6},{8,11},{9,8},{10,9... | collective-permute-start | bytes 393224 | tf_op jit(solution)/shard_map/ppermute | solution.py:24
  124.4 5.1 %collective-permute-start.32 = (bf16[128,512]{1,0:T(8,128)(2,1)S(1)}, bf16[128,512]{1,0:T(8,128)(2,1)S(1)}, u32[]{:S(2)}, u32[]{:S(2)}) collective-permute-start(bf16[128,512]{1,0:T(8,128)(2,1)S(1)} %get-tuple-element.29), channel_id=1, source_target_pairs={{0,4},{4,0},{1,5},{5,1},{2,6},{6,2},{3,7},{7,3},{8,12},{12,8},{9,1... | collective-permute-start | bytes 393224 | tf_op jit(solution)/shard_map/ppermute | solution.py:24

commit v8 on v7

--- a/solution.py
+++ b/solution.py
@@ -396,7 +396,7 @@
     mine = jnp.where(p == 0, local, swapped)
     across = moved(local, ("yh", "p"), lambda a, b: (1 - a, 0) if b == 0 else None)
     corner = moved(local, ("yh", "p"), lambda a, b: (1 - a, 1) if b == 0 else None)
-    theirs = jnp.where(p == 0, across, corner)
+    theirs = after(jnp.where(p == 0, across, corner), far)
     decoding = jnp.where(p == 0, swapped[:128], local[128:])
     gain_rows = jnp.broadcast_to(final_gain[None], (16, 512))
     tokens = around(jnp.concatenate([mine, theirs, decoding, gain_rows]), 256)

time: 130 us -> 130 us (level)
  waiting for transfers between devices: 37.1 us -> 34.4 us
    ppermute x33, waiting for transfers between devices: 37.1 us -> 34.4 us  [moved(): return lax.ppermute(value, axes, pairs)]
  transfers between devices with their start and end apart: 33 -> 33, of which waited for: 18 -> 16; matrix products, arithmetic and copies ran while one was open for 0% -> 0% of each run, Pallas kernels for 6% -> 6%
where the time goes in v8:
time: 130 us
  starting transfers between devices  42.3 us (33%)
  waiting for transfers between devices  34.4 us (26%)
  blocking collectives  31.9 us (25%)
  Pallas kernels  15.5 us (12%)
  local copies, waits for them, and re-layouts  4.05 us (3%)
    ppermute x33, starting transfers between devices, moved(): return lax.ppermute(value, axes, pairs)  42.3 us
    ppermute x33, waiting for transfers between devices, moved(): return lax.ppermute(value, axes, pairs)  34.4 us
    all_to_all x1, blocking collectives, shards(): terms = lax.all_to_all(terms, ('yh', 'p', 'x'), 0, 0)  31.9 us
    pallas_call x1, Pallas kernels, ffn(): pl.pallas_call(first_kernel, grid_spec=grid_spec, out_shape=[jax.ShapeDty...  5.12 us
    pallas_call x1, Pallas kernels, ffn(): pl.pallas_call(second_kernel, grid_spec=grid_spec, out_shape=jax.ShapeDty...  4.4 us
    pallas_call x1, Pallas kernels, query_rows(): pl.pallas_call(query_kernel, grid_spec=grid_spec, out_shape=[jax.ShapeDty...  2.99 us
  transfers between devices with their start and end apart: 33, of which 16 were waited for; matrix products, arithmetic and copies ran while one was open for 0% of the time, Pallas kernels for 6%

profile of v8, /device:TPU:6, one launch (start us, length us, event | category | flops | bytes accessed | tf_op | source)
XLA Modules:
  0.0 129.6 jit_solution(12158279614701240543)
XLA Ops:
  0.0 0.9 dynamic-slice_bitcast_fusion
  0.9 1.0 constant_dynamic-slice_fusion
  2.0 3.1 %collective-permute-start.3 = (bf16[192,512]{1,0:T(8,128)(2,1)S(1)}, bf16[192,512]{1,0:T(8,128)(2,1)S(1)}, u32[]{:S(2)}, u32[]{:S(2)}) collective-permute-start(bf16[192,512]{1,0:T(8,128)(2,1)S(1)} %pad_maximum_fusion.3), channel_id=1, source_target_pairs={{0,132},{4,128},{128,4},{132,0},{1,133},{5,129},{129,5},{133,1},{2... | collective-permute-start | bytes 589832 | tf_op jit(solution)/shard_map/ppermute | solution.py:24
  5.3 3.5 %collective-permute-start.1 = (bf16[256,512]{1,0:T(8,128)(2,1)}, bf16[256,512]{1,0:T(8,128)(2,1)S(1)}, u32[]{:S(2)}, u32[]{:S(2)}) collective-permute-start(bf16[256,512]{1,0:T(8,128)(2,1)} %bitcast.15), channel_id=1, source_target_pairs={{0,128},{128,0},{1,129},{129,1},{2,130},{130,2},{3,131},{131,3},{8... | collective-permute-start | bytes 786440 | tf_op jit(solution)/shard_map/ppermute | solution.py:24
  8.8 1.3 %collective-permute-start.2 = (bf16[256,512]{1,0:T(8,128)(2,1)}, bf16[256,512]{1,0:T(8,128)(2,1)S(1)}, u32[]{:S(2)}, u32[]{:S(2)}) collective-permute-start(bf16[256,512]{1,0:T(8,128)(2,1)} %bitcast.16), channel_id=1, source_target_pairs={{0,132},{128,4},{1,133},{129,5},{2,134},{130,6},{3,135},{131,7},{8... | collective-permute-start | bytes 786440 | tf_op jit(solution)/shard_map/ppermute | solution.py:24
  10.1 2.0 %collective-permute-start.10 = (bf16[384,512]{1,0:T(8,128)(2,1)S(1)}, bf16[384,512]{1,0:T(8,128)(2,1)S(1)}, u32[]{:S(2)}, u32[]{:S(2)}) collective-permute-start(bf16[384,512]{1,0:T(8,128)(2,1)S(1)} %pad_maximum_fusion.1.refs_9_.refs_0_), channel_id=1, source_target_pairs={{0,16},{8,120},{16,32},{24,8},{32,48},{40,24},{48,64},{56,40},{64,... | collective-permute-start | bytes 1179656 | tf_op jit(solution)/shard_map/ppermute | solution.py:24
  12.1 3.5 %collective-permute-start.4 = (bf16[192,512]{1,0:T(8,128)(2,1)S(1)}, bf16[192,512]{1,0:T(8,128)(2,1)S(1)}, u32[]{:S(2)}, u32[]{:S(2)}) collective-permute-start(bf16[192,512]{1,0:T(8,128)(2,1)S(1)} %collective-permute-done.3), channel_id=1, source_target_pairs={{0,8},{8,0},{1,9},{9,1},{2,10},{10,2},{3,11},{11,3},{4,12},{12,4},... | collective-permute-start | bytes 589832 | tf_op jit(solution)/shard_map/ppermute | solution.py:24
  15.7 3.5 %collective-permute-done.1.refs_2_ = bf16[256,512]{1,0:T(8,128)(2,1)S(1)} collective-permute-done((bf16[256,512]{1,0:T(8,128)(2,1)}, bf16[256,512]{1,0:T(8,128)(2,1)S(1)}, u32[]{:S(2)}, u32[]{:S(2)}) %collective-permute-start.1) | collective-permute-done | bytes 262176 | tf_op jit(solution)/shard_map/ppermute | solution.py:24
  19.3 2.0 %collective-permute-start.16 = (bf16[384,512]{1,0:T(8,128)(2,1)S(1)}, bf16[384,512]{1,0:T(8,128)(2,1)}, u32[]{:S(2)}, u32[]{:S(2)}) collective-permute-start(bf16[384,512]{1,0:T(8,128)(2,1)S(1)} %constant_dynamic-update-slice_fusion.refs_1_.refs_16_.refs_9_), channel_id=1, source_target_pairs={{0,16},{8,120},{16,32},{24,8},{32,48},{40,24},{48,64},{56,40},{64,... | collective-permute-start | bytes 1179656 | tf_op jit(solution)/shard_map/ppermute | solution.py:24
  21.4 0.7 collective-permute-start.5
  22.1 1.4 %collective-permute-start.6 = (bf16[656,512]{1,0:T(8,128)(2,1)S(1)}, bf16[656,512]{1,0:T(8,128)(2,1)S(1)}, u32[]{:S(2)}, u32[]{:S(2)}) collective-permute-start(bf16[656,512]{1,0:T(8,128)(2,1)S(1)} %pad_maximum_fusion.t0.refs_0_.refs_4_), channel_id=1, source_target_pairs={{0,3},{1,0},{2,1},{3,2},{4,7},{5,4},{6,5},{7,6},{8,11},{9,8},{10,9... | collective-permute-start | bytes 2015240 | tf_op jit(solution)/shard_map/ppermute | solution.py:24
  23.5 0.9 copy-done.3
  24.5 0.9 copy-done.5
  25.4 1.9 %collective-permute-start.11 = (bf16[384,512]{1,0:T(8,128)(2,1)S(1)}, bf16[384,512]{1,0:T(8,128)(2,1)}, u32[]{:S(2)}, u32[]{:S(2)}) collective-permute-start(bf16[384,512]{1,0:T(8,128)(2,1)S(1)} %shard_map.120.refs_10_.refs_1_), channel_id=1, source_target_pairs={{0,16},{8,120},{16,32},{24,8},{32,48},{40,24},{48,64},{56,40},{64,... | collective-permute-start | bytes 1179656 | tf_op jit(solution)/shard_map/ppermute | solution.py:24
  27.4 3.8 %collective-permute-done.16.refs_17_.refs_10_ = bf16[384,512]{1,0:T(8,128)(2,1)} collective-permute-done((bf16[384,512]{1,0:T(8,128)(2,1)S(1)}, bf16[384,512]{1,0:T(8,128)(2,1)}, u32[]{:S(2)}, u32[]{:S(2)}) %collective-permute-start.16) | collective-permute-done | bytes 393248 | tf_op jit(solution)/shard_map/ppermute | solution.py:24
  31.1 1.5 %collective-permute-start.13 = (bf16[384,512]{1,0:T(8,128)(2,1)S(1)}, bf16[384,512]{1,0:T(8,128)(2,1)}, u32[]{:S(2)}, u32[]{:S(2)}) collective-permute-start(bf16[384,512]{1,0:T(8,128)(2,1)S(1)} %shard_map.120.refs_10_.refs_1_), channel_id=1, source_target_pairs={{0,8},{8,0},{1,9},{9,1},{2,10},{10,2},{3,11},{11,3},{4,12},{12,4},... | collective-permute-start | bytes 1179656 | tf_op jit(solution)/shard_map/ppermute | solution.py:24
  32.8 2.9 %collective-permute-done.11.refs_0_ = bf16[384,512]{1,0:T(8,128)(2,1)} collective-permute-done((bf16[384,512]{1,0:T(8,128)(2,1)S(1)}, bf16[384,512]{1,0:T(8,128)(2,1)}, u32[]{:S(2)}, u32[]{:S(2)}) %collective-permute-start.11) | collective-permute-done | bytes 393248 | tf_op jit(solution)/shard_map/ppermute | solution.py:24
  35.7 1.5 %collective-permute-done.5.t1.refs_1_.refs_5_ = bf16[656,512]{1,0:T(8,128)(2,1)S(1)} collective-permute-done((bf16[656,512]{1,0:T(8,128)(2,1)S(1)}, bf16[656,512]{1,0:T(8,128)(2,1)S(1)}, u32[]{:S(2)}, u32[]{:S(2)}) %collective-permute-start.5) | collective-permute-done | bytes 671776 | tf_op jit(solution)/shard_map/ppermute | solution.py:24
  37.2 2.5 %collective-permute-start.19 = (bf16[384,512]{1,0:T(8,128)(2,1)}, bf16[384,512]{1,0:T(8,128)(2,1)S(1)}, u32[]{:S(2)}, u32[]{:S(2)}) collective-permute-start(bf16[384,512]{1,0:T(8,128)(2,1)} %collective-permute-done.16.refs_17_.refs_10_), channel_id=1, source_target_pairs={{0,8},{8,0},{1,9},{9,1},{2,10},{10,2},{3,11},{11,3},{4,12},{12,4},... | collective-permute-start | bytes 1179656 | tf_op jit(solution)/shard_map/ppermute | solution.py:24
  39.7 0.8 collective-permute-done.17.refs_18_.refs_11_
  40.5 1.2 collective-permute-start.8
  41.7 1.0 collective-permute-start.7
  42.7 2.2 %collective-permute-done.12.refs_0_ = bf16[384,512]{1,0:T(8,128)(2,1)S(1)} collective-permute-done((bf16[384,512]{1,0:T(8,128)(2,1)}, bf16[384,512]{1,0:T(8,128)(2,1)S(1)}, u32[]{:S(2)}, u32[]{:S(2)}) %collective-permute-start.12) | collective-permute-done | bytes 393248 | tf_op jit(solution)/shard_map/ppermute | solution.py:24
  44.9 0.5 collective-permute-start.20
  45.4 2.7 %collective-permute-done.8.refs_2_ = bf16[256,512]{1,0:T(8,128)(2,1)S(1)} collective-permute-done((bf16[256,512]{1,0:T(8,128)(2,1)S(1)}, bf16[256,512]{1,0:T(8,128)(2,1)S(1)}, u32[]{:S(2)}, u32[]{:S(2)}) %collective-permute-start.8) | collective-permute-done | bytes 262176 | tf_op jit(solution)/shard_map/ppermute | solution.py:24
  48.1 1.7 %collective-permute-start.15 = (bf16[384,512]{1,0:T(8,128)(2,1)S(1)}, bf16[384,512]{1,0:T(8,128)(2,1)S(1)}, u32[]{:S(2)}, u32[]{:S(2)}) collective-permute-start(bf16[384,512]{1,0:T(8,128)(2,1)S(1)} %shard_map.122.refs_12_.refs_3_), channel_id=1, source_target_pairs={{0,8},{8,0},{1,9},{9,1},{2,10},{10,2},{3,11},{11,3},{4,12},{12,4},... | collective-permute-start | bytes 1179656 | tf_op jit(solution)/shard_map/ppermute | solution.py:24
  50.4 3.1 %collective-permute-done.7.t2.refs_6_ = bf16[400,512]{1,0:T(8,128)(2,1)S(1)} collective-permute-done((bf16[400,512]{1,0:T(8,128)(2,1)S(1)}, bf16[400,512]{1,0:T(8,128)(2,1)S(1)}, u32[]{:S(2)}, u32[]{:S(2)}) %collective-permute-start.7) | collective-permute-done | bytes 409632 | tf_op jit(solution)/shard_map/ppermute | solution.py:24
  53.5 2.3 %collective-permute-start.24 = (bf16[192,512]{1,0:T(8,128)(2,1)S(1)}, bf16[192,512]{1,0:T(8,128)(2,1)S(1)}, u32[]{:S(2)}, u32[]{:S(2)}) collective-permute-start(bf16[192,512]{1,0:T(8,128)(2,1)S(1)} %slice.32), channel_id=1, source_target_pairs={{0,16},{8,120},{16,32},{24,8},{32,48},{40,24},{48,64},{56,40},{64,... | collective-permute-start | bytes 589832 | tf_op jit(solution)/shard_map/ppermute | solution.py:24
  55.8 5.1 %shard_map.123 = (f32[512,512]{1,0:T(8,128)S(1)}, f32[512,512]{1,0:T(8,128)S(1)}, bf16[2,512,128]{2,1,0:T(8,128)(2,1)S(1)}) custom-call(s32[5]{0:T(128)S(1)} %stack.23.place.refs_1_, bf16[656,512]{1,0:T(8,128)(2,1)S(1)} %pad_maximum_fusion.t0.refs_0_.refs_4_, bf16[656,512]{1,0:T(8,128)(2,1)S(1)} %collective-permute-done.5.t1.refs_1_.refs_5_, ...), custom_call_target="tpu_custom_call" | custom-call | flops 1879048192 | bytes 4194304 | tf_op jit(solution)/shard_map/pallas_call | solution.py:211
  60.9 2.0 %collective-permute-start.23 = (bf16[192,512]{1,0:T(8,128)(2,1)S(1)}, bf16[192,512]{1,0:T(8,128)(2,1)S(1)}, u32[]{:S(2)}, u32[]{:S(2)}) collective-permute-start(bf16[192,512]{1,0:T(8,128)(2,1)S(1)} %shard_map.124.refs_4_), channel_id=1, source_target_pairs={{0,8},{8,0},{1,9},{9,1},{2,10},{10,2},{3,11},{11,3},{4,12},{12,4},... | collective-permute-start | bytes 589832 | tf_op jit(solution)/shard_map/ppermute | solution.py:24
  63.0 0.9 collective-permute-done.23.refs_8_
  64.4 4.4 %shard_map.126 = bf16[16,4,32,512]{3,2,1,0:T(8,128)(2,1)S(1)} custom-call(s32[5]{0:T(128)S(1)} %stack.23.place.refs_1_, f32[512,512]{1,0:T(8,128)S(1)} %get-tuple-element.18.gate, f32[512,512]{1,0:T(8,128)S(1)} %get-tuple-element.19.lift, bf16[2,512,128]{2,1,0:T(8,128)(2,1)S(1)} %get-tuple-element.20.refs_1_.last, ...), custom_call_target="tpu_custom_call" | custom-call | flops 1207959552 | bytes 4194304 | tf_op jit(solution)/shard_map/pallas_call | solution.py:234
  68.8 31.9 %all_to_all.5.terms = bf16[16,4,32,512]{3,2,1,0:T(8,128)(2,1)S(1)} all-to-all(bf16[16,4,32,512]{3,2,1,0:T(8,128)(2,1)S(1)} %shard_map.126), channel_id=1, replica_groups=mesh['yh'=2,'z'=8,'c'=2,'p'=2,'x'=4] {'yh','p','x'}, dimensions={0} | all-to-all | bytes 4194304 | tf_op jit(solution)/shard_map/all_to_all | solution.py:409
  100.7 0.9 shard_map.127.m0
  101.6 0.9 collective-permute-start.28
  102.6 3.3 %collective-permute-start.27 = (bf16[32,2048]{1,0:T(8,128)(2,1)S(1)}, bf16[32,2048]{1,0:T(8,128)(2,1)S(1)}, u32[]{:S(2)}, u32[]{:S(2)}) collective-permute-start(bf16[32,2048]{1,0:T(8,128)(2,1)S(1)} %shard_map.127.m0), channel_id=1, source_target_pairs={{0,2},{1,3},{2,0},{3,1},{4,6},{5,7},{6,4},{7,5},{8,10},{9,11},{10,... | collective-permute-start | bytes 393224 | tf_op jit(solution)/shard_map/ppermute | solution.py:24
  105.9 1.2 collective-permute-start.26
  107.1 3.0 %shard_map.119 = (bf16[128,512]{1,0:T(8,128)(2,1)S(1)}, bf16[2048,512]{1,0:T(8,128)(2,1)S(1)}, bf16[2048,512]{1,0:T(8,128)(2,1)S(1)}, bf16[512,2048]{1,0:T(8,128)(2,1)S(1)}) custom-call(s32[5]{0:T(128)S(1)} %stack.23.place.refs_1_, bf16[656,512]{1,0:T(8,128)(2,1)S(1)} %pad_maximum_fusion.t0.refs_0_.refs_4_, ...), custom_call_target="tpu_custom_call" | custom-call | flops 268435456 | bytes 10485760 | tf_op jit(solution)/shard_map/pallas_call | solution.py:312
  110.1 0.9 collective-permute-done.27.m2
  111.0 2.0 %shard_map.128 = (bf16[128,512]{1,0:T(8,128)(2,1)S(1)}, bf16[128,512]{1,0:T(8,128)(2,1)S(1)}, bf16[128,512]{1,0:T(8,128)(2,1)S(1)}, bf16[128,512]{1,0:T(8,128)(2,1)S(1)}, bf16[128,512]{1,0:T(8,128)(2,1)S(1)}) custom-call(s32[5]{0:T(128)S(1)} %stack.23.place.refs_1_, s32[2]{0:T(128)S(1)} %copy-done.6, bf16[128,512]{1,0:T(8,128)(2,1)S(1)} %get-tuple-element.17.query, ...), custom_call_target="tpu_custom_call" | custom-call | flops 805306368 | bytes 8388608 | tf_op jit(solution)/shard_map/pallas_call | solution.py:356
  113.0 2.7 %collective-permute-start.29 = (bf16[128,512]{1,0:T(8,128)(2,1)S(1)}, bf16[128,512]{1,0:T(8,128)(2,1)S(1)}, u32[]{:S(2)}, u32[]{:S(2)}) collective-permute-start(bf16[128,512]{1,0:T(8,128)(2,1)S(1)} %get-tuple-element.26), channel_id=1, source_target_pairs={{0,1},{1,2},{2,3},{3,0},{4,5},{5,6},{6,7},{7,4},{8,9},{9,10},{10,1... | collective-permute-start | bytes 393224 | tf_op jit(solution)/shard_map/ppermute | solution.py:24
  115.8 0.6 collective-permute-start.30
  116.4 0.6 collective-permute-start.31
  116.9 2.8 %collective-permute-done.29 = bf16[128,512]{1,0:T(8,128)(2,1)S(1)} collective-permute-done((bf16[128,512]{1,0:T(8,128)(2,1)S(1)}, bf16[128,512]{1,0:T(8,128)(2,1)S(1)}, u32[]{:S(2)}, u32[]{:S(2)}) %collective-permute-start.29) | collective-permute-done | bytes 131104 | tf_op jit(solution)/shard_map/ppermute | solution.py:24
  119.7 2.7 %collective-permute-done.30 = bf16[128,512]{1,0:T(8,128)(2,1)S(1)} collective-permute-done((bf16[128,512]{1,0:T(8,128)(2,1)S(1)}, bf16[128,512]{1,0:T(8,128)(2,1)S(1)}, u32[]{:S(2)}, u32[]{:S(2)}) %collective-permute-start.30) | collective-permute-done | bytes 131104 | tf_op jit(solution)/shard_map/ppermute | solution.py:24
  122.4 1.3 %collective-permute-done.31 = bf16[128,512]{1,0:T(8,128)(2,1)S(1)} collective-permute-done((bf16[128,512]{1,0:T(8,128)(2,1)S(1)}, bf16[128,512]{1,0:T(8,128)(2,1)S(1)}, u32[]{:S(2)}, u32[]{:S(2)}) %collective-permute-start.31) | collective-permute-done | bytes 131104 | tf_op jit(solution)/shard_map/ppermute | solution.py:24
  123.9 5.0 %collective-permute-done.32 = bf16[128,512]{1,0:T(8,128)(2,1)S(1)} collective-permute-done((bf16[128,512]{1,0:T(8,128)(2,1)S(1)}, bf16[128,512]{1,0:T(8,128)(2,1)S(1)}, u32[]{:S(2)}, u32[]{:S(2)}) %collective-permute-start.32) | collective-permute-done | bytes 131104 | tf_op jit(solution)/shard_map/ppermute | solution.py:24
  128.9 0.7 pad_maximum_fusion.2
  (78 shorter events, 2.0 us)
Async XLA Ops:
  0.0 15.6 %copy-start.9 = (bf16[1,2,128,512]{3,2,1,0:T(8,128)(2,1)S(1)}, bf16[1,2,128,512]{3,2,1,0:T(8,128)(2,1)}, u32[]{:S(2)}) copy-start(bf16[1,2,128,512]{3,2,1,0:T(8,128)(2,1)} %param.12) | copy-start | bytes 786436
  1.9 8.2 %collective-permute-start.9 = (bf16[192,512]{1,0:T(8,128)(2,1)S(1)}, bf16[192,512]{1,0:T(8,128)(2,1)S(1)}, u32[]{:S(2)}, u32[]{:S(2)}) collective-permute-start(bf16[192,512]{1,0:T(8,128)(2,1)S(1)} %pad_maximum_fusion.4), channel_id=1, source_target_pairs={{0,8},{8,0},{1,9},{9,1},{2,10},{10,2},{3,11},{11,3},{4,12},{12,4},... | collective-permute-start | bytes 589832 | tf_op jit(solution)/shard_map/ppermute | solution.py:24
  2.0 10.1 %collective-permute-start.3 = (bf16[192,512]{1,0:T(8,128)(2,1)S(1)}, bf16[192,512]{1,0:T(8,128)(2,1)S(1)}, u32[]{:S(2)}, u32[]{:S(2)}) collective-permute-start(bf16[192,512]{1,0:T(8,128)(2,1)S(1)} %pad_maximum_fusion.3), channel_id=1, source_target_pairs={{0,132},{4,128},{128,4},{132,0},{1,133},{5,129},{129,5},{133,1},{2... | collective-permute-start | bytes 589832 | tf_op jit(solution)/shard_map/ppermute | solution.py:24
  5.1 10.5 %collective-permute-start = (bf16[256,512]{1,0:T(8,128)(2,1)}, bf16[256,512]{1,0:T(8,128)(2,1)S(1)}, u32[]{:S(2)}, u32[]{:S(2)}) collective-permute-start(bf16[256,512]{1,0:T(8,128)(2,1)} %bitcast.14), channel_id=1, source_target_pairs={{0,4},{4,0},{1,5},{5,1},{2,6},{6,2},{3,7},{7,3},{8,12},{12,8},{9,1... | collective-permute-start | bytes 786440 | tf_op jit(solution)/shard_map/ppermute | solution.py:24
  5.3 13.9 %collective-permute-start.1 = (bf16[256,512]{1,0:T(8,128)(2,1)}, bf16[256,512]{1,0:T(8,128)(2,1)S(1)}, u32[]{:S(2)}, u32[]{:S(2)}) collective-permute-start(bf16[256,512]{1,0:T(8,128)(2,1)} %bitcast.15), channel_id=1, source_target_pairs={{0,128},{128,0},{1,129},{129,1},{2,130},{130,2},{3,131},{131,3},{8... | collective-permute-start | bytes 786440 | tf_op jit(solution)/shard_map/ppermute | solution.py:24
  8.8 10.5 %collective-permute-start.2 = (bf16[256,512]{1,0:T(8,128)(2,1)}, bf16[256,512]{1,0:T(8,128)(2,1)S(1)}, u32[]{:S(2)}, u32[]{:S(2)}) collective-permute-start(bf16[256,512]{1,0:T(8,128)(2,1)} %bitcast.16), channel_id=1, source_target_pairs={{0,132},{128,4},{1,133},{129,5},{2,134},{130,6},{3,135},{131,7},{8... | collective-permute-start | bytes 786440 | tf_op jit(solution)/shard_map/ppermute | solution.py:24
  10.1 11.3 %copy-start.12 = (bf16[512]{0:T(512)(128)(2,1)S(1)}, bf16[512]{0:T(512)(128)(2,1)}, u32[]{:S(2)}) copy-start(bf16[512]{0:T(512)(128)(2,1)} %param.18) | copy-start | bytes 3076
  10.1 13.4 %collective-permute-start.10 = (bf16[384,512]{1,0:T(8,128)(2,1)S(1)}, bf16[384,512]{1,0:T(8,128)(2,1)S(1)}, u32[]{:S(2)}, u32[]{:S(2)}) collective-permute-start(bf16[384,512]{1,0:T(8,128)(2,1)S(1)} %pad_maximum_fusion.1.refs_9_.refs_0_), channel_id=1, source_target_pairs={{0,16},{8,120},{16,32},{24,8},{32,48},{40,24},{48,64},{56,40},{64,... | collective-permute-start | bytes 1179656 | tf_op jit(solution)/shard_map/ppermute | solution.py:24
  12.1 7.2 %collective-permute-start.4 = (bf16[192,512]{1,0:T(8,128)(2,1)S(1)}, bf16[192,512]{1,0:T(8,128)(2,1)S(1)}, u32[]{:S(2)}, u32[]{:S(2)}) collective-permute-start(bf16[192,512]{1,0:T(8,128)(2,1)S(1)} %collective-permute-done.3), channel_id=1, source_target_pairs={{0,8},{8,0},{1,9},{9,1},{2,10},{10,2},{3,11},{11,3},{4,12},{12,4},... | collective-permute-start | bytes 589832 | tf_op jit(solution)/shard_map/ppermute | solution.py:24
  19.2 2.2 %copy-start.2 = (bf16[256,512]{1,0:T(8,128)(2,1)}, bf16[256,512]{1,0:T(8,128)(2,1)S(1)}, u32[]{:S(2)}) copy-start(bf16[256,512]{1,0:T(8,128)(2,1)S(1)} %collective-permute-done.1.refs_2_) | copy-start | bytes 786436
  19.2 2.2 %copy-start.4 = (bf16[256,512]{1,0:T(8,128)(2,1)}, bf16[256,512]{1,0:T(8,128)(2,1)S(1)}, u32[]{:S(2)}) copy-start(bf16[256,512]{1,0:T(8,128)(2,1)S(1)} %collective-permute-done.2.refs_3_) | copy-start | bytes 786436
  19.3 2.1 %copy-start.7 = (bf16[128,512]{1,0:T(8,128)(2,1)}, bf16[128,512]{1,0:T(8,128)(2,1)S(1)}, u32[]{:S(2)}) copy-start(bf16[128,512]{1,0:T(8,128)(2,1)S(1)} %slice_select_fusion) | copy-start | bytes 393220
  19.3 13.4 %copy-start.10 = (bf16[2048]{0:T(1024)(128)(2,1)S(1)}, bf16[2048]{0:T(1024)(128)(2,1)}, u32[]{:S(2)}) copy-start(bf16[2048]{0:T(1024)(128)(2,1)} %param.14) | copy-start | bytes 12292
  19.3 13.4 %copy-start.11 = (bf16[2048]{0:T(1024)(128)(2,1)S(1)}, bf16[2048]{0:T(1024)(128)(2,1)}, u32[]{:S(2)}) copy-start(bf16[2048]{0:T(1024)(128)(2,1)} %param.19) | copy-start | bytes 12292
  19.3 11.8 %collective-permute-start.16 = (bf16[384,512]{1,0:T(8,128)(2,1)S(1)}, bf16[384,512]{1,0:T(8,128)(2,1)}, u32[]{:S(2)}, u32[]{:S(2)}) collective-permute-start(bf16[384,512]{1,0:T(8,128)(2,1)S(1)} %constant_dynamic-update-slice_fusion.refs_1_.refs_16_.refs_9_), channel_id=1, source_target_pairs={{0,16},{8,120},{16,32},{24,8},{32,48},{40,24},{48,64},{56,40},{64,... | collective-permute-start | bytes 1179656 | tf_op jit(solution)/shard_map/ppermute | solution.py:24
  21.4 15.7 %collective-permute-start.5 = (bf16[656,512]{1,0:T(8,128)(2,1)S(1)}, bf16[656,512]{1,0:T(8,128)(2,1)S(1)}, u32[]{:S(2)}, u32[]{:S(2)}) collective-permute-start(bf16[656,512]{1,0:T(8,128)(2,1)S(1)} %pad_maximum_fusion.t0.refs_0_.refs_4_), channel_id=1, source_target_pairs={{0,1},{1,2},{2,3},{3,0},{4,5},{5,6},{6,7},{7,4},{8,9},{9,10},{10,1... | collective-permute-start | bytes 2015240 | tf_op jit(solution)/shard_map/ppermute | solution.py:24
  22.1 18.4 %collective-permute-start.6 = (bf16[656,512]{1,0:T(8,128)(2,1)S(1)}, bf16[656,512]{1,0:T(8,128)(2,1)S(1)}, u32[]{:S(2)}, u32[]{:S(2)}) collective-permute-start(bf16[656,512]{1,0:T(8,128)(2,1)S(1)} %pad_maximum_fusion.t0.refs_0_.refs_4_), channel_id=1, source_target_pairs={{0,3},{1,0},{2,1},{3,2},{4,7},{5,4},{6,5},{7,6},{8,11},{9,8},{10,9... | collective-permute-start | bytes 2015240 | tf_op jit(solution)/shard_map/ppermute | solution.py:24
  23.5 1.0 copy-start.3
  24.5 0.9 copy-start.5
  25.4 10.2 %collective-permute-start.11 = (bf16[384,512]{1,0:T(8,128)(2,1)S(1)}, bf16[384,512]{1,0:T(8,128)(2,1)}, u32[]{:S(2)}, u32[]{:S(2)}) collective-permute-start(bf16[384,512]{1,0:T(8,128)(2,1)S(1)} %shard_map.120.refs_10_.refs_1_), channel_id=1, source_target_pairs={{0,16},{8,120},{16,32},{24,8},{32,48},{40,24},{48,64},{56,40},{64,... | collective-permute-start | bytes 1179656 | tf_op jit(solution)/shard_map/ppermute | solution.py:24
  31.1 9.3 %collective-permute-start.17 = (bf16[384,512]{1,0:T(8,128)(2,1)}, bf16[384,512]{1,0:T(8,128)(2,1)}, u32[]{:S(2)}, u32[]{:S(2)}) collective-permute-start(bf16[384,512]{1,0:T(8,128)(2,1)} %collective-permute-done.16.refs_17_.refs_10_), channel_id=1, source_target_pairs={{0,16},{8,120},{16,32},{24,8},{32,48},{40,24},{48,64},{56,40},{64,... | collective-permute-start | bytes 1179656 | tf_op jit(solution)/shard_map/ppermute | solution.py:24
  31.1 10.6 %collective-permute-start.13 = (bf16[384,512]{1,0:T(8,128)(2,1)S(1)}, bf16[384,512]{1,0:T(8,128)(2,1)}, u32[]{:S(2)}, u32[]{:S(2)}) collective-permute-start(bf16[384,512]{1,0:T(8,128)(2,1)S(1)} %shard_map.120.refs_10_.refs_1_), channel_id=1, source_target_pairs={{0,8},{8,0},{1,9},{9,1},{2,10},{10,2},{3,11},{11,3},{4,12},{12,4},... | collective-permute-start | bytes 1179656 | tf_op jit(solution)/shard_map/ppermute | solution.py:24
  35.7 9.2 %collective-permute-start.12 = (bf16[384,512]{1,0:T(8,128)(2,1)}, bf16[384,512]{1,0:T(8,128)(2,1)S(1)}, u32[]{:S(2)}, u32[]{:S(2)}) collective-permute-start(bf16[384,512]{1,0:T(8,128)(2,1)} %shard_map.121.refs_11_.refs_2_), channel_id=1, source_target_pairs={{0,16},{8,120},{16,32},{24,8},{32,48},{40,24},{48,64},{56,40},{64,... | collective-permute-start | bytes 1179656 | tf_op jit(solution)/shard_map/ppermute | solution.py:24
  37.2 7.7 %collective-permute-start.19 = (bf16[384,512]{1,0:T(8,128)(2,1)}, bf16[384,512]{1,0:T(8,128)(2,1)S(1)}, u32[]{:S(2)}, u32[]{:S(2)}) collective-permute-start(bf16[384,512]{1,0:T(8,128)(2,1)} %collective-permute-done.16.refs_17_.refs_10_), channel_id=1, source_target_pairs={{0,8},{8,0},{1,9},{9,1},{2,10},{10,2},{3,11},{11,3},{4,12},{12,4},... | collective-permute-start | bytes 1179656 | tf_op jit(solution)/shard_map/ppermute | solution.py:24
  40.4 9.4 %collective-permute-start.18 = (bf16[384,512]{1,0:T(8,128)(2,1)}, bf16[384,512]{1,0:T(8,128)(2,1)S(1)}, u32[]{:S(2)}, u32[]{:S(2)}) collective-permute-start(bf16[384,512]{1,0:T(8,128)(2,1)} %collective-permute-done.17.refs_18_.refs_11_), channel_id=1, source_target_pairs={{0,16},{8,120},{16,32},{24,8},{32,48},{40,24},{48,64},{56,40},{64,... | collective-permute-start | bytes 1179656 | tf_op jit(solution)/shard_map/ppermute | solution.py:24
  40.5 7.7 %collective-permute-start.8 = (bf16[256,512]{1,0:T(8,128)(2,1)S(1)}, bf16[256,512]{1,0:T(8,128)(2,1)S(1)}, u32[]{:S(2)}, u32[]{:S(2)}) collective-permute-start(bf16[256,512]{1,0:T(8,128)(2,1)S(1)} %slice.30), channel_id=1, source_target_pairs={{0,1},{1,2},{2,3},{3,0},{4,5},{5,6},{6,7},{7,4},{8,9},{9,10},{10,1... | collective-permute-start | bytes 786440 | tf_op jit(solution)/shard_map/ppermute | solution.py:24
  41.7 11.8 %collective-permute-start.7 = (bf16[400,512]{1,0:T(8,128)(2,1)S(1)}, bf16[400,512]{1,0:T(8,128)(2,1)S(1)}, u32[]{:S(2)}, u32[]{:S(2)}) collective-permute-start(bf16[400,512]{1,0:T(8,128)(2,1)S(1)} %slice.29), channel_id=1, source_target_pairs={{0,3},{1,0},{2,1},{3,2},{4,7},{5,4},{6,5},{7,6},{8,11},{9,8},{10,9... | collective-permute-start | bytes 1228808 | tf_op jit(solution)/shard_map/ppermute | solution.py:24
  44.9 5.0 %collective-permute-start.14 = (bf16[384,512]{1,0:T(8,128)(2,1)}, bf16[384,512]{1,0:T(8,128)(2,1)S(1)}, u32[]{:S(2)}, u32[]{:S(2)}) collective-permute-start(bf16[384,512]{1,0:T(8,128)(2,1)} %shard_map.121.refs_11_.refs_2_), channel_id=1, source_target_pairs={{0,8},{8,0},{1,9},{9,1},{2,10},{10,2},{3,11},{11,3},{4,12},{12,4},... | collective-permute-start | bytes 1179656 | tf_op jit(solution)/shard_map/ppermute | solution.py:24
  44.9 10.9 %collective-permute-start.20 = (bf16[384,512]{1,0:T(8,128)(2,1)}, bf16[384,512]{1,0:T(8,128)(2,1)S(1)}, u32[]{:S(2)}, u32[]{:S(2)}) collective-permute-start(bf16[384,512]{1,0:T(8,128)(2,1)} %collective-permute-done.17.refs_18_.refs_11_), channel_id=1, source_target_pairs={{0,8},{8,0},{1,9},{9,1},{2,10},{10,2},{3,11},{11,3},{4,12},{12,4},... | collective-permute-start | bytes 1179656 | tf_op jit(solution)/shard_map/ppermute | solution.py:24
  48.1 7.6 %collective-permute-start.15 = (bf16[384,512]{1,0:T(8,128)(2,1)S(1)}, bf16[384,512]{1,0:T(8,128)(2,1)S(1)}, u32[]{:S(2)}, u32[]{:S(2)}) collective-permute-start(bf16[384,512]{1,0:T(8,128)(2,1)S(1)} %shard_map.122.refs_12_.refs_3_), channel_id=1, source_target_pairs={{0,8},{8,0},{1,9},{9,1},{2,10},{10,2},{3,11},{11,3},{4,12},{12,4},... | collective-permute-start | bytes 1179656 | tf_op jit(solution)/shard_map/ppermute | solution.py:24
  49.9 5.9 %collective-permute-start.21 = (bf16[384,512]{1,0:T(8,128)(2,1)S(1)}, bf16[384,512]{1,0:T(8,128)(2,1)S(1)}, u32[]{:S(2)}, u32[]{:S(2)}) collective-permute-start(bf16[384,512]{1,0:T(8,128)(2,1)S(1)} %collective-permute-done.18.refs_19_.refs_12_), channel_id=1, source_target_pairs={{0,8},{8,0},{1,9},{9,1},{2,10},{10,2},{3,11},{11,3},{4,12},{12,4},... | collective-permute-start | bytes 1179656 | tf_op jit(solution)/shard_map/ppermute | solution.py:24
  49.9 11.0 %collective-permute-start.22 = (bf16[192,512]{1,0:T(8,128)(2,1)S(1)}, bf16[192,512]{1,0:T(8,128)(2,1)S(1)}, u32[]{:S(2)}, u32[]{:S(2)}) collective-permute-start(bf16[192,512]{1,0:T(8,128)(2,1)S(1)} %slice.31), channel_id=1, source_target_pairs={{0,16},{8,120},{16,32},{24,8},{32,48},{40,24},{48,64},{56,40},{64,... | collective-permute-start | bytes 589832 | tf_op jit(solution)/shard_map/ppermute | solution.py:24
  53.5 9.4 %collective-permute-start.24 = (bf16[192,512]{1,0:T(8,128)(2,1)S(1)}, bf16[192,512]{1,0:T(8,128)(2,1)S(1)}, u32[]{:S(2)}, u32[]{:S(2)}) collective-permute-start(bf16[192,512]{1,0:T(8,128)(2,1)S(1)} %slice.32), channel_id=1, source_target_pairs={{0,16},{8,120},{16,32},{24,8},{32,48},{40,24},{48,64},{56,40},{64,... | collective-permute-start | bytes 589832 | tf_op jit(solution)/shard_map/ppermute | solution.py:24
  60.9 3.1 %collective-permute-start.23 = (bf16[192,512]{1,0:T(8,128)(2,1)S(1)}, bf16[192,512]{1,0:T(8,128)(2,1)S(1)}, u32[]{:S(2)}, u32[]{:S(2)}) collective-permute-start(bf16[192,512]{1,0:T(8,128)(2,1)S(1)} %shard_map.124.refs_4_), channel_id=1, source_target_pairs={{0,8},{8,0},{1,9},{9,1},{2,10},{10,2},{3,11},{11,3},{4,12},{12,4},... | collective-permute-start | bytes 589832 | tf_op jit(solution)/shard_map/ppermute | solution.py:24
  62.9 1.4 %collective-permute-start.25 = (bf16[192,512]{1,0:T(8,128)(2,1)S(1)}, bf16[192,512]{1,0:T(8,128)(2,1)S(1)}, u32[]{:S(2)}, u32[]{:S(2)}) collective-permute-start(bf16[192,512]{1,0:T(8,128)(2,1)S(1)} %shard_map.125.refs_13_), channel_id=1, source_target_pairs={{0,8},{8,0},{1,9},{9,1},{2,10},{10,2},{3,11},{11,3},{4,12},{12,4},... | collective-permute-start | bytes 589832 | tf_op jit(solution)/shard_map/ppermute | solution.py:24
  100.7 6.4 %copy-start = (bf16[2048,512]{1,0:T(8,128)(2,1)S(1)}, bf16[2048,512]{1,0:T(8,128)(2,1)}, u32[]{:S(2)}) copy-start(bf16[2048,512]{1,0:T(8,128)(2,1)} %weight.1) | copy-start | bytes 6291460
  100.7 6.4 %copy-start.1 = (bf16[2048,512]{1,0:T(8,128)(2,1)S(1)}, bf16[2048,512]{1,0:T(8,128)(2,1)}, u32[]{:S(2)}) copy-start(bf16[2048,512]{1,0:T(8,128)(2,1)} %wk.1) | copy-start | bytes 6291460
  101.6 9.4 %copy-start.6 = (s32[2]{0:T(128)S(1)}, s32[2]{0:T(128)}, u32[]{:S(2)}) copy-start(s32[2]{0:T(128)} %lengths.1) | copy-start | bytes 28
  101.6 8.4 %collective-permute-start.28 = (bf16[32,2048]{1,0:T(8,128)(2,1)S(1)}, bf16[32,2048]{1,0:T(8,128)(2,1)S(1)}, u32[]{:S(2)}, u32[]{:S(2)}) collective-permute-start(bf16[32,2048]{1,0:T(8,128)(2,1)S(1)} %shard_map.127.m0), channel_id=1, source_target_pairs={{0,3},{1,0},{2,1},{3,2},{4,7},{5,4},{6,5},{7,6},{8,11},{9,8},{10,9... | collective-permute-start | bytes 393224 | tf_op jit(solution)/shard_map/ppermute | solution.py:24
  102.6 8.4 %collective-permute-start.27 = (bf16[32,2048]{1,0:T(8,128)(2,1)S(1)}, bf16[32,2048]{1,0:T(8,128)(2,1)S(1)}, u32[]{:S(2)}, u32[]{:S(2)}) collective-permute-start(bf16[32,2048]{1,0:T(8,128)(2,1)S(1)} %shard_map.127.m0), channel_id=1, source_target_pairs={{0,2},{1,3},{2,0},{3,1},{4,6},{5,7},{6,4},{7,5},{8,10},{9,11},{10,... | collective-permute-start | bytes 393224 | tf_op jit(solution)/shard_map/ppermute | solution.py:24
  105.9 5.1 %collective-permute-start.26 = (bf16[32,2048]{1,0:T(8,128)(2,1)S(1)}, bf16[32,2048]{1,0:T(8,128)(2,1)S(1)}, u32[]{:S(2)}, u32[]{:S(2)}) collective-permute-start(bf16[32,2048]{1,0:T(8,128)(2,1)S(1)} %shard_map.127.m0), channel_id=1, source_target_pairs={{0,1},{1,2},{2,3},{3,0},{4,5},{5,6},{6,7},{7,4},{8,9},{9,10},{10,1... | collective-permute-start | bytes 393224 | tf_op jit(solution)/shard_map/ppermute | solution.py:24
  111.0 12.6 %copy-start.8 = (bf16[128,512]{1,0:T(8,128)(2,1)S(1)}, bf16[128,512]{1,0:T(8,128)(2,1)}, u32[]{:S(2)}) copy-start(bf16[128,512]{1,0:T(8,128)(2,1)} %copy-done.7) | copy-start | bytes 393220
  113.0 6.7 %collective-permute-start.29 = (bf16[128,512]{1,0:T(8,128)(2,1)S(1)}, bf16[128,512]{1,0:T(8,128)(2,1)S(1)}, u32[]{:S(2)}, u32[]{:S(2)}) collective-permute-start(bf16[128,512]{1,0:T(8,128)(2,1)S(1)} %get-tuple-element.26), channel_id=1, source_target_pairs={{0,1},{1,2},{2,3},{3,0},{4,5},{5,6},{6,7},{7,4},{8,9},{9,10},{10,1... | collective-permute-start | bytes 393224 | tf_op jit(solution)/shard_map/ppermute | solution.py:24
  115.8 6.6 %collective-permute-start.30 = (bf16[128,512]{1,0:T(8,128)(2,1)S(1)}, bf16[128,512]{1,0:T(8,128)(2,1)S(1)}, u32[]{:S(2)}, u32[]{:S(2)}) collective-permute-start(bf16[128,512]{1,0:T(8,128)(2,1)S(1)} %get-tuple-element.27), channel_id=1, source_target_pairs={{0,2},{1,3},{2,0},{3,1},{4,6},{5,7},{6,4},{7,5},{8,10},{9,11},{10,... | collective-permute-start | bytes 393224 | tf_op jit(solution)/shard_map/ppermute | solution.py:24
  116.4 7.3 %collective-permute-start.31 = (bf16[128,512]{1,0:T(8,128)(2,1)S(1)}, bf16[128,512]{1,0:T(8,128)(2,1)S(1)}, u32[]{:S(2)}, u32[]{:S(2)}) collective-permute-start(bf16[128,512]{1,0:T(8,128)(2,1)S(1)} %get-tuple-element.28), channel_id=1, source_target_pairs={{0,3},{1,0},{2,1},{3,2},{4,7},{5,4},{6,5},{7,6},{8,11},{9,8},{10,9... | collective-permute-start | bytes 393224 | tf_op jit(solution)/shard_map/ppermute | solution.py:24
  123.8 5.1 %collective-permute-start.32 = (bf16[128,512]{1,0:T(8,128)(2,1)S(1)}, bf16[128,512]{1,0:T(8,128)(2,1)S(1)}, u32[]{:S(2)}, u32[]{:S(2)}) collective-permute-start(bf16[128,512]{1,0:T(8,128)(2,1)S(1)} %get-tuple-element.29), channel_id=1, source_target_pairs={{0,4},{4,0},{1,5},{5,1},{2,6},{6,2},{3,7},{7,3},{8,12},{12,8},{9,1... | collective-permute-start | bytes 393224 | tf_op jit(solution)/shard_map/ppermute | solution.py:24
